TPU v7x, 512 devices: a whole 4x4x16 slice. The times are simulated.
512 devices in a mesh: blk: 32 (over z_lo, x), dp: 16 (over y, z_hi, core).
Axes of the slice: x: 4, y: 4, z: 16 (z_hi: 2, z_lo: 8; z = z_hi * 8 + z_lo), core: 2. Of those that a mesh axis runs over, the one named last changes fastest.
Arguments:
- inputs: bfloat16 [512, 128, 4096], P(('blk', 'dp')), may hold values from -6 to 6
- queries: bfloat16 [512, 128, 4096], P(('blk', 'dp'))
- keys: bfloat16 [512, 128, 512], P(('blk', 'dp'))
- values: bfloat16 [512, 128, 512], P(('blk', 'dp')), may hold values from -6 to 6
- out_grad: bfloat16 [512, 128, 4096], P(('blk', 'dp')), may hold values from -6 to 6
- lengths: int32 [512], P(('blk', 'dp')), may hold values from 1 to 128, as said below
- value_weight: bfloat16 [4096, 512], P('blk'), may hold values from -0.25 to 0.25
Outputs:
- input_grad: bfloat16 [512, 128, 4096], P(('blk', 'dp'))
- key_grad: bfloat16 [512, 128, 512], P(('blk', 'dp'))
- weight_grad: float32 [4096, 512], P('blk')
Inputs may be any that keep to these rules, and one draw needn't show every extreme that they name: `lengths`: some microbatch has all 128 slots live.
All inputs are finite; a program needn't handle non-finite values.
Results may differ from a plain program's by a relative error of at most 0.01.
Values may be sent and summed in bfloat16 or wider, within the bound.
No kernel may reach another device: no remote copies, remote signals or barrier semaphores. Data moves between devices by JAX's collectives and lax.ppermute only.
A program may use at most 64 MiB of HBM per device.

v0:
```python
import jax
import jax.numpy as jnp
from jax import lax
from jax.sharding import PartitionSpec as P

HEAD_DIM = 128


def shifted(array, axis, by):
    count = lax.axis_size(axis)
    return lax.ppermute(array, axis, [(i, (i + by) % count) for i in range(count)])


def attend_back(query, key_rows, value_rows, grad_rows, length):
    tok_count = query.shape[0]
    kv_dim = key_rows.shape[1]
    heads_kv = kv_dim // HEAD_DIM
    group_size = query.shape[1] // kv_dim
    scaling = HEAD_DIM ** (-0.5)
    query_heads = query.reshape(tok_count, heads_kv, group_size, HEAD_DIM)
    key_heads = key_rows.reshape(tok_count, heads_kv, HEAD_DIM)
    value_heads = value_rows.reshape(tok_count, heads_kv, HEAD_DIM)
    grad_heads = grad_rows.reshape(tok_count, heads_kv, group_size, HEAD_DIM)
    scores = (
        jnp.einsum("tkgd,skd->kgts", query_heads, key_heads, preferred_element_type=jnp.float32)
        * scaling
    )
    position = jnp.arange(tok_count)
    allowed = position[None, :] <= position[:, None]
    scores = jnp.where(allowed, scores, jnp.float32(-1e30))
    highest = jnp.max(scores, axis=-1, keepdims=True)
    expd = jnp.exp(scores - highest)
    attn_probs = expd / jnp.sum(expd, axis=-1, keepdims=True)
    is_valid = (position < length).astype(jnp.float32)
    attn_probs = attn_probs * is_valid[None, None, :, None]
    probs_low = attn_probs.astype(jnp.bfloat16)
    attended = jnp.einsum(
        "kgts,skd->tkgd",
        attn_probs,
        value_heads.astype(jnp.float32),
        precision=lax.Precision.HIGHEST,
    )
    row_delta = jnp.sum(grad_heads.astype(jnp.float32) * attended, axis=-1)
    dprob = jnp.einsum(
        "tkgd,skd->kgts", grad_heads, value_heads, preferred_element_type=jnp.float32
    )
    dscore = attn_probs * (dprob - jnp.transpose(row_delta, (1, 2, 0))[..., None])
    dscore_low = dscore.astype(jnp.bfloat16)
    value_grad = jnp.einsum(
        "kgts,tkgd->skd", probs_low, grad_heads, preferred_element_type=jnp.float32
    )
    key_grad = (
        jnp.einsum("kgts,tkgd->skd", dscore_low, query_heads, preferred_element_type=jnp.float32)
        * scaling
    )
    value_grad = value_grad.reshape(tok_count, kv_dim).astype(jnp.bfloat16)
    key_grad = key_grad.reshape(tok_count, kv_dim).astype(jnp.bfloat16)
    return (value_grad, key_grad)


def per_device(inputs, queries, keys, values, out_grad, lengths, value_weight):
    tokens = inputs[0]
    value_grad, key_grad = attend_back(queries[0], keys[0], values[0], out_grad[0], lengths[0])
    input_grad = lax.dot_general(
        value_grad,
        lax.all_gather(value_weight, "blk", axis=0, tiled=True),
        (((1,), (1,)), ((), ())),
        preferred_element_type=jnp.float32,
    ).astype(jnp.bfloat16)
    blk_count = lax.axis_size("blk")
    shard_rows = value_weight.shape[0]
    kv_dim = value_weight.shape[1]

    def term_rows(first_row, row_count):
        columns = lax.dynamic_slice_in_dim(tokens, first_row, row_count, 1)
        return lax.dot_general(
            columns, value_grad, (((0,), (0,)), ((), ())), preferred_element_type=jnp.float32
        )

    own_index = lax.axis_index("blk")

    def grad_term(hop_index):
        block_index = (own_index + hop_index + 1) % blk_count
        rounded = lax.optimization_barrier(
            term_rows(block_index * shard_rows, shard_rows).astype(jnp.bfloat16)
        )
        return rounded.astype(jnp.float32)

    def advance(hop_index, running):
        return shifted(running + grad_term(hop_index), "blk", -1)

    running = lax.fori_loop(0, blk_count - 1, advance, jnp.zeros((shard_rows, kv_dim), jnp.float32))
    running = running + grad_term(blk_count - 1)
    replica_total = lax.psum(running, "dp")
    weight_grad = replica_total / (blk_count * lax.axis_size("dp"))
    return (input_grad[None], key_grad[None], weight_grad)


def solution(mesh):
    placed = (
        P(("blk", "dp"), None, None),
        P(("blk", "dp"), None, None),
        P(("blk", "dp"), None, None),
        P(("blk", "dp"), None, None),
        P(("blk", "dp"), None, None),
        P(("blk", "dp")),
        P("blk", None),
    )
    return jax.shard_map(
        per_device,
        mesh=mesh,
        in_specs=placed,
        out_specs=(P(("blk", "dp"), None, None), P(("blk", "dp"), None, None), P("blk", None)),
        check_vma=False,
    )
```

profile of v0, /device:TPU:1, one launch (start us, length us, event | category | flops | bytes accessed | tf_op | source)
XLA Modules:
  0.0 888.6 jit_solution(12854610650266653895)
XLA Ops:
  18.1 565.7 %while.15 = (s32[]{:T(128)}, f32[128,512]{1,0:T(8,128)S(1)}, s32[]{:T(128)}, bf16[128,4096]{1,0:T(8,128)(2,1)}, bf16[128,512]{1,0:T(8,128)(2,1)S(1)}, /*index=5*...) while((s32[]{:T(128)}, f32[128,512]{1,0:T(8,128)S(1)}, s32[]{:T(128)}, ...), condition=%wide.region_4.5_spmd, body=%wide.region_3.4_spmd.sunk | while | flops 16973844 | bytes 1999180 | solution.py:92
  19.8 15.9 %collective-permute-start = (f32[128,512]{1,0:T(8,128)}, f32[128,512]{1,0:T(8,128)S(1)}, u32[]{:S(2)}, u32[]{:S(2)}) collective-permute-start(f32[128,512]{1,0:T(8,128)} %convert_add_fusion.3), channel_id=1, source_target_pairs={{0,496},{16,0},{32,16},{48,32},{64,48},{80,64},{96,80},{112,96},{1... | collective-permute-start | bytes 786440 | tf_op jit(solution)/shard_map/while/body/eval_jaxpr/ppermute | solution.py:11
  42.7 12.7 %collective-permute-start = (f32[128,512]{1,0:T(8,128)}, f32[128,512]{1,0:T(8,128)S(1)}, u32[]{:S(2)}, u32[]{:S(2)}) collective-permute-start(f32[128,512]{1,0:T(8,128)} %convert_add_fusion.3), channel_id=1, source_target_pairs={{0,496},{16,0},{32,16},{48,32},{64,48},{80,64},{96,80},{112,96},{1... | collective-permute-start | bytes 786440 | tf_op jit(solution)/shard_map/while/body/eval_jaxpr/ppermute | solution.py:11
  61.4 12.7 %collective-permute-start = (f32[128,512]{1,0:T(8,128)}, f32[128,512]{1,0:T(8,128)S(1)}, u32[]{:S(2)}, u32[]{:S(2)}) collective-permute-start(f32[128,512]{1,0:T(8,128)} %convert_add_fusion.3), channel_id=1, source_target_pairs={{0,496},{16,0},{32,16},{48,32},{64,48},{80,64},{96,80},{112,96},{1... | collective-permute-start | bytes 786440 | tf_op jit(solution)/shard_map/while/body/eval_jaxpr/ppermute | solution.py:11
  79.5 12.4 %collective-permute-start = (f32[128,512]{1,0:T(8,128)}, f32[128,512]{1,0:T(8,128)S(1)}, u32[]{:S(2)}, u32[]{:S(2)}) collective-permute-start(f32[128,512]{1,0:T(8,128)} %convert_add_fusion.3), channel_id=1, source_target_pairs={{0,496},{16,0},{32,16},{48,32},{64,48},{80,64},{96,80},{112,96},{1... | collective-permute-start | bytes 786440 | tf_op jit(solution)/shard_map/while/body/eval_jaxpr/ppermute | solution.py:11
  97.2 12.4 %collective-permute-start = (f32[128,512]{1,0:T(8,128)}, f32[128,512]{1,0:T(8,128)S(1)}, u32[]{:S(2)}, u32[]{:S(2)}) collective-permute-start(f32[128,512]{1,0:T(8,128)} %convert_add_fusion.3), channel_id=1, source_target_pairs={{0,496},{16,0},{32,16},{48,32},{64,48},{80,64},{96,80},{112,96},{1... | collective-permute-start | bytes 786440 | tf_op jit(solution)/shard_map/while/body/eval_jaxpr/ppermute | solution.py:11
  115.0 12.4 %collective-permute-start = (f32[128,512]{1,0:T(8,128)}, f32[128,512]{1,0:T(8,128)S(1)}, u32[]{:S(2)}, u32[]{:S(2)}) collective-permute-start(f32[128,512]{1,0:T(8,128)} %convert_add_fusion.3), channel_id=1, source_target_pairs={{0,496},{16,0},{32,16},{48,32},{64,48},{80,64},{96,80},{112,96},{1... | collective-permute-start | bytes 786440 | tf_op jit(solution)/shard_map/while/body/eval_jaxpr/ppermute | solution.py:11
  132.7 12.4 %collective-permute-start = (f32[128,512]{1,0:T(8,128)}, f32[128,512]{1,0:T(8,128)S(1)}, u32[]{:S(2)}, u32[]{:S(2)}) collective-permute-start(f32[128,512]{1,0:T(8,128)} %convert_add_fusion.3), channel_id=1, source_target_pairs={{0,496},{16,0},{32,16},{48,32},{64,48},{80,64},{96,80},{112,96},{1... | collective-permute-start | bytes 786440 | tf_op jit(solution)/shard_map/while/body/eval_jaxpr/ppermute | solution.py:11
  150.4 12.4 %collective-permute-start = (f32[128,512]{1,0:T(8,128)}, f32[128,512]{1,0:T(8,128)S(1)}, u32[]{:S(2)}, u32[]{:S(2)}) collective-permute-start(f32[128,512]{1,0:T(8,128)} %convert_add_fusion.3), channel_id=1, source_target_pairs={{0,496},{16,0},{32,16},{48,32},{64,48},{80,64},{96,80},{112,96},{1... | collective-permute-start | bytes 786440 | tf_op jit(solution)/shard_map/while/body/eval_jaxpr/ppermute | solution.py:11
  168.2 12.4 %collective-permute-start = (f32[128,512]{1,0:T(8,128)}, f32[128,512]{1,0:T(8,128)S(1)}, u32[]{:S(2)}, u32[]{:S(2)}) collective-permute-start(f32[128,512]{1,0:T(8,128)} %convert_add_fusion.3), channel_id=1, source_target_pairs={{0,496},{16,0},{32,16},{48,32},{64,48},{80,64},{96,80},{112,96},{1... | collective-permute-start | bytes 786440 | tf_op jit(solution)/shard_map/while/body/eval_jaxpr/ppermute | solution.py:11
  185.9 12.4 %collective-permute-start = (f32[128,512]{1,0:T(8,128)}, f32[128,512]{1,0:T(8,128)S(1)}, u32[]{:S(2)}, u32[]{:S(2)}) collective-permute-start(f32[128,512]{1,0:T(8,128)} %convert_add_fusion.3), channel_id=1, source_target_pairs={{0,496},{16,0},{32,16},{48,32},{64,48},{80,64},{96,80},{112,96},{1... | collective-permute-start | bytes 786440 | tf_op jit(solution)/shard_map/while/body/eval_jaxpr/ppermute | solution.py:11
  203.6 12.4 %collective-permute-start = (f32[128,512]{1,0:T(8,128)}, f32[128,512]{1,0:T(8,128)S(1)}, u32[]{:S(2)}, u32[]{:S(2)}) collective-permute-start(f32[128,512]{1,0:T(8,128)} %convert_add_fusion.3), channel_id=1, source_target_pairs={{0,496},{16,0},{32,16},{48,32},{64,48},{80,64},{96,80},{112,96},{1... | collective-permute-start | bytes 786440 | tf_op jit(solution)/shard_map/while/body/eval_jaxpr/ppermute | solution.py:11
  221.4 12.4 %collective-permute-start = (f32[128,512]{1,0:T(8,128)}, f32[128,512]{1,0:T(8,128)S(1)}, u32[]{:S(2)}, u32[]{:S(2)}) collective-permute-start(f32[128,512]{1,0:T(8,128)} %convert_add_fusion.3), channel_id=1, source_target_pairs={{0,496},{16,0},{32,16},{48,32},{64,48},{80,64},{96,80},{112,96},{1... | collective-permute-start | bytes 786440 | tf_op jit(solution)/shard_map/while/body/eval_jaxpr/ppermute | solution.py:11
  239.1 12.4 %collective-permute-start = (f32[128,512]{1,0:T(8,128)}, f32[128,512]{1,0:T(8,128)S(1)}, u32[]{:S(2)}, u32[]{:S(2)}) collective-permute-start(f32[128,512]{1,0:T(8,128)} %convert_add_fusion.3), channel_id=1, source_target_pairs={{0,496},{16,0},{32,16},{48,32},{64,48},{80,64},{96,80},{112,96},{1... | collective-permute-start | bytes 786440 | tf_op jit(solution)/shard_map/while/body/eval_jaxpr/ppermute | solution.py:11
  256.9 12.4 %collective-permute-start = (f32[128,512]{1,0:T(8,128)}, f32[128,512]{1,0:T(8,128)S(1)}, u32[]{:S(2)}, u32[]{:S(2)}) collective-permute-start(f32[128,512]{1,0:T(8,128)} %convert_add_fusion.3), channel_id=1, source_target_pairs={{0,496},{16,0},{32,16},{48,32},{64,48},{80,64},{96,80},{112,96},{1... | collective-permute-start | bytes 786440 | tf_op jit(solution)/shard_map/while/body/eval_jaxpr/ppermute | solution.py:11
  274.6 12.4 %collective-permute-start = (f32[128,512]{1,0:T(8,128)}, f32[128,512]{1,0:T(8,128)S(1)}, u32[]{:S(2)}, u32[]{:S(2)}) collective-permute-start(f32[128,512]{1,0:T(8,128)} %convert_add_fusion.3), channel_id=1, source_target_pairs={{0,496},{16,0},{32,16},{48,32},{64,48},{80,64},{96,80},{112,96},{1... | collective-permute-start | bytes 786440 | tf_op jit(solution)/shard_map/while/body/eval_jaxpr/ppermute | solution.py:11
  293.0 12.4 %collective-permute-start = (f32[128,512]{1,0:T(8,128)}, f32[128,512]{1,0:T(8,128)S(1)}, u32[]{:S(2)}, u32[]{:S(2)}) collective-permute-start(f32[128,512]{1,0:T(8,128)} %convert_add_fusion.3), channel_id=1, source_target_pairs={{0,496},{16,0},{32,16},{48,32},{64,48},{80,64},{96,80},{112,96},{1... | collective-permute-start | bytes 786440 | tf_op jit(solution)/shard_map/while/body/eval_jaxpr/ppermute | solution.py:11
  312.5 12.4 %collective-permute-start = (f32[128,512]{1,0:T(8,128)}, f32[128,512]{1,0:T(8,128)S(1)}, u32[]{:S(2)}, u32[]{:S(2)}) collective-permute-start(f32[128,512]{1,0:T(8,128)} %convert_add_fusion.3), channel_id=1, source_target_pairs={{0,496},{16,0},{32,16},{48,32},{64,48},{80,64},{96,80},{112,96},{1... | collective-permute-start | bytes 786440 | tf_op jit(solution)/shard_map/while/body/eval_jaxpr/ppermute | solution.py:11
  333.0 12.7 %collective-permute-start = (f32[128,512]{1,0:T(8,128)}, f32[128,512]{1,0:T(8,128)S(1)}, u32[]{:S(2)}, u32[]{:S(2)}) collective-permute-start(f32[128,512]{1,0:T(8,128)} %convert_add_fusion.3), channel_id=1, source_target_pairs={{0,496},{16,0},{32,16},{48,32},{64,48},{80,64},{96,80},{112,96},{1... | collective-permute-start | bytes 786440 | tf_op jit(solution)/shard_map/while/body/eval_jaxpr/ppermute | solution.py:11
  352.9 12.7 %collective-permute-start = (f32[128,512]{1,0:T(8,128)}, f32[128,512]{1,0:T(8,128)S(1)}, u32[]{:S(2)}, u32[]{:S(2)}) collective-permute-start(f32[128,512]{1,0:T(8,128)} %convert_add_fusion.3), channel_id=1, source_target_pairs={{0,496},{16,0},{32,16},{48,32},{64,48},{80,64},{96,80},{112,96},{1... | collective-permute-start | bytes 786440 | tf_op jit(solution)/shard_map/while/body/eval_jaxpr/ppermute | solution.py:11
  371.9 12.7 %collective-permute-start = (f32[128,512]{1,0:T(8,128)}, f32[128,512]{1,0:T(8,128)S(1)}, u32[]{:S(2)}, u32[]{:S(2)}) collective-permute-start(f32[128,512]{1,0:T(8,128)} %convert_add_fusion.3), channel_id=1, source_target_pairs={{0,496},{16,0},{32,16},{48,32},{64,48},{80,64},{96,80},{112,96},{1... | collective-permute-start | bytes 786440 | tf_op jit(solution)/shard_map/while/body/eval_jaxpr/ppermute | solution.py:11
  389.9 12.8 %collective-permute-start = (f32[128,512]{1,0:T(8,128)}, f32[128,512]{1,0:T(8,128)S(1)}, u32[]{:S(2)}, u32[]{:S(2)}) collective-permute-start(f32[128,512]{1,0:T(8,128)} %convert_add_fusion.3), channel_id=1, source_target_pairs={{0,496},{16,0},{32,16},{48,32},{64,48},{80,64},{96,80},{112,96},{1... | collective-permute-start | bytes 786440 | tf_op jit(solution)/shard_map/while/body/eval_jaxpr/ppermute | solution.py:11
  408.0 12.4 %collective-permute-start = (f32[128,512]{1,0:T(8,128)}, f32[128,512]{1,0:T(8,128)S(1)}, u32[]{:S(2)}, u32[]{:S(2)}) collective-permute-start(f32[128,512]{1,0:T(8,128)} %convert_add_fusion.3), channel_id=1, source_target_pairs={{0,496},{16,0},{32,16},{48,32},{64,48},{80,64},{96,80},{112,96},{1... | collective-permute-start | bytes 786440 | tf_op jit(solution)/shard_map/while/body/eval_jaxpr/ppermute | solution.py:11
  425.8 12.4 %collective-permute-start = (f32[128,512]{1,0:T(8,128)}, f32[128,512]{1,0:T(8,128)S(1)}, u32[]{:S(2)}, u32[]{:S(2)}) collective-permute-start(f32[128,512]{1,0:T(8,128)} %convert_add_fusion.3), channel_id=1, source_target_pairs={{0,496},{16,0},{32,16},{48,32},{64,48},{80,64},{96,80},{112,96},{1... | collective-permute-start | bytes 786440 | tf_op jit(solution)/shard_map/while/body/eval_jaxpr/ppermute | solution.py:11
  443.5 12.4 %collective-permute-start = (f32[128,512]{1,0:T(8,128)}, f32[128,512]{1,0:T(8,128)S(1)}, u32[]{:S(2)}, u32[]{:S(2)}) collective-permute-start(f32[128,512]{1,0:T(8,128)} %convert_add_fusion.3), channel_id=1, source_target_pairs={{0,496},{16,0},{32,16},{48,32},{64,48},{80,64},{96,80},{112,96},{1... | collective-permute-start | bytes 786440 | tf_op jit(solution)/shard_map/while/body/eval_jaxpr/ppermute | solution.py:11
  461.3 12.4 %collective-permute-start = (f32[128,512]{1,0:T(8,128)}, f32[128,512]{1,0:T(8,128)S(1)}, u32[]{:S(2)}, u32[]{:S(2)}) collective-permute-start(f32[128,512]{1,0:T(8,128)} %convert_add_fusion.3), channel_id=1, source_target_pairs={{0,496},{16,0},{32,16},{48,32},{64,48},{80,64},{96,80},{112,96},{1... | collective-permute-start | bytes 786440 | tf_op jit(solution)/shard_map/while/body/eval_jaxpr/ppermute | solution.py:11
  479.0 12.4 %collective-permute-start = (f32[128,512]{1,0:T(8,128)}, f32[128,512]{1,0:T(8,128)S(1)}, u32[]{:S(2)}, u32[]{:S(2)}) collective-permute-start(f32[128,512]{1,0:T(8,128)} %convert_add_fusion.3), channel_id=1, source_target_pairs={{0,496},{16,0},{32,16},{48,32},{64,48},{80,64},{96,80},{112,96},{1... | collective-permute-start | bytes 786440 | tf_op jit(solution)/shard_map/while/body/eval_jaxpr/ppermute | solution.py:11
  496.7 12.4 %collective-permute-start = (f32[128,512]{1,0:T(8,128)}, f32[128,512]{1,0:T(8,128)S(1)}, u32[]{:S(2)}, u32[]{:S(2)}) collective-permute-start(f32[128,512]{1,0:T(8,128)} %convert_add_fusion.3), channel_id=1, source_target_pairs={{0,496},{16,0},{32,16},{48,32},{64,48},{80,64},{96,80},{112,96},{1... | collective-permute-start | bytes 786440 | tf_op jit(solution)/shard_map/while/body/eval_jaxpr/ppermute | solution.py:11
  514.5 12.4 %collective-permute-start = (f32[128,512]{1,0:T(8,128)}, f32[128,512]{1,0:T(8,128)S(1)}, u32[]{:S(2)}, u32[]{:S(2)}) collective-permute-start(f32[128,512]{1,0:T(8,128)} %convert_add_fusion.3), channel_id=1, source_target_pairs={{0,496},{16,0},{32,16},{48,32},{64,48},{80,64},{96,80},{112,96},{1... | collective-permute-start | bytes 786440 | tf_op jit(solution)/shard_map/while/body/eval_jaxpr/ppermute | solution.py:11
  532.2 12.4 %collective-permute-start = (f32[128,512]{1,0:T(8,128)}, f32[128,512]{1,0:T(8,128)S(1)}, u32[]{:S(2)}, u32[]{:S(2)}) collective-permute-start(f32[128,512]{1,0:T(8,128)} %convert_add_fusion.3), channel_id=1, source_target_pairs={{0,496},{16,0},{32,16},{48,32},{64,48},{80,64},{96,80},{112,96},{1... | collective-permute-start | bytes 786440 | tf_op jit(solution)/shard_map/while/body/eval_jaxpr/ppermute | solution.py:11
  567.7 12.4 %collective-permute-start = (f32[128,512]{1,0:T(8,128)}, f32[128,512]{1,0:T(8,128)S(1)}, u32[]{:S(2)}, u32[]{:S(2)}) collective-permute-start(f32[128,512]{1,0:T(8,128)} %convert_add_fusion.3), channel_id=1, source_target_pairs={{0,496},{16,0},{32,16},{48,32},{64,48},{80,64},{96,80},{112,96},{1... | collective-permute-start | bytes 786440 | tf_op jit(solution)/shard_map/while/body/eval_jaxpr/ppermute | solution.py:11
  596.0 278.8 %all-reduce.2.cloned.1.call-done = f32[128,512]{1,0:T(8,128)} async-done(((f32[128,512]{1,0:T(8,128)}), f32[128,512]{1,0:T(8,128)}) %all-reduce.2.cloned.1.call-update) | async-done | bytes 262160 | tf_op jit(solution)/shard_map/psum | solution.py:94
  (134 shorter events, 215.1 us)
Async XLA Ops:
  8.0 866.8 %all-reduce.2.cloned.1.call-start = ((), (), s32[]{:S(2)}) async-start(), calls=%async_computation.1 | async-start | bytes 524288 | tf_op jit(solution)/shard_map/psum | solution.py:94
  19.8 21.2 %collective-permute-start = (f32[128,512]{1,0:T(8,128)}, f32[128,512]{1,0:T(8,128)S(1)}, u32[]{:S(2)}, u32[]{:S(2)}) collective-permute-start(f32[128,512]{1,0:T(8,128)} %convert_add_fusion.3), channel_id=1, source_target_pairs={{0,496},{16,0},{32,16},{48,32},{64,48},{80,64},{96,80},{112,96},{1... | collective-permute-start | bytes 786440 | tf_op jit(solution)/shard_map/while/body/eval_jaxpr/ppermute | solution.py:11
  42.7 17.1 %collective-permute-start = (f32[128,512]{1,0:T(8,128)}, f32[128,512]{1,0:T(8,128)S(1)}, u32[]{:S(2)}, u32[]{:S(2)}) collective-permute-start(f32[128,512]{1,0:T(8,128)} %convert_add_fusion.3), channel_id=1, source_target_pairs={{0,496},{16,0},{32,16},{48,32},{64,48},{80,64},{96,80},{112,96},{1... | collective-permute-start | bytes 786440 | tf_op jit(solution)/shard_map/while/body/eval_jaxpr/ppermute | solution.py:11
  61.4 16.3 %collective-permute-start = (f32[128,512]{1,0:T(8,128)}, f32[128,512]{1,0:T(8,128)S(1)}, u32[]{:S(2)}, u32[]{:S(2)}) collective-permute-start(f32[128,512]{1,0:T(8,128)} %convert_add_fusion.3), channel_id=1, source_target_pairs={{0,496},{16,0},{32,16},{48,32},{64,48},{80,64},{96,80},{112,96},{1... | collective-permute-start | bytes 786440 | tf_op jit(solution)/shard_map/while/body/eval_jaxpr/ppermute | solution.py:11
  79.5 16.0 %collective-permute-start = (f32[128,512]{1,0:T(8,128)}, f32[128,512]{1,0:T(8,128)S(1)}, u32[]{:S(2)}, u32[]{:S(2)}) collective-permute-start(f32[128,512]{1,0:T(8,128)} %convert_add_fusion.3), channel_id=1, source_target_pairs={{0,496},{16,0},{32,16},{48,32},{64,48},{80,64},{96,80},{112,96},{1... | collective-permute-start | bytes 786440 | tf_op jit(solution)/shard_map/while/body/eval_jaxpr/ppermute | solution.py:11
  97.2 16.0 %collective-permute-start = (f32[128,512]{1,0:T(8,128)}, f32[128,512]{1,0:T(8,128)S(1)}, u32[]{:S(2)}, u32[]{:S(2)}) collective-permute-start(f32[128,512]{1,0:T(8,128)} %convert_add_fusion.3), channel_id=1, source_target_pairs={{0,496},{16,0},{32,16},{48,32},{64,48},{80,64},{96,80},{112,96},{1... | collective-permute-start | bytes 786440 | tf_op jit(solution)/shard_map/while/body/eval_jaxpr/ppermute | solution.py:11
  115.0 16.0 %collective-permute-start = (f32[128,512]{1,0:T(8,128)}, f32[128,512]{1,0:T(8,128)S(1)}, u32[]{:S(2)}, u32[]{:S(2)}) collective-permute-start(f32[128,512]{1,0:T(8,128)} %convert_add_fusion.3), channel_id=1, source_target_pairs={{0,496},{16,0},{32,16},{48,32},{64,48},{80,64},{96,80},{112,96},{1... | collective-permute-start | bytes 786440 | tf_op jit(solution)/shard_map/while/body/eval_jaxpr/ppermute | solution.py:11
  132.7 16.0 %collective-permute-start = (f32[128,512]{1,0:T(8,128)}, f32[128,512]{1,0:T(8,128)S(1)}, u32[]{:S(2)}, u32[]{:S(2)}) collective-permute-start(f32[128,512]{1,0:T(8,128)} %convert_add_fusion.3), channel_id=1, source_target_pairs={{0,496},{16,0},{32,16},{48,32},{64,48},{80,64},{96,80},{112,96},{1... | collective-permute-start | bytes 786440 | tf_op jit(solution)/shard_map/while/body/eval_jaxpr/ppermute | solution.py:11
  150.4 16.0 %collective-permute-start = (f32[128,512]{1,0:T(8,128)}, f32[128,512]{1,0:T(8,128)S(1)}, u32[]{:S(2)}, u32[]{:S(2)}) collective-permute-start(f32[128,512]{1,0:T(8,128)} %convert_add_fusion.3), channel_id=1, source_target_pairs={{0,496},{16,0},{32,16},{48,32},{64,48},{80,64},{96,80},{112,96},{1... | collective-permute-start | bytes 786440 | tf_op jit(solution)/shard_map/while/body/eval_jaxpr/ppermute | solution.py:11
  168.2 16.0 %collective-permute-start = (f32[128,512]{1,0:T(8,128)}, f32[128,512]{1,0:T(8,128)S(1)}, u32[]{:S(2)}, u32[]{:S(2)}) collective-permute-start(f32[128,512]{1,0:T(8,128)} %convert_add_fusion.3), channel_id=1, source_target_pairs={{0,496},{16,0},{32,16},{48,32},{64,48},{80,64},{96,80},{112,96},{1... | collective-permute-start | bytes 786440 | tf_op jit(solution)/shard_map/while/body/eval_jaxpr/ppermute | solution.py:11
  185.9 16.0 %collective-permute-start = (f32[128,512]{1,0:T(8,128)}, f32[128,512]{1,0:T(8,128)S(1)}, u32[]{:S(2)}, u32[]{:S(2)}) collective-permute-start(f32[128,512]{1,0:T(8,128)} %convert_add_fusion.3), channel_id=1, source_target_pairs={{0,496},{16,0},{32,16},{48,32},{64,48},{80,64},{96,80},{112,96},{1... | collective-permute-start | bytes 786440 | tf_op jit(solution)/shard_map/while/body/eval_jaxpr/ppermute | solution.py:11
  203.6 16.0 %collective-permute-start = (f32[128,512]{1,0:T(8,128)}, f32[128,512]{1,0:T(8,128)S(1)}, u32[]{:S(2)}, u32[]{:S(2)}) collective-permute-start(f32[128,512]{1,0:T(8,128)} %convert_add_fusion.3), channel_id=1, source_target_pairs={{0,496},{16,0},{32,16},{48,32},{64,48},{80,64},{96,80},{112,96},{1... | collective-permute-start | bytes 786440 | tf_op jit(solution)/shard_map/while/body/eval_jaxpr/ppermute | solution.py:11
  221.4 16.0 %collective-permute-start = (f32[128,512]{1,0:T(8,128)}, f32[128,512]{1,0:T(8,128)S(1)}, u32[]{:S(2)}, u32[]{:S(2)}) collective-permute-start(f32[128,512]{1,0:T(8,128)} %convert_add_fusion.3), channel_id=1, source_target_pairs={{0,496},{16,0},{32,16},{48,32},{64,48},{80,64},{96,80},{112,96},{1... | collective-permute-start | bytes 786440 | tf_op jit(solution)/shard_map/while/body/eval_jaxpr/ppermute | solution.py:11
  239.1 16.0 %collective-permute-start = (f32[128,512]{1,0:T(8,128)}, f32[128,512]{1,0:T(8,128)S(1)}, u32[]{:S(2)}, u32[]{:S(2)}) collective-permute-start(f32[128,512]{1,0:T(8,128)} %convert_add_fusion.3), channel_id=1, source_target_pairs={{0,496},{16,0},{32,16},{48,32},{64,48},{80,64},{96,80},{112,96},{1... | collective-permute-start | bytes 786440 | tf_op jit(solution)/shard_map/while/body/eval_jaxpr/ppermute | solution.py:11
  256.9 16.0 %collective-permute-start = (f32[128,512]{1,0:T(8,128)}, f32[128,512]{1,0:T(8,128)S(1)}, u32[]{:S(2)}, u32[]{:S(2)}) collective-permute-start(f32[128,512]{1,0:T(8,128)} %convert_add_fusion.3), channel_id=1, source_target_pairs={{0,496},{16,0},{32,16},{48,32},{64,48},{80,64},{96,80},{112,96},{1... | collective-permute-start | bytes 786440 | tf_op jit(solution)/shard_map/while/body/eval_jaxpr/ppermute | solution.py:11
  274.6 16.7 %collective-permute-start = (f32[128,512]{1,0:T(8,128)}, f32[128,512]{1,0:T(8,128)S(1)}, u32[]{:S(2)}, u32[]{:S(2)}) collective-permute-start(f32[128,512]{1,0:T(8,128)} %convert_add_fusion.3), channel_id=1, source_target_pairs={{0,496},{16,0},{32,16},{48,32},{64,48},{80,64},{96,80},{112,96},{1... | collective-permute-start | bytes 786440 | tf_op jit(solution)/shard_map/while/body/eval_jaxpr/ppermute | solution.py:11
  293.0 17.8 %collective-permute-start = (f32[128,512]{1,0:T(8,128)}, f32[128,512]{1,0:T(8,128)S(1)}, u32[]{:S(2)}, u32[]{:S(2)}) collective-permute-start(f32[128,512]{1,0:T(8,128)} %convert_add_fusion.3), channel_id=1, source_target_pairs={{0,496},{16,0},{32,16},{48,32},{64,48},{80,64},{96,80},{112,96},{1... | collective-permute-start | bytes 786440 | tf_op jit(solution)/shard_map/while/body/eval_jaxpr/ppermute | solution.py:11
  312.5 18.8 %collective-permute-start = (f32[128,512]{1,0:T(8,128)}, f32[128,512]{1,0:T(8,128)S(1)}, u32[]{:S(2)}, u32[]{:S(2)}) collective-permute-start(f32[128,512]{1,0:T(8,128)} %convert_add_fusion.3), channel_id=1, source_target_pairs={{0,496},{16,0},{32,16},{48,32},{64,48},{80,64},{96,80},{112,96},{1... | collective-permute-start | bytes 786440 | tf_op jit(solution)/shard_map/while/body/eval_jaxpr/ppermute | solution.py:11
  333.0 18.2 %collective-permute-start = (f32[128,512]{1,0:T(8,128)}, f32[128,512]{1,0:T(8,128)S(1)}, u32[]{:S(2)}, u32[]{:S(2)}) collective-permute-start(f32[128,512]{1,0:T(8,128)} %convert_add_fusion.3), channel_id=1, source_target_pairs={{0,496},{16,0},{32,16},{48,32},{64,48},{80,64},{96,80},{112,96},{1... | collective-permute-start | bytes 786440 | tf_op jit(solution)/shard_map/while/body/eval_jaxpr/ppermute | solution.py:11
  352.9 17.3 %collective-permute-start = (f32[128,512]{1,0:T(8,128)}, f32[128,512]{1,0:T(8,128)S(1)}, u32[]{:S(2)}, u32[]{:S(2)}) collective-permute-start(f32[128,512]{1,0:T(8,128)} %convert_add_fusion.3), channel_id=1, source_target_pairs={{0,496},{16,0},{32,16},{48,32},{64,48},{80,64},{96,80},{112,96},{1... | collective-permute-start | bytes 786440 | tf_op jit(solution)/shard_map/while/body/eval_jaxpr/ppermute | solution.py:11
  371.9 16.3 %collective-permute-start = (f32[128,512]{1,0:T(8,128)}, f32[128,512]{1,0:T(8,128)S(1)}, u32[]{:S(2)}, u32[]{:S(2)}) collective-permute-start(f32[128,512]{1,0:T(8,128)} %convert_add_fusion.3), channel_id=1, source_target_pairs={{0,496},{16,0},{32,16},{48,32},{64,48},{80,64},{96,80},{112,96},{1... | collective-permute-start | bytes 786440 | tf_op jit(solution)/shard_map/while/body/eval_jaxpr/ppermute | solution.py:11
  389.9 16.4 %collective-permute-start = (f32[128,512]{1,0:T(8,128)}, f32[128,512]{1,0:T(8,128)S(1)}, u32[]{:S(2)}, u32[]{:S(2)}) collective-permute-start(f32[128,512]{1,0:T(8,128)} %convert_add_fusion.3), channel_id=1, source_target_pairs={{0,496},{16,0},{32,16},{48,32},{64,48},{80,64},{96,80},{112,96},{1... | collective-permute-start | bytes 786440 | tf_op jit(solution)/shard_map/while/body/eval_jaxpr/ppermute | solution.py:11
  408.0 16.0 %collective-permute-start = (f32[128,512]{1,0:T(8,128)}, f32[128,512]{1,0:T(8,128)S(1)}, u32[]{:S(2)}, u32[]{:S(2)}) collective-permute-start(f32[128,512]{1,0:T(8,128)} %convert_add_fusion.3), channel_id=1, source_target_pairs={{0,496},{16,0},{32,16},{48,32},{64,48},{80,64},{96,80},{112,96},{1... | collective-permute-start | bytes 786440 | tf_op jit(solution)/shard_map/while/body/eval_jaxpr/ppermute | solution.py:11
  425.8 16.0 %collective-permute-start = (f32[128,512]{1,0:T(8,128)}, f32[128,512]{1,0:T(8,128)S(1)}, u32[]{:S(2)}, u32[]{:S(2)}) collective-permute-start(f32[128,512]{1,0:T(8,128)} %convert_add_fusion.3), channel_id=1, source_target_pairs={{0,496},{16,0},{32,16},{48,32},{64,48},{80,64},{96,80},{112,96},{1... | collective-permute-start | bytes 786440 | tf_op jit(solution)/shard_map/while/body/eval_jaxpr/ppermute | solution.py:11
  443.5 16.0 %collective-permute-start = (f32[128,512]{1,0:T(8,128)}, f32[128,512]{1,0:T(8,128)S(1)}, u32[]{:S(2)}, u32[]{:S(2)}) collective-permute-start(f32[128,512]{1,0:T(8,128)} %convert_add_fusion.3), channel_id=1, source_target_pairs={{0,496},{16,0},{32,16},{48,32},{64,48},{80,64},{96,80},{112,96},{1... | collective-permute-start | bytes 786440 | tf_op jit(solution)/shard_map/while/body/eval_jaxpr/ppermute | solution.py:11
  461.3 16.0 %collective-permute-start = (f32[128,512]{1,0:T(8,128)}, f32[128,512]{1,0:T(8,128)S(1)}, u32[]{:S(2)}, u32[]{:S(2)}) collective-permute-start(f32[128,512]{1,0:T(8,128)} %convert_add_fusion.3), channel_id=1, source_target_pairs={{0,496},{16,0},{32,16},{48,32},{64,48},{80,64},{96,80},{112,96},{1... | collective-permute-start | bytes 786440 | tf_op jit(solution)/shard_map/while/body/eval_jaxpr/ppermute | solution.py:11
  479.0 16.0 %collective-permute-start = (f32[128,512]{1,0:T(8,128)}, f32[128,512]{1,0:T(8,128)S(1)}, u32[]{:S(2)}, u32[]{:S(2)}) collective-permute-start(f32[128,512]{1,0:T(8,128)} %convert_add_fusion.3), channel_id=1, source_target_pairs={{0,496},{16,0},{32,16},{48,32},{64,48},{80,64},{96,80},{112,96},{1... | collective-permute-start | bytes 786440 | tf_op jit(solution)/shard_map/while/body/eval_jaxpr/ppermute | solution.py:11
  496.7 16.0 %collective-permute-start = (f32[128,512]{1,0:T(8,128)}, f32[128,512]{1,0:T(8,128)S(1)}, u32[]{:S(2)}, u32[]{:S(2)}) collective-permute-start(f32[128,512]{1,0:T(8,128)} %convert_add_fusion.3), channel_id=1, source_target_pairs={{0,496},{16,0},{32,16},{48,32},{64,48},{80,64},{96,80},{112,96},{1... | collective-permute-start | bytes 786440 | tf_op jit(solution)/shard_map/while/body/eval_jaxpr/ppermute | solution.py:11
  514.5 16.0 %collective-permute-start = (f32[128,512]{1,0:T(8,128)}, f32[128,512]{1,0:T(8,128)S(1)}, u32[]{:S(2)}, u32[]{:S(2)}) collective-permute-start(f32[128,512]{1,0:T(8,128)} %convert_add_fusion.3), channel_id=1, source_target_pairs={{0,496},{16,0},{32,16},{48,32},{64,48},{80,64},{96,80},{112,96},{1... | collective-permute-start | bytes 786440 | tf_op jit(solution)/shard_map/while/body/eval_jaxpr/ppermute | solution.py:11
  532.2 16.0 %collective-permute-start = (f32[128,512]{1,0:T(8,128)}, f32[128,512]{1,0:T(8,128)S(1)}, u32[]{:S(2)}, u32[]{:S(2)}) collective-permute-start(f32[128,512]{1,0:T(8,128)} %convert_add_fusion.3), channel_id=1, source_target_pairs={{0,496},{16,0},{32,16},{48,32},{64,48},{80,64},{96,80},{112,96},{1... | collective-permute-start | bytes 786440 | tf_op jit(solution)/shard_map/while/body/eval_jaxpr/ppermute | solution.py:11
  567.7 16.0 %collective-permute-start = (f32[128,512]{1,0:T(8,128)}, f32[128,512]{1,0:T(8,128)S(1)}, u32[]{:S(2)}, u32[]{:S(2)}) collective-permute-start(f32[128,512]{1,0:T(8,128)} %convert_add_fusion.3), channel_id=1, source_target_pairs={{0,496},{16,0},{32,16},{48,32},{64,48},{80,64},{96,80},{112,96},{1... | collective-permute-start | bytes 786440 | tf_op jit(solution)/shard_map/while/body/eval_jaxpr/ppermute | solution.py:11
  585.4 291.1 %all-gather.2.cloned.1.call-start = ((), (), s32[]{:S(2)}) async-start(), calls=%async_computation | async-start | bytes 4325376 | tf_op jit(solution)/shard_map/all_gather | solution.py:66
  (8 other events, 312.7 us)
Sparse Core Ops, SparseCore 0:
  585.5 289.2 all-reduce.1
Sparse Core Ops, SparseCore 1:
  587.9 243.3 all-gather.1
where the time goes:
time: 892 us; the launch traced here: 889 us
  waiting for transfers between devices  402 us (45%)
  starting transfers between devices  390 us (44%)
  matrix products  44.7 us (5%)
  other arithmetic  28.1 us (3%)
  between operations  16.4 us (2%)
    ppermute x31, starting transfers between devices, shifted(): lax.ppermute(array, axis, [(i, (i + by) % count) for i in range(count)])  390 us
    psum x1, waiting for transfers between devices, per_device(): replica_total = lax.psum(running, 'dp')  279 us
    ppermute x31, waiting for transfers between devices, shifted(): lax.ppermute(array, axis, [(i, (i + by) % count) for i in range(count)])  122 us
    dot_general x32, matrix products, term_rows(): lax.dot_general(columns, value_grad, (((0,), (0,)), ((), ())), preferred_...  31.4 us
    add x31, other arithmetic, advance(): return shifted(running + grad_term(hop_index), 'blk', -1)  23 us
  transfers between devices with their start and end apart: 33, of which 32 were waited for; matrix products, arithmetic and copies ran while one was open for 1% of the time, Pallas kernels for 0%

commit v1 on v0

v1 whole, which is shorter than its diff:
```python
import jax
import jax.numpy as jnp
from jax import lax
from jax.experimental import pallas as pl
from jax.experimental.pallas import tpu as pltpu
from jax.sharding import Mesh
from jax.sharding import PartitionSpec as P

ZL, XN, YN, ZH, CN = 8, 4, 4, 2, 2
QN = CN * YN
TOK, WIDTH, KV, HD = 128, 4096, 512, 128
GROUP = 8
SUB = 16
BF, F32 = jnp.bfloat16, jnp.float32


def nt(a, b):
    return lax.dot_general(a, b, (((1,), (1,)), ((), ())), preferred_element_type=F32)


def attend_kernel(length_ref, q_ref, k_ref, v_ref, g_ref, vg_ref, kg_ref):
    scaling = HD ** (-0.5)
    keys, vals = k_ref[...], v_ref[...]
    length = length_ref[0]
    step = 2
    wide = step * TOK
    pos_s = lax.broadcasted_iota(jnp.int32, (TOK, wide), 0)
    pos_t = lax.broadcasted_iota(jnp.int32, (TOK, wide), 1) & (TOK - 1)
    allowed = pos_s <= pos_t
    live = ((lax.broadcasted_iota(jnp.int32, (1, wide), 1) & (TOK - 1)) < length).astype(F32)
    vg = jnp.zeros((TOK, HD), F32)
    kg = jnp.zeros((TOK, HD), F32)
    for first in range(0, GROUP, step):
        heads = range(first, first + step)
        qs = jnp.concatenate([q_ref[:, h * HD : (h + 1) * HD] for h in heads], axis=0)
        gs = jnp.concatenate([g_ref[:, h * HD : (h + 1) * HD] for h in heads], axis=0)
        scores = jnp.where(allowed, nt(keys, qs) * scaling, F32(-1e30))
        expd = jnp.exp(scores - jnp.max(scores, axis=0, keepdims=True))
        probs = expd * (live / jnp.sum(expd, axis=0, keepdims=True))
        dprob = nt(vals, gs)
        delta = jnp.sum(probs * dprob, axis=0, keepdims=True)
        dscore = probs * (dprob - delta)
        vg += jnp.dot(probs.astype(BF), gs, preferred_element_type=F32)
        kg += jnp.dot(dscore.astype(BF), qs, preferred_element_type=F32)
    vg_ref[...] = vg.astype(BF)
    kg_ref[...] = (kg * scaling).astype(BF)


def attend_back(query, key_rows, value_rows, grad_rows, length):
    heads = KV // HD
    wide = pl.BlockSpec((TOK, GROUP * HD), lambda g: (0, g))
    thin = pl.BlockSpec((TOK, HD), lambda g: (0, g))
    return pl.pallas_call(
        attend_kernel,
        grid=(heads,),
        in_specs=[pl.BlockSpec(memory_space=pltpu.SMEM), wide, thin, thin, wide],
        out_specs=[thin, thin],
        out_shape=[jax.ShapeDtypeStruct((TOK, KV), BF)] * 2,
        compiler_params=pltpu.CompilerParams(vmem_limit_bytes=24 << 20),
        cost_estimate=pl.CostEstimate(
            flops=10 * 32 * TOK * TOK * HD, bytes_accessed=3 << 20, transcendentals=32 * TOK * TOK
        ),
        name="attend",
    )(length, query, key_rows, value_rows, grad_rows)


def swap_groups(tiles):
    lane = lax.broadcasted_iota(jnp.int32, tiles[0].shape, 1)
    for bit in (1, 2, 4):
        shift = bit * SUB
        high = (lane & shift) != 0
        after = list(tiles)
        for i in range(8):
            if i & bit == 0:
                low_tile, high_tile = tiles[i], tiles[i | bit]
                after[i] = jnp.where(high, pltpu.roll(high_tile, shift, 1), low_tile)
                after[i | bit] = jnp.where(high, high_tile, pltpu.roll(low_tile, 128 - shift, 1))
        tiles = after
    return tiles


def to_pieces_kernel(in_ref, out_ref):
    for x in range(XN):
        tiles = [in_ref[:, (zl * XN + x) * 128 : (zl * XN + x + 1) * 128].astype(F32) for zl in range(8)]
        for q, tile in enumerate(swap_groups(tiles)):
            out_ref[q, :, x * 128 : (x + 1) * 128] = tile.astype(BF)


def from_pieces_kernel(in_ref, out_ref):
    for x in range(XN):
        tiles = [in_ref[q, :, x * 128 : (x + 1) * 128].astype(F32) for q in range(8)]
        for zl, tile in enumerate(swap_groups(tiles)):
            out_ref[:, (zl * XN + x) * 128 : (zl * XN + x + 1) * 128] = tile.astype(BF)


def to_pieces(rows):
    part = 32
    return pl.pallas_call(
        to_pieces_kernel,
        grid=(TOK // part,),
        in_specs=[pl.BlockSpec((part, WIDTH), lambda i: (i, 0))],
        out_specs=pl.BlockSpec((QN, part, KV), lambda i: (0, i, 0)),
        out_shape=jax.ShapeDtypeStruct((QN, TOK, KV), BF),
        compiler_params=pltpu.CompilerParams(vmem_limit_bytes=24 << 20),
        cost_estimate=pl.CostEstimate(flops=1 << 22, bytes_accessed=2 << 20, transcendentals=0),
        name="to_pieces",
    )(rows)


def from_pieces(pieces):
    part = 32
    return pl.pallas_call(
        from_pieces_kernel,
        grid=(TOK // part,),
        in_specs=[pl.BlockSpec((QN, part, KV), lambda i: (0, i, 0))],
        out_specs=pl.BlockSpec((part, WIDTH), lambda i: (i, 0)),
        out_shape=jax.ShapeDtypeStruct((TOK, WIDTH), BF),
        compiler_params=pltpu.CompilerParams(vmem_limit_bytes=24 << 20),
        cost_estimate=pl.CostEstimate(flops=1 << 22, bytes_accessed=2 << 20, transcendentals=0),
        name="from_pieces",
    )(pieces)


def exchange(array, axes):
    return lax.all_to_all(array, axes, 0, 0, tiled=True)


def spread(array, axes, count):
    return exchange(jnp.broadcast_to(array[None], (count,) + array.shape), axes)


def per_device(inputs, queries, keys, values, out_grad, lengths, value_weight):
    with jax.named_scope("send_inputs"):
        columns = exchange(to_pieces(inputs[0]), ("core", "y"))
    with jax.named_scope("gather_weight"):
        q = lax.axis_index("core") * YN + lax.axis_index("y")
        own = lax.dynamic_slice_in_dim(value_weight, q * SUB, SUB, 0)
        weight = spread(own, "zl", ZL)
        weight = spread(weight.reshape(ZL * SUB, KV), "x", XN).reshape(XN * ZL * SUB, KV)
    with jax.named_scope("attention"):
        value_grad, key_grad = attend_back(queries[0], keys[0], values[0], out_grad[0], lengths)
    with jax.named_scope("gather_value_grad"):
        grads = spread(value_grad, "y", YN)
        grads = lax.all_gather(grads, "core", axis=0, tiled=True).reshape(QN * TOK, KV)
    with jax.named_scope("weight_term"):
        term = lax.dot_general(
            columns.reshape(QN * TOK, KV), grads, (((0,), (0,)), ((), ())), preferred_element_type=F32
        ).astype(BF)
    with jax.named_scope("sum_x"):
        got = exchange(term.reshape(XN, ZL * SUB, KV), "x")
        plane = jnp.sum(got.astype(F32), axis=0).astype(BF).reshape(1, ZL, SUB, KV)
    with jax.named_scope("sum_z"):
        both = jnp.broadcast_to(plane, (ZH, ZL, SUB, KV)).reshape(ZH * ZL, SUB, KV)
        got = exchange(both, ("zh", "zl"))
        total = jnp.sum(got.astype(F32), axis=0) * F32(1.0 / 512)
    with jax.named_scope("share_rows"):
        weight_grad = spread(total, ("core", "y"), QN).reshape(QN * SUB, KV)
    with jax.named_scope("input_grad"):
        parts = nt(grads, weight).astype(BF).reshape(QN, TOK, KV)
        input_grad = from_pieces(exchange(parts, ("core", "y")))
    return (input_grad[None], key_grad[None], weight_grad)


def solution(mesh):
    fine = Mesh(mesh.devices.reshape(ZL, XN, YN, ZH, CN), ("zl", "x", "y", "zh", "core"))
    micro = ("zl", "x", "y", "zh", "core")
    blk = ("zl", "x")
    rows = P(micro, None, None)
    return jax.shard_map(
        per_device,
        mesh=fine,
        in_specs=(rows, rows, rows, rows, rows, P(micro), P(blk, None)),
        out_specs=(rows, rows, P(blk, None)),
        check_vma=False,
    )
```

time: 892 us -> 165 us (0.18)
  starting transfers between devices: 390 us -> 50.3 us
  waiting for transfers between devices: 402 us -> 63.6 us
  matrix products: 44.7 us -> 3.69 us
  other arithmetic: 28.1 us -> 0.13 us
  Pallas kernels: 0 us -> 11 us
  blocking collectives: 0 us -> 10.7 us
    ppermute x31 -> x0, starting transfers between devices: 390 us -> none  [shifted(): lax.ppermute(array, axis, [(i, (i + by) % count) for i in range(count)])]
    psum x1 -> x0, waiting for transfers between devices: 279 us -> none  [per_device(): replica_total = lax.psum(running, 'dp')]
    ppermute x31 -> x0, waiting for transfers between devices: 122 us -> none  [shifted(): lax.ppermute(array, axis, [(i, (i + by) % count) for i in range(count)])]
    all_to_all x0 -> x7, waiting for transfers between devices: none -> 62.8 us  [exchange(): return lax.all_to_all(array, axes, 0, 0, tiled=True)]
    all_to_all x0 -> x7, starting transfers between devices: none -> 50.3 us  [exchange(): return lax.all_to_all(array, axes, 0, 0, tiled=True)]
    dot_general x36 -> x2, matrix products: 42.5 us -> 3.69 us  [the longest x1 1.97 us: per_device(): lax.dot_general(columns.reshape(QN * TOK, KV), grads, (((0,), (0,)), ((),...]
    add x32 -> x0, other arithmetic: 24.6 us -> none  [the longest x31 23 us: advance(): return shifted(running + grad_term(hop_index), 'blk', -1)]
    pallas_call x0 -> x3, Pallas kernels: none -> 11 us  [the longest x1 4.98 us: attend_back(): pl.pallas_call(attend_kernel, grid=(heads,), in_specs=[pl.BlockSpec(memor...]
  transfers between devices with their start and end apart: 33 -> 8, of which waited for: 32 -> 8; matrix products, arithmetic and copies ran while one was open for 1% -> 3% of each run, Pallas kernels for 0% -> 4%
where the time goes in v1:
time: 165 us; the launch traced here: 164 us
  waiting for transfers between devices  63.6 us (39%)
  starting transfers between devices  50.3 us (30%)
  between operations  14.8 us (9%)
  Pallas kernels  11 us (7%)
  blocking collectives  10.7 us (6%)
  local copies, waits for them, and re-layouts  9.58 us (6%)
  matrix products  3.69 us (2%)
    all_to_all x7, waiting for transfers between devices, exchange(): return lax.all_to_all(array, axes, 0, 0, tiled=True)  62.8 us
    all_to_all x7, starting transfers between devices, exchange(): return lax.all_to_all(array, axes, 0, 0, tiled=True)  50.3 us
    all_to_all x1, blocking collectives, exchange(): return lax.all_to_all(array, axes, 0, 0, tiled=True)  10.7 us
    unnamed x17, local copies, waits for them, and re-layouts  5.78 us
    pallas_call x1, Pallas kernels, attend_back(): pl.pallas_call(attend_kernel, grid=(heads,), in_specs=[pl.BlockSpec(memor...  4.98 us
  transfers between devices with their start and end apart: 8, of which 8 were waited for; matrix products, arithmetic and copies ran while one was open for 3% of the time, Pallas kernels for 4%

profile of v1, /device:TPU:1, one launch (start us, length us, event | category | flops | bytes accessed | tf_op | source)
XLA Modules:
  0.0 163.8 jit_solution(16012610905797712179)
XLA Ops:
  7.9 1.2 copy-done.2
  9.1 1.2 copy-done.3
  10.3 0.9 copy-done.4
  11.2 0.9 copy-done.5
  12.1 5.0 %attend.1 = (bf16[128,512]{1,0:T(8,128)(2,1)S(1)}, bf16[128,512]{1,0:T(8,128)(2,1)}) custom-call(s32[1]{0:T(128)S(6)} %copy.15.length_ref, bf16[128,4096]{1,0:T(8,128)(2,1)S(1)} %bitcast.26, bf16[128,512]{1,0:T(8,128)(2,1)S(1)} %bitcast.28, bf16[128,512]{1,0:T(8,128)(2,1)S(1)} %bitcast.29, bf16[128,4096]{1,0:T(8,128)(2,1)S(1)} %bitcast.27), custom_call_target="tpu_custom_call" | custom-call | flops 671088640 | bytes 3145728 | tf_op jit(solution)/shard_map/attention/attend/pallas_call | solution.py:53
  17.1 0.8 broadcast_in_dim.18
  17.9 5.0 %all-to-all-start = ((bf16[4,128,512]{2,1,0:T(8,128)(2,1)}), bf16[4,128,512]{2,1,0:T(8,128)(2,1)S(1)}, u32[]{:S(2)}, u32[]{:S(2)}) async-start(bf16[4,128,512]{2,1,0:T(8,128)(2,1)} %broadcast_in_dim.18), calls=%async_computation | async-start | bytes 1048576 | tf_op jit(solution)/shard_map/gather_value_grad/all_to_all | solution.py:125
  22.9 3.0 %to_pieces.1 = bf16[8,128,512]{2,1,0:T(8,128)(2,1)} custom-call(bf16[128,4096]{1,0:T(8,128)(2,1)S(1)} %bitcast.25), custom_call_target="tpu_custom_call" | custom-call | flops 4194304 | bytes 2097152 | tf_op jit(solution)/shard_map/send_inputs/to_pieces/pallas_call | solution.py:98
  25.9 4.0 %all-to-all-done = bf16[4,128,512]{2,1,0:T(8,128)(2,1)S(1)} async-done(((bf16[4,128,512]{2,1,0:T(8,128)(2,1)}), bf16[4,128,512]{2,1,0:T(8,128)(2,1)S(1)}, u32[]{:S(2)}, u32[]{:S(2)}) %all-to-all-start) | async-done | bytes 524320 | tf_op jit(solution)/shard_map/gather_value_grad/all_to_all | solution.py:125
  29.9 0.8 copy-done.6
  30.7 9.9 %all-to-all-start.4 = ((bf16[8,128,512]{2,1,0:T(8,128)(2,1)}), bf16[8,128,512]{2,1,0:T(8,128)(2,1)S(1)}, u32[]{:S(2)}, u32[]{:S(2)}) async-start(bf16[8,128,512]{2,1,0:T(8,128)(2,1)} %to_pieces.1), calls=%async_computation.4 | async-start | bytes 2097152 | tf_op jit(solution)/shard_map/send_inputs/all_to_all | solution.py:125
  40.6 0.7 all-gather.2.cloned.1.call-update
  41.4 14.2 %all-to-all-done.4 = bf16[8,128,512]{2,1,0:T(8,128)(2,1)S(1)} async-done(((bf16[8,128,512]{2,1,0:T(8,128)(2,1)}), bf16[8,128,512]{2,1,0:T(8,128)(2,1)S(1)}, u32[]{:S(2)}, u32[]{:S(2)}) %all-to-all-start.4) | async-done | bytes 1048608 | tf_op jit(solution)/shard_map/send_inputs/all_to_all | solution.py:125
  55.6 0.7 broadcast_in_dim.19
  56.3 9.3 %all-to-all-start.1 = ((bf16[8,16,512]{2,1,0:T(8,128)(2,1)}), bf16[8,16,512]{2,1,0:T(8,128)(2,1)S(1)}, u32[]{:S(2)}, u32[]{:S(2)}) async-start(bf16[8,16,512]{2,1,0:T(8,128)(2,1)} %broadcast_in_dim.19), calls=%async_computation.1 | async-start | bytes 262144 | tf_op jit(solution)/shard_map/gather_weight/all_to_all | solution.py:125
  65.7 2.0 %fusion = bf16[512,512]{0,1:T(8,128)(2,1)S(1)} fusion(bf16[8,128,512]{2,1,0:T(8,128)(2,1)} %all-gather.2.cloned.1.call-done, bf16[8,128,512]{2,1,0:T(8,128)(2,1)S(1)} %all-to-all-done.4), kind=kOutput, calls=%fused_computation.2 | convolution fusion | flops 537133056 | bytes 2621440 | tf_op jit(solution)/shard_map/weight_term/dot_general | solution.py:146
  67.7 8.3 %all-to-all-done.1 = bf16[8,16,512]{2,1,0:T(8,128)(2,1)S(1)} async-done(((bf16[8,16,512]{2,1,0:T(8,128)(2,1)}), bf16[8,16,512]{2,1,0:T(8,128)(2,1)S(1)}, u32[]{:S(2)}, u32[]{:S(2)}) %all-to-all-start.1) | async-done | bytes 131104 | tf_op jit(solution)/shard_map/gather_weight/all_to_all | solution.py:125
  75.9 10.7 %all_to_all.40 = bf16[4,128,512]{2,1,0:T(8,128)(2,1)S(1)} all-to-all(bf16[4,128,512]{2,1,0:T(8,128)(2,1)S(1)} %bitcast.34), channel_id=1, replica_groups=mesh['zl'=8,'x'=4,'y'=4,'zh'=2,'core'=2] {'x'}, dimensions={0} | all-to-all | bytes 1048576 | tf_op jit(solution)/shard_map/sum_x/all_to_all | solution.py:125
  86.7 0.8 broadcast_in_dim.41
  87.5 3.5 %all-to-all-start.2 = ((bf16[4,128,512]{2,1,0:T(8,128)(2,1)}), bf16[4,128,512]{2,1,0:T(8,128)(2,1)S(1)}, u32[]{:S(2)}, u32[]{:S(2)}) async-start(bf16[4,128,512]{2,1,0:T(8,128)(2,1)} %broadcast_in_dim.41), calls=%async_computation.2 | async-start | bytes 1048576 | tf_op jit(solution)/shard_map/gather_weight/all_to_all | solution.py:125
  91.1 6.8 %all-to-all-done.2 = bf16[4,128,512]{2,1,0:T(8,128)(2,1)S(1)} async-done(((bf16[4,128,512]{2,1,0:T(8,128)(2,1)}), bf16[4,128,512]{2,1,0:T(8,128)(2,1)S(1)}, u32[]{:S(2)}, u32[]{:S(2)}) %all-to-all-start.2) | async-done | bytes 524320 | tf_op jit(solution)/shard_map/gather_weight/all_to_all | solution.py:125
  97.9 0.7 broadcast_in_dim.45
  98.6 7.4 %all-to-all-start.6 = ((bf16[16,16,512]{2,1,0:T(8,128)(2,1)}), bf16[16,16,512]{2,1,0:T(8,128)(2,1)S(1)}, u32[]{:S(2)}, u32[]{:S(2)}) async-start(bf16[16,16,512]{2,1,0:T(8,128)(2,1)} %bitcast.15), calls=%async_computation.6 | async-start | bytes 524288 | tf_op jit(solution)/shard_map/sum_z/all_to_all | solution.py:125
  106.1 1.7 %convolution_convert_fusion = bf16[1024,512]{1,0:T(8,128)(2,1)} fusion(bf16[1024,512]{1,0:T(8,128)(2,1)S(1)} %bitcast.36, bf16[512,512]{1,0:T(8,128)(2,1)S(1)} %bitcast.33), kind=kOutput, calls=%fused_computation | convolution fusion | flops 537395200 | bytes 2621440 | tf_op jit(solution)/shard_map/input_grad/dot_general | solution.py:18
  107.8 11.1 %all-to-all-done.6 = bf16[16,16,512]{2,1,0:T(8,128)(2,1)S(1)} async-done(((bf16[16,16,512]{2,1,0:T(8,128)(2,1)}), bf16[16,16,512]{2,1,0:T(8,128)(2,1)S(1)}, u32[]{:S(2)}, u32[]{:S(2)}) %all-to-all-start.6) | async-done | bytes 262176 | tf_op jit(solution)/shard_map/sum_z/all_to_all | solution.py:125
  118.8 11.5 %all-to-all-start.3 = ((bf16[8,128,512]{2,1,0:T(8,128)(2,1)}), bf16[8,128,512]{2,1,0:T(8,128)(2,1)S(1)}, u32[]{:S(2)}, u32[]{:S(2)}) async-start(bf16[8,128,512]{2,1,0:T(8,128)(2,1)} %bitcast.7), calls=%async_computation.3 | async-start | bytes 2097152 | tf_op jit(solution)/shard_map/input_grad/all_to_all | solution.py:125
  130.3 14.9 %all-to-all-done.3.in_ref = bf16[8,128,512]{2,1,0:T(8,128)(2,1)S(1)} async-done(((bf16[8,128,512]{2,1,0:T(8,128)(2,1)}), bf16[8,128,512]{2,1,0:T(8,128)(2,1)S(1)}, u32[]{:S(2)}, u32[]{:S(2)}) %all-to-all-start.3) | async-done | bytes 1048608 | tf_op jit(solution)/shard_map/input_grad/all_to_all | solution.py:125
  145.3 0.7 broadcast_in_dim.46
  146.0 3.7 %all-to-all-start.7 = ((f32[8,16,512]{2,1,0:T(8,128)}), f32[8,16,512]{2,1,0:T(8,128)S(1)}, u32[]{:S(2)}, u32[]{:S(2)}) async-start(f32[8,16,512]{2,1,0:T(8,128)} %broadcast_in_dim.46), calls=%async_computation.7 | async-start | bytes 524288 | tf_op jit(solution)/shard_map/share_rows/all_to_all | solution.py:125
  149.7 3.0 %from_pieces.1 = bf16[128,4096]{1,0:T(8,128)(2,1)} custom-call(bf16[8,128,512]{2,1,0:T(8,128)(2,1)S(1)} %all-to-all-done.3.in_ref), custom_call_target="tpu_custom_call" | custom-call | flops 4194304 | bytes 2097152 | tf_op jit(solution)/shard_map/input_grad/from_pieces/pallas_call | solution.py:112
  152.8 3.5 %all-to-all-done.7 = f32[8,16,512]{2,1,0:T(8,128)S(1)} async-done(((f32[8,16,512]{2,1,0:T(8,128)}), f32[8,16,512]{2,1,0:T(8,128)S(1)}, u32[]{:S(2)}, u32[]{:S(2)}) %all-to-all-start.7) | async-done | bytes 262176 | tf_op jit(solution)/shard_map/share_rows/all_to_all | solution.py:125
  156.3 0.7 copy.16
  (17 shorter events, 0.3 us)
Async XLA Ops:
  7.2 34.2 %copy-start = (bf16[128,512]{1,0:T(8,128)(2,1)S(1)}, bf16[128,512]{1,0:T(8,128)(2,1)}, u32[]{:S(2)}) copy-start(bf16[128,512]{1,0:T(8,128)(2,1)} %param.13) | copy-start | bytes 393220
  7.9 1.2 copy-start.2
  9.1 1.2 copy-start.3
  10.3 0.9 copy-start.4
  11.2 0.9 copy-start.5
  17.1 5.8 %copy-start.1 = (bf16[1,128,4096]{2,1,0:T(8,128)(2,1)S(1)}, bf16[1,128,4096]{2,1,0:T(8,128)(2,1)}, u32[]{:S(2)}) copy-start(bf16[1,128,4096]{2,1,0:T(8,128)(2,1)} %param.7) | copy-start | bytes 3145732
  17.9 11.9 %all-to-all-start = ((bf16[4,128,512]{2,1,0:T(8,128)(2,1)}), bf16[4,128,512]{2,1,0:T(8,128)(2,1)S(1)}, u32[]{:S(2)}, u32[]{:S(2)}) async-start(bf16[4,128,512]{2,1,0:T(8,128)(2,1)} %broadcast_in_dim.18), calls=%async_computation | async-start | bytes 1048576 | tf_op jit(solution)/shard_map/gather_value_grad/all_to_all | solution.py:125
  29.9 0.8 copy-start.6
  30.7 24.9 %all-to-all-start.4 = ((bf16[8,128,512]{2,1,0:T(8,128)(2,1)}), bf16[8,128,512]{2,1,0:T(8,128)(2,1)S(1)}, u32[]{:S(2)}, u32[]{:S(2)}) async-start(bf16[8,128,512]{2,1,0:T(8,128)(2,1)} %to_pieces.1), calls=%async_computation.4 | async-start | bytes 2097152 | tf_op jit(solution)/shard_map/send_inputs/all_to_all | solution.py:125
  40.6 25.1 %all-gather.2.cloned.1.call-start = ((), (), s32[]{:S(2)}) async-start(), calls=%async_computation.8 | async-start | bytes 1572864 | tf_op jit(solution)/shard_map/gather_value_grad/all_gather | solution.py:144
  56.3 19.7 %all-to-all-start.1 = ((bf16[8,16,512]{2,1,0:T(8,128)(2,1)}), bf16[8,16,512]{2,1,0:T(8,128)(2,1)S(1)}, u32[]{:S(2)}, u32[]{:S(2)}) async-start(bf16[8,16,512]{2,1,0:T(8,128)(2,1)} %broadcast_in_dim.19), calls=%async_computation.1 | async-start | bytes 262144 | tf_op jit(solution)/shard_map/gather_weight/all_to_all | solution.py:125
  87.5 10.4 %all-to-all-start.2 = ((bf16[4,128,512]{2,1,0:T(8,128)(2,1)}), bf16[4,128,512]{2,1,0:T(8,128)(2,1)S(1)}, u32[]{:S(2)}, u32[]{:S(2)}) async-start(bf16[4,128,512]{2,1,0:T(8,128)(2,1)} %broadcast_in_dim.41), calls=%async_computation.2 | async-start | bytes 1048576 | tf_op jit(solution)/shard_map/gather_weight/all_to_all | solution.py:125
  91.0 15.1 %copy-start.7 = (bf16[8,128,512]{2,1,0:T(8,128)(2,1)S(1)}, bf16[8,128,512]{2,1,0:T(8,128)(2,1)}, u32[]{:S(2)}) copy-start(bf16[8,128,512]{2,1,0:T(8,128)(2,1)} %all-gather.2.cloned.1.call-done) | copy-start | bytes 3145732
  98.6 20.2 %all-to-all-start.6 = ((bf16[16,16,512]{2,1,0:T(8,128)(2,1)}), bf16[16,16,512]{2,1,0:T(8,128)(2,1)S(1)}, u32[]{:S(2)}, u32[]{:S(2)}) async-start(bf16[16,16,512]{2,1,0:T(8,128)(2,1)} %bitcast.15), calls=%async_computation.6 | async-start | bytes 524288 | tf_op jit(solution)/shard_map/sum_z/all_to_all | solution.py:125
  118.8 26.4 %all-to-all-start.3 = ((bf16[8,128,512]{2,1,0:T(8,128)(2,1)}), bf16[8,128,512]{2,1,0:T(8,128)(2,1)S(1)}, u32[]{:S(2)}, u32[]{:S(2)}) async-start(bf16[8,128,512]{2,1,0:T(8,128)(2,1)} %bitcast.7), calls=%async_computation.3 | async-start | bytes 2097152 | tf_op jit(solution)/shard_map/input_grad/all_to_all | solution.py:125
  146.0 10.3 %all-to-all-start.7 = ((f32[8,16,512]{2,1,0:T(8,128)}), f32[8,16,512]{2,1,0:T(8,128)S(1)}, u32[]{:S(2)}, u32[]{:S(2)}) async-start(f32[8,16,512]{2,1,0:T(8,128)} %broadcast_in_dim.46), calls=%async_computation.7 | async-start | bytes 524288 | tf_op jit(solution)/shard_map/share_rows/all_to_all | solution.py:125
Sparse Core Ops, SparseCore 0:
  43.5 22.0 all-gather.1

commit v2 on v1

--- a/solution.py
+++ b/solution.py
@@ -18,7 +18,7 @@
     return lax.dot_general(a, b, (((1,), (1,)), ((), ())), preferred_element_type=F32)
 
 
-def attend_kernel(length_ref, q_ref, k_ref, v_ref, g_ref, vg_ref, kg_ref):
+def attend_kernel(length_ref, q_ref, k_ref, v_ref, g_ref, _, vg_ref, kg_ref):
     scaling = HD ** (-0.5)
     keys, vals = k_ref[...], v_ref[...]
     length = length_ref[0]
@@ -46,22 +46,21 @@
     kg_ref[...] = (kg * scaling).astype(BF)
 
 
-def attend_back(query, key_rows, value_rows, grad_rows, length):
+def attend_back(query, key_rows, value_rows, grad_rows, length, earlier):
     heads = KV // HD
     wide = pl.BlockSpec((TOK, GROUP * HD), lambda g: (0, g))
     thin = pl.BlockSpec((TOK, HD), lambda g: (0, g))
     return pl.pallas_call(
         attend_kernel,
         grid=(heads,),
-        in_specs=[pl.BlockSpec(memory_space=pltpu.SMEM), wide, thin, thin, wide],
+        in_specs=[pl.BlockSpec(memory_space=pltpu.SMEM), wide, thin, thin, wide, pl.BlockSpec(memory_space=pl.ANY)],
         out_specs=[thin, thin],
         out_shape=[jax.ShapeDtypeStruct((TOK, KV), BF)] * 2,
-        compiler_params=pltpu.CompilerParams(vmem_limit_bytes=24 << 20),
         cost_estimate=pl.CostEstimate(
             flops=10 * 32 * TOK * TOK * HD, bytes_accessed=3 << 20, transcendentals=32 * TOK * TOK
         ),
         name="attend",
-    )(length, query, key_rows, value_rows, grad_rows)
+    )(length, query, key_rows, value_rows, grad_rows, earlier)
 
 
 def swap_groups(tiles):
@@ -86,9 +85,12 @@
             out_ref[q, :, x * 128 : (x + 1) * 128] = tile.astype(BF)
 
 
-def from_pieces_kernel(in_ref, out_ref):
+def from_pieces_kernel(places_ref, *refs):
+    out_ref, held = refs[-2:]
+    for i in range(QN):
+        held[places_ref[i]] = refs[i // CN][i % CN]
     for x in range(XN):
-        tiles = [in_ref[q, :, x * 128 : (x + 1) * 128].astype(F32) for q in range(8)]
+        tiles = [held[q, :, x * 128 : (x + 1) * 128].astype(F32) for q in range(8)]
         for zl, tile in enumerate(swap_groups(tiles)):
             out_ref[:, (zl * XN + x) * 128 : (zl * XN + x + 1) * 128] = tile.astype(BF)
 
@@ -101,24 +103,25 @@
         in_specs=[pl.BlockSpec((part, WIDTH), lambda i: (i, 0))],
         out_specs=pl.BlockSpec((QN, part, KV), lambda i: (0, i, 0)),
         out_shape=jax.ShapeDtypeStruct((QN, TOK, KV), BF),
-        compiler_params=pltpu.CompilerParams(vmem_limit_bytes=24 << 20),
         cost_estimate=pl.CostEstimate(flops=1 << 22, bytes_accessed=2 << 20, transcendentals=0),
         name="to_pieces",
     )(rows)
 
 
-def from_pieces(pieces):
+def from_pieces(pieces, places):
     part = 32
     return pl.pallas_call(
         from_pieces_kernel,
         grid=(TOK // part,),
-        in_specs=[pl.BlockSpec((QN, part, KV), lambda i: (0, i, 0))],
+        in_specs=[pl.BlockSpec(memory_space=pltpu.SMEM)]
+        + [pl.BlockSpec((CN, part, KV), lambda i: (0, i, 0))] * YN,
         out_specs=pl.BlockSpec((part, WIDTH), lambda i: (i, 0)),
         out_shape=jax.ShapeDtypeStruct((TOK, WIDTH), BF),
-        compiler_params=pltpu.CompilerParams(vmem_limit_bytes=24 << 20),
+        scratch_shapes=[pltpu.VMEM((QN, part, KV), BF)],
         cost_estimate=pl.CostEstimate(flops=1 << 22, bytes_accessed=2 << 20, transcendentals=0),
+        compiler_params=pltpu.CompilerParams(vmem_limit_bytes=16 << 20),
         name="from_pieces",
-    )(pieces)
+    )(jnp.stack(places).astype(jnp.int32), *pieces)
 
 
 def exchange(array, axes):
@@ -129,19 +132,103 @@
     return exchange(jnp.broadcast_to(array[None], (count,) + array.shape), axes)
 
 
+def shifted(array, axes, count, by):
+    return lax.ppermute(array, axes, [(i, (i + by) % count) for i in range(count)])
+
+
+def along_z(array, by):
+    places = []
+    for z in range(ZH * ZL):
+        to = (z + by) % (ZH * ZL)
+        places.append(((z % ZL) * ZH + z // ZL, (to % ZL) * ZH + to // ZL))
+    return lax.ppermute(array, ("zl", "zh"), places)
+
+
+def ring_spread(array, axes, count):
+    return [array] + [shifted(array, axes, count, by) for by in range(1, count)]
+
+
+def place_kernel(places_ref, *refs):
+    out_ref = refs[-1]
+    at = 0
+    for ref in refs[:-1]:
+        if ref.ndim < out_ref.ndim:
+            out_ref[places_ref[at]] = ref[...]
+            at += 1
+        else:
+            for i in range(ref.shape[0]):
+                out_ref[places_ref[at]] = ref[i]
+                at += 1
+
+
+def place(parts, places):
+    shape = parts[0].shape
+    places = jnp.stack(places).astype(jnp.int32)
+    return pl.pallas_call(
+        place_kernel,
+        in_specs=[pl.BlockSpec(memory_space=pltpu.SMEM)] + [pl.BlockSpec(memory_space=pltpu.VMEM)] * len(parts),
+        out_specs=pl.BlockSpec(memory_space=pltpu.VMEM),
+        out_shape=jax.ShapeDtypeStruct((len(places),) + shape, parts[0].dtype),
+        cost_estimate=pl.CostEstimate(
+            flops=0, bytes_accessed=4 * len(places) * shape[0] * shape[1], transcendentals=0
+        ),
+        compiler_params=pltpu.CompilerParams(vmem_limit_bytes=16 << 20),
+        name="place",
+    )(places, *parts)
+
+
+def place_rows_kernel(at_ref, *refs):
+    out_ref = refs[-1]
+    for j, ref in enumerate(refs[:-1]):
+        for k in range(ZL):
+            row = ((at_ref[1] + XN - j) % XN) * ZL + (at_ref[0] + ZL - k) % ZL
+            out_ref[pl.ds(pl.multiple_of(row * SUB, SUB), SUB), :] = ref[k * SUB : (k + 1) * SUB, :]
+
+
+def place_rows(parts, zl, x):
+    return pl.pallas_call(
+        place_rows_kernel,
+        in_specs=[pl.BlockSpec(memory_space=pltpu.SMEM)] + [pl.BlockSpec(memory_space=pltpu.VMEM)] * len(parts),
+        out_specs=pl.BlockSpec(memory_space=pltpu.VMEM),
+        out_shape=jax.ShapeDtypeStruct((KV, KV), BF),
+        compiler_params=pltpu.CompilerParams(vmem_limit_bytes=16 << 20),
+        name="place_rows",
+    )(jnp.stack([zl, x]).astype(jnp.int32), *parts)
+
+
+def own_rows_kernel(q_ref, rows_ref, _, out_ref):
+    out_ref[...] = rows_ref[...]
+
+
+def own_rows(rows, q, earlier):
+    return pl.pallas_call(
+        own_rows_kernel,
+        grid_spec=pltpu.PrefetchScalarGridSpec(
+            num_scalar_prefetch=1,
+            grid=(1,),
+            in_specs=[pl.BlockSpec((SUB, KV), lambda i, q: (q[0], 0)), pl.BlockSpec(memory_space=pl.ANY)],
+            out_specs=pl.BlockSpec((SUB, KV), lambda i, q: (0, 0)),
+        ),
+        out_shape=jax.ShapeDtypeStruct((SUB, KV), BF),
+        name="own_rows",
+    )(q[None].astype(jnp.int32), rows, earlier)
+
+
 def per_device(inputs, queries, keys, values, out_grad, lengths, value_weight):
+    core, y, x = (lax.axis_index(name) for name in ("core", "y", "x"))
+    zl = lax.axis_index("zl")
+    q = core * YN + y
     with jax.named_scope("send_inputs"):
-        columns = exchange(to_pieces(inputs[0]), ("core", "y"))
-    with jax.named_scope("gather_weight"):
-        q = lax.axis_index("core") * YN + lax.axis_index("y")
-        own = lax.dynamic_slice_in_dim(value_weight, q * SUB, SUB, 0)
-        weight = spread(own, "zl", ZL)
-        weight = spread(weight.reshape(ZL * SUB, KV), "x", XN).reshape(XN * ZL * SUB, KV)
+        pieces = to_pieces(inputs[0])
+        columns = exchange(pieces, ("core", "y"))
     with jax.named_scope("attention"):
-        value_grad, key_grad = attend_back(queries[0], keys[0], values[0], out_grad[0], lengths)
+        value_grad, key_grad = attend_back(queries[0], keys[0], values[0], out_grad[0], lengths, pieces)
     with jax.named_scope("gather_value_grad"):
-        grads = spread(value_grad, "y", YN)
-        grads = lax.all_gather(grads, "core", axis=0, tiled=True).reshape(QN * TOK, KV)
+        ring = ring_spread(value_grad, "y", YN)
+        other = shifted(jnp.stack(ring), "core", CN, 1)
+        sources = [(y - k) % YN for k in range(YN)]
+        grads = place(ring + [other], [core * YN + p for p in sources] + [(1 - core) * YN + p for p in sources])
+        grads = grads.reshape(QN * TOK, KV)
     with jax.named_scope("weight_term"):
         term = lax.dot_general(
             columns.reshape(QN * TOK, KV), grads, (((0,), (0,)), ((), ())), preferred_element_type=F32
@@ -149,15 +236,29 @@
     with jax.named_scope("sum_x"):
         got = exchange(term.reshape(XN, ZL * SUB, KV), "x")
         plane = jnp.sum(got.astype(F32), axis=0).astype(BF).reshape(1, ZL, SUB, KV)
+    with jax.named_scope("gather_weight"):
+        ring = own_rows(value_weight, q, value_grad)[None]
+        for by in (1, 2, 4):
+            ring = jnp.concatenate([ring, along_z(ring, by)])
+        ring = ring.reshape(ZL * SUB, KV)
+        weight = place_rows(ring_spread(ring, "x", XN), zl, x)
+    with jax.named_scope("input_grad"):
+        parts = nt(grads, weight).astype(BF).reshape(CN, YN, TOK, KV)
+        mine = lax.dynamic_index_in_dim(parts, core, 0, False)
+        theirs = shifted(lax.dynamic_index_in_dim(parts, 1 - core, 0, False), "core", CN, 1)
+        parts = jnp.stack([mine, theirs], axis=1)
+        places, back = [], []
+        for by in range(YN):
+            piece = lax.dynamic_index_in_dim(parts, (y + by) % YN, 0, False)
+            back.append(shifted(piece, "y", YN, by) if by else piece)
+            places += [c * YN + (y - by) % YN for c in (core, 1 - core)]
+        input_grad = from_pieces(back, places)
     with jax.named_scope("sum_z"):
         both = jnp.broadcast_to(plane, (ZH, ZL, SUB, KV)).reshape(ZH * ZL, SUB, KV)
         got = exchange(both, ("zh", "zl"))
         total = jnp.sum(got.astype(F32), axis=0) * F32(1.0 / 512)
     with jax.named_scope("share_rows"):
         weight_grad = spread(total, ("core", "y"), QN).reshape(QN * SUB, KV)
-    with jax.named_scope("input_grad"):
-        parts = nt(grads, weight).astype(BF).reshape(QN, TOK, KV)
-        input_grad = from_pieces(exchange(parts, ("core", "y")))
     return (input_grad[None], key_grad[None], weight_grad)
 
 

time: 165 us -> 129 us (0.78)
  waiting for transfers between devices: 63.6 us -> 27.5 us
  starting transfers between devices: 50.3 us -> 76 us
  between operations: 14.8 us -> 1.67 us
  blocking collectives: 10.7 us -> 0 us
  local copies, waits for them, and re-layouts: 9.58 us -> 2.42 us
  Pallas kernels: 11 us -> 16.5 us
  other arithmetic: 0.13 us -> 2.02 us
    all_to_all x7 -> x4, waiting for transfers between devices: 62.8 us -> 2 us  [exchange(): return lax.all_to_all(array, axes, 0, 0, tiled=True)]
    ppermute x0 -> x14, starting transfers between devices: none -> 42.6 us  [the longest x11 34.8 us: shifted(): lax.ppermute(array, axes, [(i, (i + by) % count) for i in range(count)])]
    ppermute x0 -> x14, waiting for transfers between devices: none -> 25.5 us  [the longest x11 14.6 us: shifted(): lax.ppermute(array, axes, [(i, (i + by) % count) for i in range(count)])]
    all_to_all x7 -> x4, starting transfers between devices: 50.3 us -> 33.4 us  [exchange(): return lax.all_to_all(array, axes, 0, 0, tiled=True)]
    all_to_all x1 -> x0, blocking collectives: 10.7 us -> none  [exchange(): return lax.all_to_all(array, axes, 0, 0, tiled=True)]
    unnamed x17 -> x5, local copies, waits for them, and re-layouts: 5.78 us -> 0.71 us
    pallas_call x0 -> x3, Pallas kernels: none -> 2.6 us  [the longest x1 1.33 us: own_rows(): pl.pallas_call(own_rows_kernel, grid_spec=pltpu.PrefetchScalarGridSpec(nu...]
    broadcast_in_dim x4 -> x1, local copies, waits for them, and re-layouts: 3.06 us -> 0.73 us  [spread(): return exchange(jnp.broadcast_to(array[None], (count,) + array.shape), axes)]
  transfers between devices with their start and end apart: 8 -> 18, of which waited for: 8 -> 10; matrix products, arithmetic and copies ran while one was open for 3% -> 4% of each run, Pallas kernels for 4% -> 9%
where the time goes in v2:
time: 129 us; the launch traced here: 128 us
  starting transfers between devices  76 us (59%)
  waiting for transfers between devices  27.5 us (21%)
  Pallas kernels  16.5 us (13%)
  local copies, waits for them, and re-layouts  2.42 us (2%)
  matrix products  2.31 us (2%)
  other arithmetic  2.02 us (2%)
  between operations  1.67 us (1%)
    ppermute x11, starting transfers between devices, shifted(): lax.ppermute(array, axes, [(i, (i + by) % count) for i in range(count)])  34.8 us
    all_to_all x4, starting transfers between devices, exchange(): return lax.all_to_all(array, axes, 0, 0, tiled=True)  33.4 us
    ppermute x11, waiting for transfers between devices, shifted(): lax.ppermute(array, axes, [(i, (i + by) % count) for i in range(count)])  14.6 us
    ppermute x3, waiting for transfers between devices, along_z(): return lax.ppermute(array, ('zl', 'zh'), places)  10.9 us
    ppermute x3, starting transfers between devices, along_z(): return lax.ppermute(array, ('zl', 'zh'), places)  7.85 us
    pallas_call x1, Pallas kernels, attend_back(): pl.pallas_call(attend_kernel, grid=(heads,), in_specs=[pl.BlockSpec(memor...  5.9 us
    pallas_call x1, Pallas kernels, to_pieces(): pl.pallas_call(to_pieces_kernel, grid=(TOK // part,), in_specs=[pl.BlockS...  4.36 us
    pallas_call x1, Pallas kernels, from_pieces(): pl.pallas_call(from_pieces_kernel, grid=(TOK // part,), in_specs=[pl.Bloc...  3.62 us
  transfers between devices with their start and end apart: 18, of which 10 were waited for; matrix products, arithmetic and copies ran while one was open for 4% of the time, Pallas kernels for 9%

profile of v2, /device:TPU:1, one launch (start us, length us, event | category | flops | bytes accessed | tf_op | source)
XLA Modules:
  0.0 128.4 jit_solution(9623641073956439672)
XLA Ops:
  0.6 4.4 %to_pieces.1._ = bf16[8,128,512]{2,1,0:T(8,128)(2,1)} custom-call(bf16[128,4096]{1,0:T(8,128)(2,1)} %bitcast.63), custom_call_target="tpu_custom_call" | custom-call | flops 4194304 | bytes 2097152 | tf_op jit(solution)/shard_map/send_inputs/to_pieces/pallas_call | solution.py:100
  5.0 10.4 %all-to-all-start = ((bf16[8,128,512]{2,1,0:T(8,128)(2,1)}), bf16[8,128,512]{2,1,0:T(8,128)(2,1)S(1)}, u32[]{:S(2)}, u32[]{:S(2)}) async-start(bf16[8,128,512]{2,1,0:T(8,128)(2,1)} %to_pieces.1._), calls=%async_computation | async-start | bytes 2097152 | tf_op jit(solution)/shard_map/send_inputs/all_to_all | solution.py:128
  16.0 5.9 %attend.1 = (bf16[128,512]{1,0:T(8,128)(2,1)}, bf16[128,512]{1,0:T(8,128)(2,1)}) custom-call(s32[1]{0:T(128)S(6)} %copy.14.length_ref, bf16[128,4096]{1,0:T(8,128)(2,1)} %bitcast.64, bf16[128,512]{1,0:T(8,128)(2,1)} %bitcast.74, bf16[128,512]{1,0:T(8,128)(2,1)} %bitcast.75, bf16[128,4096]{1,0:T(8,128)(2,1)} %bitcast.65, bf16[8,128,512]{2,1,0:T(8,128)(2,1)} %to_pieces.1._), custom_call_target="tpu_custom_call" | custom-call | flops 671088640 | bytes 3145728 | tf_op jit(solution)/shard_map/attention/attend/pallas_call | solution.py:53
  21.9 4.6 %collective-permute-start.2 = (bf16[128,512]{1,0:T(8,128)(2,1)}, bf16[128,512]{1,0:T(8,128)(2,1)S(1)}, u32[]{:S(2)}, u32[]{:S(2)}) collective-permute-start(bf16[128,512]{1,0:T(8,128)(2,1)} %get-tuple-element.5.refs_0_._), channel_id=1, source_target_pairs={{0,12},{4,0},{8,4},{12,8},{1,13},{5,1},{9,5},{13,9},{2,14},{6,2},{... | collective-permute-start | bytes 393224 | tf_op jit(solution)/shard_map/gather_value_grad/ppermute | solution.py:136
  26.5 2.5 %collective-permute-start.1 = (bf16[128,512]{1,0:T(8,128)(2,1)}, bf16[128,512]{1,0:T(8,128)(2,1)S(1)}, u32[]{:S(2)}, u32[]{:S(2)}) collective-permute-start(bf16[128,512]{1,0:T(8,128)(2,1)} %get-tuple-element.5.refs_0_._), channel_id=1, source_target_pairs={{0,8},{4,12},{8,0},{12,4},{1,9},{5,13},{9,1},{13,5},{2,10},{6,14},... | collective-permute-start | bytes 393224 | tf_op jit(solution)/shard_map/gather_value_grad/ppermute | solution.py:136
  29.0 2.5 %collective-permute-start = (bf16[128,512]{1,0:T(8,128)(2,1)}, bf16[128,512]{1,0:T(8,128)(2,1)S(1)}, u32[]{:S(2)}, u32[]{:S(2)}) collective-permute-start(bf16[128,512]{1,0:T(8,128)(2,1)} %get-tuple-element.5.refs_0_._), channel_id=1, source_target_pairs={{0,4},{4,8},{8,12},{12,0},{1,5},{5,9},{9,13},{13,1},{2,6},{6,10},{... | collective-permute-start | bytes 393224 | tf_op jit(solution)/shard_map/gather_value_grad/ppermute | solution.py:136
  31.7 2.8 %collective-permute-done.1.refs_2_ = bf16[128,512]{1,0:T(8,128)(2,1)S(1)} collective-permute-done((bf16[128,512]{1,0:T(8,128)(2,1)}, bf16[128,512]{1,0:T(8,128)(2,1)S(1)}, u32[]{:S(2)}, u32[]{:S(2)}) %collective-permute-start.1) | collective-permute-done | bytes 131104 | tf_op jit(solution)/shard_map/gather_value_grad/ppermute | solution.py:136
  34.5 3.3 %collective-permute-done.refs_1_ = bf16[128,512]{1,0:T(8,128)(2,1)S(1)} collective-permute-done((bf16[128,512]{1,0:T(8,128)(2,1)}, bf16[128,512]{1,0:T(8,128)(2,1)S(1)}, u32[]{:S(2)}, u32[]{:S(2)}) %collective-permute-start) | collective-permute-done | bytes 131104 | tf_op jit(solution)/shard_map/gather_value_grad/ppermute | solution.py:136
  37.9 1.0 pad_maximum_fusion
  38.9 3.0 %collective-permute-start.3 = (bf16[4,128,512]{2,1,0:T(8,128)(2,1)S(1)}, bf16[4,128,512]{2,1,0:T(8,128)(2,1)S(1)}, u32[]{:S(2)}, u32[]{:S(2)}) collective-permute-start(bf16[4,128,512]{2,1,0:T(8,128)(2,1)S(1)} %pad_maximum_fusion), channel_id=1, source_target_pairs={{0,1},{1,0},{2,3},{3,2},{4,5},{5,4},{6,7},{7,6},{8,9},{9,8},{10,11... | collective-permute-start | bytes 1572872 | tf_op jit(solution)/shard_map/gather_value_grad/ppermute | solution.py:136
  41.9 1.3 %own_rows.1 = bf16[16,512]{1,0:T(8,128)(2,1)} custom-call(s32[1]{0:T(128)} %bitcast.20.q_ref, bf16[128,512]{1,0:T(8,128)(2,1)} %rows_ref.1, bf16[128,512]{1,0:T(8,128)(2,1)} %get-tuple-element.5.refs_0_._), custom_call_target="tpu_custom_call" | custom-call | tf_op jit(solution)/shard_map/gather_weight/own_rows/pallas_call | solution.py:204
  43.2 1.9 %collective-permute-start.4 = (bf16[1,16,512]{2,1,0:T(8,128)(2,1)}, bf16[1,16,512]{2,1,0:T(8,128)(2,1)S(1)}, u32[]{:S(2)}, u32[]{:S(2)}) collective-permute-start(bf16[1,16,512]{2,1,0:T(8,128)(2,1)} %bitcast.70), channel_id=1, source_target_pairs={{0,64},{64,128},{128,192},{192,256},{256,320},{320,384},{384,448},... | collective-permute-start | bytes 49160 | tf_op jit(solution)/shard_map/gather_weight/ppermute | solution.py:144
  45.3 6.0 %collective-permute-done.4 = bf16[1,16,512]{2,1,0:T(8,128)(2,1)S(1)} collective-permute-done((bf16[1,16,512]{2,1,0:T(8,128)(2,1)}, bf16[1,16,512]{2,1,0:T(8,128)(2,1)S(1)}, u32[]{:S(2)}, u32[]{:S(2)}) %collective-permute-start.4) | collective-permute-done | bytes 16416 | tf_op jit(solution)/shard_map/gather_weight/ppermute | solution.py:144
  52.0 1.9 %collective-permute-start.5 = (bf16[2,16,512]{2,1,0:T(8,128)(2,1)S(1)}, bf16[2,16,512]{2,1,0:T(8,128)(2,1)S(1)}, u32[]{:S(2)}, u32[]{:S(2)}) collective-permute-start(bf16[2,16,512]{2,1,0:T(8,128)(2,1)S(1)} %pad_maximum_fusion.3), channel_id=1, source_target_pairs={{0,128},{64,192},{128,256},{192,320},{256,384},{320,448},{384,2},{... | collective-permute-start | bytes 98312 | tf_op jit(solution)/shard_map/gather_weight/ppermute | solution.py:144
  54.6 1.6 %fusion = bf16[512,512]{0,1:T(8,128)(2,1)} fusion(bf16[8,128,512]{2,1,0:T(8,128)(2,1)S(1)} %place.1, bf16[8,128,512]{2,1,0:T(8,128)(2,1)S(1)} %all-to-all-done), kind=kOutput, calls=%fused_computation.10 | convolution fusion | flops 537133056 | bytes 2621440 | tf_op jit(solution)/shard_map/weight_term/dot_general | solution.py:233
  56.2 4.2 %all-to-all-start.1 = ((bf16[4,128,512]{2,1,0:T(8,128)(2,1)}), bf16[4,128,512]{2,1,0:T(8,128)(2,1)S(1)}, u32[]{:S(2)}, u32[]{:S(2)}) async-start(bf16[4,128,512]{2,1,0:T(8,128)(2,1)} %bitcast.35), calls=%async_computation.1 | async-start | bytes 1048576 | tf_op jit(solution)/shard_map/sum_x/all_to_all | solution.py:128
  60.3 4.0 %collective-permute-start.6 = (bf16[4,16,512]{2,1,0:T(8,128)(2,1)S(1)}, bf16[4,16,512]{2,1,0:T(8,128)(2,1)S(1)}, u32[]{:S(2)}, u32[]{:S(2)}) collective-permute-start(bf16[4,16,512]{2,1,0:T(8,128)(2,1)S(1)} %pad_maximum_fusion.2), channel_id=1, source_target_pairs={{0,256},{64,320},{128,384},{192,448},{256,2},{320,66},{384,130},{4... | collective-permute-start | bytes 196616 | tf_op jit(solution)/shard_map/gather_weight/ppermute | solution.py:144
  64.4 4.9 %collective-permute-done.6 = bf16[4,16,512]{2,1,0:T(8,128)(2,1)S(1)} collective-permute-done((bf16[4,16,512]{2,1,0:T(8,128)(2,1)S(1)}, bf16[4,16,512]{2,1,0:T(8,128)(2,1)S(1)}, u32[]{:S(2)}, u32[]{:S(2)}) %collective-permute-start.6) | collective-permute-done | bytes 65568 | tf_op jit(solution)/shard_map/gather_weight/ppermute | solution.py:144
  69.3 4.5 %collective-permute-start.9 = (bf16[128,512]{1,0:T(8,128)(2,1)S(1)}, bf16[128,512]{1,0:T(8,128)(2,1)S(1)}, u32[]{:S(2)}, u32[]{:S(2)}) collective-permute-start(bf16[128,512]{1,0:T(8,128)(2,1)S(1)} %bitcast.58), channel_id=1, source_target_pairs={{0,48},{16,0},{32,16},{48,32},{1,49},{17,1},{33,17},{49,33},{2,50}... | collective-permute-start | bytes 393224 | tf_op jit(solution)/shard_map/gather_weight/ppermute | solution.py:136
  73.9 2.5 %collective-permute-start.8 = (bf16[128,512]{1,0:T(8,128)(2,1)S(1)}, bf16[128,512]{1,0:T(8,128)(2,1)S(1)}, u32[]{:S(2)}, u32[]{:S(2)}) collective-permute-start(bf16[128,512]{1,0:T(8,128)(2,1)S(1)} %bitcast.59), channel_id=1, source_target_pairs={{0,32},{16,48},{32,0},{48,16},{1,33},{17,49},{33,1},{49,17},{2,34}... | collective-permute-start | bytes 393224 | tf_op jit(solution)/shard_map/gather_weight/ppermute | solution.py:136
  76.4 2.5 %collective-permute-start.7 = (bf16[128,512]{1,0:T(8,128)(2,1)S(1)}, bf16[128,512]{1,0:T(8,128)(2,1)S(1)}, u32[]{:S(2)}, u32[]{:S(2)}) collective-permute-start(bf16[128,512]{1,0:T(8,128)(2,1)S(1)} %bitcast.60), channel_id=1, source_target_pairs={{0,16},{16,32},{32,48},{48,0},{1,17},{17,33},{33,49},{49,1},{2,18}... | collective-permute-start | bytes 393224 | tf_op jit(solution)/shard_map/gather_weight/ppermute | solution.py:136
  79.0 2.1 %collective-permute-done.8.refs_2_ = bf16[128,512]{1,0:T(8,128)(2,1)S(1)} collective-permute-done((bf16[128,512]{1,0:T(8,128)(2,1)S(1)}, bf16[128,512]{1,0:T(8,128)(2,1)S(1)}, u32[]{:S(2)}, u32[]{:S(2)}) %collective-permute-start.8) | collective-permute-done | bytes 131104 | tf_op jit(solution)/shard_map/gather_weight/ppermute | solution.py:136
  81.1 3.7 %collective-permute-done.7.refs_1_ = bf16[128,512]{1,0:T(8,128)(2,1)S(1)} collective-permute-done((bf16[128,512]{1,0:T(8,128)(2,1)S(1)}, bf16[128,512]{1,0:T(8,128)(2,1)S(1)}, u32[]{:S(2)}, u32[]{:S(2)}) %collective-permute-start.7) | collective-permute-done | bytes 131104 | tf_op jit(solution)/shard_map/gather_weight/ppermute | solution.py:136
  86.3 11.2 %all-to-all-start.2 = ((bf16[16,16,512]{2,1,0:T(8,128)(2,1)}), bf16[16,16,512]{2,1,0:T(8,128)(2,1)S(1)}, u32[]{:S(2)}, u32[]{:S(2)}) async-start(bf16[16,16,512]{2,1,0:T(8,128)(2,1)} %bitcast.37), calls=%async_computation.2 | async-start | bytes 524288 | tf_op jit(solution)/shard_map/sum_z/all_to_all | solution.py:128
  98.3 4.9 %collective-permute-start.10 = (bf16[4,128,512]{2,1,0:T(8,128)(2,1)S(1)}, bf16[4,128,512]{2,1,0:T(8,128)(2,1)S(1)}, u32[]{:S(2)}, u32[]{:S(2)}) collective-permute-start(bf16[4,128,512]{2,1,0:T(8,128)(2,1)S(1)} %get-tuple-element.11), channel_id=1, source_target_pairs={{0,1},{1,0},{2,3},{3,2},{4,5},{5,4},{6,7},{7,6},{8,9},{9,8},{10,11... | collective-permute-start | bytes 1572872 | tf_op jit(solution)/shard_map/input_grad/ppermute | solution.py:136
  103.3 1.5 %collective-permute-done.10 = bf16[4,128,512]{2,1,0:T(8,128)(2,1)S(1)} collective-permute-done((bf16[4,128,512]{2,1,0:T(8,128)(2,1)S(1)}, bf16[4,128,512]{2,1,0:T(8,128)(2,1)S(1)}, u32[]{:S(2)}, u32[]{:S(2)}) %collective-permute-start.10) | collective-permute-done | bytes 524320 | tf_op jit(solution)/shard_map/input_grad/ppermute | solution.py:136
  104.9 2.0 %collective-permute-start.13 = (bf16[2,128,512]{2,1,0:T(8,128)(2,1)S(1)}, bf16[2,128,512]{2,1,0:T(8,128)(2,1)S(1)}, u32[]{:S(2)}, u32[]{:S(2)}) collective-permute-start(bf16[2,128,512]{2,1,0:T(8,128)(2,1)S(1)} %get-tuple-element.7), channel_id=1, source_target_pairs={{0,12},{4,0},{8,4},{12,8},{1,13},{5,1},{9,5},{13,9},{2,14},{6,2},{... | collective-permute-start | bytes 786440 | tf_op jit(solution)/shard_map/input_grad/ppermute | solution.py:136
  106.9 3.2 %collective-permute-start.11 = (bf16[2,128,512]{2,1,0:T(8,128)(2,1)S(1)}, bf16[2,128,512]{2,1,0:T(8,128)(2,1)S(1)}, u32[]{:S(2)}, u32[]{:S(2)}) collective-permute-start(bf16[2,128,512]{2,1,0:T(8,128)(2,1)S(1)} %get-tuple-element.9), channel_id=1, source_target_pairs={{0,4},{4,8},{8,12},{12,0},{1,5},{5,9},{9,13},{13,1},{2,6},{6,10},{... | collective-permute-start | bytes 786440 | tf_op jit(solution)/shard_map/input_grad/ppermute | solution.py:136
  110.2 2.5 %collective-permute-start.12 = (bf16[2,128,512]{2,1,0:T(8,128)(2,1)S(1)}, bf16[2,128,512]{2,1,0:T(8,128)(2,1)S(1)}, u32[]{:S(2)}, u32[]{:S(2)}) collective-permute-start(bf16[2,128,512]{2,1,0:T(8,128)(2,1)S(1)} %get-tuple-element.10), channel_id=1, source_target_pairs={{0,8},{4,12},{8,0},{12,4},{1,9},{5,13},{9,1},{13,5},{2,10},{6,14},... | collective-permute-start | bytes 786440 | tf_op jit(solution)/shard_map/input_grad/ppermute | solution.py:136
  113.4 7.7 %all-to-all-start.3 = ((f32[8,16,512]{2,1,0:T(8,128)}), f32[8,16,512]{2,1,0:T(8,128)S(1)}, u32[]{:S(2)}, u32[]{:S(2)}) async-start(f32[8,16,512]{2,1,0:T(8,128)} %broadcast_in_dim.31), calls=%async_computation.3 | async-start | bytes 524288 | tf_op jit(solution)/shard_map/share_rows/all_to_all | solution.py:128
  122.1 3.6 %from_pieces.1 = bf16[128,4096]{1,0:T(8,128)(2,1)} custom-call(s32[8]{0:T(128)S(1)} %stack.79.places_ref, bf16[2,128,512]{2,1,0:T(8,128)(2,1)S(1)} %get-tuple-element.8.refs_0_, bf16[2,128,512]{2,1,0:T(8,128)(2,1)S(1)} %collective-permute-done.11.refs_1_, bf16[2,128,512]{2,1,0:T(8,128)(2,1)S(1)} %collective-permute-done.12.refs_2_, ...), custom_call_target="tpu_custom_call" | custom-call | flops 4194304 | bytes 2097152 | tf_op jit(solution)/shard_map/input_grad/from_pieces/pallas_call | solution.py:113
  125.7 2.0 %all-to-all-done.3 = f32[8,16,512]{2,1,0:T(8,128)S(1)} async-done(((f32[8,16,512]{2,1,0:T(8,128)}), f32[8,16,512]{2,1,0:T(8,128)S(1)}, u32[]{:S(2)}, u32[]{:S(2)}) %all-to-all-start.3) | async-done | bytes 262176 | tf_op jit(solution)/shard_map/share_rows/all_to_all | solution.py:128
  (31 shorter events, 6.6 us)
Async XLA Ops:
  5.0 49.6 %all-to-all-start = ((bf16[8,128,512]{2,1,0:T(8,128)(2,1)}), bf16[8,128,512]{2,1,0:T(8,128)(2,1)S(1)}, u32[]{:S(2)}, u32[]{:S(2)}) async-start(bf16[8,128,512]{2,1,0:T(8,128)(2,1)} %to_pieces.1._), calls=%async_computation | async-start | bytes 2097152 | tf_op jit(solution)/shard_map/send_inputs/all_to_all | solution.py:128
  21.9 32.0 %copy-start = (bf16[128,512]{1,0:T(8,128)(2,1)S(1)}, bf16[128,512]{1,0:T(8,128)(2,1)}, u32[]{:S(2)}) copy-start(bf16[128,512]{1,0:T(8,128)(2,1)} %get-tuple-element.5.refs_0_._) | copy-start | bytes 393220
  21.9 9.8 %collective-permute-start.2 = (bf16[128,512]{1,0:T(8,128)(2,1)}, bf16[128,512]{1,0:T(8,128)(2,1)S(1)}, u32[]{:S(2)}, u32[]{:S(2)}) collective-permute-start(bf16[128,512]{1,0:T(8,128)(2,1)} %get-tuple-element.5.refs_0_._), channel_id=1, source_target_pairs={{0,12},{4,0},{8,4},{12,8},{1,13},{5,1},{9,5},{13,9},{2,14},{6,2},{... | collective-permute-start | bytes 393224 | tf_op jit(solution)/shard_map/gather_value_grad/ppermute | solution.py:136
  26.5 8.0 %collective-permute-start.1 = (bf16[128,512]{1,0:T(8,128)(2,1)}, bf16[128,512]{1,0:T(8,128)(2,1)S(1)}, u32[]{:S(2)}, u32[]{:S(2)}) collective-permute-start(bf16[128,512]{1,0:T(8,128)(2,1)} %get-tuple-element.5.refs_0_._), channel_id=1, source_target_pairs={{0,8},{4,12},{8,0},{12,4},{1,9},{5,13},{9,1},{13,5},{2,10},{6,14},... | collective-permute-start | bytes 393224 | tf_op jit(solution)/shard_map/gather_value_grad/ppermute | solution.py:136
  29.0 8.9 %collective-permute-start = (bf16[128,512]{1,0:T(8,128)(2,1)}, bf16[128,512]{1,0:T(8,128)(2,1)S(1)}, u32[]{:S(2)}, u32[]{:S(2)}) collective-permute-start(bf16[128,512]{1,0:T(8,128)(2,1)} %get-tuple-element.5.refs_0_._), channel_id=1, source_target_pairs={{0,4},{4,8},{8,12},{12,0},{1,5},{5,9},{9,13},{13,1},{2,6},{6,10},{... | collective-permute-start | bytes 393224 | tf_op jit(solution)/shard_map/gather_value_grad/ppermute | solution.py:136
  38.9 15.1 %collective-permute-start.3 = (bf16[4,128,512]{2,1,0:T(8,128)(2,1)S(1)}, bf16[4,128,512]{2,1,0:T(8,128)(2,1)S(1)}, u32[]{:S(2)}, u32[]{:S(2)}) collective-permute-start(bf16[4,128,512]{2,1,0:T(8,128)(2,1)S(1)} %pad_maximum_fusion), channel_id=1, source_target_pairs={{0,1},{1,0},{2,3},{3,2},{4,5},{5,4},{6,7},{7,6},{8,9},{9,8},{10,11... | collective-permute-start | bytes 1572872 | tf_op jit(solution)/shard_map/gather_value_grad/ppermute | solution.py:136
  43.2 8.0 %collective-permute-start.4 = (bf16[1,16,512]{2,1,0:T(8,128)(2,1)}, bf16[1,16,512]{2,1,0:T(8,128)(2,1)S(1)}, u32[]{:S(2)}, u32[]{:S(2)}) collective-permute-start(bf16[1,16,512]{2,1,0:T(8,128)(2,1)} %bitcast.70), channel_id=1, source_target_pairs={{0,64},{64,128},{128,192},{192,256},{256,320},{320,384},{384,448},... | collective-permute-start | bytes 49160 | tf_op jit(solution)/shard_map/gather_weight/ppermute | solution.py:144
  52.0 8.3 %collective-permute-start.5 = (bf16[2,16,512]{2,1,0:T(8,128)(2,1)S(1)}, bf16[2,16,512]{2,1,0:T(8,128)(2,1)S(1)}, u32[]{:S(2)}, u32[]{:S(2)}) collective-permute-start(bf16[2,16,512]{2,1,0:T(8,128)(2,1)S(1)} %pad_maximum_fusion.3), channel_id=1, source_target_pairs={{0,128},{64,192},{128,256},{192,320},{256,384},{320,448},{384,2},{... | collective-permute-start | bytes 98312 | tf_op jit(solution)/shard_map/gather_weight/ppermute | solution.py:144
  56.2 4.2 %copy-start.1 = (bf16[16,512]{1,0:T(8,128)(2,1)S(1)}, bf16[16,512]{1,0:T(8,128)(2,1)}, u32[]{:S(2)}) copy-start(bf16[16,512]{1,0:T(8,128)(2,1)} %own_rows.1) | copy-start | bytes 49156
  56.2 29.3 %all-to-all-start.1 = ((bf16[4,128,512]{2,1,0:T(8,128)(2,1)}), bf16[4,128,512]{2,1,0:T(8,128)(2,1)S(1)}, u32[]{:S(2)}, u32[]{:S(2)}) async-start(bf16[4,128,512]{2,1,0:T(8,128)(2,1)} %bitcast.35), calls=%async_computation.1 | async-start | bytes 1048576 | tf_op jit(solution)/shard_map/sum_x/all_to_all | solution.py:128
  60.3 9.0 %collective-permute-start.6 = (bf16[4,16,512]{2,1,0:T(8,128)(2,1)S(1)}, bf16[4,16,512]{2,1,0:T(8,128)(2,1)S(1)}, u32[]{:S(2)}, u32[]{:S(2)}) collective-permute-start(bf16[4,16,512]{2,1,0:T(8,128)(2,1)S(1)} %pad_maximum_fusion.2), channel_id=1, source_target_pairs={{0,256},{64,320},{128,384},{192,448},{256,2},{320,66},{384,130},{4... | collective-permute-start | bytes 196616 | tf_op jit(solution)/shard_map/gather_weight/ppermute | solution.py:144
  69.3 9.6 %collective-permute-start.9 = (bf16[128,512]{1,0:T(8,128)(2,1)S(1)}, bf16[128,512]{1,0:T(8,128)(2,1)S(1)}, u32[]{:S(2)}, u32[]{:S(2)}) collective-permute-start(bf16[128,512]{1,0:T(8,128)(2,1)S(1)} %bitcast.58), channel_id=1, source_target_pairs={{0,48},{16,0},{32,16},{48,32},{1,49},{17,1},{33,17},{49,33},{2,50}... | collective-permute-start | bytes 393224 | tf_op jit(solution)/shard_map/gather_weight/ppermute | solution.py:136
  73.9 7.2 %collective-permute-start.8 = (bf16[128,512]{1,0:T(8,128)(2,1)S(1)}, bf16[128,512]{1,0:T(8,128)(2,1)S(1)}, u32[]{:S(2)}, u32[]{:S(2)}) collective-permute-start(bf16[128,512]{1,0:T(8,128)(2,1)S(1)} %bitcast.59), channel_id=1, source_target_pairs={{0,32},{16,48},{32,0},{48,16},{1,33},{17,49},{33,1},{49,17},{2,34}... | collective-permute-start | bytes 393224 | tf_op jit(solution)/shard_map/gather_weight/ppermute | solution.py:136
  76.4 8.4 %collective-permute-start.7 = (bf16[128,512]{1,0:T(8,128)(2,1)S(1)}, bf16[128,512]{1,0:T(8,128)(2,1)S(1)}, u32[]{:S(2)}, u32[]{:S(2)}) collective-permute-start(bf16[128,512]{1,0:T(8,128)(2,1)S(1)} %bitcast.60), channel_id=1, source_target_pairs={{0,16},{16,32},{32,48},{48,0},{1,17},{17,33},{33,49},{49,1},{2,18}... | collective-permute-start | bytes 393224 | tf_op jit(solution)/shard_map/gather_weight/ppermute | solution.py:136
  86.3 26.3 %all-to-all-start.2 = ((bf16[16,16,512]{2,1,0:T(8,128)(2,1)}), bf16[16,16,512]{2,1,0:T(8,128)(2,1)S(1)}, u32[]{:S(2)}, u32[]{:S(2)}) async-start(bf16[16,16,512]{2,1,0:T(8,128)(2,1)} %bitcast.37), calls=%async_computation.2 | async-start | bytes 524288 | tf_op jit(solution)/shard_map/sum_z/all_to_all | solution.py:128
  98.3 6.4 %collective-permute-start.10 = (bf16[4,128,512]{2,1,0:T(8,128)(2,1)S(1)}, bf16[4,128,512]{2,1,0:T(8,128)(2,1)S(1)}, u32[]{:S(2)}, u32[]{:S(2)}) collective-permute-start(bf16[4,128,512]{2,1,0:T(8,128)(2,1)S(1)} %get-tuple-element.11), channel_id=1, source_target_pairs={{0,1},{1,0},{2,3},{3,2},{4,5},{5,4},{6,7},{7,6},{8,9},{9,8},{10,11... | collective-permute-start | bytes 1572872 | tf_op jit(solution)/shard_map/input_grad/ppermute | solution.py:136
  104.9 16.3 %collective-permute-start.13 = (bf16[2,128,512]{2,1,0:T(8,128)(2,1)S(1)}, bf16[2,128,512]{2,1,0:T(8,128)(2,1)S(1)}, u32[]{:S(2)}, u32[]{:S(2)}) collective-permute-start(bf16[2,128,512]{2,1,0:T(8,128)(2,1)S(1)} %get-tuple-element.7), channel_id=1, source_target_pairs={{0,12},{4,0},{8,4},{12,8},{1,13},{5,1},{9,5},{13,9},{2,14},{6,2},{... | collective-permute-start | bytes 786440 | tf_op jit(solution)/shard_map/input_grad/ppermute | solution.py:136
  106.9 14.3 %collective-permute-start.11 = (bf16[2,128,512]{2,1,0:T(8,128)(2,1)S(1)}, bf16[2,128,512]{2,1,0:T(8,128)(2,1)S(1)}, u32[]{:S(2)}, u32[]{:S(2)}) collective-permute-start(bf16[2,128,512]{2,1,0:T(8,128)(2,1)S(1)} %get-tuple-element.9), channel_id=1, source_target_pairs={{0,4},{4,8},{8,12},{12,0},{1,5},{5,9},{9,13},{13,1},{2,6},{6,10},{... | collective-permute-start | bytes 786440 | tf_op jit(solution)/shard_map/input_grad/ppermute | solution.py:136
  110.2 11.9 %collective-permute-start.12 = (bf16[2,128,512]{2,1,0:T(8,128)(2,1)S(1)}, bf16[2,128,512]{2,1,0:T(8,128)(2,1)S(1)}, u32[]{:S(2)}, u32[]{:S(2)}) collective-permute-start(bf16[2,128,512]{2,1,0:T(8,128)(2,1)S(1)} %get-tuple-element.10), channel_id=1, source_target_pairs={{0,8},{4,12},{8,0},{12,4},{1,9},{5,13},{9,1},{13,5},{2,10},{6,14},... | collective-permute-start | bytes 786440 | tf_op jit(solution)/shard_map/input_grad/ppermute | solution.py:136
  113.4 14.3 %all-to-all-start.3 = ((f32[8,16,512]{2,1,0:T(8,128)}), f32[8,16,512]{2,1,0:T(8,128)S(1)}, u32[]{:S(2)}, u32[]{:S(2)}) async-start(f32[8,16,512]{2,1,0:T(8,128)} %broadcast_in_dim.31), calls=%async_computation.3 | async-start | bytes 524288 | tf_op jit(solution)/shard_map/share_rows/all_to_all | solution.py:128

commit v3 on v1

v3 whole, which is shorter than its diff:
```python
import jax
import jax.numpy as jnp
from jax import lax
from jax.experimental import pallas as pl
from jax.experimental.pallas import tpu as pltpu
from jax.sharding import Mesh
from jax.sharding import PartitionSpec as P

ZL, XN, YN, ZH, CN = 8, 4, 4, 2, 2
TOK, WIDTH, KV, HD = 128, 4096, 512, 128
GROUP = 8
HALF = KV // CN
QUART = 128 // YN
HELD = ZL // CN
BF, F32 = jnp.bfloat16, jnp.float32
SMEM = pl.BlockSpec(memory_space=pltpu.SMEM)
VMEM = pl.BlockSpec(memory_space=pltpu.VMEM)
UNREAD = pl.BlockSpec(memory_space=pl.ANY)
SMALL = pltpu.CompilerParams(vmem_limit_bytes=20 << 20)


def nt(a, b):
    return lax.dot_general(a, b, (((1,), (1,)), ((), ())), preferred_element_type=F32)


def attend_kernel(length_ref, q_ref, k_ref, v_ref, g_ref, vg_ref, kg_ref):
    scaling = HD ** (-0.5)
    keys, vals = k_ref[...], v_ref[...]
    length = length_ref[0]
    step = 2
    wide = step * TOK
    pos_s = lax.broadcasted_iota(jnp.int32, (TOK, wide), 0)
    pos_t = lax.broadcasted_iota(jnp.int32, (TOK, wide), 1) & (TOK - 1)
    allowed = pos_s <= pos_t
    live = ((lax.broadcasted_iota(jnp.int32, (1, wide), 1) & (TOK - 1)) < length).astype(F32)
    vg = jnp.zeros((TOK, HD), F32)
    kg = jnp.zeros((TOK, HD), F32)
    for first in range(0, GROUP, step):
        heads = range(first, first + step)
        qs = jnp.concatenate([q_ref[:, h * HD : (h + 1) * HD] for h in heads], axis=0)
        gs = jnp.concatenate([g_ref[:, h * HD : (h + 1) * HD] for h in heads], axis=0)
        scores = jnp.where(allowed, nt(keys, qs) * scaling, F32(-1e30))
        expd = jnp.exp(scores - jnp.max(scores, axis=0, keepdims=True))
        probs = expd * (live / jnp.sum(expd, axis=0, keepdims=True))
        dprob = nt(vals, gs)
        delta = jnp.sum(probs * dprob, axis=0, keepdims=True)
        dscore = probs * (dprob - delta)
        vg += jnp.dot(probs.astype(BF), gs, preferred_element_type=F32)
        kg += jnp.dot(dscore.astype(BF), qs, preferred_element_type=F32)
    vg_ref[...] = vg.astype(BF)
    kg_ref[...] = (kg * scaling).astype(BF)


def attend_back(query, key_rows, value_rows, grad_rows, length):
    heads = KV // HD
    wide = pl.BlockSpec((TOK, GROUP * HD), lambda g: (0, g))
    thin = pl.BlockSpec((TOK, HD), lambda g: (0, g))
    return pl.pallas_call(
        attend_kernel,
        grid=(heads,),
        in_specs=[pl.BlockSpec(memory_space=pltpu.SMEM), wide, thin, thin, wide],
        out_specs=[thin, thin],
        out_shape=[jax.ShapeDtypeStruct((TOK, KV), BF)] * 2,
        cost_estimate=pl.CostEstimate(
            flops=10 * 32 * TOK * TOK * HD, bytes_accessed=3 << 20, transcendentals=32 * TOK * TOK
        ),
        name="attend",
    )(length, query, key_rows, value_rows, grad_rows)


def term_kernel(core_ref, own_ref, other_ref, own_grad_ref, other_grad_ref, out_ref):
    rows = jnp.concatenate([own_ref[...], other_ref[...]], axis=0)
    grads = jnp.concatenate([own_grad_ref[...], other_grad_ref[...]], axis=0)
    term = lax.dot_general(rows, grads, (((0,), (0,)), ((), ())), preferred_element_type=F32).astype(BF)
    for piece in range(XN * YN):
        out_ref[piece, 0] = term[piece * QUART : (piece + 1) * QUART]


def term_pieces(own, other, own_grad, other_grad, core):
    rows = pl.BlockSpec((TOK, XN * 128), lambda i, c: (0, i))
    grads = pl.BlockSpec((TOK, HALF), lambda i, c: (0, c[0]))
    return pl.pallas_call(
        term_kernel,
        grid_spec=pltpu.PrefetchScalarGridSpec(
            num_scalar_prefetch=1,
            grid=(ZL,),
            in_specs=[rows, rows, grads, grads],
            out_specs=pl.BlockSpec((XN * YN, 1, QUART, HALF), lambda i, c: (0, i, 0, 0)),
        ),
        out_shape=jax.ShapeDtypeStruct((XN * YN, ZL, QUART, HALF), BF),
        cost_estimate=pl.CostEstimate(flops=2 * 256 * WIDTH * HALF, bytes_accessed=4 << 20, transcendentals=0),
        compiler_params=SMALL,
        name="term_pieces",
    )(core[None].astype(jnp.int32), own, other, own_grad, other_grad)


def own_rows_kernel(at_ref, rows_ref, _, out_ref):
    out_ref[...] = rows_ref[...]


def own_rows(rows, y, earlier):
    return pl.pallas_call(
        own_rows_kernel,
        grid_spec=pltpu.PrefetchScalarGridSpec(
            num_scalar_prefetch=1,
            grid=(1,),
            in_specs=[pl.BlockSpec((QUART, KV), lambda i, at: (at[0], 0)), UNREAD],
            out_specs=pl.BlockSpec((QUART, KV), lambda i, at: (0, 0)),
        ),
        out_shape=jax.ShapeDtypeStruct((QUART, KV), BF),
        name="own_rows",
    )(y[None].astype(jnp.int32), rows, earlier)


def input_parts_kernel(at_ref, own_grad_ref, other_grad_ref, *refs):
    own_ref, other_ref, held = refs[-3:]
    k = pl.program_id(0)
    for i, ref in enumerate(refs[:-3]):
        first = ((at_ref[0] + YN - i) % YN) * QUART
        for j in range(XN):
            rows = ref[pl.ds(pl.multiple_of((j * HELD + k) * QUART, QUART), QUART), :]
            held[pl.ds(pl.multiple_of(j * 128 + first, QUART), QUART), :] = rows
    own_ref[...] = nt(own_grad_ref[...], held[...]).astype(BF)
    other_ref[...] = nt(other_grad_ref[...], held[...]).astype(BF)


def input_parts(own_grad, other_grad, weights, y):
    out = pl.BlockSpec((TOK, XN * 128), lambda k: (0, k))
    return pl.pallas_call(
        input_parts_kernel,
        grid=(HELD,),
        in_specs=[SMEM] + [VMEM] * (2 + YN),
        out_specs=[out, out],
        out_shape=[jax.ShapeDtypeStruct((TOK, WIDTH // CN), BF)] * 2,
        scratch_shapes=[pltpu.VMEM((XN * 128, KV), BF)],
        cost_estimate=pl.CostEstimate(flops=2 * 256 * 2048 * KV, bytes_accessed=4 << 20, transcendentals=0),
        compiler_params=SMALL,
        name="input_parts",
    )(y[None].astype(jnp.int32), own_grad, other_grad, *weights)


def merge_kernel(at_ref, own_ref, other_ref, out_ref):
    for which, ref in enumerate((own_ref, other_ref)):
        for k in range(HELD):
            for j in range(XN):
                zl = (at_ref[which] + ZL - k) % ZL
                tile = zl * XN + (at_ref[2] + XN - j) % XN
                first = (k * XN + j) * 128
                out_ref[:, pl.ds(pl.multiple_of(tile * 128, 128), 128)] = ref[:, first : first + 128]


def merge(own, other, zl, x, core):
    part = 32
    half = pl.BlockSpec((part, WIDTH // CN), lambda i: (i, 0))
    places = jnp.stack([(zl + ZL - HELD * core) % ZL, (zl + HELD + HELD * core) % ZL, x]).astype(jnp.int32)
    return pl.pallas_call(
        merge_kernel,
        grid=(TOK // part,),
        in_specs=[SMEM, half, half],
        out_specs=pl.BlockSpec((part, WIDTH), lambda i: (i, 0)),
        out_shape=jax.ShapeDtypeStruct((TOK, WIDTH), BF),
        cost_estimate=pl.CostEstimate(flops=0, bytes_accessed=2 << 20, transcendentals=0),
        compiler_params=SMALL,
        name="merge",
    )(places, own, other)


def exchange(array, axes):
    return lax.all_to_all(array, axes, 0, 0, tiled=True)


def spread(array, axes, count):
    return exchange(jnp.broadcast_to(array[None], (count,) + array.shape), axes)


def shifted(array, axis, by):
    count = lax.axis_size(axis)
    return lax.ppermute(array, axis, [(i, (i + by) % count) for i in range(count)])


def along_z(array, steps):
    pairs = []
    for z in range(ZH * ZL):
        for core, by in enumerate(steps):
            to = (z + by) % (ZH * ZL)
            pairs.append((((z % ZL) * ZH + z // ZL) * CN + core, ((to % ZL) * ZH + to // ZL) * CN + core))
    return lax.ppermute(array, ("zl", "zh", "core"), pairs)


def ring(array, axis):
    return [array] + [shifted(array, axis, by) for by in range(1, lax.axis_size(axis))]


def per_device(inputs, queries, keys, values, out_grad, lengths, value_weight):
    core, y, x, zl = (lax.axis_index(name) for name in ("core", "y", "x", "zl"))
    with jax.named_scope("swap_inputs"):
        other_inputs = shifted(inputs[0], "core", 1)
    with jax.named_scope("attention"):
        value_grad, key_grad = attend_back(queries[0], keys[0], values[0], out_grad[0], lengths)
    with jax.named_scope("swap_value_grad"):
        other_grad = shifted(value_grad, "core", 1)
    with jax.named_scope("weight_term"):
        term = term_pieces(inputs[0], other_inputs, value_grad, other_grad, core)
    with jax.named_scope("sum_xy"):
        got = exchange(term.reshape(XN * YN, ZL * QUART, HALF), ("x", "y"))
        plane = jnp.sum(got.astype(F32), axis=0).astype(BF).reshape(1, ZL, QUART, HALF)
    with jax.named_scope("sum_z"):
        both = jnp.broadcast_to(plane, (ZH, ZL, QUART, HALF)).reshape(ZH * ZL, QUART, HALF)
        got = exchange(both, ("zh", "zl"))
        total = jnp.sum(got.astype(F32), axis=0) * F32(1.0 / 512)
    with jax.named_scope("share_rows"):
        shared = spread(total, ("core", "y"), CN * YN).reshape(CN, YN * QUART, HALF)
        weight_grad = jnp.concatenate([shared[0], shared[1]], axis=1)
    with jax.named_scope("gather_weight"):
        rows = own_rows(value_weight, y, term)
        rows = jnp.concatenate([along_z(rows, (k, HELD + k if k == 0 else k - HELD)) for k in range(HELD)])
        rows = jnp.concatenate(ring(rows, "x"))
        weights = ring(rows, "y")
    with jax.named_scope("input_grad"):
        own_part, other_part = input_parts(value_grad, other_grad, weights, y)
        input_grad = merge(own_part, shifted(other_part, "core", 1), zl, x, core)
    return (input_grad[None], key_grad[None], weight_grad)


def solution(mesh):
    fine = Mesh(mesh.devices.reshape(ZL, XN, YN, ZH, CN), ("zl", "x", "y", "zh", "core"))
    micro = ("zl", "x", "y", "zh", "core")
    blk = ("zl", "x")
    rows = P(micro, None, None)
    return jax.shard_map(
        per_device,
        mesh=fine,
        in_specs=(rows, rows, rows, rows, rows, P(micro), P(blk, None)),
        out_specs=(rows, rows, P(blk, None)),
        check_vma=False,
    )
```

time: 165 us -> 133 us (0.81)
  waiting for transfers between devices: 63.6 us -> 38.1 us
  starting transfers between devices: 50.3 us -> 70.6 us
  between operations: 14.8 us -> 1.56 us
  blocking collectives: 10.7 us -> 0 us
  local copies, waits for them, and re-layouts: 9.58 us -> 2.44 us
  Pallas kernels: 11 us -> 16.2 us
  matrix products: 3.69 us -> 0 us
  other arithmetic: 0.13 us -> 2.74 us
    all_to_all x7 -> x3, waiting for transfers between devices: 62.8 us -> 7.57 us  [exchange(): return lax.all_to_all(array, axes, 0, 0, tiled=True)]
    ppermute x0 -> x13, starting transfers between devices: none -> 51.1 us  [the longest x9 31.2 us: shifted(): lax.ppermute(array, axis, [(i, (i + by) % count) for i in range(count)])]
    all_to_all x7 -> x3, starting transfers between devices: 50.3 us -> 19.5 us  [exchange(): return lax.all_to_all(array, axes, 0, 0, tiled=True)]
    ppermute x0 -> x13, waiting for transfers between devices: none -> 30.5 us  [the longest x9 29.2 us: shifted(): lax.ppermute(array, axis, [(i, (i + by) % count) for i in range(count)])]
    all_to_all x1 -> x0, blocking collectives: 10.7 us -> none  [exchange(): return lax.all_to_all(array, axes, 0, 0, tiled=True)]
    unnamed x17 -> x11, local copies, waits for them, and re-layouts: 5.78 us -> 0.95 us
    pallas_call x2 -> x4, Pallas kernels: 6 us -> 10.3 us  [the longest x1 4.46 us: term_pieces(): pl.pallas_call(term_kernel, grid_spec=pltpu.PrefetchScalarGridSpec(num_sc...]
    dot_general x2 -> x0, matrix products: 3.69 us -> none  [the longest x1 1.97 us: per_device(): lax.dot_general(columns.reshape(QN * TOK, KV), grads, (((0,), (0,)), ((),...]
  transfers between devices with their start and end apart: 8 -> 16, of which waited for: 8 -> 9; matrix products, arithmetic and copies ran while one was open for 3% -> 3% of each run, Pallas kernels for 4% -> 9%
where the time goes in v3:
time: 133 us; the launch traced here: 132 us
  starting transfers between devices  70.6 us (53%)
  waiting for transfers between devices  38.1 us (29%)
  Pallas kernels  16.2 us (12%)
  other arithmetic  2.74 us (2%)
  local copies, waits for them, and re-layouts  2.44 us (2%)
  between operations  1.56 us (1%)
    ppermute x9, starting transfers between devices, shifted(): lax.ppermute(array, axis, [(i, (i + by) % count) for i in range(count)])  31.2 us
    ppermute x9, waiting for transfers between devices, shifted(): lax.ppermute(array, axis, [(i, (i + by) % count) for i in range(count)])  29.2 us
    ppermute x4, starting transfers between devices, along_z(): return lax.ppermute(array, ('zl', 'zh', 'core'), pairs)  19.9 us
    all_to_all x3, starting transfers between devices, exchange(): return lax.all_to_all(array, axes, 0, 0, tiled=True)  19.5 us
    all_to_all x3, waiting for transfers between devices, exchange(): return lax.all_to_all(array, axes, 0, 0, tiled=True)  7.57 us
    pallas_call x1, Pallas kernels, attend_back(): pl.pallas_call(attend_kernel, grid=(heads,), in_specs=[pl.BlockSpec(memor...  5.9 us
    pallas_call x1, Pallas kernels, term_pieces(): pl.pallas_call(term_kernel, grid_spec=pltpu.PrefetchScalarGridSpec(num_sc...  4.46 us
  transfers between devices with their start and end apart: 16, of which 9 were waited for; matrix products, arithmetic and copies ran while one was open for 3% of the time, Pallas kernels for 9%

profile of v3, /device:TPU:1, one launch (start us, length us, event | category | flops | bytes accessed | tf_op | source)
XLA Modules:
  0.0 131.7 jit_solution(12881492662771682686)
XLA Ops:
  0.6 8.9 %collective-permute-start.1 = (bf16[128,4096]{1,0:T(8,128)(2,1)}, bf16[128,4096]{1,0:T(8,128)(2,1)S(1)}, u32[]{:S(2)}, u32[]{:S(2)}) collective-permute-start(bf16[128,4096]{1,0:T(8,128)(2,1)} %bitcast.17), channel_id=1, source_target_pairs={{0,1},{1,0},{2,3},{3,2},{4,5},{5,4},{6,7},{7,6},{8,9},{9,8},{10,11... | collective-permute-start | bytes 3145736 | tf_op jit(solution)/shard_map/swap_inputs/ppermute | solution.py:178
  10.2 5.9 %attend.1 = (bf16[128,512]{1,0:T(8,128)(2,1)}, bf16[128,512]{1,0:T(8,128)(2,1)}) custom-call(s32[1]{0:T(128)S(6)} %copy.19.length_ref, bf16[128,4096]{1,0:T(8,128)(2,1)} %bitcast.23, bf16[128,512]{1,0:T(8,128)(2,1)} %bitcast.25, bf16[128,512]{1,0:T(8,128)(2,1)} %bitcast.26, bf16[128,4096]{1,0:T(8,128)(2,1)} %bitcast.24), custom_call_target="tpu_custom_call" | custom-call | flops 671088640 | bytes 3145728 | tf_op jit(solution)/shard_map/attention/attend/pallas_call | solution.py:58
  16.1 1.9 %collective-permute-start = (bf16[128,512]{1,0:T(8,128)(2,1)}, bf16[128,512]{1,0:T(8,128)(2,1)S(1)}, u32[]{:S(2)}, u32[]{:S(2)}) collective-permute-start(bf16[128,512]{1,0:T(8,128)(2,1)} %get-tuple-element.7.own_grad_ref), channel_id=1, source_target_pairs={{0,1},{1,0},{2,3},{3,2},{4,5},{5,4},{6,7},{7,6},{8,9},{9,8},{10,11... | collective-permute-start | bytes 393224 | tf_op jit(solution)/shard_map/swap_value_grad/ppermute | solution.py:178
  18.0 1.5 %collective-permute-done.other_grad_ref = bf16[128,512]{1,0:T(8,128)(2,1)S(1)} collective-permute-done((bf16[128,512]{1,0:T(8,128)(2,1)}, bf16[128,512]{1,0:T(8,128)(2,1)S(1)}, u32[]{:S(2)}, u32[]{:S(2)}) %collective-permute-start) | collective-permute-done | bytes 131104 | tf_op jit(solution)/shard_map/swap_value_grad/ppermute | solution.py:178
  19.6 0.9 copy-done.1
  20.5 4.5 %term_pieces.1._ = bf16[16,8,32,256]{3,2,1,0:T(8,128)(2,1)} custom-call(s32[1]{0:T(128)} %bitcast.8.core_ref, bf16[128,4096]{1,0:T(8,128)(2,1)S(1)} %bitcast.18, bf16[128,4096]{1,0:T(8,128)(2,1)S(1)} %collective-permute-done.1.other_ref, bf16[128,512]{1,0:T(8,128)(2,1)S(1)} %copy-done.1, bf16[128,512]{1,0:T(8,128)(2,1)S(1)} %collective-permute-done.other_grad_ref), custom_call_target="tpu_custom_call" | custom-call | flops 536870912 | bytes 4194304 | tf_op jit(solution)/shard_map/weight_term/term_pieces/pallas_call | solution.py:82
  24.9 4.4 %all-to-all-start = ((bf16[16,256,256]{2,1,0:T(8,128)(2,1)}), bf16[16,256,256]{2,1,0:T(8,128)(2,1)}, u32[]{:S(2)}, u32[]{:S(2)}) async-start(bf16[16,256,256]{2,1,0:T(8,128)(2,1)} %bitcast.12), calls=%async_computation | async-start | bytes 4194304 | tf_op jit(solution)/shard_map/sum_xy/all_to_all | solution.py:169
  29.4 1.4 %own_rows.1 = bf16[32,512]{1,0:T(8,128)(2,1)} custom-call(s32[1]{0:T(128)} %bitcast.3.at_ref, bf16[128,512]{1,0:T(8,128)(2,1)} %rows_ref.1, bf16[16,8,32,256]{3,2,1,0:T(8,128)(2,1)} %term_pieces.1._), custom_call_target="tpu_custom_call" | custom-call | tf_op jit(solution)/shard_map/gather_weight/own_rows/pallas_call | solution.py:102
  30.8 5.8 %collective-permute-start.2 = (bf16[32,512]{1,0:T(8,128)(2,1)}, bf16[32,512]{1,0:T(8,128)(2,1)S(1)}, u32[]{:S(2)}, u32[]{:S(2)}) collective-permute-start(bf16[32,512]{1,0:T(8,128)(2,1)} %own_rows.1), channel_id=1, source_target_pairs={{0,0},{1,257},{64,64},{65,321},{128,128},{129,385},{192,192},{193,... | collective-permute-start | bytes 98312 | tf_op jit(solution)/shard_map/gather_weight/ppermute | solution.py:187
  36.6 4.2 %collective-permute-start.5 = (bf16[32,512]{1,0:T(8,128)(2,1)}, bf16[32,512]{1,0:T(8,128)(2,1)S(1)}, u32[]{:S(2)}, u32[]{:S(2)}) collective-permute-start(bf16[32,512]{1,0:T(8,128)(2,1)} %own_rows.1), channel_id=1, source_target_pairs={{0,192},{1,451},{64,256},{65,1},{128,320},{129,65},{192,384},{193,... | collective-permute-start | bytes 98312 | tf_op jit(solution)/shard_map/gather_weight/ppermute | solution.py:187
  40.8 3.1 %collective-permute-start.4 = (bf16[32,512]{1,0:T(8,128)(2,1)}, bf16[32,512]{1,0:T(8,128)(2,1)S(1)}, u32[]{:S(2)}, u32[]{:S(2)}) collective-permute-start(bf16[32,512]{1,0:T(8,128)(2,1)} %own_rows.1), channel_id=1, source_target_pairs={{0,128},{1,387},{64,192},{65,451},{128,256},{129,1},{192,320},{193... | collective-permute-start | bytes 98312 | tf_op jit(solution)/shard_map/gather_weight/ppermute | solution.py:187
  43.9 6.8 %collective-permute-start.3 = (bf16[32,512]{1,0:T(8,128)(2,1)}, bf16[32,512]{1,0:T(8,128)(2,1)S(1)}, u32[]{:S(2)}, u32[]{:S(2)}) collective-permute-start(bf16[32,512]{1,0:T(8,128)(2,1)} %own_rows.1), channel_id=1, source_target_pairs={{0,64},{1,323},{64,128},{65,387},{128,192},{129,451},{192,256},{19... | collective-permute-start | bytes 98312 | tf_op jit(solution)/shard_map/gather_weight/ppermute | solution.py:187
  50.7 1.3 collective-permute-done.3
  52.1 3.2 %collective-permute-start.6 = (bf16[128,512]{1,0:T(8,128)(2,1)S(1)}, bf16[128,512]{1,0:T(8,128)(2,1)S(1)}, u32[]{:S(2)}, u32[]{:S(2)}) collective-permute-start(bf16[128,512]{1,0:T(8,128)(2,1)S(1)} %get-tuple-element.13), channel_id=1, source_target_pairs={{0,16},{16,32},{32,48},{48,0},{1,17},{17,33},{33,49},{49,1},{2,18}... | collective-permute-start | bytes 393224 | tf_op jit(solution)/shard_map/gather_weight/ppermute | solution.py:178
  55.3 3.4 %all-to-all-done = bf16[16,256,256]{2,1,0:T(8,128)(2,1)} async-done(((bf16[16,256,256]{2,1,0:T(8,128)(2,1)}), bf16[16,256,256]{2,1,0:T(8,128)(2,1)}, u32[]{:S(2)}, u32[]{:S(2)}) %all-to-all-start) | async-done | bytes 2097184 | tf_op jit(solution)/shard_map/sum_xy/all_to_all | solution.py:169
  58.7 1.9 %reduce_sum.21 = bf16[256,256]{1,0:T(8,128)(2,1)S(1)} reduce(bf16[16,256,256]{2,1,0:T(8,128)(2,1)} %all-to-all-done, bf16[]{:T(256)} %constant.41.clone.1), dimensions={0}, to_apply=%region_0.0 | reduce | flops 983040 | bytes 2228226 | tf_op jit(solution)/shard_map/sum_xy/reduce_sum | solution.py:206
  61.4 11.7 %all-to-all-start.1 = ((bf16[16,32,256]{2,1,0:T(8,128)(2,1)}), bf16[16,32,256]{2,1,0:T(8,128)(2,1)S(1)}, u32[]{:S(2)}, u32[]{:S(2)}) async-start(bf16[16,32,256]{2,1,0:T(8,128)(2,1)} %bitcast.14), calls=%async_computation.1 | async-start | bytes 524288 | tf_op jit(solution)/shard_map/sum_z/all_to_all | solution.py:169
  73.1 2.5 %collective-permute-start.7 = (bf16[128,512]{1,0:T(8,128)(2,1)S(1)}, bf16[128,512]{1,0:T(8,128)(2,1)S(1)}, u32[]{:S(2)}, u32[]{:S(2)}) collective-permute-start(bf16[128,512]{1,0:T(8,128)(2,1)S(1)} %get-tuple-element.13), channel_id=1, source_target_pairs={{0,32},{16,48},{32,0},{48,16},{1,33},{17,49},{33,1},{49,17},{2,34}... | collective-permute-start | bytes 393224 | tf_op jit(solution)/shard_map/gather_weight/ppermute | solution.py:178
  75.5 3.1 %collective-permute-start.8 = (bf16[128,512]{1,0:T(8,128)(2,1)S(1)}, bf16[128,512]{1,0:T(8,128)(2,1)S(1)}, u32[]{:S(2)}, u32[]{:S(2)}) collective-permute-start(bf16[128,512]{1,0:T(8,128)(2,1)S(1)} %get-tuple-element.13), channel_id=1, source_target_pairs={{0,48},{16,0},{32,16},{48,32},{1,49},{17,1},{33,17},{49,33},{2,50}... | collective-permute-start | bytes 393224 | tf_op jit(solution)/shard_map/gather_weight/ppermute | solution.py:178
  78.6 1.7 %collective-permute-done.7 = bf16[128,512]{1,0:T(8,128)(2,1)S(1)} collective-permute-done((bf16[128,512]{1,0:T(8,128)(2,1)S(1)}, bf16[128,512]{1,0:T(8,128)(2,1)S(1)}, u32[]{:S(2)}, u32[]{:S(2)}) %collective-permute-start.7) | collective-permute-done | bytes 131104 | tf_op jit(solution)/shard_map/gather_weight/ppermute | solution.py:178
  80.3 2.2 %collective-permute-done.8 = bf16[128,512]{1,0:T(8,128)(2,1)S(1)} collective-permute-done((bf16[128,512]{1,0:T(8,128)(2,1)S(1)}, bf16[128,512]{1,0:T(8,128)(2,1)S(1)}, u32[]{:S(2)}, u32[]{:S(2)}) %collective-permute-start.8) | collective-permute-done | bytes 131104 | tf_op jit(solution)/shard_map/gather_weight/ppermute | solution.py:178
  82.5 4.6 %collective-permute-start.11 = (bf16[512,512]{1,0:T(8,128)(2,1)S(1)}, bf16[512,512]{1,0:T(8,128)(2,1)S(1)}, u32[]{:S(2)}, u32[]{:S(2)}) collective-permute-start(bf16[512,512]{1,0:T(8,128)(2,1)S(1)} %constant_dynamic-update-slice_fusion.4.refs_0_), channel_id=1, source_target_pairs={{0,12},{4,0},{8,4},{12,8},{1,13},{5,1},{9,5},{13,9},{2,14},{6,2},{... | collective-permute-start | bytes 1572872 | tf_op jit(solution)/shard_map/gather_weight/ppermute | solution.py:178
  87.1 1.9 %collective-permute-start.10 = (bf16[512,512]{1,0:T(8,128)(2,1)S(1)}, bf16[512,512]{1,0:T(8,128)(2,1)S(1)}, u32[]{:S(2)}, u32[]{:S(2)}) collective-permute-start(bf16[512,512]{1,0:T(8,128)(2,1)S(1)} %constant_dynamic-update-slice_fusion.4.refs_0_), channel_id=1, source_target_pairs={{0,8},{4,12},{8,0},{12,4},{1,9},{5,13},{9,1},{13,5},{2,10},{6,14},... | collective-permute-start | bytes 1572872 | tf_op jit(solution)/shard_map/gather_weight/ppermute | solution.py:178
  89.1 2.7 %collective-permute-start.9 = (bf16[512,512]{1,0:T(8,128)(2,1)S(1)}, bf16[512,512]{1,0:T(8,128)(2,1)S(1)}, u32[]{:S(2)}, u32[]{:S(2)}) collective-permute-start(bf16[512,512]{1,0:T(8,128)(2,1)S(1)} %constant_dynamic-update-slice_fusion.4.refs_0_), channel_id=1, source_target_pairs={{0,4},{4,8},{8,12},{12,0},{1,5},{5,9},{9,13},{13,1},{2,6},{6,10},{... | collective-permute-start | bytes 1572872 | tf_op jit(solution)/shard_map/gather_weight/ppermute | solution.py:178
  91.8 5.1 %collective-permute-done.11.refs_3_ = bf16[512,512]{1,0:T(8,128)(2,1)S(1)} collective-permute-done((bf16[512,512]{1,0:T(8,128)(2,1)S(1)}, bf16[512,512]{1,0:T(8,128)(2,1)S(1)}, u32[]{:S(2)}, u32[]{:S(2)}) %collective-permute-start.11) | collective-permute-done | bytes 524320 | tf_op jit(solution)/shard_map/gather_weight/ppermute | solution.py:178
  96.9 4.1 %collective-permute-done.10.refs_2_ = bf16[512,512]{1,0:T(8,128)(2,1)S(1)} collective-permute-done((bf16[512,512]{1,0:T(8,128)(2,1)S(1)}, bf16[512,512]{1,0:T(8,128)(2,1)S(1)}, u32[]{:S(2)}, u32[]{:S(2)}) %collective-permute-start.10) | collective-permute-done | bytes 524320 | tf_op jit(solution)/shard_map/gather_weight/ppermute | solution.py:178
  101.0 14.6 %collective-permute-done.9.refs_1_ = bf16[512,512]{1,0:T(8,128)(2,1)S(1)} collective-permute-done((bf16[512,512]{1,0:T(8,128)(2,1)S(1)}, bf16[512,512]{1,0:T(8,128)(2,1)S(1)}, u32[]{:S(2)}, u32[]{:S(2)}) %collective-permute-start.9) | collective-permute-done | bytes 524320 | tf_op jit(solution)/shard_map/gather_weight/ppermute | solution.py:178
  115.6 2.2 %input_parts.1 = (bf16[128,2048]{1,0:T(8,128)(2,1)S(1)}, bf16[128,2048]{1,0:T(8,128)(2,1)S(1)}) custom-call(s32[1]{0:T(128)} %bitcast.3.at_ref, bf16[128,512]{1,0:T(8,128)(2,1)S(1)} %copy-done.2, bf16[128,512]{1,0:T(8,128)(2,1)S(1)} %collective-permute-done.other_grad_ref, bf16[512,512]{1,0:T(8,128)(2,1)S(1)} %constant_dynamic-update-slice_fusion.4.refs_0_, ...), custom_call_target="tpu_custom_call" | custom-call | flops 536870912 | bytes 4194304 | tf_op jit(solution)/shard_map/input_grad/input_parts/pallas_call | solution.py:129
  117.8 2.4 %collective-permute-start.12 = (bf16[128,2048]{1,0:T(8,128)(2,1)S(1)}, bf16[128,2048]{1,0:T(8,128)(2,1)S(1)}, u32[]{:S(2)}, u32[]{:S(2)}) collective-permute-start(bf16[128,2048]{1,0:T(8,128)(2,1)S(1)} %get-tuple-element.9), channel_id=1, source_target_pairs={{0,1},{1,0},{2,3},{3,2},{4,5},{5,4},{6,7},{7,6},{8,9},{9,8},{10,11... | collective-permute-start | bytes 1572872 | tf_op jit(solution)/shard_map/input_grad/ppermute | solution.py:178
  121.0 3.4 %all-to-all-start.2 = ((f32[8,32,256]{2,1,0:T(8,128)}), f32[8,32,256]{2,1,0:T(8,128)S(1)}, u32[]{:S(2)}, u32[]{:S(2)}) async-start(f32[8,32,256]{2,1,0:T(8,128)} %broadcast_in_dim.32), calls=%async_computation.2 | async-start | bytes 524288 | tf_op jit(solution)/shard_map/share_rows/all_to_all | solution.py:169
  124.5 2.3 %merge.1 = bf16[128,4096]{1,0:T(8,128)(2,1)} custom-call(s32[3]{0:T(128)S(1)} %pad_add_fusion.at_ref, bf16[128,2048]{1,0:T(8,128)(2,1)S(1)} %get-tuple-element.8.own_ref, bf16[128,2048]{1,0:T(8,128)(2,1)S(1)} %collective-permute-done.12.other_ref), custom_call_target="tpu_custom_call" | custom-call | bytes 2097152 | tf_op jit(solution)/shard_map/input_grad/merge/pallas_call | solution.py:156
  126.8 4.1 %all-to-all-done.2 = f32[8,32,256]{2,1,0:T(8,128)S(1)} async-done(((f32[8,32,256]{2,1,0:T(8,128)}), f32[8,32,256]{2,1,0:T(8,128)S(1)}, u32[]{:S(2)}, u32[]{:S(2)}) %all-to-all-start.2) | async-done | bytes 262176 | tf_op jit(solution)/shard_map/share_rows/all_to_all | solution.py:169
  (26 shorter events, 2.4 us)
Async XLA Ops:
  0.6 18.9 %copy-start = (bf16[1,128,4096]{2,1,0:T(8,128)(2,1)S(1)}, bf16[1,128,4096]{2,1,0:T(8,128)(2,1)}, u32[]{:S(2)}) copy-start(bf16[1,128,4096]{2,1,0:T(8,128)(2,1)} %param.7) | copy-start | bytes 3145732
  0.6 18.9 %collective-permute-start.1 = (bf16[128,4096]{1,0:T(8,128)(2,1)}, bf16[128,4096]{1,0:T(8,128)(2,1)S(1)}, u32[]{:S(2)}, u32[]{:S(2)}) collective-permute-start(bf16[128,4096]{1,0:T(8,128)(2,1)} %bitcast.17), channel_id=1, source_target_pairs={{0,1},{1,0},{2,3},{3,2},{4,5},{5,4},{6,7},{7,6},{8,9},{9,8},{10,11... | collective-permute-start | bytes 3145736 | tf_op jit(solution)/shard_map/swap_inputs/ppermute | solution.py:178
  16.1 3.4 %collective-permute-start = (bf16[128,512]{1,0:T(8,128)(2,1)}, bf16[128,512]{1,0:T(8,128)(2,1)S(1)}, u32[]{:S(2)}, u32[]{:S(2)}) collective-permute-start(bf16[128,512]{1,0:T(8,128)(2,1)} %get-tuple-element.7.own_grad_ref), channel_id=1, source_target_pairs={{0,1},{1,0},{2,3},{3,2},{4,5},{5,4},{6,7},{7,6},{8,9},{9,8},{10,11... | collective-permute-start | bytes 393224 | tf_op jit(solution)/shard_map/swap_value_grad/ppermute | solution.py:178
  19.6 0.9 copy-start.1
  24.9 33.8 %all-to-all-start = ((bf16[16,256,256]{2,1,0:T(8,128)(2,1)}), bf16[16,256,256]{2,1,0:T(8,128)(2,1)}, u32[]{:S(2)}, u32[]{:S(2)}) async-start(bf16[16,256,256]{2,1,0:T(8,128)(2,1)} %bitcast.12), calls=%async_computation | async-start | bytes 4194304 | tf_op jit(solution)/shard_map/sum_xy/all_to_all | solution.py:169
  30.8 20.0 %collective-permute-start.2 = (bf16[32,512]{1,0:T(8,128)(2,1)}, bf16[32,512]{1,0:T(8,128)(2,1)S(1)}, u32[]{:S(2)}, u32[]{:S(2)}) collective-permute-start(bf16[32,512]{1,0:T(8,128)(2,1)} %own_rows.1), channel_id=1, source_target_pairs={{0,0},{1,257},{64,64},{65,321},{128,128},{129,385},{192,192},{193,... | collective-permute-start | bytes 98312 | tf_op jit(solution)/shard_map/gather_weight/ppermute | solution.py:187
  36.6 15.5 %collective-permute-start.5 = (bf16[32,512]{1,0:T(8,128)(2,1)}, bf16[32,512]{1,0:T(8,128)(2,1)S(1)}, u32[]{:S(2)}, u32[]{:S(2)}) collective-permute-start(bf16[32,512]{1,0:T(8,128)(2,1)} %own_rows.1), channel_id=1, source_target_pairs={{0,192},{1,451},{64,256},{65,1},{128,320},{129,65},{192,384},{193,... | collective-permute-start | bytes 98312 | tf_op jit(solution)/shard_map/gather_weight/ppermute | solution.py:187
  40.8 11.2 %collective-permute-start.4 = (bf16[32,512]{1,0:T(8,128)(2,1)}, bf16[32,512]{1,0:T(8,128)(2,1)S(1)}, u32[]{:S(2)}, u32[]{:S(2)}) collective-permute-start(bf16[32,512]{1,0:T(8,128)(2,1)} %own_rows.1), channel_id=1, source_target_pairs={{0,128},{1,387},{64,192},{65,451},{128,256},{129,1},{192,320},{193... | collective-permute-start | bytes 98312 | tf_op jit(solution)/shard_map/gather_weight/ppermute | solution.py:187
  43.9 8.1 %collective-permute-start.3 = (bf16[32,512]{1,0:T(8,128)(2,1)}, bf16[32,512]{1,0:T(8,128)(2,1)S(1)}, u32[]{:S(2)}, u32[]{:S(2)}) collective-permute-start(bf16[32,512]{1,0:T(8,128)(2,1)} %own_rows.1), channel_id=1, source_target_pairs={{0,64},{1,323},{64,128},{65,387},{128,192},{129,451},{192,256},{19... | collective-permute-start | bytes 98312 | tf_op jit(solution)/shard_map/gather_weight/ppermute | solution.py:187
  52.0 63.6 %copy-start.2 = (bf16[128,512]{1,0:T(8,128)(2,1)S(1)}, bf16[128,512]{1,0:T(8,128)(2,1)}, u32[]{:S(2)}) copy-start(bf16[128,512]{1,0:T(8,128)(2,1)} %get-tuple-element.7.own_grad_ref) | copy-start | bytes 393220
  52.1 26.5 %collective-permute-start.6 = (bf16[128,512]{1,0:T(8,128)(2,1)S(1)}, bf16[128,512]{1,0:T(8,128)(2,1)S(1)}, u32[]{:S(2)}, u32[]{:S(2)}) collective-permute-start(bf16[128,512]{1,0:T(8,128)(2,1)S(1)} %get-tuple-element.13), channel_id=1, source_target_pairs={{0,16},{16,32},{32,48},{48,0},{1,17},{17,33},{33,49},{49,1},{2,18}... | collective-permute-start | bytes 393224 | tf_op jit(solution)/shard_map/gather_weight/ppermute | solution.py:178
  61.4 58.9 %all-to-all-start.1 = ((bf16[16,32,256]{2,1,0:T(8,128)(2,1)}), bf16[16,32,256]{2,1,0:T(8,128)(2,1)S(1)}, u32[]{:S(2)}, u32[]{:S(2)}) async-start(bf16[16,32,256]{2,1,0:T(8,128)(2,1)} %bitcast.14), calls=%async_computation.1 | async-start | bytes 524288 | tf_op jit(solution)/shard_map/sum_z/all_to_all | solution.py:169
  73.1 7.2 %collective-permute-start.7 = (bf16[128,512]{1,0:T(8,128)(2,1)S(1)}, bf16[128,512]{1,0:T(8,128)(2,1)S(1)}, u32[]{:S(2)}, u32[]{:S(2)}) collective-permute-start(bf16[128,512]{1,0:T(8,128)(2,1)S(1)} %get-tuple-element.13), channel_id=1, source_target_pairs={{0,32},{16,48},{32,0},{48,16},{1,33},{17,49},{33,1},{49,17},{2,34}... | collective-permute-start | bytes 393224 | tf_op jit(solution)/shard_map/gather_weight/ppermute | solution.py:178
  75.5 6.9 %collective-permute-start.8 = (bf16[128,512]{1,0:T(8,128)(2,1)S(1)}, bf16[128,512]{1,0:T(8,128)(2,1)S(1)}, u32[]{:S(2)}, u32[]{:S(2)}) collective-permute-start(bf16[128,512]{1,0:T(8,128)(2,1)S(1)} %get-tuple-element.13), channel_id=1, source_target_pairs={{0,48},{16,0},{32,16},{48,32},{1,49},{17,1},{33,17},{49,33},{2,50}... | collective-permute-start | bytes 393224 | tf_op jit(solution)/shard_map/gather_weight/ppermute | solution.py:178
  82.5 14.4 %collective-permute-start.11 = (bf16[512,512]{1,0:T(8,128)(2,1)S(1)}, bf16[512,512]{1,0:T(8,128)(2,1)S(1)}, u32[]{:S(2)}, u32[]{:S(2)}) collective-permute-start(bf16[512,512]{1,0:T(8,128)(2,1)S(1)} %constant_dynamic-update-slice_fusion.4.refs_0_), channel_id=1, source_target_pairs={{0,12},{4,0},{8,4},{12,8},{1,13},{5,1},{9,5},{13,9},{2,14},{6,2},{... | collective-permute-start | bytes 1572872 | tf_op jit(solution)/shard_map/gather_weight/ppermute | solution.py:178
  87.1 13.9 %collective-permute-start.10 = (bf16[512,512]{1,0:T(8,128)(2,1)S(1)}, bf16[512,512]{1,0:T(8,128)(2,1)S(1)}, u32[]{:S(2)}, u32[]{:S(2)}) collective-permute-start(bf16[512,512]{1,0:T(8,128)(2,1)S(1)} %constant_dynamic-update-slice_fusion.4.refs_0_), channel_id=1, source_target_pairs={{0,8},{4,12},{8,0},{12,4},{1,9},{5,13},{9,1},{13,5},{2,10},{6,14},... | collective-permute-start | bytes 1572872 | tf_op jit(solution)/shard_map/gather_weight/ppermute | solution.py:178
  89.1 26.6 %collective-permute-start.9 = (bf16[512,512]{1,0:T(8,128)(2,1)S(1)}, bf16[512,512]{1,0:T(8,128)(2,1)S(1)}, u32[]{:S(2)}, u32[]{:S(2)}) collective-permute-start(bf16[512,512]{1,0:T(8,128)(2,1)S(1)} %constant_dynamic-update-slice_fusion.4.refs_0_), channel_id=1, source_target_pairs={{0,4},{4,8},{8,12},{12,0},{1,5},{5,9},{9,13},{13,1},{2,6},{6,10},{... | collective-permute-start | bytes 1572872 | tf_op jit(solution)/shard_map/gather_weight/ppermute | solution.py:178
  117.8 6.7 %collective-permute-start.12 = (bf16[128,2048]{1,0:T(8,128)(2,1)S(1)}, bf16[128,2048]{1,0:T(8,128)(2,1)S(1)}, u32[]{:S(2)}, u32[]{:S(2)}) collective-permute-start(bf16[128,2048]{1,0:T(8,128)(2,1)S(1)} %get-tuple-element.9), channel_id=1, source_target_pairs={{0,1},{1,0},{2,3},{3,2},{4,5},{5,4},{6,7},{7,6},{8,9},{9,8},{10,11... | collective-permute-start | bytes 1572872 | tf_op jit(solution)/shard_map/input_grad/ppermute | solution.py:178
  121.0 9.9 %all-to-all-start.2 = ((f32[8,32,256]{2,1,0:T(8,128)}), f32[8,32,256]{2,1,0:T(8,128)S(1)}, u32[]{:S(2)}, u32[]{:S(2)}) async-start(f32[8,32,256]{2,1,0:T(8,128)} %broadcast_in_dim.32), calls=%async_computation.2 | async-start | bytes 524288 | tf_op jit(solution)/shard_map/share_rows/all_to_all | solution.py:169

commit v4 on v1

v4 whole, which is shorter than its diff:
```python
import jax
import jax.numpy as jnp
from jax import lax
from jax.experimental import pallas as pl
from jax.experimental.pallas import tpu as pltpu
from jax.sharding import Mesh
from jax.sharding import PartitionSpec as P

ZL, XN, YN, ZH, CN = 8, 4, 4, 2, 2
ZM, ZR = 2, 4
STEPS = (-1, 0, 1, 2, 3, 4, -3, -2)
QN = CN * YN
TOK, WIDTH, KV, HD = 128, 4096, 512, 128
GROUP = 8
SUB = 16
BF, F32 = jnp.bfloat16, jnp.float32


def nt(a, b):
    return lax.dot_general(a, b, (((1,), (1,)), ((), ())), preferred_element_type=F32)


def attend_kernel(length_ref, q_ref, k_ref, v_ref, g_ref, vg_ref, kg_ref):
    scaling = HD ** (-0.5)
    keys, vals = k_ref[...], v_ref[...]
    length = length_ref[0]
    step = 2
    wide = step * TOK
    pos_s = lax.broadcasted_iota(jnp.int32, (TOK, wide), 0)
    pos_t = lax.broadcasted_iota(jnp.int32, (TOK, wide), 1) & (TOK - 1)
    allowed = pos_s <= pos_t
    live = ((lax.broadcasted_iota(jnp.int32, (1, wide), 1) & (TOK - 1)) < length).astype(F32)
    vg = jnp.zeros((TOK, HD), F32)
    kg = jnp.zeros((TOK, HD), F32)
    for first in range(0, GROUP, step):
        heads = range(first, first + step)
        qs = jnp.concatenate([q_ref[:, h * HD : (h + 1) * HD] for h in heads], axis=0)
        gs = jnp.concatenate([g_ref[:, h * HD : (h + 1) * HD] for h in heads], axis=0)
        scores = jnp.where(allowed, nt(keys, qs) * scaling, F32(-1e30))
        expd = jnp.exp(scores - jnp.max(scores, axis=0, keepdims=True))
        probs = expd * (live / jnp.sum(expd, axis=0, keepdims=True))
        dprob = nt(vals, gs)
        delta = jnp.sum(probs * dprob, axis=0, keepdims=True)
        dscore = probs * (dprob - delta)
        vg += jnp.dot(probs.astype(BF), gs, preferred_element_type=F32)
        kg += jnp.dot(dscore.astype(BF), qs, preferred_element_type=F32)
    for copy in range(YN):
        vg_ref[copy] = vg.astype(BF)
    kg_ref[...] = (kg * scaling).astype(BF)


def attend_back(query, key_rows, value_rows, grad_rows, length):
    heads = KV // HD
    wide = pl.BlockSpec((TOK, GROUP * HD), lambda g: (0, g))
    thin = pl.BlockSpec((TOK, HD), lambda g: (0, g))
    return pl.pallas_call(
        attend_kernel,
        grid=(heads,),
        in_specs=[pl.BlockSpec(memory_space=pltpu.SMEM), wide, thin, thin, wide],
        out_specs=[pl.BlockSpec((YN, TOK, HD), lambda g: (0, 0, g)), thin],
        out_shape=[jax.ShapeDtypeStruct((YN, TOK, KV), BF), jax.ShapeDtypeStruct((TOK, KV), BF)],
        cost_estimate=pl.CostEstimate(
            flops=10 * 32 * TOK * TOK * HD, bytes_accessed=3 << 20, transcendentals=32 * TOK * TOK
        ),
        name="attend",
    )(length, query, key_rows, value_rows, grad_rows)


def swap_groups(tiles):
    lane = lax.broadcasted_iota(jnp.int32, tiles[0].shape, 1)
    for bit in (1, 2, 4):
        shift = bit * SUB
        high = (lane & shift) != 0
        after = list(tiles)
        for i in range(8):
            if i & bit == 0:
                low_tile, high_tile = tiles[i], tiles[i | bit]
                after[i] = jnp.where(high, pltpu.roll(high_tile, shift, 1), low_tile)
                after[i | bit] = jnp.where(high, high_tile, pltpu.roll(low_tile, 128 - shift, 1))
        tiles = after
    return tiles


def to_pieces_kernel(in_ref, _, out_ref):
    for x in range(XN):
        tiles = [in_ref[:, (zl * XN + x) * 128 : (zl * XN + x + 1) * 128].astype(F32) for zl in range(8)]
        for q, tile in enumerate(swap_groups(tiles)):
            out_ref[q, :, x * 128 : (x + 1) * 128] = tile.astype(BF)


def from_pieces_kernel(places_ref, *refs):
    out_ref, held = refs[-2:]
    for i in range(QN):
        held[places_ref[i]] = refs[i // CN][i % CN]
    for x in range(XN):
        tiles = [held[q, :, x * 128 : (x + 1) * 128].astype(F32) for q in range(8)]
        for zl, tile in enumerate(swap_groups(tiles)):
            out_ref[:, (zl * XN + x) * 128 : (zl * XN + x + 1) * 128] = tile.astype(BF)


def to_pieces(rows, earlier):
    part = 32
    return pl.pallas_call(
        to_pieces_kernel,
        grid=(TOK // part,),
        in_specs=[pl.BlockSpec((part, WIDTH), lambda i: (i, 0)), pl.BlockSpec(memory_space=pl.ANY)],
        out_specs=pl.BlockSpec((QN, part, KV), lambda i: (0, i, 0)),
        out_shape=jax.ShapeDtypeStruct((QN, TOK, KV), BF),
        cost_estimate=pl.CostEstimate(flops=1 << 22, bytes_accessed=2 << 20, transcendentals=0),
        name="to_pieces",
    )(rows, earlier)


def from_pieces(pieces, places):
    part = 32
    return pl.pallas_call(
        from_pieces_kernel,
        grid=(TOK // part,),
        in_specs=[pl.BlockSpec(memory_space=pltpu.SMEM)]
        + [pl.BlockSpec((CN, part, KV), lambda i: (0, i, 0))] * YN,
        out_specs=pl.BlockSpec((part, WIDTH), lambda i: (i, 0)),
        out_shape=jax.ShapeDtypeStruct((TOK, WIDTH), BF),
        scratch_shapes=[pltpu.VMEM((QN, part, KV), BF)],
        cost_estimate=pl.CostEstimate(flops=1 << 22, bytes_accessed=2 << 20, transcendentals=0),
        compiler_params=pltpu.CompilerParams(vmem_limit_bytes=16 << 20),
        name="from_pieces",
    )(jnp.stack(places).astype(jnp.int32), *pieces)


def exchange(array, axes):
    return lax.all_to_all(array, axes, 0, 0, tiled=True)


def spread(array, axes, count):
    return exchange(jnp.broadcast_to(array[None], (count,) + array.shape), axes)


def shifted(array, axes, count, by):
    return lax.ppermute(array, axes, [(i, (i + by) % count) for i in range(count)])


def along_z(array, by):
    places = []
    for z in range(ZH * ZL):
        to = (z + by) % (ZH * ZL)
        places.append(((z % ZL) * ZH + z // ZL, (to % ZL) * ZH + to // ZL))
    return lax.ppermute(array, ("zm", "zr", "zh"), places)


def ring_spread(array, axes, count):
    return [array] + [shifted(array, axes, count, by) for by in range(1, count)]


def pair_kernel(core_ref, own_ref, other_ref, _, out_ref):
    core = core_ref[0]
    out_ref[core] = own_ref[...]
    out_ref[1 - core] = other_ref[...]


def pair(own, other, core, earlier):
    vmem = pl.BlockSpec(memory_space=pltpu.VMEM)
    return pl.pallas_call(
        pair_kernel,
        in_specs=[pl.BlockSpec(memory_space=pltpu.SMEM), vmem, vmem, pl.BlockSpec(memory_space=pl.ANY)],
        out_specs=vmem,
        out_shape=jax.ShapeDtypeStruct((CN,) + own.shape, own.dtype),
        compiler_params=pltpu.CompilerParams(vmem_limit_bytes=16 << 20),
        name="pair",
    )(core[None].astype(jnp.int32), own, other, earlier)


def join_kernel(*refs):
    out_ref = refs[-1]
    at = 0
    for ref in refs[:-2]:
        out_ref[at : at + ref.shape[0], :] = ref[...]
        at += ref.shape[0]


def join(parts, earlier):
    vmem = pl.BlockSpec(memory_space=pltpu.VMEM)
    return pl.pallas_call(
        join_kernel,
        in_specs=[vmem] * len(parts) + [pl.BlockSpec(memory_space=pl.ANY)],
        out_specs=vmem,
        out_shape=jax.ShapeDtypeStruct((sum(part.shape[0] for part in parts), KV), BF),
        compiler_params=pltpu.CompilerParams(vmem_limit_bytes=16 << 20),
        name="join",
    )(*parts, earlier)


def place_rows_kernel(at_ref, *refs):
    out_ref = refs[-1]
    for j, ref in enumerate(refs[:-2]):
        for i, k in enumerate(STEPS):
            row = ((at_ref[1] + XN - j) % XN) * ZL + (at_ref[0] + ZL - k) % ZL
            out_ref[pl.ds(pl.multiple_of(row * SUB, SUB), SUB), :] = ref[i * SUB : (i + 1) * SUB, :]


def place_rows(parts, zl, x, earlier):
    return pl.pallas_call(
        place_rows_kernel,
        in_specs=[pl.BlockSpec(memory_space=pltpu.SMEM)]
        + [pl.BlockSpec(memory_space=pltpu.VMEM)] * len(parts)
        + [pl.BlockSpec(memory_space=pl.ANY)],
        out_specs=pl.BlockSpec(memory_space=pltpu.VMEM),
        out_shape=jax.ShapeDtypeStruct((KV, KV), BF),
        compiler_params=pltpu.CompilerParams(vmem_limit_bytes=16 << 20),
        name="place_rows",
    )(jnp.stack([zl, x]).astype(jnp.int32), *parts, earlier)


def per_device(inputs, queries, keys, values, out_grad, lengths, value_weight):
    core, y, x, zr, zm = (lax.axis_index(name) for name in ("core", "y", "x", "zr", "zm"))
    q = core * YN + y
    with jax.named_scope("weight_along_z"):
        own_rows = lax.dynamic_slice_in_dim(value_weight, q * SUB, SUB, 0)
        ring = jnp.concatenate([along_z(own_rows, -1), own_rows, along_z(own_rows, 1)])
    with jax.named_scope("attention"):
        copies, key_grad = attend_back(queries[0], keys[0], values[0], out_grad[0], lengths)
    with jax.named_scope("gather_value_grad"):
        mine = exchange(copies, "y")
        other = shifted(mine, "core", CN, 1)
        grads = pair(mine, other, core, ring).reshape(QN * TOK, KV)
    with jax.named_scope("send_inputs"):
        columns = exchange(to_pieces(inputs[0], own_rows), ("core", "y"))
    with jax.named_scope("weight_term"):
        term = lax.dot_general(
            columns.reshape(QN * TOK, KV), grads, (((0,), (0,)), ((), ())), preferred_element_type=F32
        ).astype(BF)
    with jax.named_scope("sum_x"):
        got = exchange(term.reshape(XN, ZL * SUB, KV), "x")
        plane = jnp.sum(got.astype(F32), axis=0).astype(BF)
    with jax.named_scope("sum_near_z"):
        pieces = jnp.swapaxes(plane.reshape(ZM, ZR, SUB, KV), 0, 1)
        got = exchange(pieces.reshape(ZR, ZM * SUB, KV), "zr")
        near = jnp.sum(got.astype(F32), axis=0).astype(BF).reshape(1, ZM, SUB, KV)
    with jax.named_scope("sum_far_z"):
        both = jnp.broadcast_to(near, (ZH, ZM, SUB, KV)).reshape(ZH * ZM, SUB, KV)
        got = exchange(both, ("zh", "zm"))
        total = jnp.sum(got.astype(F32), axis=0) * F32(1.0 / 512)
    with jax.named_scope("share_rows"):
        weight_grad = spread(total, ("core", "y"), QN).reshape(QN * SUB, KV)
    with jax.named_scope("gather_weight"):
        ring = join([ring, along_z(ring, 3), along_z(ring[SUB:], -3)], term)
        weight = place_rows(ring_spread(ring, "x", XN), zm * ZR + zr, x, plane)
    with jax.named_scope("input_grad"):
        parts = nt(grads, weight).astype(BF).reshape(CN, YN, TOK, KV)
        kept = lax.dynamic_index_in_dim(parts, core, 0, False)
        theirs = shifted(lax.dynamic_index_in_dim(parts, 1 - core, 0, False), "core", CN, 1)
        parts = jnp.stack([kept, theirs], axis=1)
        places, back = [], []
        for by in range(YN):
            piece = lax.dynamic_index_in_dim(parts, (y + by) % YN, 0, False)
            back.append(shifted(piece, "y", YN, by) if by else piece)
            places += [c * YN + (y - by) % YN for c in (core, 1 - core)]
        input_grad = from_pieces(back, places)
    return (input_grad[None], key_grad[None], weight_grad)


def solution(mesh):
    names = ("zm", "zr", "x", "y", "zh", "core")
    fine = Mesh(mesh.devices.reshape(ZM, ZR, XN, YN, ZH, CN), names)
    blk = names[:3]
    rows = P(names, None, None)
    return jax.shard_map(
        per_device,
        mesh=fine,
        in_specs=(rows, rows, rows, rows, rows, P(names), P(blk, None)),
        out_specs=(rows, rows, P(blk, None)),
        check_vma=False,
    )
```

time: 165 us -> 130 us (0.79)
  waiting for transfers between devices: 63.6 us -> 15 us
  starting transfers between devices: 50.3 us -> 81.6 us
  between operations: 14.8 us -> 1.56 us
  local copies, waits for them, and re-layouts: 9.58 us -> 2.86 us
  Pallas kernels: 11 us -> 14.7 us
    all_to_all x7 -> x5, waiting for transfers between devices: 62.8 us -> 9.88 us  [exchange(): return lax.all_to_all(array, axes, 0, 0, tiled=True)]
    ppermute x0 -> x12, starting transfers between devices: none -> 48.3 us  [the longest x8 26.7 us: shifted(): lax.ppermute(array, axes, [(i, (i + by) % count) for i in range(count)])]
    all_to_all x7 -> x5, starting transfers between devices: 50.3 us -> 33.3 us  [exchange(): return lax.all_to_all(array, axes, 0, 0, tiled=True)]
    ppermute x0 -> x12, waiting for transfers between devices: none -> 5.09 us  [the longest x8 3.18 us: shifted(): lax.ppermute(array, axes, [(i, (i + by) % count) for i in range(count)])]
    unnamed x17 -> x5, local copies, waits for them, and re-layouts: 5.78 us -> 0.72 us
    broadcast_in_dim x4 -> x1, local copies, waits for them, and re-layouts: 3.06 us -> 0.73 us  [spread(): return exchange(jnp.broadcast_to(array[None], (count,) + array.shape), axes)]
  transfers between devices with their start and end apart: 8 -> 17, of which waited for: 8 -> 8; matrix products, arithmetic and copies ran while one was open for 3% -> 2% of each run, Pallas kernels for 4% -> 6%
where the time goes in v4:
time: 130 us; the launch traced here: 129 us
  starting transfers between devices  81.6 us (63%)
  waiting for transfers between devices  15 us (12%)
  Pallas kernels  14.7 us (11%)
  blocking collectives  10.3 us (8%)
  local copies, waits for them, and re-layouts  2.86 us (2%)
  matrix products  2.26 us (2%)
  between operations  1.56 us (1%)
    all_to_all x5, starting transfers between devices, exchange(): return lax.all_to_all(array, axes, 0, 0, tiled=True)  33.3 us
    ppermute x8, starting transfers between devices, shifted(): lax.ppermute(array, axes, [(i, (i + by) % count) for i in range(count)])  26.7 us
    ppermute x4, starting transfers between devices, along_z(): return lax.ppermute(array, ('zm', 'zr', 'zh'), places)  21.6 us
    all_to_all x1, blocking collectives, exchange(): return lax.all_to_all(array, axes, 0, 0, tiled=True)  10.3 us
    all_to_all x5, waiting for transfers between devices, exchange(): return lax.all_to_all(array, axes, 0, 0, tiled=True)  9.88 us
    pallas_call x1, Pallas kernels, attend_back(): pl.pallas_call(attend_kernel, grid=(heads,), in_specs=[pl.BlockSpec(memor...  5.97 us
    pallas_call x1, Pallas kernels, to_pieces(): pl.pallas_call(to_pieces_kernel, grid=(TOK // part,), in_specs=[pl.BlockS...  4.35 us
    pallas_call x1, Pallas kernels, from_pieces(): pl.pallas_call(from_pieces_kernel, grid=(TOK // part,), in_specs=[pl.Bloc...  3.63 us
  transfers between devices with their start and end apart: 17, of which 8 were waited for; matrix products, arithmetic and copies ran while one was open for 2% of the time, Pallas kernels for 6%

profile of v4, /device:TPU:1, one launch (start us, length us, event | category | flops | bytes accessed | tf_op | source)
XLA Modules:
  0.0 128.5 jit_solution(12088311840613085091)
XLA Ops:
  1.3 6.0 %attend.1 = (bf16[4,128,512]{2,1,0:T(8,128)(2,1)}, bf16[128,512]{1,0:T(8,128)(2,1)}) custom-call(s32[1]{0:T(128)S(6)} %copy.13.length_ref, bf16[128,4096]{1,0:T(8,128)(2,1)} %bitcast.57, bf16[128,512]{1,0:T(8,128)(2,1)} %bitcast.59, bf16[128,512]{1,0:T(8,128)(2,1)} %bitcast.60, bf16[128,4096]{1,0:T(8,128)(2,1)} %bitcast.58), custom_call_target="tpu_custom_call" | custom-call | flops 671088640 | bytes 3145728 | tf_op jit(solution)/shard_map/attention/attend/pallas_call | solution.py:56
  7.3 5.0 %all-to-all-start = ((bf16[4,128,512]{2,1,0:T(8,128)(2,1)}), bf16[4,128,512]{2,1,0:T(8,128)(2,1)S(1)}, u32[]{:S(2)}, u32[]{:S(2)}) async-start(bf16[4,128,512]{2,1,0:T(8,128)(2,1)} %get-tuple-element.5), calls=%async_computation | async-start | bytes 1048576 | tf_op jit(solution)/shard_map/gather_value_grad/all_to_all | solution.py:131
  12.9 4.3 %to_pieces.1 = bf16[8,128,512]{2,1,0:T(8,128)(2,1)} custom-call(bf16[128,4096]{1,0:T(8,128)(2,1)} %bitcast.50, bf16[16,512]{1,0:T(8,128)(2,1)} %constant_dynamic-slice_fusion._), custom_call_target="tpu_custom_call" | custom-call | flops 4194304 | bytes 2097152 | tf_op jit(solution)/shard_map/send_inputs/to_pieces/pallas_call | solution.py:103
  17.3 2.0 %all-to-all-done.own_ref = bf16[4,128,512]{2,1,0:T(8,128)(2,1)S(1)} async-done(((bf16[4,128,512]{2,1,0:T(8,128)(2,1)}), bf16[4,128,512]{2,1,0:T(8,128)(2,1)S(1)}, u32[]{:S(2)}, u32[]{:S(2)}) %all-to-all-start) | async-done | bytes 524320 | tf_op jit(solution)/shard_map/gather_value_grad/all_to_all | solution.py:131
  19.2 9.9 %all-to-all-start.1 = ((bf16[8,128,512]{2,1,0:T(8,128)(2,1)}), bf16[8,128,512]{2,1,0:T(8,128)(2,1)S(1)}, u32[]{:S(2)}, u32[]{:S(2)}) async-start(bf16[8,128,512]{2,1,0:T(8,128)(2,1)} %to_pieces.1), calls=%async_computation.1 | async-start | bytes 2097152 | tf_op jit(solution)/shard_map/send_inputs/all_to_all | solution.py:131
  29.2 2.0 %collective-permute-start = (bf16[4,128,512]{2,1,0:T(8,128)(2,1)S(1)}, bf16[4,128,512]{2,1,0:T(8,128)(2,1)S(1)}, u32[]{:S(2)}, u32[]{:S(2)}) collective-permute-start(bf16[4,128,512]{2,1,0:T(8,128)(2,1)S(1)} %all-to-all-done.own_ref), channel_id=1, source_target_pairs={{0,1},{1,0},{2,3},{3,2},{4,5},{5,4},{6,7},{7,6},{8,9},{9,8},{10,11... | collective-permute-start | bytes 1572872 | tf_op jit(solution)/shard_map/gather_value_grad/ppermute | solution.py:139
  31.2 1.9 %collective-permute-start.2 = (bf16[16,512]{1,0:T(8,128)(2,1)S(1)}, bf16[16,512]{1,0:T(8,128)(2,1)S(1)}, u32[]{:S(2)}, u32[]{:S(2)}) collective-permute-start(bf16[16,512]{1,0:T(8,128)(2,1)S(1)} %copy-done.1), channel_id=1, source_target_pairs={{0,64},{64,128},{128,192},{192,256},{256,320},{320,384},{384,448},... | collective-permute-start | bytes 49160 | tf_op jit(solution)/shard_map/weight_along_z/ppermute | solution.py:147
  33.1 8.2 %collective-permute-start.1 = (bf16[16,512]{1,0:T(8,128)(2,1)S(1)}, bf16[16,512]{1,0:T(8,128)(2,1)S(1)}, u32[]{:S(2)}, u32[]{:S(2)}) collective-permute-start(bf16[16,512]{1,0:T(8,128)(2,1)S(1)} %copy-done.1), channel_id=1, source_target_pairs={{0,450},{64,0},{128,64},{192,128},{256,192},{320,256},{384,320},{4... | collective-permute-start | bytes 49160 | tf_op jit(solution)/shard_map/weight_along_z/ppermute | solution.py:147
  41.3 0.8 collective-permute-done.1
  42.2 2.0 %all-to-all-done.1 = bf16[8,128,512]{2,1,0:T(8,128)(2,1)S(1)} async-done(((bf16[8,128,512]{2,1,0:T(8,128)(2,1)}), bf16[8,128,512]{2,1,0:T(8,128)(2,1)S(1)}, u32[]{:S(2)}, u32[]{:S(2)}) %all-to-all-start.1) | async-done | bytes 1048608 | tf_op jit(solution)/shard_map/send_inputs/all_to_all | solution.py:131
  44.2 1.5 %convolution_convert_fusion.1.refs_3_ = bf16[512,512]{1,0:T(8,128)(2,1)} fusion(bf16[1024,512]{1,0:T(8,128)(2,1)S(1)} %bitcast.51, bf16[1024,512]{1,0:T(8,128)(2,1)S(1)} %bitcast.47), kind=kOutput, calls=%fused_computation.9 | convolution fusion | flops 537133056 | bytes 2621440 | tf_op jit(solution)/shard_map/weight_term/dot_general | solution.py:228
  45.7 3.5 %all-to-all-start.2 = ((bf16[4,128,512]{2,1,0:T(8,128)(2,1)}), bf16[4,128,512]{2,1,0:T(8,128)(2,1)S(1)}, u32[]{:S(2)}, u32[]{:S(2)}) async-start(bf16[4,128,512]{2,1,0:T(8,128)(2,1)} %bitcast.18), calls=%async_computation.2 | async-start | bytes 1048576 | tf_op jit(solution)/shard_map/sum_x/all_to_all | solution.py:131
  49.2 3.8 %collective-permute-start.3 = (bf16[48,512]{1,0:T(8,128)(2,1)S(1)}, bf16[48,512]{1,0:T(8,128)(2,1)S(1)}, u32[]{:S(2)}, u32[]{:S(2)}) collective-permute-start(bf16[48,512]{1,0:T(8,128)(2,1)S(1)} %pad_maximum_fusion._.refs_0_), channel_id=1, source_target_pairs={{0,192},{64,256},{128,320},{192,384},{256,448},{320,2},{384,66},{4... | collective-permute-start | bytes 147464 | tf_op jit(solution)/shard_map/gather_weight/ppermute | solution.py:147
  53.0 7.7 %collective-permute-start.4 = (bf16[32,512]{1,0:T(8,128)(2,1)S(1)}, bf16[32,512]{1,0:T(8,128)(2,1)S(1)}, u32[]{:S(2)}, u32[]{:S(2)}) collective-permute-start(bf16[32,512]{1,0:T(8,128)(2,1)S(1)} %pad_maximum_fusion.1), channel_id=1, source_target_pairs={{0,322},{64,386},{128,450},{192,0},{256,64},{320,128},{384,192},{4... | collective-permute-start | bytes 98312 | tf_op jit(solution)/shard_map/gather_weight/ppermute | solution.py:147
  60.7 1.1 collective-permute-done.4.refs_2_
  61.8 3.4 %collective-permute-start.5 = (bf16[128,512]{1,0:T(8,128)(2,1)S(1)}, bf16[128,512]{1,0:T(8,128)(2,1)S(1)}, u32[]{:S(2)}, u32[]{:S(2)}) collective-permute-start(bf16[128,512]{1,0:T(8,128)(2,1)S(1)} %join.1.refs_0_), channel_id=1, source_target_pairs={{0,16},{16,32},{32,48},{48,0},{1,17},{17,33},{33,49},{49,1},{2,18}... | collective-permute-start | bytes 393224 | tf_op jit(solution)/shard_map/gather_weight/ppermute | solution.py:139
  65.2 4.3 %collective-permute-start.6 = (bf16[128,512]{1,0:T(8,128)(2,1)S(1)}, bf16[128,512]{1,0:T(8,128)(2,1)S(1)}, u32[]{:S(2)}, u32[]{:S(2)}) collective-permute-start(bf16[128,512]{1,0:T(8,128)(2,1)S(1)} %join.1.refs_0_), channel_id=1, source_target_pairs={{0,32},{16,48},{32,0},{48,16},{1,33},{17,49},{33,1},{49,17},{2,34}... | collective-permute-start | bytes 393224 | tf_op jit(solution)/shard_map/gather_weight/ppermute | solution.py:139
  69.5 3.1 %collective-permute-start.7 = (bf16[128,512]{1,0:T(8,128)(2,1)S(1)}, bf16[128,512]{1,0:T(8,128)(2,1)S(1)}, u32[]{:S(2)}, u32[]{:S(2)}) collective-permute-start(bf16[128,512]{1,0:T(8,128)(2,1)S(1)} %join.1.refs_0_), channel_id=1, source_target_pairs={{0,48},{16,0},{32,16},{48,32},{1,49},{17,1},{33,17},{49,33},{2,50}... | collective-permute-start | bytes 393224 | tf_op jit(solution)/shard_map/gather_weight/ppermute | solution.py:139
  73.4 2.5 %collective-permute-done.7.refs_3_ = bf16[128,512]{1,0:T(8,128)(2,1)S(1)} collective-permute-done((bf16[128,512]{1,0:T(8,128)(2,1)S(1)}, bf16[128,512]{1,0:T(8,128)(2,1)S(1)}, u32[]{:S(2)}, u32[]{:S(2)}) %collective-permute-start.7) | collective-permute-done | bytes 131104 | tf_op jit(solution)/shard_map/gather_weight/ppermute | solution.py:139
  76.6 0.7 convolution_convert_fusion
  77.4 5.4 %collective-permute-start.8 = (bf16[4,128,512]{2,1,0:T(8,128)(2,1)S(1)}, bf16[4,128,512]{2,1,0:T(8,128)(2,1)S(1)}, u32[]{:S(2)}, u32[]{:S(2)}) collective-permute-start(bf16[4,128,512]{2,1,0:T(8,128)(2,1)S(1)} %get-tuple-element.11), channel_id=1, source_target_pairs={{0,1},{1,0},{2,3},{3,2},{4,5},{5,4},{6,7},{7,6},{8,9},{9,8},{10,11... | collective-permute-start | bytes 1572872 | tf_op jit(solution)/shard_map/input_grad/ppermute | solution.py:139
  82.8 10.3 %all_to_all.30 = bf16[4,32,512]{2,1,0:T(8,128)(2,1)S(1)} all-to-all(bf16[4,32,512]{2,1,0:T(8,128)(2,1)S(1)} %bitcast.55), channel_id=1, replica_groups=mesh['zm'=2,'zr'=4,'x'=4,'y'=4,'zh'=2,'core'=2] {'zr'}, dimensions={0} | all-to-all | bytes 262144 | tf_op jit(solution)/shard_map/sum_near_z/all_to_all | solution.py:131
  93.8 8.3 %all-to-all-start.4 = ((bf16[4,16,512]{2,1,0:T(8,128)(2,1)}), bf16[4,16,512]{2,1,0:T(8,128)(2,1)S(1)}, u32[]{:S(2)}, u32[]{:S(2)}) async-start(bf16[4,16,512]{2,1,0:T(8,128)(2,1)} %bitcast.33), calls=%async_computation.4 | async-start | bytes 131072 | tf_op jit(solution)/shard_map/sum_far_z/all_to_all | solution.py:131
  102.1 2.6 %collective-permute-start.10 = (bf16[2,128,512]{2,1,0:T(8,128)(2,1)S(1)}, bf16[2,128,512]{2,1,0:T(8,128)(2,1)S(1)}, u32[]{:S(2)}, u32[]{:S(2)}) collective-permute-start(bf16[2,128,512]{2,1,0:T(8,128)(2,1)S(1)} %get-tuple-element.10), channel_id=1, source_target_pairs={{0,8},{4,12},{8,0},{12,4},{1,9},{5,13},{9,1},{13,5},{2,10},{6,14},... | collective-permute-start | bytes 786440 | tf_op jit(solution)/shard_map/input_grad/ppermute | solution.py:139
  104.7 4.1 %collective-permute-start.11 = (bf16[2,128,512]{2,1,0:T(8,128)(2,1)S(1)}, bf16[2,128,512]{2,1,0:T(8,128)(2,1)S(1)}, u32[]{:S(2)}, u32[]{:S(2)}) collective-permute-start(bf16[2,128,512]{2,1,0:T(8,128)(2,1)S(1)} %get-tuple-element.7), channel_id=1, source_target_pairs={{0,12},{4,0},{8,4},{12,8},{1,13},{5,1},{9,5},{13,9},{2,14},{6,2},{... | collective-permute-start | bytes 786440 | tf_op jit(solution)/shard_map/input_grad/ppermute | solution.py:139
  108.8 1.9 %collective-permute-start.9 = (bf16[2,128,512]{2,1,0:T(8,128)(2,1)S(1)}, bf16[2,128,512]{2,1,0:T(8,128)(2,1)S(1)}, u32[]{:S(2)}, u32[]{:S(2)}) collective-permute-start(bf16[2,128,512]{2,1,0:T(8,128)(2,1)S(1)} %get-tuple-element.9), channel_id=1, source_target_pairs={{0,4},{4,8},{8,12},{12,0},{1,5},{5,9},{9,13},{13,1},{2,6},{6,10},{... | collective-permute-start | bytes 786440 | tf_op jit(solution)/shard_map/input_grad/ppermute | solution.py:139
  110.7 3.1 %all-to-all-done.4 = bf16[4,16,512]{2,1,0:T(8,128)(2,1)S(1)} async-done(((bf16[4,16,512]{2,1,0:T(8,128)(2,1)}), bf16[4,16,512]{2,1,0:T(8,128)(2,1)S(1)}, u32[]{:S(2)}, u32[]{:S(2)}) %all-to-all-start.4) | async-done | bytes 65568 | tf_op jit(solution)/shard_map/sum_far_z/all_to_all | solution.py:131
  113.9 0.7 broadcast_in_dim.27
  114.6 6.6 %all-to-all-start.5 = ((f32[8,16,512]{2,1,0:T(8,128)}), f32[8,16,512]{2,1,0:T(8,128)S(1)}, u32[]{:S(2)}, u32[]{:S(2)}) async-start(f32[8,16,512]{2,1,0:T(8,128)} %broadcast_in_dim.27), calls=%async_computation.5 | async-start | bytes 524288 | tf_op jit(solution)/shard_map/share_rows/all_to_all | solution.py:131
  121.4 3.6 %from_pieces.1 = bf16[128,4096]{1,0:T(8,128)(2,1)} custom-call(s32[8]{0:T(128)S(1)} %stack.53.places_ref, bf16[2,128,512]{2,1,0:T(8,128)(2,1)S(1)} %get-tuple-element.8.refs_0_, bf16[2,128,512]{2,1,0:T(8,128)(2,1)S(1)} %collective-permute-done.9.refs_1_, bf16[2,128,512]{2,1,0:T(8,128)(2,1)S(1)} %collective-permute-done.10.refs_2_, ...), custom_call_target="tpu_custom_call" | custom-call | flops 4194304 | bytes 2097152 | tf_op jit(solution)/shard_map/input_grad/from_pieces/pallas_call | solution.py:116
  125.0 2.8 %all-to-all-done.5 = f32[8,16,512]{2,1,0:T(8,128)S(1)} async-done(((f32[8,16,512]{2,1,0:T(8,128)}), f32[8,16,512]{2,1,0:T(8,128)S(1)}, u32[]{:S(2)}, u32[]{:S(2)}) %all-to-all-start.5) | async-done | bytes 262176 | tf_op jit(solution)/shard_map/share_rows/all_to_all | solution.py:131
  127.8 0.7 copy.14
  (30 shorter events, 3.1 us)
Async XLA Ops:
  0.6 11.7 %copy-start = (bf16[128,512]{1,0:T(8,128)(2,1)S(1)}, bf16[128,512]{1,0:T(8,128)(2,1)}, u32[]{:S(2)}) copy-start(bf16[128,512]{1,0:T(8,128)(2,1)} %param.13) | copy-start | bytes 393220
  7.3 11.9 %all-to-all-start = ((bf16[4,128,512]{2,1,0:T(8,128)(2,1)}), bf16[4,128,512]{2,1,0:T(8,128)(2,1)S(1)}, u32[]{:S(2)}, u32[]{:S(2)}) async-start(bf16[4,128,512]{2,1,0:T(8,128)(2,1)} %get-tuple-element.5), calls=%async_computation | async-start | bytes 1048576 | tf_op jit(solution)/shard_map/gather_value_grad/all_to_all | solution.py:131
  17.3 13.9 %copy-start.1 = (bf16[16,512]{1,0:T(8,128)(2,1)S(1)}, bf16[16,512]{1,0:T(8,128)(2,1)}, u32[]{:S(2)}) copy-start(bf16[16,512]{1,0:T(8,128)(2,1)} %constant_dynamic-slice_fusion._) | copy-start | bytes 49156
  19.2 24.9 %all-to-all-start.1 = ((bf16[8,128,512]{2,1,0:T(8,128)(2,1)}), bf16[8,128,512]{2,1,0:T(8,128)(2,1)S(1)}, u32[]{:S(2)}, u32[]{:S(2)}) async-start(bf16[8,128,512]{2,1,0:T(8,128)(2,1)} %to_pieces.1), calls=%async_computation.1 | async-start | bytes 2097152 | tf_op jit(solution)/shard_map/send_inputs/all_to_all | solution.py:131
  29.2 13.0 %collective-permute-start = (bf16[4,128,512]{2,1,0:T(8,128)(2,1)S(1)}, bf16[4,128,512]{2,1,0:T(8,128)(2,1)S(1)}, u32[]{:S(2)}, u32[]{:S(2)}) collective-permute-start(bf16[4,128,512]{2,1,0:T(8,128)(2,1)S(1)} %all-to-all-done.own_ref), channel_id=1, source_target_pairs={{0,1},{1,0},{2,3},{3,2},{4,5},{5,4},{6,7},{7,6},{8,9},{9,8},{10,11... | collective-permute-start | bytes 1572872 | tf_op jit(solution)/shard_map/gather_value_grad/ppermute | solution.py:139
  31.2 10.1 %collective-permute-start.2 = (bf16[16,512]{1,0:T(8,128)(2,1)S(1)}, bf16[16,512]{1,0:T(8,128)(2,1)S(1)}, u32[]{:S(2)}, u32[]{:S(2)}) collective-permute-start(bf16[16,512]{1,0:T(8,128)(2,1)S(1)} %copy-done.1), channel_id=1, source_target_pairs={{0,64},{64,128},{128,192},{192,256},{256,320},{320,384},{384,448},... | collective-permute-start | bytes 49160 | tf_op jit(solution)/shard_map/weight_along_z/ppermute | solution.py:147
  33.1 9.0 %collective-permute-start.1 = (bf16[16,512]{1,0:T(8,128)(2,1)S(1)}, bf16[16,512]{1,0:T(8,128)(2,1)S(1)}, u32[]{:S(2)}, u32[]{:S(2)}) collective-permute-start(bf16[16,512]{1,0:T(8,128)(2,1)S(1)} %copy-done.1), channel_id=1, source_target_pairs={{0,450},{64,0},{128,64},{192,128},{256,192},{320,256},{384,320},{4... | collective-permute-start | bytes 49160 | tf_op jit(solution)/shard_map/weight_along_z/ppermute | solution.py:147
  45.7 27.0 %all-to-all-start.2 = ((bf16[4,128,512]{2,1,0:T(8,128)(2,1)}), bf16[4,128,512]{2,1,0:T(8,128)(2,1)S(1)}, u32[]{:S(2)}, u32[]{:S(2)}) async-start(bf16[4,128,512]{2,1,0:T(8,128)(2,1)} %bitcast.18), calls=%async_computation.2 | async-start | bytes 1048576 | tf_op jit(solution)/shard_map/sum_x/all_to_all | solution.py:131
  49.2 12.6 %collective-permute-start.3 = (bf16[48,512]{1,0:T(8,128)(2,1)S(1)}, bf16[48,512]{1,0:T(8,128)(2,1)S(1)}, u32[]{:S(2)}, u32[]{:S(2)}) collective-permute-start(bf16[48,512]{1,0:T(8,128)(2,1)S(1)} %pad_maximum_fusion._.refs_0_), channel_id=1, source_target_pairs={{0,192},{64,256},{128,320},{192,384},{256,448},{320,2},{384,66},{4... | collective-permute-start | bytes 147464 | tf_op jit(solution)/shard_map/gather_weight/ppermute | solution.py:147
  53.0 8.8 %collective-permute-start.4 = (bf16[32,512]{1,0:T(8,128)(2,1)S(1)}, bf16[32,512]{1,0:T(8,128)(2,1)S(1)}, u32[]{:S(2)}, u32[]{:S(2)}) collective-permute-start(bf16[32,512]{1,0:T(8,128)(2,1)S(1)} %pad_maximum_fusion.1), channel_id=1, source_target_pairs={{0,322},{64,386},{128,450},{192,0},{256,64},{320,128},{384,192},{4... | collective-permute-start | bytes 98312 | tf_op jit(solution)/shard_map/gather_weight/ppermute | solution.py:147
  61.8 11.0 %collective-permute-start.5 = (bf16[128,512]{1,0:T(8,128)(2,1)S(1)}, bf16[128,512]{1,0:T(8,128)(2,1)S(1)}, u32[]{:S(2)}, u32[]{:S(2)}) collective-permute-start(bf16[128,512]{1,0:T(8,128)(2,1)S(1)} %join.1.refs_0_), channel_id=1, source_target_pairs={{0,16},{16,32},{32,48},{48,0},{1,17},{17,33},{33,49},{49,1},{2,18}... | collective-permute-start | bytes 393224 | tf_op jit(solution)/shard_map/gather_weight/ppermute | solution.py:139
  65.2 8.2 %collective-permute-start.6 = (bf16[128,512]{1,0:T(8,128)(2,1)S(1)}, bf16[128,512]{1,0:T(8,128)(2,1)S(1)}, u32[]{:S(2)}, u32[]{:S(2)}) collective-permute-start(bf16[128,512]{1,0:T(8,128)(2,1)S(1)} %join.1.refs_0_), channel_id=1, source_target_pairs={{0,32},{16,48},{32,0},{48,16},{1,33},{17,49},{33,1},{49,17},{2,34}... | collective-permute-start | bytes 393224 | tf_op jit(solution)/shard_map/gather_weight/ppermute | solution.py:139
  69.5 6.4 %collective-permute-start.7 = (bf16[128,512]{1,0:T(8,128)(2,1)S(1)}, bf16[128,512]{1,0:T(8,128)(2,1)S(1)}, u32[]{:S(2)}, u32[]{:S(2)}) collective-permute-start(bf16[128,512]{1,0:T(8,128)(2,1)S(1)} %join.1.refs_0_), channel_id=1, source_target_pairs={{0,48},{16,0},{32,16},{48,32},{1,49},{17,1},{33,17},{49,33},{2,50}... | collective-permute-start | bytes 393224 | tf_op jit(solution)/shard_map/gather_weight/ppermute | solution.py:139
  77.4 24.6 %collective-permute-start.8 = (bf16[4,128,512]{2,1,0:T(8,128)(2,1)S(1)}, bf16[4,128,512]{2,1,0:T(8,128)(2,1)S(1)}, u32[]{:S(2)}, u32[]{:S(2)}) collective-permute-start(bf16[4,128,512]{2,1,0:T(8,128)(2,1)S(1)} %get-tuple-element.11), channel_id=1, source_target_pairs={{0,1},{1,0},{2,3},{3,2},{4,5},{5,4},{6,7},{7,6},{8,9},{9,8},{10,11... | collective-permute-start | bytes 1572872 | tf_op jit(solution)/shard_map/input_grad/ppermute | solution.py:139
  93.8 20.1 %all-to-all-start.4 = ((bf16[4,16,512]{2,1,0:T(8,128)(2,1)}), bf16[4,16,512]{2,1,0:T(8,128)(2,1)S(1)}, u32[]{:S(2)}, u32[]{:S(2)}) async-start(bf16[4,16,512]{2,1,0:T(8,128)(2,1)} %bitcast.33), calls=%async_computation.4 | async-start | bytes 131072 | tf_op jit(solution)/shard_map/sum_far_z/all_to_all | solution.py:131
  102.1 19.2 %collective-permute-start.10 = (bf16[2,128,512]{2,1,0:T(8,128)(2,1)S(1)}, bf16[2,128,512]{2,1,0:T(8,128)(2,1)S(1)}, u32[]{:S(2)}, u32[]{:S(2)}) collective-permute-start(bf16[2,128,512]{2,1,0:T(8,128)(2,1)S(1)} %get-tuple-element.10), channel_id=1, source_target_pairs={{0,8},{4,12},{8,0},{12,4},{1,9},{5,13},{9,1},{13,5},{2,10},{6,14},... | collective-permute-start | bytes 786440 | tf_op jit(solution)/shard_map/input_grad/ppermute | solution.py:139
  104.7 16.6 %collective-permute-start.11 = (bf16[2,128,512]{2,1,0:T(8,128)(2,1)S(1)}, bf16[2,128,512]{2,1,0:T(8,128)(2,1)S(1)}, u32[]{:S(2)}, u32[]{:S(2)}) collective-permute-start(bf16[2,128,512]{2,1,0:T(8,128)(2,1)S(1)} %get-tuple-element.7), channel_id=1, source_target_pairs={{0,12},{4,0},{8,4},{12,8},{1,13},{5,1},{9,5},{13,9},{2,14},{6,2},{... | collective-permute-start | bytes 786440 | tf_op jit(solution)/shard_map/input_grad/ppermute | solution.py:139
  108.8 12.6 %collective-permute-start.9 = (bf16[2,128,512]{2,1,0:T(8,128)(2,1)S(1)}, bf16[2,128,512]{2,1,0:T(8,128)(2,1)S(1)}, u32[]{:S(2)}, u32[]{:S(2)}) collective-permute-start(bf16[2,128,512]{2,1,0:T(8,128)(2,1)S(1)} %get-tuple-element.9), channel_id=1, source_target_pairs={{0,4},{4,8},{8,12},{12,0},{1,5},{5,9},{9,13},{13,1},{2,6},{6,10},{... | collective-permute-start | bytes 786440 | tf_op jit(solution)/shard_map/input_grad/ppermute | solution.py:139
  114.6 13.2 %all-to-all-start.5 = ((f32[8,16,512]{2,1,0:T(8,128)}), f32[8,16,512]{2,1,0:T(8,128)S(1)}, u32[]{:S(2)}, u32[]{:S(2)}) async-start(f32[8,16,512]{2,1,0:T(8,128)} %broadcast_in_dim.27), calls=%async_computation.5 | async-start | bytes 524288 | tf_op jit(solution)/shard_map/share_rows/all_to_all | solution.py:131

commit v5 on v4

--- a/solution.py
+++ b/solution.py
@@ -7,12 +7,12 @@
 from jax.sharding import PartitionSpec as P
 
 ZL, XN, YN, ZH, CN = 8, 4, 4, 2, 2
-ZM, ZR = 2, 4
 STEPS = (-1, 0, 1, 2, 3, 4, -3, -2)
 QN = CN * YN
 TOK, WIDTH, KV, HD = 128, 4096, 512, 128
 GROUP = 8
 SUB = 16
+HALF = 64
 BF, F32 = jnp.bfloat16, jnp.float32
 
 
@@ -44,7 +44,7 @@
         dscore = probs * (dprob - delta)
         vg += jnp.dot(probs.astype(BF), gs, preferred_element_type=F32)
         kg += jnp.dot(dscore.astype(BF), qs, preferred_element_type=F32)
-    for copy in range(YN):
+    for copy in range(XN):
         vg_ref[copy] = vg.astype(BF)
     kg_ref[...] = (kg * scaling).astype(BF)
 
@@ -57,8 +57,8 @@
         attend_kernel,
         grid=(heads,),
         in_specs=[pl.BlockSpec(memory_space=pltpu.SMEM), wide, thin, thin, wide],
-        out_specs=[pl.BlockSpec((YN, TOK, HD), lambda g: (0, 0, g)), thin],
-        out_shape=[jax.ShapeDtypeStruct((YN, TOK, KV), BF), jax.ShapeDtypeStruct((TOK, KV), BF)],
+        out_specs=[pl.BlockSpec((XN, TOK, HD), lambda g: (0, 0, g)), thin],
+        out_shape=[jax.ShapeDtypeStruct((XN, TOK, KV), BF), jax.ShapeDtypeStruct((TOK, KV), BF)],
         cost_estimate=pl.CostEstimate(
             flops=10 * 32 * TOK * TOK * HD, bytes_accessed=3 << 20, transcendentals=32 * TOK * TOK
         ),
@@ -85,7 +85,8 @@
     for x in range(XN):
         tiles = [in_ref[:, (zl * XN + x) * 128 : (zl * XN + x + 1) * 128].astype(F32) for zl in range(8)]
         for q, tile in enumerate(swap_groups(tiles)):
-            out_ref[q, :, x * 128 : (x + 1) * 128] = tile.astype(BF)
+            y = q % YN
+            out_ref[q // YN * XN + x, :, y * 128 : (y + 1) * 128] = tile.astype(BF)
 
 
 def from_pieces_kernel(places_ref, *refs):
@@ -93,7 +94,9 @@
     for i in range(QN):
         held[places_ref[i]] = refs[i // CN][i % CN]
     for x in range(XN):
-        tiles = [held[q, :, x * 128 : (x + 1) * 128].astype(F32) for q in range(8)]
+        tiles = [
+            held[c * XN + x, :, y * 128 : (y + 1) * 128].astype(F32) for c in range(CN) for y in range(YN)
+        ]
         for zl, tile in enumerate(swap_groups(tiles)):
             out_ref[:, (zl * XN + x) * 128 : (zl * XN + x + 1) * 128] = tile.astype(BF)
 
@@ -117,7 +120,7 @@
         from_pieces_kernel,
         grid=(TOK // part,),
         in_specs=[pl.BlockSpec(memory_space=pltpu.SMEM)]
-        + [pl.BlockSpec((CN, part, KV), lambda i: (0, i, 0))] * YN,
+        + [pl.BlockSpec((CN, part, KV), lambda i: (0, i, 0))] * XN,
         out_specs=pl.BlockSpec((part, WIDTH), lambda i: (i, 0)),
         out_shape=jax.ShapeDtypeStruct((TOK, WIDTH), BF),
         scratch_shapes=[pltpu.VMEM((QN, part, KV), BF)],
@@ -144,11 +147,7 @@
     for z in range(ZH * ZL):
         to = (z + by) % (ZH * ZL)
         places.append(((z % ZL) * ZH + z // ZL, (to % ZL) * ZH + to // ZL))
-    return lax.ppermute(array, ("zm", "zr", "zh"), places)
-
-
-def ring_spread(array, axes, count):
-    return [array] + [shifted(array, axes, count, by) for by in range(1, count)]
+    return lax.ppermute(array, ("zl", "zh"), places)
 
 
 def pair_kernel(core_ref, own_ref, other_ref, _, out_ref):
@@ -169,99 +168,74 @@
     )(core[None].astype(jnp.int32), own, other, earlier)
 
 
-def join_kernel(*refs):
+def place_rows_kernel(zl_ref, *refs):
     out_ref = refs[-1]
-    at = 0
-    for ref in refs[:-2]:
-        out_ref[at : at + ref.shape[0], :] = ref[...]
-        at += ref.shape[0]
-
-
-def join(parts, earlier):
+    for i, step in enumerate(STEPS):
+        ref = refs[0 if i < 3 else 1 if i < 6 else 2]
+        first = (i if i < 3 else i - 3 if i < 6 else i - 6) * YN
+        for y in range(YN):
+            row = (y * ZL + (zl_ref[0] + ZL - step) % ZL) * SUB
+            out_ref[pl.ds(pl.multiple_of(row, SUB), SUB), :] = ref[(first + y) * SUB : (first + y + 1) * SUB, :]
+
+
+def place_rows(parts, zl, earlier):
     vmem = pl.BlockSpec(memory_space=pltpu.VMEM)
     return pl.pallas_call(
-        join_kernel,
-        in_specs=[vmem] * len(parts) + [pl.BlockSpec(memory_space=pl.ANY)],
+        place_rows_kernel,
+        in_specs=[pl.BlockSpec(memory_space=pltpu.SMEM), vmem, vmem, vmem, pl.BlockSpec(memory_space=pl.ANY)],
         out_specs=vmem,
-        out_shape=jax.ShapeDtypeStruct((sum(part.shape[0] for part in parts), KV), BF),
-        compiler_params=pltpu.CompilerParams(vmem_limit_bytes=16 << 20),
-        name="join",
-    )(*parts, earlier)
-
-
-def place_rows_kernel(at_ref, *refs):
-    out_ref = refs[-1]
-    for j, ref in enumerate(refs[:-2]):
-        for i, k in enumerate(STEPS):
-            row = ((at_ref[1] + XN - j) % XN) * ZL + (at_ref[0] + ZL - k) % ZL
-            out_ref[pl.ds(pl.multiple_of(row * SUB, SUB), SUB), :] = ref[i * SUB : (i + 1) * SUB, :]
-
-
-def place_rows(parts, zl, x, earlier):
-    return pl.pallas_call(
-        place_rows_kernel,
-        in_specs=[pl.BlockSpec(memory_space=pltpu.SMEM)]
-        + [pl.BlockSpec(memory_space=pltpu.VMEM)] * len(parts)
-        + [pl.BlockSpec(memory_space=pl.ANY)],
-        out_specs=pl.BlockSpec(memory_space=pltpu.VMEM),
         out_shape=jax.ShapeDtypeStruct((KV, KV), BF),
         compiler_params=pltpu.CompilerParams(vmem_limit_bytes=16 << 20),
         name="place_rows",
-    )(jnp.stack([zl, x]).astype(jnp.int32), *parts, earlier)
+    )(zl[None].astype(jnp.int32), *parts, earlier)
 
 
 def per_device(inputs, queries, keys, values, out_grad, lengths, value_weight):
-    core, y, x, zr, zm = (lax.axis_index(name) for name in ("core", "y", "x", "zr", "zm"))
-    q = core * YN + y
+    core, x, zl = (lax.axis_index(name) for name in ("core", "x", "zl"))
     with jax.named_scope("weight_along_z"):
-        own_rows = lax.dynamic_slice_in_dim(value_weight, q * SUB, SUB, 0)
+        own_rows = lax.dynamic_slice_in_dim(value_weight, core * HALF, HALF, 0)
         ring = jnp.concatenate([along_z(own_rows, -1), own_rows, along_z(own_rows, 1)])
     with jax.named_scope("attention"):
         copies, key_grad = attend_back(queries[0], keys[0], values[0], out_grad[0], lengths)
     with jax.named_scope("gather_value_grad"):
-        mine = exchange(copies, "y")
+        mine = exchange(copies, "x")
         other = shifted(mine, "core", CN, 1)
-        grads = pair(mine, other, core, ring).reshape(QN * TOK, KV)
+        grads = pair(mine, other, core, ring).reshape(CN * XN * TOK, KV)
     with jax.named_scope("send_inputs"):
-        columns = exchange(to_pieces(inputs[0], own_rows), ("core", "y"))
+        columns = exchange(to_pieces(inputs[0], own_rows), ("core", "x"))
     with jax.named_scope("weight_term"):
         term = lax.dot_general(
-            columns.reshape(QN * TOK, KV), grads, (((0,), (0,)), ((), ())), preferred_element_type=F32
+            columns.reshape(CN * XN * TOK, KV), grads, (((0,), (0,)), ((), ())), preferred_element_type=F32
         ).astype(BF)
-    with jax.named_scope("sum_x"):
-        got = exchange(term.reshape(XN, ZL * SUB, KV), "x")
-        plane = jnp.sum(got.astype(F32), axis=0).astype(BF)
-    with jax.named_scope("sum_near_z"):
-        pieces = jnp.swapaxes(plane.reshape(ZM, ZR, SUB, KV), 0, 1)
-        got = exchange(pieces.reshape(ZR, ZM * SUB, KV), "zr")
-        near = jnp.sum(got.astype(F32), axis=0).astype(BF).reshape(1, ZM, SUB, KV)
-    with jax.named_scope("sum_far_z"):
-        both = jnp.broadcast_to(near, (ZH, ZM, SUB, KV)).reshape(ZH * ZM, SUB, KV)
-        got = exchange(both, ("zh", "zm"))
+    with jax.named_scope("sum_y"):
+        got = exchange(term.reshape(YN, ZL * SUB, KV), "y")
+        plane = jnp.sum(got.astype(F32), axis=0).astype(BF).reshape(1, ZL, SUB, KV)
+    with jax.named_scope("sum_z"):
+        both = jnp.broadcast_to(plane, (ZH, ZL, SUB, KV)).reshape(ZH * ZL, SUB, KV)
+        got = exchange(both, ("zh", "zl"))
         total = jnp.sum(got.astype(F32), axis=0) * F32(1.0 / 512)
     with jax.named_scope("share_rows"):
         weight_grad = spread(total, ("core", "y"), QN).reshape(QN * SUB, KV)
     with jax.named_scope("gather_weight"):
-        ring = join([ring, along_z(ring, 3), along_z(ring[SUB:], -3)], term)
-        weight = place_rows(ring_spread(ring, "x", XN), zm * ZR + zr, x, plane)
+        weight = place_rows([ring, along_z(ring, 3), along_z(ring[HALF:], -3)], zl, plane)
     with jax.named_scope("input_grad"):
-        parts = nt(grads, weight).astype(BF).reshape(CN, YN, TOK, KV)
+        parts = nt(grads, weight).astype(BF).reshape(CN, XN, TOK, KV)
         kept = lax.dynamic_index_in_dim(parts, core, 0, False)
         theirs = shifted(lax.dynamic_index_in_dim(parts, 1 - core, 0, False), "core", CN, 1)
         parts = jnp.stack([kept, theirs], axis=1)
         places, back = [], []
-        for by in range(YN):
-            piece = lax.dynamic_index_in_dim(parts, (y + by) % YN, 0, False)
-            back.append(shifted(piece, "y", YN, by) if by else piece)
-            places += [c * YN + (y - by) % YN for c in (core, 1 - core)]
+        for by in range(XN):
+            piece = lax.dynamic_index_in_dim(parts, (x + by) % XN, 0, False)
+            back.append(shifted(piece, "x", XN, by) if by else piece)
+            places += [c * XN + (x - by) % XN for c in (core, 1 - core)]
         input_grad = from_pieces(back, places)
     return (input_grad[None], key_grad[None], weight_grad)
 
 
 def solution(mesh):
-    names = ("zm", "zr", "x", "y", "zh", "core")
-    fine = Mesh(mesh.devices.reshape(ZM, ZR, XN, YN, ZH, CN), names)
-    blk = names[:3]
+    names = ("zl", "x", "y", "zh", "core")
+    fine = Mesh(mesh.devices.reshape(ZL, XN, YN, ZH, CN), names)
+    blk = names[:2]
     rows = P(names, None, None)
     return jax.shard_map(
         per_device,

time: 130 us -> 104 us (0.80)
  blocking collectives: 10.3 us -> 0 us
  starting transfers between devices: 81.6 us -> 72.6 us
  waiting for transfers between devices: 15 us -> 9.2 us
    ppermute x8 -> x5, starting transfers between devices: 26.7 us -> 14.4 us  [shifted(): lax.ppermute(array, axes, [(i, (i + by) % count) for i in range(count)])]
    all_to_all x1 -> x0, blocking collectives: 10.3 us -> none  [exchange(): return lax.all_to_all(array, axes, 0, 0, tiled=True)]
    all_to_all x5, waiting for transfers between devices: 9.88 us -> 6.09 us  [exchange(): return lax.all_to_all(array, axes, 0, 0, tiled=True)]
    all_to_all x5, starting transfers between devices: 33.3 us -> 36.8 us  [exchange(): return lax.all_to_all(array, axes, 0, 0, tiled=True)]
    ppermute x8 -> x5, waiting for transfers between devices: 3.18 us -> 1.8 us  [shifted(): lax.ppermute(array, axes, [(i, (i + by) % count) for i in range(count)])]
  transfers between devices with their start and end apart: 17 -> 14, of which waited for: 8 -> 7; matrix products, arithmetic and copies ran while one was open for 2% -> 3% of each run, Pallas kernels for 6% -> 8%
where the time goes in v5:
time: 104 us; the launch traced here: 103 us
  starting transfers between devices  72.6 us (70%)
  Pallas kernels  14.1 us (14%)
  waiting for transfers between devices  9.2 us (9%)
  local copies, waits for them, and re-layouts  2.97 us (3%)
  matrix products  2.26 us (2%)
  between operations  1.6 us (2%)
    all_to_all x5, starting transfers between devices, exchange(): return lax.all_to_all(array, axes, 0, 0, tiled=True)  36.8 us
    ppermute x4, starting transfers between devices, along_z(): return lax.ppermute(array, ('zl', 'zh'), places)  21.4 us
    ppermute x5, starting transfers between devices, shifted(): lax.ppermute(array, axes, [(i, (i + by) % count) for i in range(count)])  14.4 us
    all_to_all x5, waiting for transfers between devices, exchange(): return lax.all_to_all(array, axes, 0, 0, tiled=True)  6.09 us
    pallas_call x1, Pallas kernels, attend_back(): pl.pallas_call(attend_kernel, grid=(heads,), in_specs=[pl.BlockSpec(memor...  5.96 us
    pallas_call x1, Pallas kernels, to_pieces(): pl.pallas_call(to_pieces_kernel, grid=(TOK // part,), in_specs=[pl.BlockS...  4.35 us
    pallas_call x1, Pallas kernels, from_pieces(): pl.pallas_call(from_pieces_kernel, grid=(TOK // part,), in_specs=[pl.Bloc...  3.61 us
  transfers between devices with their start and end apart: 14, of which 7 were waited for; matrix products, arithmetic and copies ran while one was open for 3% of the time, Pallas kernels for 8%

profile of v5, /device:TPU:1, one launch (start us, length us, event | category | flops | bytes accessed | tf_op | source)
XLA Modules:
  0.0 103.0 jit_solution(13238648927295621493)
XLA Ops:
  1.3 6.0 %attend.1 = (bf16[4,128,512]{2,1,0:T(8,128)(2,1)}, bf16[128,512]{1,0:T(8,128)(2,1)}) custom-call(s32[1]{0:T(128)S(6)} %copy.11.length_ref, bf16[128,4096]{1,0:T(8,128)(2,1)} %bitcast.52, bf16[128,512]{1,0:T(8,128)(2,1)} %bitcast.54, bf16[128,512]{1,0:T(8,128)(2,1)} %bitcast.55, bf16[128,4096]{1,0:T(8,128)(2,1)} %bitcast.53), custom_call_target="tpu_custom_call" | custom-call | flops 671088640 | bytes 3145728 | tf_op jit(solution)/shard_map/attention/attend/pallas_call | solution.py:56
  7.3 4.8 %all-to-all-start = ((bf16[4,128,512]{2,1,0:T(8,128)(2,1)}), bf16[4,128,512]{2,1,0:T(8,128)(2,1)S(1)}, u32[]{:S(2)}, u32[]{:S(2)}) async-start(bf16[4,128,512]{2,1,0:T(8,128)(2,1)} %get-tuple-element.5), calls=%async_computation | async-start | bytes 1048576 | tf_op jit(solution)/shard_map/gather_value_grad/all_to_all | solution.py:134
  12.1 0.6 constant_dynamic-slice_fusion._
  12.8 4.3 %to_pieces.1 = bf16[8,128,512]{2,1,0:T(8,128)(2,1)} custom-call(bf16[128,4096]{1,0:T(8,128)(2,1)} %bitcast.47, bf16[64,512]{1,0:T(8,128)(2,1)} %constant_dynamic-slice_fusion._), custom_call_target="tpu_custom_call" | custom-call | flops 4194304 | bytes 2097152 | tf_op jit(solution)/shard_map/send_inputs/to_pieces/pallas_call | solution.py:106
  17.1 1.9 %all-to-all-done.own_ref = bf16[4,128,512]{2,1,0:T(8,128)(2,1)S(1)} async-done(((bf16[4,128,512]{2,1,0:T(8,128)(2,1)}), bf16[4,128,512]{2,1,0:T(8,128)(2,1)S(1)}, u32[]{:S(2)}, u32[]{:S(2)}) %all-to-all-start) | async-done | bytes 524320 | tf_op jit(solution)/shard_map/gather_value_grad/all_to_all | solution.py:134
  19.1 10.1 %all-to-all-start.1 = ((bf16[8,128,512]{2,1,0:T(8,128)(2,1)}), bf16[8,128,512]{2,1,0:T(8,128)(2,1)S(1)}, u32[]{:S(2)}, u32[]{:S(2)}) async-start(bf16[8,128,512]{2,1,0:T(8,128)(2,1)} %to_pieces.1), calls=%async_computation.1 | async-start | bytes 2097152 | tf_op jit(solution)/shard_map/send_inputs/all_to_all | solution.py:134
  29.2 2.0 %collective-permute-start = (bf16[4,128,512]{2,1,0:T(8,128)(2,1)S(1)}, bf16[4,128,512]{2,1,0:T(8,128)(2,1)S(1)}, u32[]{:S(2)}, u32[]{:S(2)}) collective-permute-start(bf16[4,128,512]{2,1,0:T(8,128)(2,1)S(1)} %all-to-all-done.own_ref), channel_id=1, source_target_pairs={{0,1},{1,0},{2,3},{3,2},{4,5},{5,4},{6,7},{7,6},{8,9},{9,8},{10,11... | collective-permute-start | bytes 1572872 | tf_op jit(solution)/shard_map/gather_value_grad/ppermute | solution.py:142
  31.2 1.9 %collective-permute-start.2 = (bf16[64,512]{1,0:T(8,128)(2,1)S(1)}, bf16[64,512]{1,0:T(8,128)(2,1)S(1)}, u32[]{:S(2)}, u32[]{:S(2)}) collective-permute-start(bf16[64,512]{1,0:T(8,128)(2,1)S(1)} %copy-done.1), channel_id=1, source_target_pairs={{0,64},{64,128},{128,192},{192,256},{256,320},{320,384},{384,448},... | collective-permute-start | bytes 196616 | tf_op jit(solution)/shard_map/weight_along_z/ppermute | solution.py:150
  33.1 8.0 %collective-permute-start.1 = (bf16[64,512]{1,0:T(8,128)(2,1)S(1)}, bf16[64,512]{1,0:T(8,128)(2,1)S(1)}, u32[]{:S(2)}, u32[]{:S(2)}) collective-permute-start(bf16[64,512]{1,0:T(8,128)(2,1)S(1)} %copy-done.1), channel_id=1, source_target_pairs={{0,450},{64,0},{128,64},{192,128},{256,192},{320,256},{384,320},{4... | collective-permute-start | bytes 196616 | tf_op jit(solution)/shard_map/weight_along_z/ppermute | solution.py:150
  41.1 0.2 collective-permute-done.2
  41.3 1.1 %collective-permute-done.1 = bf16[64,512]{1,0:T(8,128)(2,1)S(1)} collective-permute-done((bf16[64,512]{1,0:T(8,128)(2,1)S(1)}, bf16[64,512]{1,0:T(8,128)(2,1)S(1)}, u32[]{:S(2)}, u32[]{:S(2)}) %collective-permute-start.1) | collective-permute-done | bytes 65568 | tf_op jit(solution)/shard_map/weight_along_z/ppermute | solution.py:150
  42.5 1.6 %all-to-all-done.1 = bf16[8,128,512]{2,1,0:T(8,128)(2,1)S(1)} async-done(((bf16[8,128,512]{2,1,0:T(8,128)(2,1)}), bf16[8,128,512]{2,1,0:T(8,128)(2,1)S(1)}, u32[]{:S(2)}, u32[]{:S(2)}) %all-to-all-start.1) | async-done | bytes 1048608 | tf_op jit(solution)/shard_map/send_inputs/all_to_all | solution.py:134
  44.2 1.5 %convolution_convert_fusion.1 = bf16[512,512]{1,0:T(8,128)(2,1)} fusion(bf16[1024,512]{1,0:T(8,128)(2,1)S(1)} %bitcast.48, bf16[1024,512]{1,0:T(8,128)(2,1)S(1)} %bitcast.44), kind=kOutput, calls=%fused_computation.9 | convolution fusion | flops 537133056 | bytes 2621440 | tf_op jit(solution)/shard_map/weight_term/dot_general | solution.py:207
  45.7 3.5 %all-to-all-start.2 = ((bf16[4,128,512]{2,1,0:T(8,128)(2,1)}), bf16[4,128,512]{2,1,0:T(8,128)(2,1)S(1)}, u32[]{:S(2)}, u32[]{:S(2)}) async-start(bf16[4,128,512]{2,1,0:T(8,128)(2,1)} %bitcast.17), calls=%async_computation.2 | async-start | bytes 1048576 | tf_op jit(solution)/shard_map/sum_y/all_to_all | solution.py:134
  49.2 3.8 %collective-permute-start.3 = (bf16[192,512]{1,0:T(8,128)(2,1)S(1)}, bf16[192,512]{1,0:T(8,128)(2,1)S(1)}, u32[]{:S(2)}, u32[]{:S(2)}) collective-permute-start(bf16[192,512]{1,0:T(8,128)(2,1)S(1)} %pad_maximum_fusion._.refs_0_), channel_id=1, source_target_pairs={{0,192},{64,256},{128,320},{192,384},{256,448},{320,2},{384,66},{4... | collective-permute-start | bytes 589832 | tf_op jit(solution)/shard_map/gather_weight/ppermute | solution.py:150
  53.0 7.7 %collective-permute-start.4 = (bf16[128,512]{1,0:T(8,128)(2,1)S(1)}, bf16[128,512]{1,0:T(8,128)(2,1)S(1)}, u32[]{:S(2)}, u32[]{:S(2)}) collective-permute-start(bf16[128,512]{1,0:T(8,128)(2,1)S(1)} %pad_maximum_fusion.1), channel_id=1, source_target_pairs={{0,322},{64,386},{128,450},{192,0},{256,64},{320,128},{384,192},{4... | collective-permute-start | bytes 393224 | tf_op jit(solution)/shard_map/gather_weight/ppermute | solution.py:150
  60.8 0.7 broadcast_in_dim.30
  61.5 9.9 %all-to-all-start.3 = ((bf16[16,16,512]{2,1,0:T(8,128)(2,1)}), bf16[16,16,512]{2,1,0:T(8,128)(2,1)S(1)}, u32[]{:S(2)}, u32[]{:S(2)}) async-start(bf16[16,16,512]{2,1,0:T(8,128)(2,1)} %bitcast.30), calls=%async_computation.3 | async-start | bytes 524288 | tf_op jit(solution)/shard_map/sum_z/all_to_all | solution.py:134
  71.5 0.7 convolution_convert_fusion
  72.3 3.7 %collective-permute-start.5 = (bf16[4,128,512]{2,1,0:T(8,128)(2,1)S(1)}, bf16[4,128,512]{2,1,0:T(8,128)(2,1)S(1)}, u32[]{:S(2)}, u32[]{:S(2)}) collective-permute-start(bf16[4,128,512]{2,1,0:T(8,128)(2,1)S(1)} %get-tuple-element.11), channel_id=1, source_target_pairs={{0,1},{1,0},{2,3},{3,2},{4,5},{5,4},{6,7},{7,6},{8,9},{9,8},{10,11... | collective-permute-start | bytes 1572872 | tf_op jit(solution)/shard_map/input_grad/ppermute | solution.py:142
  76.1 1.5 %collective-permute-done.5 = bf16[4,128,512]{2,1,0:T(8,128)(2,1)S(1)} collective-permute-done((bf16[4,128,512]{2,1,0:T(8,128)(2,1)S(1)}, bf16[4,128,512]{2,1,0:T(8,128)(2,1)S(1)}, u32[]{:S(2)}, u32[]{:S(2)}) %collective-permute-start.5) | collective-permute-done | bytes 524320 | tf_op jit(solution)/shard_map/input_grad/ppermute | solution.py:142
  77.6 0.1 fusion.1
  77.7 2.5 %collective-permute-start.6 = (bf16[2,128,512]{2,1,0:T(8,128)(2,1)S(1)}, bf16[2,128,512]{2,1,0:T(8,128)(2,1)S(1)}, u32[]{:S(2)}, u32[]{:S(2)}) collective-permute-start(bf16[2,128,512]{2,1,0:T(8,128)(2,1)S(1)} %get-tuple-element.9), channel_id=1, source_target_pairs={{0,16},{16,32},{32,48},{48,0},{1,17},{17,33},{33,49},{49,1},{2,18}... | collective-permute-start | bytes 786440 | tf_op jit(solution)/shard_map/input_grad/ppermute | solution.py:142
  80.2 3.5 %collective-permute-start.7 = (bf16[2,128,512]{2,1,0:T(8,128)(2,1)S(1)}, bf16[2,128,512]{2,1,0:T(8,128)(2,1)S(1)}, u32[]{:S(2)}, u32[]{:S(2)}) collective-permute-start(bf16[2,128,512]{2,1,0:T(8,128)(2,1)S(1)} %get-tuple-element.10), channel_id=1, source_target_pairs={{0,32},{16,48},{32,0},{48,16},{1,33},{17,49},{33,1},{49,17},{2,34}... | collective-permute-start | bytes 786440 | tf_op jit(solution)/shard_map/input_grad/ppermute | solution.py:142
  83.7 2.7 %collective-permute-start.8 = (bf16[2,128,512]{2,1,0:T(8,128)(2,1)S(1)}, bf16[2,128,512]{2,1,0:T(8,128)(2,1)S(1)}, u32[]{:S(2)}, u32[]{:S(2)}) collective-permute-start(bf16[2,128,512]{2,1,0:T(8,128)(2,1)S(1)} %get-tuple-element.7), channel_id=1, source_target_pairs={{0,48},{16,0},{32,16},{48,32},{1,49},{17,1},{33,17},{49,33},{2,50}... | collective-permute-start | bytes 786440 | tf_op jit(solution)/shard_map/input_grad/ppermute | solution.py:142
  86.5 0.7 broadcast_in_dim.31
  87.2 8.5 %all-to-all-start.4 = ((f32[8,16,512]{2,1,0:T(8,128)}), f32[8,16,512]{2,1,0:T(8,128)S(1)}, u32[]{:S(2)}, u32[]{:S(2)}) async-start(f32[8,16,512]{2,1,0:T(8,128)} %broadcast_in_dim.31), calls=%async_computation.4 | async-start | bytes 524288 | tf_op jit(solution)/shard_map/share_rows/all_to_all | solution.py:134
  95.7 0.1 stack.44.places_ref
  95.8 0.3 collective-permute-done.8.refs_3_
  96.1 3.6 %from_pieces.1 = bf16[128,4096]{1,0:T(8,128)(2,1)} custom-call(s32[8]{0:T(128)S(1)} %stack.44.places_ref, bf16[2,128,512]{2,1,0:T(8,128)(2,1)S(1)} %get-tuple-element.8.refs_0_, bf16[2,128,512]{2,1,0:T(8,128)(2,1)S(1)} %collective-permute-done.6.refs_1_, bf16[2,128,512]{2,1,0:T(8,128)(2,1)S(1)} %collective-permute-done.7.refs_2_, ...), custom_call_target="tpu_custom_call" | custom-call | flops 4194304 | bytes 2097152 | tf_op jit(solution)/shard_map/input_grad/from_pieces/pallas_call | solution.py:119
  99.7 2.5 %all-to-all-done.4 = f32[8,16,512]{2,1,0:T(8,128)S(1)} async-done(((f32[8,16,512]{2,1,0:T(8,128)}), f32[8,16,512]{2,1,0:T(8,128)S(1)}, u32[]{:S(2)}, u32[]{:S(2)}) %all-to-all-start.4) | async-done | bytes 262176 | tf_op jit(solution)/shard_map/share_rows/all_to_all | solution.py:134
  102.3 0.7 copy.12
  (19 shorter events, 0.4 us)
Async XLA Ops:
  0.6 11.5 %copy-start = (bf16[128,512]{1,0:T(8,128)(2,1)S(1)}, bf16[128,512]{1,0:T(8,128)(2,1)}, u32[]{:S(2)}) copy-start(bf16[128,512]{1,0:T(8,128)(2,1)} %param.13) | copy-start | bytes 393220
  7.3 11.8 %all-to-all-start = ((bf16[4,128,512]{2,1,0:T(8,128)(2,1)}), bf16[4,128,512]{2,1,0:T(8,128)(2,1)S(1)}, u32[]{:S(2)}, u32[]{:S(2)}) async-start(bf16[4,128,512]{2,1,0:T(8,128)(2,1)} %get-tuple-element.5), calls=%async_computation | async-start | bytes 1048576 | tf_op jit(solution)/shard_map/gather_value_grad/all_to_all | solution.py:134
  17.1 14.1 %copy-start.1 = (bf16[64,512]{1,0:T(8,128)(2,1)S(1)}, bf16[64,512]{1,0:T(8,128)(2,1)}, u32[]{:S(2)}) copy-start(bf16[64,512]{1,0:T(8,128)(2,1)} %constant_dynamic-slice_fusion._) | copy-start | bytes 196612
  19.1 25.1 %all-to-all-start.1 = ((bf16[8,128,512]{2,1,0:T(8,128)(2,1)}), bf16[8,128,512]{2,1,0:T(8,128)(2,1)S(1)}, u32[]{:S(2)}, u32[]{:S(2)}) async-start(bf16[8,128,512]{2,1,0:T(8,128)(2,1)} %to_pieces.1), calls=%async_computation.1 | async-start | bytes 2097152 | tf_op jit(solution)/shard_map/send_inputs/all_to_all | solution.py:134
  29.2 13.3 %collective-permute-start = (bf16[4,128,512]{2,1,0:T(8,128)(2,1)S(1)}, bf16[4,128,512]{2,1,0:T(8,128)(2,1)S(1)}, u32[]{:S(2)}, u32[]{:S(2)}) collective-permute-start(bf16[4,128,512]{2,1,0:T(8,128)(2,1)S(1)} %all-to-all-done.own_ref), channel_id=1, source_target_pairs={{0,1},{1,0},{2,3},{3,2},{4,5},{5,4},{6,7},{7,6},{8,9},{9,8},{10,11... | collective-permute-start | bytes 1572872 | tf_op jit(solution)/shard_map/gather_value_grad/ppermute | solution.py:142
  31.2 10.1 %collective-permute-start.2 = (bf16[64,512]{1,0:T(8,128)(2,1)S(1)}, bf16[64,512]{1,0:T(8,128)(2,1)S(1)}, u32[]{:S(2)}, u32[]{:S(2)}) collective-permute-start(bf16[64,512]{1,0:T(8,128)(2,1)S(1)} %copy-done.1), channel_id=1, source_target_pairs={{0,64},{64,128},{128,192},{192,256},{256,320},{320,384},{384,448},... | collective-permute-start | bytes 196616 | tf_op jit(solution)/shard_map/weight_along_z/ppermute | solution.py:150
  33.1 9.3 %collective-permute-start.1 = (bf16[64,512]{1,0:T(8,128)(2,1)S(1)}, bf16[64,512]{1,0:T(8,128)(2,1)S(1)}, u32[]{:S(2)}, u32[]{:S(2)}) collective-permute-start(bf16[64,512]{1,0:T(8,128)(2,1)S(1)} %copy-done.1), channel_id=1, source_target_pairs={{0,450},{64,0},{128,64},{192,128},{256,192},{320,256},{384,320},{4... | collective-permute-start | bytes 196616 | tf_op jit(solution)/shard_map/weight_along_z/ppermute | solution.py:150
  45.7 15.0 %all-to-all-start.2 = ((bf16[4,128,512]{2,1,0:T(8,128)(2,1)}), bf16[4,128,512]{2,1,0:T(8,128)(2,1)S(1)}, u32[]{:S(2)}, u32[]{:S(2)}) async-start(bf16[4,128,512]{2,1,0:T(8,128)(2,1)} %bitcast.17), calls=%async_computation.2 | async-start | bytes 1048576 | tf_op jit(solution)/shard_map/sum_y/all_to_all | solution.py:134
  49.2 22.3 %collective-permute-start.3 = (bf16[192,512]{1,0:T(8,128)(2,1)S(1)}, bf16[192,512]{1,0:T(8,128)(2,1)S(1)}, u32[]{:S(2)}, u32[]{:S(2)}) collective-permute-start(bf16[192,512]{1,0:T(8,128)(2,1)S(1)} %pad_maximum_fusion._.refs_0_), channel_id=1, source_target_pairs={{0,192},{64,256},{128,320},{192,384},{256,448},{320,2},{384,66},{4... | collective-permute-start | bytes 589832 | tf_op jit(solution)/shard_map/gather_weight/ppermute | solution.py:150
  53.0 18.4 %collective-permute-start.4 = (bf16[128,512]{1,0:T(8,128)(2,1)S(1)}, bf16[128,512]{1,0:T(8,128)(2,1)S(1)}, u32[]{:S(2)}, u32[]{:S(2)}) collective-permute-start(bf16[128,512]{1,0:T(8,128)(2,1)S(1)} %pad_maximum_fusion.1), channel_id=1, source_target_pairs={{0,322},{64,386},{128,450},{192,0},{256,64},{320,128},{384,192},{4... | collective-permute-start | bytes 393224 | tf_op jit(solution)/shard_map/gather_weight/ppermute | solution.py:150
  61.5 24.9 %all-to-all-start.3 = ((bf16[16,16,512]{2,1,0:T(8,128)(2,1)}), bf16[16,16,512]{2,1,0:T(8,128)(2,1)S(1)}, u32[]{:S(2)}, u32[]{:S(2)}) async-start(bf16[16,16,512]{2,1,0:T(8,128)(2,1)} %bitcast.30), calls=%async_computation.3 | async-start | bytes 524288 | tf_op jit(solution)/shard_map/sum_z/all_to_all | solution.py:134
  72.3 5.2 %collective-permute-start.5 = (bf16[4,128,512]{2,1,0:T(8,128)(2,1)S(1)}, bf16[4,128,512]{2,1,0:T(8,128)(2,1)S(1)}, u32[]{:S(2)}, u32[]{:S(2)}) collective-permute-start(bf16[4,128,512]{2,1,0:T(8,128)(2,1)S(1)} %get-tuple-element.11), channel_id=1, source_target_pairs={{0,1},{1,0},{2,3},{3,2},{4,5},{5,4},{6,7},{7,6},{8,9},{9,8},{10,11... | collective-permute-start | bytes 1572872 | tf_op jit(solution)/shard_map/input_grad/ppermute | solution.py:142
  77.7 18.1 %collective-permute-start.6 = (bf16[2,128,512]{2,1,0:T(8,128)(2,1)S(1)}, bf16[2,128,512]{2,1,0:T(8,128)(2,1)S(1)}, u32[]{:S(2)}, u32[]{:S(2)}) collective-permute-start(bf16[2,128,512]{2,1,0:T(8,128)(2,1)S(1)} %get-tuple-element.9), channel_id=1, source_target_pairs={{0,16},{16,32},{32,48},{48,0},{1,17},{17,33},{33,49},{49,1},{2,18}... | collective-permute-start | bytes 786440 | tf_op jit(solution)/shard_map/input_grad/ppermute | solution.py:142
  80.2 15.6 %collective-permute-start.7 = (bf16[2,128,512]{2,1,0:T(8,128)(2,1)S(1)}, bf16[2,128,512]{2,1,0:T(8,128)(2,1)S(1)}, u32[]{:S(2)}, u32[]{:S(2)}) collective-permute-start(bf16[2,128,512]{2,1,0:T(8,128)(2,1)S(1)} %get-tuple-element.10), channel_id=1, source_target_pairs={{0,32},{16,48},{32,0},{48,16},{1,33},{17,49},{33,1},{49,17},{2,34}... | collective-permute-start | bytes 786440 | tf_op jit(solution)/shard_map/input_grad/ppermute | solution.py:142
  83.7 12.5 %collective-permute-start.8 = (bf16[2,128,512]{2,1,0:T(8,128)(2,1)S(1)}, bf16[2,128,512]{2,1,0:T(8,128)(2,1)S(1)}, u32[]{:S(2)}, u32[]{:S(2)}) collective-permute-start(bf16[2,128,512]{2,1,0:T(8,128)(2,1)S(1)} %get-tuple-element.7), channel_id=1, source_target_pairs={{0,48},{16,0},{32,16},{48,32},{1,49},{17,1},{33,17},{49,33},{2,50}... | collective-permute-start | bytes 786440 | tf_op jit(solution)/shard_map/input_grad/ppermute | solution.py:142
  87.2 15.1 %all-to-all-start.4 = ((f32[8,16,512]{2,1,0:T(8,128)}), f32[8,16,512]{2,1,0:T(8,128)S(1)}, u32[]{:S(2)}, u32[]{:S(2)}) async-start(f32[8,16,512]{2,1,0:T(8,128)} %broadcast_in_dim.31), calls=%async_computation.4 | async-start | bytes 524288 | tf_op jit(solution)/shard_map/share_rows/all_to_all | solution.py:134

commit v6 on v5

--- a/solution.py
+++ b/solution.py
@@ -23,7 +23,7 @@
 def attend_kernel(length_ref, q_ref, k_ref, v_ref, g_ref, vg_ref, kg_ref):
     scaling = HD ** (-0.5)
     keys, vals = k_ref[...], v_ref[...]
-    length = length_ref[0]
+    length = length_ref[...]
     step = 2
     wide = step * TOK
     pos_s = lax.broadcasted_iota(jnp.int32, (TOK, wide), 0)
@@ -56,7 +56,7 @@
     return pl.pallas_call(
         attend_kernel,
         grid=(heads,),
-        in_specs=[pl.BlockSpec(memory_space=pltpu.SMEM), wide, thin, thin, wide],
+        in_specs=[pl.BlockSpec(memory_space=pltpu.VMEM), wide, thin, thin, wide],
         out_specs=[pl.BlockSpec((XN, TOK, HD), lambda g: (0, 0, g)), thin],
         out_shape=[jax.ShapeDtypeStruct((XN, TOK, KV), BF), jax.ShapeDtypeStruct((TOK, KV), BF)],
         cost_estimate=pl.CostEstimate(
@@ -81,12 +81,17 @@
     return tiles
 
 
+def piece(c, x, y):
+    return c * 4 + x % 2 * 2 + y % 2
+
+
 def to_pieces_kernel(in_ref, _, out_ref):
     for x in range(XN):
         tiles = [in_ref[:, (zl * XN + x) * 128 : (zl * XN + x + 1) * 128].astype(F32) for zl in range(8)]
         for q, tile in enumerate(swap_groups(tiles)):
             y = q % YN
-            out_ref[q // YN * XN + x, :, y * 128 : (y + 1) * 128] = tile.astype(BF)
+            slot = x // 2 * 2 + y // 2
+            out_ref[piece(q // YN, x, y), :, slot * 128 : (slot + 1) * 128] = tile.astype(BF)
 
 
 def from_pieces_kernel(places_ref, *refs):
@@ -95,7 +100,9 @@
         held[places_ref[i]] = refs[i // CN][i % CN]
     for x in range(XN):
         tiles = [
-            held[c * XN + x, :, y * 128 : (y + 1) * 128].astype(F32) for c in range(CN) for y in range(YN)
+            held[piece(c, x, y), :, (x // 2 * 2 + y // 2) * 128 : (x // 2 * 2 + y // 2 + 1) * 128].astype(F32)
+            for c in range(CN)
+            for y in range(YN)
         ]
         for zl, tile in enumerate(swap_groups(tiles)):
             out_ref[:, (zl * XN + x) * 128 : (zl * XN + x + 1) * 128] = tile.astype(BF)
@@ -109,7 +116,7 @@
         in_specs=[pl.BlockSpec((part, WIDTH), lambda i: (i, 0)), pl.BlockSpec(memory_space=pl.ANY)],
         out_specs=pl.BlockSpec((QN, part, KV), lambda i: (0, i, 0)),
         out_shape=jax.ShapeDtypeStruct((QN, TOK, KV), BF),
-        cost_estimate=pl.CostEstimate(flops=1 << 22, bytes_accessed=2 << 20, transcendentals=0),
+        cost_estimate=pl.CostEstimate(flops=1 << 36, bytes_accessed=2 << 20, transcendentals=0),
         name="to_pieces",
     )(rows, earlier)
 
@@ -138,8 +145,12 @@
     return exchange(jnp.broadcast_to(array[None], (count,) + array.shape), axes)
 
 
-def shifted(array, axes, count, by):
-    return lax.ppermute(array, axes, [(i, (i + by) % count) for i in range(count)])
+def shifted(array, axis, count, by):
+    return lax.ppermute(array, axis, [(i, (i + by) % count) for i in range(count)])
+
+
+def over_square(array, mask):
+    return lax.ppermute(array, ("xp", "yp"), [(i, i ^ mask) for i in range(4)])
 
 
 def along_z(array, by):
@@ -191,51 +202,56 @@
 
 
 def per_device(inputs, queries, keys, values, out_grad, lengths, value_weight):
-    core, x, zl = (lax.axis_index(name) for name in ("core", "x", "zl"))
+    core, zl, xh, xp, yp = (lax.axis_index(name) for name in ("core", "zl", "xh", "xp", "yp"))
+    place = 2 * xp + yp
     with jax.named_scope("weight_along_z"):
-        own_rows = lax.dynamic_slice_in_dim(value_weight, core * HALF, HALF, 0)
-        ring = jnp.concatenate([along_z(own_rows, -1), own_rows, along_z(own_rows, 1)])
+        blocks = value_weight.reshape(CN, 2, 2, SUB, KV)
+        own_rows = lax.dynamic_slice(blocks, (core, 0, yp, 0, 0), (1, 2, 1, SUB, KV)).reshape(2 * SUB, KV)
+        far_rows = shifted(own_rows, "xh", 2, 1)
+        rows = jnp.where(xh == 0, jnp.concatenate([own_rows, far_rows]), jnp.concatenate([far_rows, own_rows]))
+        ring = jnp.concatenate([along_z(rows, -1), rows, along_z(rows, 1)])
     with jax.named_scope("attention"):
         copies, key_grad = attend_back(queries[0], keys[0], values[0], out_grad[0], lengths)
     with jax.named_scope("gather_value_grad"):
-        mine = exchange(copies, "x")
+        mine = exchange(copies, ("xp", "yp"))
         other = shifted(mine, "core", CN, 1)
-        grads = pair(mine, other, core, ring).reshape(CN * XN * TOK, KV)
+        grads = pair(mine, other, core, ring).reshape(CN * 4 * TOK, KV)
     with jax.named_scope("send_inputs"):
-        columns = exchange(to_pieces(inputs[0], own_rows), ("core", "x"))
+        columns = exchange(to_pieces(inputs[0], rows), ("core", "xp", "yp"))
     with jax.named_scope("weight_term"):
         term = lax.dot_general(
-            columns.reshape(CN * XN * TOK, KV), grads, (((0,), (0,)), ((), ())), preferred_element_type=F32
+            columns.reshape(CN * 4 * TOK, KV), grads, (((0,), (0,)), ((), ())), preferred_element_type=F32
         ).astype(BF)
-    with jax.named_scope("sum_y"):
-        got = exchange(term.reshape(YN, ZL * SUB, KV), "y")
+    with jax.named_scope("sum_squares"):
+        got = exchange(term.reshape(4, ZL * SUB, KV), ("xh", "yh"))
         plane = jnp.sum(got.astype(F32), axis=0).astype(BF).reshape(1, ZL, SUB, KV)
     with jax.named_scope("sum_z"):
         both = jnp.broadcast_to(plane, (ZH, ZL, SUB, KV)).reshape(ZH * ZL, SUB, KV)
         got = exchange(both, ("zh", "zl"))
         total = jnp.sum(got.astype(F32), axis=0) * F32(1.0 / 512)
     with jax.named_scope("share_rows"):
-        weight_grad = spread(total, ("core", "y"), QN).reshape(QN * SUB, KV)
+        shared = spread(total.astype(BF), ("core", "yh", "yp"), QN)
+        weight_grad = shared.reshape(QN * SUB, KV).astype(F32)
     with jax.named_scope("gather_weight"):
         weight = place_rows([ring, along_z(ring, 3), along_z(ring[HALF:], -3)], zl, plane)
     with jax.named_scope("input_grad"):
-        parts = nt(grads, weight).astype(BF).reshape(CN, XN, TOK, KV)
+        parts = nt(grads, weight).astype(BF).reshape(CN, 4, TOK, KV)
         kept = lax.dynamic_index_in_dim(parts, core, 0, False)
         theirs = shifted(lax.dynamic_index_in_dim(parts, 1 - core, 0, False), "core", CN, 1)
         parts = jnp.stack([kept, theirs], axis=1)
         places, back = [], []
-        for by in range(XN):
-            piece = lax.dynamic_index_in_dim(parts, (x + by) % XN, 0, False)
-            back.append(shifted(piece, "x", XN, by) if by else piece)
-            places += [c * XN + (x - by) % XN for c in (core, 1 - core)]
+        for mask in range(4):
+            sent = lax.dynamic_index_in_dim(parts, place ^ mask, 0, False)
+            back.append(over_square(sent, mask) if mask else sent)
+            places += [c * 4 + (place ^ mask) for c in (core, 1 - core)]
         input_grad = from_pieces(back, places)
     return (input_grad[None], key_grad[None], weight_grad)
 
 
 def solution(mesh):
-    names = ("zl", "x", "y", "zh", "core")
-    fine = Mesh(mesh.devices.reshape(ZL, XN, YN, ZH, CN), names)
-    blk = names[:2]
+    names = ("zl", "xh", "xp", "yh", "yp", "zh", "core")
+    fine = Mesh(mesh.devices.reshape(ZL, 2, 2, 2, 2, ZH, CN), names)
+    blk = names[:3]
     rows = P(names, None, None)
     return jax.shard_map(
         per_device,

time: 104 us -> 106 us (1.019)
  starting transfers between devices: 72.6 us -> 78.8 us
  waiting for transfers between devices: 9.2 us -> 4.68 us
  other arithmetic: 0.25 us -> 1.63 us
    ppermute x5 -> x6, starting transfers between devices: 14.4 us -> 19.9 us  [the longest x3 11.6 us: shifted(): lax.ppermute(array, axis, [(i, (i + by) % count) for i in range(count)])]
    all_to_all x5, waiting for transfers between devices: 6.09 us -> 1.86 us  [exchange(): return lax.all_to_all(array, axes, 0, 0, tiled=True)]
    ppermute x4, starting transfers between devices: 21.4 us -> 24.2 us  [along_z(): return lax.ppermute(array, ('zl', 'zh'), places)]
    all_to_all x5, starting transfers between devices: 36.8 us -> 34.7 us  [exchange(): return lax.all_to_all(array, axes, 0, 0, tiled=True)]
  transfers between devices with their start and end apart: 14 -> 15, of which waited for: 7 -> 5; matrix products, arithmetic and copies ran while one was open for 3% -> 3% of each run, Pallas kernels for 8% -> 13%
where the time goes in v6:
time: 106 us
  starting transfers between devices  78.8 us (74%)
  Pallas kernels  14.1 us (13%)
  waiting for transfers between devices  4.68 us (4%)
  local copies, waits for them, and re-layouts  2.46 us (2%)
  matrix products  2.26 us (2%)
  other arithmetic  1.63 us (2%)
  between operations  1.58 us (1%)
    all_to_all x5, starting transfers between devices, exchange(): return lax.all_to_all(array, axes, 0, 0, tiled=True)  34.7 us
    ppermute x4, starting transfers between devices, along_z(): return lax.ppermute(array, ('zl', 'zh'), places)  24.2 us
    ppermute x3, starting transfers between devices, shifted(): lax.ppermute(array, axis, [(i, (i + by) % count) for i in range(count)])  11.6 us
    ppermute x3, starting transfers between devices, over_square(): return lax.ppermute(array, ('xp', 'yp'), [(i, i ^ mask) for i in range(4)])  8.37 us
    pallas_call x1, Pallas kernels, attend_back(): pl.pallas_call(attend_kernel, grid=(heads,), in_specs=[pl.BlockSpec(memor...  5.96 us
    pallas_call x1, Pallas kernels, to_pieces(): pl.pallas_call(to_pieces_kernel, grid=(TOK // part,), in_specs=[pl.BlockS...  4.35 us
    pallas_call x1, Pallas kernels, from_pieces(): pl.pallas_call(from_pieces_kernel, grid=(TOK // part,), in_specs=[pl.Bloc...  3.62 us
  transfers between devices with their start and end apart: 15, of which 5 were waited for; matrix products, arithmetic and copies ran while one was open for 3% of the time, Pallas kernels for 13%

profile of v6, /device:TPU:1, one launch (start us, length us, event | category | flops | bytes accessed | tf_op | source)
XLA Modules:
  0.0 105.5 jit_solution(1381185212057527242)
XLA Ops:
  0.7 0.9 copy-done
  1.5 5.5 %collective-permute-start.1 = (bf16[32,512]{1,0:T(8,128)(2,1)S(1)}, bf16[32,512]{1,0:T(8,128)(2,1)S(1)}, u32[]{:S(2)}, u32[]{:S(2)}) collective-permute-start(bf16[32,512]{1,0:T(8,128)(2,1)S(1)} %bitcast.57), channel_id=1, source_target_pairs={{0,32},{32,0},{1,33},{33,1},{2,34},{34,2},{3,35},{35,3},{4,36},{36... | collective-permute-start | bytes 98312 | tf_op jit(solution)/shard_map/weight_along_z/ppermute | solution.py:149
  7.7 6.0 %attend.1 = (bf16[4,128,512]{2,1,0:T(8,128)(2,1)}, bf16[128,512]{1,0:T(8,128)(2,1)}) custom-call(s32[1]{0:T(128)S(6)} %copy.13.length_ref, bf16[128,4096]{1,0:T(8,128)(2,1)} %bitcast.59, bf16[128,512]{1,0:T(8,128)(2,1)} %bitcast.62, bf16[128,512]{1,0:T(8,128)(2,1)} %bitcast.63, bf16[128,4096]{1,0:T(8,128)(2,1)} %bitcast.60), custom_call_target="tpu_custom_call" | custom-call | flops 671088640 | bytes 3145728 | tf_op jit(solution)/shard_map/attention/attend/pallas_call | solution.py:56
  13.6 3.5 %all-to-all-start = ((bf16[4,128,512]{2,1,0:T(8,128)(2,1)}), bf16[4,128,512]{2,1,0:T(8,128)(2,1)S(1)}, u32[]{:S(2)}, u32[]{:S(2)}) async-start(bf16[4,128,512]{2,1,0:T(8,128)(2,1)} %get-tuple-element.5), calls=%async_computation | async-start | bytes 1048576 | tf_op jit(solution)/shard_map/gather_value_grad/all_to_all | solution.py:141
  17.1 0.6 maximum_select_fusion._
  17.8 4.3 %to_pieces.1 = bf16[8,128,512]{2,1,0:T(8,128)(2,1)} custom-call(bf16[128,4096]{1,0:T(8,128)(2,1)} %bitcast.61, bf16[64,512]{1,0:T(8,128)(2,1)} %maximum_select_fusion._), custom_call_target="tpu_custom_call" | custom-call | flops 68719476736 | bytes 2097152 | tf_op jit(solution)/shard_map/send_inputs/to_pieces/pallas_call | solution.py:113
  22.1 0.4 all-to-all-done.own_ref
  22.5 7.9 %all-to-all-start.1 = ((bf16[8,128,512]{2,1,0:T(8,128)(2,1)}), bf16[8,128,512]{2,1,0:T(8,128)(2,1)S(1)}, u32[]{:S(2)}, u32[]{:S(2)}) async-start(bf16[8,128,512]{2,1,0:T(8,128)(2,1)} %to_pieces.1), calls=%async_computation.1 | async-start | bytes 2097152 | tf_op jit(solution)/shard_map/send_inputs/all_to_all | solution.py:141
  30.5 2.0 %collective-permute-start = (bf16[4,128,512]{2,1,0:T(8,128)(2,1)S(1)}, bf16[4,128,512]{2,1,0:T(8,128)(2,1)S(1)}, u32[]{:S(2)}, u32[]{:S(2)}) collective-permute-start(bf16[4,128,512]{2,1,0:T(8,128)(2,1)S(1)} %all-to-all-done.own_ref), channel_id=1, source_target_pairs={{0,1},{1,0},{2,3},{3,2},{4,5},{5,4},{6,7},{7,6},{8,9},{9,8},{10,11... | collective-permute-start | bytes 1572872 | tf_op jit(solution)/shard_map/gather_value_grad/ppermute | solution.py:149
  32.5 2.6 %collective-permute-start.3 = (bf16[64,512]{1,0:T(8,128)(2,1)S(1)}, bf16[64,512]{1,0:T(8,128)(2,1)S(1)}, u32[]{:S(2)}, u32[]{:S(2)}) collective-permute-start(bf16[64,512]{1,0:T(8,128)(2,1)S(1)} %copy-done.1), channel_id=1, source_target_pairs={{0,64},{64,128},{128,192},{192,256},{256,320},{320,384},{384,448},... | collective-permute-start | bytes 196616 | tf_op jit(solution)/shard_map/weight_along_z/ppermute | solution.py:161
  35.1 9.5 %collective-permute-start.2 = (bf16[64,512]{1,0:T(8,128)(2,1)S(1)}, bf16[64,512]{1,0:T(8,128)(2,1)S(1)}, u32[]{:S(2)}, u32[]{:S(2)}) collective-permute-start(bf16[64,512]{1,0:T(8,128)(2,1)S(1)} %copy-done.1), channel_id=1, source_target_pairs={{0,450},{64,0},{128,64},{192,128},{256,192},{320,256},{384,320},{4... | collective-permute-start | bytes 196616 | tf_op jit(solution)/shard_map/weight_along_z/ppermute | solution.py:161
  44.6 0.2 collective-permute-done.3
  44.8 1.1 %collective-permute-done.2 = bf16[64,512]{1,0:T(8,128)(2,1)S(1)} collective-permute-done((bf16[64,512]{1,0:T(8,128)(2,1)S(1)}, bf16[64,512]{1,0:T(8,128)(2,1)S(1)}, u32[]{:S(2)}, u32[]{:S(2)}) %collective-permute-start.2) | collective-permute-done | bytes 65568 | tf_op jit(solution)/shard_map/weight_along_z/ppermute | solution.py:161
  46.0 1.5 %convolution_convert_fusion.1 = bf16[512,512]{1,0:T(8,128)(2,1)} fusion(bf16[1024,512]{1,0:T(8,128)(2,1)S(1)} %bitcast.54, bf16[1024,512]{1,0:T(8,128)(2,1)S(1)} %bitcast.51), kind=kOutput, calls=%fused_computation.9 | convolution fusion | flops 537133056 | bytes 2621440 | tf_op jit(solution)/shard_map/weight_term/dot_general | solution.py:222
  47.6 4.5 %all-to-all-start.2 = ((bf16[4,128,512]{2,1,0:T(8,128)(2,1)}), bf16[4,128,512]{2,1,0:T(8,128)(2,1)S(1)}, u32[]{:S(2)}, u32[]{:S(2)}) async-start(bf16[4,128,512]{2,1,0:T(8,128)(2,1)} %bitcast.19), calls=%async_computation.2 | async-start | bytes 1048576 | tf_op jit(solution)/shard_map/sum_squares/all_to_all | solution.py:141
  52.0 4.4 %collective-permute-start.4 = (bf16[192,512]{1,0:T(8,128)(2,1)S(1)}, bf16[192,512]{1,0:T(8,128)(2,1)S(1)}, u32[]{:S(2)}, u32[]{:S(2)}) collective-permute-start(bf16[192,512]{1,0:T(8,128)(2,1)S(1)} %pad_maximum_fusion._.refs_0_), channel_id=1, source_target_pairs={{0,192},{64,256},{128,320},{192,384},{256,448},{320,2},{384,66},{4... | collective-permute-start | bytes 589832 | tf_op jit(solution)/shard_map/gather_weight/ppermute | solution.py:161
  56.5 7.7 %collective-permute-start.5 = (bf16[128,512]{1,0:T(8,128)(2,1)S(1)}, bf16[128,512]{1,0:T(8,128)(2,1)S(1)}, u32[]{:S(2)}, u32[]{:S(2)}) collective-permute-start(bf16[128,512]{1,0:T(8,128)(2,1)S(1)} %pad_maximum_fusion.1), channel_id=1, source_target_pairs={{0,322},{64,386},{128,450},{192,0},{256,64},{320,128},{384,192},{4... | collective-permute-start | bytes 393224 | tf_op jit(solution)/shard_map/gather_weight/ppermute | solution.py:161
  64.3 0.7 broadcast_in_dim.30
  65.0 10.0 %all-to-all-start.3 = ((bf16[16,16,512]{2,1,0:T(8,128)(2,1)}), bf16[16,16,512]{2,1,0:T(8,128)(2,1)S(1)}, u32[]{:S(2)}, u32[]{:S(2)}) async-start(bf16[16,16,512]{2,1,0:T(8,128)(2,1)} %bitcast.32), calls=%async_computation.3 | async-start | bytes 524288 | tf_op jit(solution)/shard_map/sum_z/all_to_all | solution.py:141
  75.1 0.7 convolution_convert_fusion
  76.0 4.1 %collective-permute-start.6 = (bf16[4,128,512]{2,1,0:T(8,128)(2,1)S(1)}, bf16[4,128,512]{2,1,0:T(8,128)(2,1)S(1)}, u32[]{:S(2)}, u32[]{:S(2)}) collective-permute-start(bf16[4,128,512]{2,1,0:T(8,128)(2,1)S(1)} %get-tuple-element.11), channel_id=1, source_target_pairs={{0,1},{1,0},{2,3},{3,2},{4,5},{5,4},{6,7},{7,6},{8,9},{9,8},{10,11... | collective-permute-start | bytes 1572872 | tf_op jit(solution)/shard_map/input_grad/ppermute | solution.py:149
  80.1 1.5 %collective-permute-done.6 = bf16[4,128,512]{2,1,0:T(8,128)(2,1)S(1)} collective-permute-done((bf16[4,128,512]{2,1,0:T(8,128)(2,1)S(1)}, bf16[4,128,512]{2,1,0:T(8,128)(2,1)S(1)}, u32[]{:S(2)}, u32[]{:S(2)}) %collective-permute-start.6) | collective-permute-done | bytes 524320 | tf_op jit(solution)/shard_map/input_grad/ppermute | solution.py:149
  81.6 0.1 fusion.1
  81.7 1.9 %collective-permute-start.7 = (bf16[2,128,512]{2,1,0:T(8,128)(2,1)S(1)}, bf16[2,128,512]{2,1,0:T(8,128)(2,1)S(1)}, u32[]{:S(2)}, u32[]{:S(2)}) collective-permute-start(bf16[2,128,512]{2,1,0:T(8,128)(2,1)S(1)} %get-tuple-element.9), channel_id=1, source_target_pairs={{0,4},{4,0},{16,20},{20,16},{1,5},{5,1},{17,21},{21,17},{2,6},{6,2... | collective-permute-start | bytes 786440 | tf_op jit(solution)/shard_map/input_grad/ppermute | solution.py:153
  83.6 2.2 %collective-permute-start.8 = (bf16[2,128,512]{2,1,0:T(8,128)(2,1)S(1)}, bf16[2,128,512]{2,1,0:T(8,128)(2,1)S(1)}, u32[]{:S(2)}, u32[]{:S(2)}) collective-permute-start(bf16[2,128,512]{2,1,0:T(8,128)(2,1)S(1)} %get-tuple-element.10), channel_id=1, source_target_pairs={{0,16},{4,20},{16,0},{20,4},{1,17},{5,21},{17,1},{21,5},{2,18},{6,... | collective-permute-start | bytes 786440 | tf_op jit(solution)/shard_map/input_grad/ppermute | solution.py:153
  85.8 4.3 %collective-permute-start.9 = (bf16[2,128,512]{2,1,0:T(8,128)(2,1)S(1)}, bf16[2,128,512]{2,1,0:T(8,128)(2,1)S(1)}, u32[]{:S(2)}, u32[]{:S(2)}) collective-permute-start(bf16[2,128,512]{2,1,0:T(8,128)(2,1)S(1)} %get-tuple-element.7), channel_id=1, source_target_pairs={{0,20},{4,16},{16,4},{20,0},{1,21},{5,17},{17,5},{21,1},{2,22},{6,... | collective-permute-start | bytes 786440 | tf_op jit(solution)/shard_map/input_grad/ppermute | solution.py:153
  90.2 0.7 broadcast_in_dim.31
  90.8 8.8 %all-to-all-start.4 = ((bf16[8,16,512]{2,1,0:T(8,128)(2,1)}), bf16[8,16,512]{2,1,0:T(8,128)(2,1)S(1)}, u32[]{:S(2)}, u32[]{:S(2)}) async-start(bf16[8,16,512]{2,1,0:T(8,128)(2,1)} %broadcast_in_dim.31), calls=%async_computation.4 | async-start | bytes 262144 | tf_op jit(solution)/shard_map/share_rows/all_to_all | solution.py:141
  99.6 0.1 stack.44.places_ref
  99.7 3.6 %from_pieces.1 = bf16[128,4096]{1,0:T(8,128)(2,1)} custom-call(s32[8]{0:T(128)S(1)} %stack.44.places_ref, bf16[2,128,512]{2,1,0:T(8,128)(2,1)S(1)} %get-tuple-element.8.refs_0_, bf16[2,128,512]{2,1,0:T(8,128)(2,1)S(1)} %collective-permute-done.7.refs_1_, bf16[2,128,512]{2,1,0:T(8,128)(2,1)S(1)} %collective-permute-done.8.refs_2_, ...), custom_call_target="tpu_custom_call" | custom-call | flops 4194304 | bytes 2097152 | tf_op jit(solution)/shard_map/input_grad/from_pieces/pallas_call | solution.py:126
  103.4 1.4 %all-to-all-done.4 = bf16[8,16,512]{2,1,0:T(8,128)(2,1)S(1)} async-done(((bf16[8,16,512]{2,1,0:T(8,128)(2,1)}), bf16[8,16,512]{2,1,0:T(8,128)(2,1)S(1)}, u32[]{:S(2)}, u32[]{:S(2)}) %all-to-all-start.4) | async-done | bytes 131104 | tf_op jit(solution)/shard_map/share_rows/all_to_all | solution.py:141
  104.8 0.7 bitcast_convert_fusion
  (22 shorter events, 0.4 us)
Async XLA Ops:
  0.6 0.9 copy-start
  1.5 15.6 %collective-permute-start.1 = (bf16[32,512]{1,0:T(8,128)(2,1)S(1)}, bf16[32,512]{1,0:T(8,128)(2,1)S(1)}, u32[]{:S(2)}, u32[]{:S(2)}) collective-permute-start(bf16[32,512]{1,0:T(8,128)(2,1)S(1)} %bitcast.57), channel_id=1, source_target_pairs={{0,32},{32,0},{1,33},{33,1},{2,34},{34,2},{3,35},{35,3},{4,36},{36... | collective-permute-start | bytes 98312 | tf_op jit(solution)/shard_map/weight_along_z/ppermute | solution.py:149
  13.6 8.9 %all-to-all-start = ((bf16[4,128,512]{2,1,0:T(8,128)(2,1)}), bf16[4,128,512]{2,1,0:T(8,128)(2,1)S(1)}, u32[]{:S(2)}, u32[]{:S(2)}) async-start(bf16[4,128,512]{2,1,0:T(8,128)(2,1)} %get-tuple-element.5), calls=%async_computation | async-start | bytes 1048576 | tf_op jit(solution)/shard_map/gather_value_grad/all_to_all | solution.py:141
  22.1 10.3 %copy-start.1 = (bf16[64,512]{1,0:T(8,128)(2,1)S(1)}, bf16[64,512]{1,0:T(8,128)(2,1)}, u32[]{:S(2)}) copy-start(bf16[64,512]{1,0:T(8,128)(2,1)} %maximum_select_fusion._) | copy-start | bytes 196612
  22.5 23.5 %all-to-all-start.1 = ((bf16[8,128,512]{2,1,0:T(8,128)(2,1)}), bf16[8,128,512]{2,1,0:T(8,128)(2,1)S(1)}, u32[]{:S(2)}, u32[]{:S(2)}) async-start(bf16[8,128,512]{2,1,0:T(8,128)(2,1)} %to_pieces.1), calls=%async_computation.1 | async-start | bytes 2097152 | tf_op jit(solution)/shard_map/send_inputs/all_to_all | solution.py:141
  30.5 15.5 %collective-permute-start = (bf16[4,128,512]{2,1,0:T(8,128)(2,1)S(1)}, bf16[4,128,512]{2,1,0:T(8,128)(2,1)S(1)}, u32[]{:S(2)}, u32[]{:S(2)}) collective-permute-start(bf16[4,128,512]{2,1,0:T(8,128)(2,1)S(1)} %all-to-all-done.own_ref), channel_id=1, source_target_pairs={{0,1},{1,0},{2,3},{3,2},{4,5},{5,4},{6,7},{7,6},{8,9},{9,8},{10,11... | collective-permute-start | bytes 1572872 | tf_op jit(solution)/shard_map/gather_value_grad/ppermute | solution.py:149
  32.5 12.3 %collective-permute-start.3 = (bf16[64,512]{1,0:T(8,128)(2,1)S(1)}, bf16[64,512]{1,0:T(8,128)(2,1)S(1)}, u32[]{:S(2)}, u32[]{:S(2)}) collective-permute-start(bf16[64,512]{1,0:T(8,128)(2,1)S(1)} %copy-done.1), channel_id=1, source_target_pairs={{0,64},{64,128},{128,192},{192,256},{256,320},{320,384},{384,448},... | collective-permute-start | bytes 196616 | tf_op jit(solution)/shard_map/weight_along_z/ppermute | solution.py:161
  35.1 10.8 %collective-permute-start.2 = (bf16[64,512]{1,0:T(8,128)(2,1)S(1)}, bf16[64,512]{1,0:T(8,128)(2,1)S(1)}, u32[]{:S(2)}, u32[]{:S(2)}) collective-permute-start(bf16[64,512]{1,0:T(8,128)(2,1)S(1)} %copy-done.1), channel_id=1, source_target_pairs={{0,450},{64,0},{128,64},{192,128},{256,192},{320,256},{384,320},{4... | collective-permute-start | bytes 196616 | tf_op jit(solution)/shard_map/weight_along_z/ppermute | solution.py:161
  47.6 16.6 %all-to-all-start.2 = ((bf16[4,128,512]{2,1,0:T(8,128)(2,1)}), bf16[4,128,512]{2,1,0:T(8,128)(2,1)S(1)}, u32[]{:S(2)}, u32[]{:S(2)}) async-start(bf16[4,128,512]{2,1,0:T(8,128)(2,1)} %bitcast.19), calls=%async_computation.2 | async-start | bytes 1048576 | tf_op jit(solution)/shard_map/sum_squares/all_to_all | solution.py:141
  52.0 23.0 %collective-permute-start.4 = (bf16[192,512]{1,0:T(8,128)(2,1)S(1)}, bf16[192,512]{1,0:T(8,128)(2,1)S(1)}, u32[]{:S(2)}, u32[]{:S(2)}) collective-permute-start(bf16[192,512]{1,0:T(8,128)(2,1)S(1)} %pad_maximum_fusion._.refs_0_), channel_id=1, source_target_pairs={{0,192},{64,256},{128,320},{192,384},{256,448},{320,2},{384,66},{4... | collective-permute-start | bytes 589832 | tf_op jit(solution)/shard_map/gather_weight/ppermute | solution.py:161
  56.5 18.6 %collective-permute-start.5 = (bf16[128,512]{1,0:T(8,128)(2,1)S(1)}, bf16[128,512]{1,0:T(8,128)(2,1)S(1)}, u32[]{:S(2)}, u32[]{:S(2)}) collective-permute-start(bf16[128,512]{1,0:T(8,128)(2,1)S(1)} %pad_maximum_fusion.1), channel_id=1, source_target_pairs={{0,322},{64,386},{128,450},{192,0},{256,64},{320,128},{384,192},{4... | collective-permute-start | bytes 393224 | tf_op jit(solution)/shard_map/gather_weight/ppermute | solution.py:161
  65.0 25.1 %all-to-all-start.3 = ((bf16[16,16,512]{2,1,0:T(8,128)(2,1)}), bf16[16,16,512]{2,1,0:T(8,128)(2,1)S(1)}, u32[]{:S(2)}, u32[]{:S(2)}) async-start(bf16[16,16,512]{2,1,0:T(8,128)(2,1)} %bitcast.32), calls=%async_computation.3 | async-start | bytes 524288 | tf_op jit(solution)/shard_map/sum_z/all_to_all | solution.py:141
  76.0 5.6 %collective-permute-start.6 = (bf16[4,128,512]{2,1,0:T(8,128)(2,1)S(1)}, bf16[4,128,512]{2,1,0:T(8,128)(2,1)S(1)}, u32[]{:S(2)}, u32[]{:S(2)}) collective-permute-start(bf16[4,128,512]{2,1,0:T(8,128)(2,1)S(1)} %get-tuple-element.11), channel_id=1, source_target_pairs={{0,1},{1,0},{2,3},{3,2},{4,5},{5,4},{6,7},{7,6},{8,9},{9,8},{10,11... | collective-permute-start | bytes 1572872 | tf_op jit(solution)/shard_map/input_grad/ppermute | solution.py:149
  81.7 18.0 %collective-permute-start.7 = (bf16[2,128,512]{2,1,0:T(8,128)(2,1)S(1)}, bf16[2,128,512]{2,1,0:T(8,128)(2,1)S(1)}, u32[]{:S(2)}, u32[]{:S(2)}) collective-permute-start(bf16[2,128,512]{2,1,0:T(8,128)(2,1)S(1)} %get-tuple-element.9), channel_id=1, source_target_pairs={{0,4},{4,0},{16,20},{20,16},{1,5},{5,1},{17,21},{21,17},{2,6},{6,2... | collective-permute-start | bytes 786440 | tf_op jit(solution)/shard_map/input_grad/ppermute | solution.py:153
  83.6 16.1 %collective-permute-start.8 = (bf16[2,128,512]{2,1,0:T(8,128)(2,1)S(1)}, bf16[2,128,512]{2,1,0:T(8,128)(2,1)S(1)}, u32[]{:S(2)}, u32[]{:S(2)}) collective-permute-start(bf16[2,128,512]{2,1,0:T(8,128)(2,1)S(1)} %get-tuple-element.10), channel_id=1, source_target_pairs={{0,16},{4,20},{16,0},{20,4},{1,17},{5,21},{17,1},{21,5},{2,18},{6,... | collective-permute-start | bytes 786440 | tf_op jit(solution)/shard_map/input_grad/ppermute | solution.py:153
  85.8 13.9 %collective-permute-start.9 = (bf16[2,128,512]{2,1,0:T(8,128)(2,1)S(1)}, bf16[2,128,512]{2,1,0:T(8,128)(2,1)S(1)}, u32[]{:S(2)}, u32[]{:S(2)}) collective-permute-start(bf16[2,128,512]{2,1,0:T(8,128)(2,1)S(1)} %get-tuple-element.7), channel_id=1, source_target_pairs={{0,20},{4,16},{16,4},{20,0},{1,21},{5,17},{17,5},{21,1},{2,22},{6,... | collective-permute-start | bytes 786440 | tf_op jit(solution)/shard_map/input_grad/ppermute | solution.py:153
  90.8 14.0 %all-to-all-start.4 = ((bf16[8,16,512]{2,1,0:T(8,128)(2,1)}), bf16[8,16,512]{2,1,0:T(8,128)(2,1)S(1)}, u32[]{:S(2)}, u32[]{:S(2)}) async-start(bf16[8,16,512]{2,1,0:T(8,128)(2,1)} %broadcast_in_dim.31), calls=%async_computation.4 | async-start | bytes 262144 | tf_op jit(solution)/shard_map/share_rows/all_to_all | solution.py:141

commit v7 on v5

--- a/solution.py
+++ b/solution.py
@@ -23,7 +23,7 @@
 def attend_kernel(length_ref, q_ref, k_ref, v_ref, g_ref, vg_ref, kg_ref):
     scaling = HD ** (-0.5)
     keys, vals = k_ref[...], v_ref[...]
-    length = length_ref[0]
+    length = length_ref[...]
     step = 2
     wide = step * TOK
     pos_s = lax.broadcasted_iota(jnp.int32, (TOK, wide), 0)
@@ -56,14 +56,14 @@
     return pl.pallas_call(
         attend_kernel,
         grid=(heads,),
-        in_specs=[pl.BlockSpec(memory_space=pltpu.SMEM), wide, thin, thin, wide],
+        in_specs=[pl.BlockSpec((1, 1), lambda g: (0, 0)), wide, thin, thin, wide],
         out_specs=[pl.BlockSpec((XN, TOK, HD), lambda g: (0, 0, g)), thin],
         out_shape=[jax.ShapeDtypeStruct((XN, TOK, KV), BF), jax.ShapeDtypeStruct((TOK, KV), BF)],
         cost_estimate=pl.CostEstimate(
             flops=10 * 32 * TOK * TOK * HD, bytes_accessed=3 << 20, transcendentals=32 * TOK * TOK
         ),
         name="attend",
-    )(length, query, key_rows, value_rows, grad_rows)
+    )(length.reshape(1, 1), query, key_rows, value_rows, grad_rows)
 
 
 def swap_groups(tiles):
@@ -81,7 +81,8 @@
     return tiles
 
 
-def to_pieces_kernel(in_ref, _, out_ref):
+def to_pieces_kernel(in_ref, *refs):
+    out_ref = refs[-1]
     for x in range(XN):
         tiles = [in_ref[:, (zl * XN + x) * 128 : (zl * XN + x + 1) * 128].astype(F32) for zl in range(8)]
         for q, tile in enumerate(swap_groups(tiles)):
@@ -103,15 +104,21 @@
 
 def to_pieces(rows, earlier):
     part = 32
-    return pl.pallas_call(
-        to_pieces_kernel,
-        grid=(TOK // part,),
-        in_specs=[pl.BlockSpec((part, WIDTH), lambda i: (i, 0)), pl.BlockSpec(memory_space=pl.ANY)],
-        out_specs=pl.BlockSpec((QN, part, KV), lambda i: (0, i, 0)),
-        out_shape=jax.ShapeDtypeStruct((QN, TOK, KV), BF),
-        cost_estimate=pl.CostEstimate(flops=1 << 22, bytes_accessed=2 << 20, transcendentals=0),
-        name="to_pieces",
-    )(rows, earlier)
+    steps = TOK // part
+    out = None
+    for first, count in ((0, steps - 1), (steps - 1, 1)):
+        block = pl.BlockSpec((part, WIDTH), lambda i, first=first: (i + first, 0))
+        out = pl.pallas_call(
+            to_pieces_kernel,
+            grid=(count,),
+            in_specs=[block] + [pl.BlockSpec(memory_space=pl.ANY)] * (2 if first else 1),
+            out_specs=pl.BlockSpec((QN, part, KV), lambda i, first=first: (0, i + first, 0)),
+            out_shape=jax.ShapeDtypeStruct((QN, TOK, KV), BF),
+            input_output_aliases={2: 0} if first else {},
+            cost_estimate=pl.CostEstimate(flops=count << 20, bytes_accessed=count << 19, transcendentals=0),
+            name="to_pieces",
+        )(*((rows, earlier[1], out) if first else (rows, earlier[0])))
+    return out
 
 
 def from_pieces(pieces, places):
@@ -185,9 +192,47 @@
         in_specs=[pl.BlockSpec(memory_space=pltpu.SMEM), vmem, vmem, vmem, pl.BlockSpec(memory_space=pl.ANY)],
         out_specs=vmem,
         out_shape=jax.ShapeDtypeStruct((KV, KV), BF),
+        cost_estimate=pl.CostEstimate(flops=1 << 36, bytes_accessed=1 << 20, transcendentals=0),
         compiler_params=pltpu.CompilerParams(vmem_limit_bytes=16 << 20),
         name="place_rows",
     )(zl[None].astype(jnp.int32), *parts, earlier)
+
+
+def sum_first_kernel(got_ref, out_ref):
+    total = got_ref[0].astype(F32)
+    for i in range(1, got_ref.shape[0]):
+        total += got_ref[i].astype(F32)
+    out_ref[...] = total.astype(BF)
+
+
+def sum_first(got):
+    vmem = pl.BlockSpec(memory_space=pltpu.VMEM)
+    return pl.pallas_call(
+        sum_first_kernel,
+        in_specs=[vmem],
+        out_specs=vmem,
+        out_shape=jax.ShapeDtypeStruct(got.shape[1:], BF),
+        cost_estimate=pl.CostEstimate(flops=1 << 36, bytes_accessed=1 << 20, transcendentals=0),
+        compiler_params=pltpu.CompilerParams(vmem_limit_bytes=16 << 20),
+        name="sum_first",
+    )(got)
+
+
+def twice_kernel(in_ref, _, out_ref):
+    for copy in range(ZH):
+        out_ref[copy] = in_ref[...]
+
+
+def twice(array, earlier):
+    vmem = pl.BlockSpec(memory_space=pltpu.VMEM)
+    return pl.pallas_call(
+        twice_kernel,
+        in_specs=[vmem, pl.BlockSpec(memory_space=pl.ANY)],
+        out_specs=vmem,
+        out_shape=jax.ShapeDtypeStruct((ZH,) + array.shape, BF),
+        compiler_params=pltpu.CompilerParams(vmem_limit_bytes=16 << 20),
+        name="twice",
+    )(array, earlier)
 
 
 def per_device(inputs, queries, keys, values, out_grad, lengths, value_weight):
@@ -202,24 +247,15 @@
         other = shifted(mine, "core", CN, 1)
         grads = pair(mine, other, core, ring).reshape(CN * XN * TOK, KV)
     with jax.named_scope("send_inputs"):
-        columns = exchange(to_pieces(inputs[0], own_rows), ("core", "x"))
+        columns = exchange(to_pieces(inputs[0], (own_rows, ring)), ("core", "x"))
     with jax.named_scope("weight_term"):
         term = lax.dot_general(
             columns.reshape(CN * XN * TOK, KV), grads, (((0,), (0,)), ((), ())), preferred_element_type=F32
         ).astype(BF)
-    with jax.named_scope("sum_y"):
-        got = exchange(term.reshape(YN, ZL * SUB, KV), "y")
-        plane = jnp.sum(got.astype(F32), axis=0).astype(BF).reshape(1, ZL, SUB, KV)
-    with jax.named_scope("sum_z"):
-        both = jnp.broadcast_to(plane, (ZH, ZL, SUB, KV)).reshape(ZH * ZL, SUB, KV)
-        got = exchange(both, ("zh", "zl"))
-        total = jnp.sum(got.astype(F32), axis=0) * F32(1.0 / 512)
-    with jax.named_scope("share_rows"):
-        weight_grad = spread(total, ("core", "y"), QN).reshape(QN * SUB, KV)
     with jax.named_scope("gather_weight"):
-        weight = place_rows([ring, along_z(ring, 3), along_z(ring[HALF:], -3)], zl, plane)
+        weight = place_rows([ring, along_z(ring, 3), along_z(ring[HALF:], -3)], zl, term)
     with jax.named_scope("input_grad"):
-        parts = nt(grads, weight).astype(BF).reshape(CN, XN, TOK, KV)
+        parts = product = nt(grads, weight).astype(BF).reshape(CN, XN, TOK, KV)
         kept = lax.dynamic_index_in_dim(parts, core, 0, False)
         theirs = shifted(lax.dynamic_index_in_dim(parts, 1 - core, 0, False), "core", CN, 1)
         parts = jnp.stack([kept, theirs], axis=1)
@@ -229,6 +265,14 @@
             back.append(shifted(piece, "x", XN, by) if by else piece)
             places += [c * XN + (x - by) % XN for c in (core, 1 - core)]
         input_grad = from_pieces(back, places)
+    with jax.named_scope("sum_y"):
+        got = exchange(term.reshape(YN, ZL * SUB, KV), "y")
+        both = twice(sum_first(got), theirs).reshape(ZH * ZL, SUB, KV)
+    with jax.named_scope("sum_z"):
+        got = exchange(both, ("zh", "zl"))
+        total = jnp.sum(got.astype(F32), axis=0) * F32(1.0 / 512)
+    with jax.named_scope("share_rows"):
+        weight_grad = spread(total.astype(BF), ("core", "y"), QN).reshape(QN * SUB, KV).astype(F32)
     return (input_grad[None], key_grad[None], weight_grad)
 
 

time: 104 us -> 110 us (1.058)
  waiting for transfers between devices: 9.2 us -> 15.9 us
  starting transfers between devices: 72.6 us -> 68.5 us
  Pallas kernels: 14.1 us -> 16.4 us
  other arithmetic: 0.25 us -> 2.43 us
  local copies, waits for them, and re-layouts: 2.97 us -> 0.85 us
  matrix products: 2.26 us -> 3.49 us
    all_to_all x5, waiting for transfers between devices: 6.09 us -> 15.9 us  [exchange(): return lax.all_to_all(array, axes, 0, 0, tiled=True)]
    all_to_all x5, starting transfers between devices: 36.8 us -> 34 us  [exchange(): return lax.all_to_all(array, axes, 0, 0, tiled=True)]
    pallas_call x2 -> x5, Pallas kernels: 10.3 us -> 12.7 us  [the longest x1 5.96 us: attend_back(): pl.pallas_call(attend_kernel, grid=(heads,), in_specs=[pl.BlockSpec((1, 1...]
    ppermute x5, waiting for transfers between devices: 1.8 us -> 0.01 us  [shifted(): lax.ppermute(array, axes, [(i, (i + by) % count) for i in range(count)])]
    concatenate x2, other arithmetic: 0.02 us -> 1.54 us  [per_device(): jnp.concatenate([along_z(own_rows, -1), own_rows, along_z(own_rows, 1)])]
    ppermute x4, waiting for transfers between devices: 1.31 us -> 0.01 us  [along_z(): return lax.ppermute(array, ('zl', 'zh'), places)]
    ppermute x5, starting transfers between devices: 14.4 us -> 13.1 us  [shifted(): lax.ppermute(array, axes, [(i, (i + by) % count) for i in range(count)])]
    dot_general x1, matrix products: 1.52 us -> 2.75 us  [per_device(): lax.dot_general(columns.reshape(CN * XN * TOK, KV), grads, (((0,), (0,)),...]
  transfers between devices with their start and end apart: 14 -> 14, of which waited for: 7 -> 4; matrix products, arithmetic and copies ran while one was open for 3% -> 6% of each run, Pallas kernels for 8% -> 9%
where the time goes in v7:
time: 110 us; the launch traced here: 109 us
  starting transfers between devices  68.5 us (62%)
  Pallas kernels  16.4 us (15%)
  waiting for transfers between devices  15.9 us (14%)
  matrix products  3.49 us (3%)
  other arithmetic  2.43 us (2%)
  between operations  1.6 us (1%)
    all_to_all x5, starting transfers between devices, exchange(): return lax.all_to_all(array, axes, 0, 0, tiled=True)  34 us
    ppermute x4, starting transfers between devices, along_z(): return lax.ppermute(array, ('zl', 'zh'), places)  21.3 us
    all_to_all x5, waiting for transfers between devices, exchange(): return lax.all_to_all(array, axes, 0, 0, tiled=True)  15.9 us
    ppermute x5, starting transfers between devices, shifted(): lax.ppermute(array, axes, [(i, (i + by) % count) for i in range(count)])  13.1 us
    pallas_call x1, Pallas kernels, attend_back(): pl.pallas_call(attend_kernel, grid=(heads,), in_specs=[pl.BlockSpec((1, 1...  5.96 us
    pallas_call x2, Pallas kernels, to_pieces(): pl.pallas_call(to_pieces_kernel, grid=(count,), in_specs=[block] + [pl.Bl...  5.91 us
    pallas_call x1, Pallas kernels, from_pieces(): pl.pallas_call(from_pieces_kernel, grid=(TOK // part,), in_specs=[pl.Bloc...  3.63 us
    dot_general x1, matrix products, per_device(): lax.dot_general(columns.reshape(CN * XN * TOK, KV), grads, (((0,), (0,)),...  2.75 us
  transfers between devices with their start and end apart: 14, of which 4 were waited for; matrix products, arithmetic and copies ran while one was open for 6% of the time, Pallas kernels for 9%

profile of v7, /device:TPU:1, one launch (start us, length us, event | category | flops | bytes accessed | tf_op | source)
XLA Modules:
  0.0 109.2 jit_solution(3084971820440809985)
XLA Ops:
  1.3 6.0 %attend.1 = (bf16[4,128,512]{2,1,0:T(8,128)(2,1)}, bf16[128,512]{1,0:T(8,128)(2,1)}) custom-call(s32[1,1]{1,0:T(1,128)} %bitcast.43.length_ref, bf16[128,4096]{1,0:T(8,128)(2,1)} %bitcast.51, bf16[128,512]{1,0:T(8,128)(2,1)} %bitcast.53, bf16[128,512]{1,0:T(8,128)(2,1)} %bitcast.54, bf16[128,4096]{1,0:T(8,128)(2,1)} %bitcast.52), custom_call_target="tpu_custom_call" | custom-call | flops 671088640 | bytes 3145728 | tf_op jit(solution)/shard_map/attention/attend/pallas_call | solution.py:56
  7.3 4.8 %all-to-all-start = ((bf16[4,128,512]{2,1,0:T(8,128)(2,1)}), bf16[4,128,512]{2,1,0:T(8,128)(2,1)S(1)}, u32[]{:S(2)}, u32[]{:S(2)}) async-start(bf16[4,128,512]{2,1,0:T(8,128)(2,1)} %get-tuple-element.5), calls=%async_computation | async-start | bytes 1048576 | tf_op jit(solution)/shard_map/gather_value_grad/all_to_all | solution.py:141
  12.2 3.5 %collective-permute-start.2 = (bf16[64,512]{1,0:T(8,128)(2,1)S(1)}, bf16[64,512]{1,0:T(8,128)(2,1)S(1)}, u32[]{:S(2)}, u32[]{:S(2)}) collective-permute-start(bf16[64,512]{1,0:T(8,128)(2,1)S(1)} %constant_dynamic-slice_fusion.refs_0_), channel_id=1, source_target_pairs={{0,64},{64,128},{128,192},{192,256},{256,320},{320,384},{384,448},... | collective-permute-start | bytes 196616 | tf_op jit(solution)/shard_map/weight_along_z/ppermute | solution.py:157
  15.7 9.5 %collective-permute-start.1 = (bf16[64,512]{1,0:T(8,128)(2,1)S(1)}, bf16[64,512]{1,0:T(8,128)(2,1)S(1)}, u32[]{:S(2)}, u32[]{:S(2)}) collective-permute-start(bf16[64,512]{1,0:T(8,128)(2,1)S(1)} %constant_dynamic-slice_fusion.refs_0_), channel_id=1, source_target_pairs={{0,450},{64,0},{128,64},{192,128},{256,192},{320,256},{384,320},{4... | collective-permute-start | bytes 196616 | tf_op jit(solution)/shard_map/weight_along_z/ppermute | solution.py:157
  25.2 3.7 %to_pieces.2.refs_1_ = bf16[8,128,512]{2,1,0:T(8,128)(2,1)} custom-call(bf16[128,4096]{1,0:T(8,128)(2,1)} %bitcast.47, bf16[64,512]{1,0:T(8,128)(2,1)} %copy-done.2), custom_call_target="tpu_custom_call" | custom-call | flops 3145728 | bytes 1572864 | tf_op jit(solution)/shard_map/send_inputs/to_pieces/pallas_call | solution.py:111
  29.0 1.5 %pad_maximum_fusion._.refs_0_ = bf16[192,512]{1,0:T(8,128)(2,1)} fusion(bf16[64,512]{1,0:T(8,128)(2,1)S(1)} %collective-permute-done.2, bf16[64,512]{1,0:T(8,128)(2,1)} %copy-done.2, bf16[64,512]{1,0:T(8,128)(2,1)S(1)} %collective-permute-done.1), kind=kLoop, calls=%fused_computation.21 | loop fusion | flops 589824 | bytes 393216 | tf_op jit(solution)/shard_map/weight_along_z/concatenate | solution.py:242
  30.5 2.2 %to_pieces.3 = bf16[8,128,512]{2,1,0:T(8,128)(2,1)} custom-call(bf16[128,4096]{1,0:T(8,128)(2,1)} %bitcast.48, bf16[192,512]{1,0:T(8,128)(2,1)} %pad_maximum_fusion._.refs_0_, bf16[8,128,512]{2,1,0:T(8,128)(2,1)} %to_pieces.2.refs_1_), custom_call_target="tpu_custom_call", output_to_operand_aliasing={{}: (2, {})} | custom-call | flops 1048576 | bytes 524288 | tf_op jit(solution)/shard_map/send_inputs/to_pieces/pallas_call | solution.py:111
  32.7 6.2 %all-to-all-start.1 = ((bf16[8,128,512]{2,1,0:T(8,128)(2,1)}), bf16[8,128,512]{2,1,0:T(8,128)(2,1)}, u32[]{:S(2)}, u32[]{:S(2)}) async-start(bf16[8,128,512]{2,1,0:T(8,128)(2,1)} %to_pieces.3), calls=%async_computation.1 | async-start | bytes 2097152 | tf_op jit(solution)/shard_map/send_inputs/all_to_all | solution.py:141
  38.9 1.9 %collective-permute-start = (bf16[4,128,512]{2,1,0:T(8,128)(2,1)S(1)}, bf16[4,128,512]{2,1,0:T(8,128)(2,1)S(1)}, u32[]{:S(2)}, u32[]{:S(2)}) collective-permute-start(bf16[4,128,512]{2,1,0:T(8,128)(2,1)S(1)} %all-to-all-done.own_ref), channel_id=1, source_target_pairs={{0,1},{1,0},{2,3},{3,2},{4,5},{5,4},{6,7},{7,6},{8,9},{9,8},{10,11... | collective-permute-start | bytes 1572872 | tf_op jit(solution)/shard_map/gather_value_grad/ppermute | solution.py:149
  40.8 1.9 %collective-permute-start.3 = (bf16[192,512]{1,0:T(8,128)(2,1)S(1)}, bf16[192,512]{1,0:T(8,128)(2,1)S(1)}, u32[]{:S(2)}, u32[]{:S(2)}) collective-permute-start(bf16[192,512]{1,0:T(8,128)(2,1)S(1)} %copy-done.1), channel_id=1, source_target_pairs={{0,192},{64,256},{128,320},{192,384},{256,448},{320,2},{384,66},{4... | collective-permute-start | bytes 589832 | tf_op jit(solution)/shard_map/gather_weight/ppermute | solution.py:157
  42.7 6.4 %collective-permute-start.4 = (bf16[128,512]{1,0:T(8,128)(2,1)S(1)}, bf16[128,512]{1,0:T(8,128)(2,1)S(1)}, u32[]{:S(2)}, u32[]{:S(2)}) collective-permute-start(bf16[128,512]{1,0:T(8,128)(2,1)S(1)} %pad_maximum_fusion.1), channel_id=1, source_target_pairs={{0,322},{64,386},{128,450},{192,0},{256,64},{320,128},{384,192},{4... | collective-permute-start | bytes 393224 | tf_op jit(solution)/shard_map/gather_weight/ppermute | solution.py:157
  49.2 4.9 %all-to-all-done.1 = bf16[8,128,512]{2,1,0:T(8,128)(2,1)} async-done(((bf16[8,128,512]{2,1,0:T(8,128)(2,1)}), bf16[8,128,512]{2,1,0:T(8,128)(2,1)}, u32[]{:S(2)}, u32[]{:S(2)}) %all-to-all-start.1) | async-done | bytes 1048608 | tf_op jit(solution)/shard_map/send_inputs/all_to_all | solution.py:141
  54.1 2.8 %convolution_convert_fusion.1.refs_3_ = bf16[512,512]{1,0:T(8,128)(2,1)} fusion(bf16[1024,512]{1,0:T(8,128)(2,1)} %bitcast.17, bf16[1024,512]{1,0:T(8,128)(2,1)S(1)} %bitcast.45), kind=kOutput, calls=%fused_computation.9 | convolution fusion | flops 537133056 | bytes 2621440 | tf_op jit(solution)/shard_map/weight_term/dot_general | solution.py:252
  56.9 4.2 %all-to-all-start.2 = ((bf16[4,128,512]{2,1,0:T(8,128)(2,1)}), bf16[4,128,512]{2,1,0:T(8,128)(2,1)S(1)}, u32[]{:S(2)}, u32[]{:S(2)}) async-start(bf16[4,128,512]{2,1,0:T(8,128)(2,1)} %bitcast.28), calls=%async_computation.2 | async-start | bytes 1048576 | tf_op jit(solution)/shard_map/sum_y/all_to_all | solution.py:141
  61.1 0.1 place_rows.1
  61.2 0.7 convolution_convert_fusion
  61.9 0.1 dynamic-slice_bitcast_fusion
  62.0 2.4 %collective-permute-start.5 = (bf16[4,128,512]{2,1,0:T(8,128)(2,1)S(1)}, bf16[4,128,512]{2,1,0:T(8,128)(2,1)S(1)}, u32[]{:S(2)}, u32[]{:S(2)}) collective-permute-start(bf16[4,128,512]{2,1,0:T(8,128)(2,1)S(1)} %get-tuple-element.11), channel_id=1, source_target_pairs={{0,1},{1,0},{2,3},{3,2},{4,5},{5,4},{6,7},{7,6},{8,9},{9,8},{10,11... | collective-permute-start | bytes 1572872 | tf_op jit(solution)/shard_map/input_grad/ppermute | solution.py:149
  64.4 5.8 %all-to-all-done.2.got_ref = bf16[4,128,512]{2,1,0:T(8,128)(2,1)S(1)} async-done(((bf16[4,128,512]{2,1,0:T(8,128)(2,1)}), bf16[4,128,512]{2,1,0:T(8,128)(2,1)S(1)}, u32[]{:S(2)}, u32[]{:S(2)}) %all-to-all-start.2) | async-done | bytes 524320 | tf_op jit(solution)/shard_map/sum_y/all_to_all | solution.py:141
  70.3 0.7 twice.1
  71.0 8.6 %all-to-all-start.3 = ((bf16[16,16,512]{2,1,0:T(8,128)(2,1)}), bf16[16,16,512]{2,1,0:T(8,128)(2,1)S(1)}, u32[]{:S(2)}, u32[]{:S(2)}) async-start(bf16[16,16,512]{2,1,0:T(8,128)(2,1)} %bitcast.29), calls=%async_computation.3 | async-start | bytes 524288 | tf_op jit(solution)/shard_map/sum_z/all_to_all | solution.py:141
  79.7 0.1 fusion.1
  79.8 2.7 %collective-permute-start.6 = (bf16[2,128,512]{2,1,0:T(8,128)(2,1)S(1)}, bf16[2,128,512]{2,1,0:T(8,128)(2,1)S(1)}, u32[]{:S(2)}, u32[]{:S(2)}) collective-permute-start(bf16[2,128,512]{2,1,0:T(8,128)(2,1)S(1)} %get-tuple-element.9), channel_id=1, source_target_pairs={{0,16},{16,32},{32,48},{48,0},{1,17},{17,33},{33,49},{49,1},{2,18}... | collective-permute-start | bytes 786440 | tf_op jit(solution)/shard_map/input_grad/ppermute | solution.py:149
  82.5 2.1 %collective-permute-start.7 = (bf16[2,128,512]{2,1,0:T(8,128)(2,1)S(1)}, bf16[2,128,512]{2,1,0:T(8,128)(2,1)S(1)}, u32[]{:S(2)}, u32[]{:S(2)}) collective-permute-start(bf16[2,128,512]{2,1,0:T(8,128)(2,1)S(1)} %get-tuple-element.10), channel_id=1, source_target_pairs={{0,32},{16,48},{32,0},{48,16},{1,33},{17,49},{33,1},{49,17},{2,34}... | collective-permute-start | bytes 786440 | tf_op jit(solution)/shard_map/input_grad/ppermute | solution.py:149
  84.6 4.1 %collective-permute-start.8 = (bf16[2,128,512]{2,1,0:T(8,128)(2,1)S(1)}, bf16[2,128,512]{2,1,0:T(8,128)(2,1)S(1)}, u32[]{:S(2)}, u32[]{:S(2)}) collective-permute-start(bf16[2,128,512]{2,1,0:T(8,128)(2,1)S(1)} %get-tuple-element.7), channel_id=1, source_target_pairs={{0,48},{16,0},{32,16},{48,32},{1,49},{17,1},{33,17},{49,33},{2,50}... | collective-permute-start | bytes 786440 | tf_op jit(solution)/shard_map/input_grad/ppermute | solution.py:149
  88.7 3.7 %all-to-all-done.3 = bf16[16,16,512]{2,1,0:T(8,128)(2,1)S(1)} async-done(((bf16[16,16,512]{2,1,0:T(8,128)(2,1)}), bf16[16,16,512]{2,1,0:T(8,128)(2,1)S(1)}, u32[]{:S(2)}, u32[]{:S(2)}) %all-to-all-start.3) | async-done | bytes 262176 | tf_op jit(solution)/shard_map/sum_z/all_to_all | solution.py:141
  92.5 0.7 broadcast_in_dim.22
  93.2 10.2 %all-to-all-start.4 = ((bf16[8,16,512]{2,1,0:T(8,128)(2,1)}), bf16[8,16,512]{2,1,0:T(8,128)(2,1)S(1)}, u32[]{:S(2)}, u32[]{:S(2)}) async-start(bf16[8,16,512]{2,1,0:T(8,128)(2,1)} %broadcast_in_dim.22), calls=%async_computation.4 | async-start | bytes 262144 | tf_op jit(solution)/shard_map/share_rows/all_to_all | solution.py:141
  103.4 0.1 stack.44.places_ref
  103.5 3.6 %from_pieces.1 = bf16[128,4096]{1,0:T(8,128)(2,1)} custom-call(s32[8]{0:T(128)S(1)} %stack.44.places_ref, bf16[2,128,512]{2,1,0:T(8,128)(2,1)S(1)} %get-tuple-element.8.refs_0_, bf16[2,128,512]{2,1,0:T(8,128)(2,1)S(1)} %collective-permute-done.6.refs_1_, bf16[2,128,512]{2,1,0:T(8,128)(2,1)S(1)} %collective-permute-done.7.refs_2_, ...), custom_call_target="tpu_custom_call" | custom-call | flops 4194304 | bytes 2097152 | tf_op jit(solution)/shard_map/input_grad/from_pieces/pallas_call | solution.py:126
  107.1 1.4 %all-to-all-done.4 = bf16[8,16,512]{2,1,0:T(8,128)(2,1)S(1)} async-done(((bf16[8,16,512]{2,1,0:T(8,128)(2,1)}), bf16[8,16,512]{2,1,0:T(8,128)(2,1)S(1)}, u32[]{:S(2)}, u32[]{:S(2)}) %all-to-all-start.4) | async-done | bytes 131104 | tf_op jit(solution)/shard_map/share_rows/all_to_all | solution.py:141
  108.5 0.7 bitcast_convert_fusion
  (24 shorter events, 0.3 us)
Async XLA Ops:
  0.6 11.5 %copy-start = (bf16[128,512]{1,0:T(8,128)(2,1)S(1)}, bf16[128,512]{1,0:T(8,128)(2,1)}, u32[]{:S(2)}) copy-start(bf16[128,512]{1,0:T(8,128)(2,1)} %param.13) | copy-start | bytes 393220
  7.3 25.4 %all-to-all-start = ((bf16[4,128,512]{2,1,0:T(8,128)(2,1)}), bf16[4,128,512]{2,1,0:T(8,128)(2,1)S(1)}, u32[]{:S(2)}, u32[]{:S(2)}) async-start(bf16[4,128,512]{2,1,0:T(8,128)(2,1)} %get-tuple-element.5), calls=%async_computation | async-start | bytes 1048576 | tf_op jit(solution)/shard_map/gather_value_grad/all_to_all | solution.py:141
  12.1 13.1 %copy-start.2 = (bf16[64,512]{1,0:T(8,128)(2,1)}, bf16[64,512]{1,0:T(8,128)(2,1)S(1)}, u32[]{:S(2)}) copy-start(bf16[64,512]{1,0:T(8,128)(2,1)S(1)} %constant_dynamic-slice_fusion.refs_0_) | copy-start | bytes 196612
  12.2 16.8 %collective-permute-start.2 = (bf16[64,512]{1,0:T(8,128)(2,1)S(1)}, bf16[64,512]{1,0:T(8,128)(2,1)S(1)}, u32[]{:S(2)}, u32[]{:S(2)}) collective-permute-start(bf16[64,512]{1,0:T(8,128)(2,1)S(1)} %constant_dynamic-slice_fusion.refs_0_), channel_id=1, source_target_pairs={{0,64},{64,128},{128,192},{192,256},{256,320},{320,384},{384,448},... | collective-permute-start | bytes 196616 | tf_op jit(solution)/shard_map/weight_along_z/ppermute | solution.py:157
  15.7 13.3 %collective-permute-start.1 = (bf16[64,512]{1,0:T(8,128)(2,1)S(1)}, bf16[64,512]{1,0:T(8,128)(2,1)S(1)}, u32[]{:S(2)}, u32[]{:S(2)}) collective-permute-start(bf16[64,512]{1,0:T(8,128)(2,1)S(1)} %constant_dynamic-slice_fusion.refs_0_), channel_id=1, source_target_pairs={{0,450},{64,0},{128,64},{192,128},{256,192},{320,256},{384,320},{4... | collective-permute-start | bytes 196616 | tf_op jit(solution)/shard_map/weight_along_z/ppermute | solution.py:157
  32.7 8.1 %copy-start.1 = (bf16[192,512]{1,0:T(8,128)(2,1)S(1)}, bf16[192,512]{1,0:T(8,128)(2,1)}, u32[]{:S(2)}) copy-start(bf16[192,512]{1,0:T(8,128)(2,1)} %pad_maximum_fusion._.refs_0_) | copy-start | bytes 589828
  32.7 10.0 %copy-start.3 = (bf16[64,512]{1,0:T(8,128)(2,1)S(1)}, bf16[64,512]{1,0:T(8,128)(2,1)}, u32[]{:S(2)}) copy-start(bf16[64,512]{1,0:T(8,128)(2,1)} %copy-done.2) | copy-start | bytes 196612
  32.7 21.5 %all-to-all-start.1 = ((bf16[8,128,512]{2,1,0:T(8,128)(2,1)}), bf16[8,128,512]{2,1,0:T(8,128)(2,1)}, u32[]{:S(2)}, u32[]{:S(2)}) async-start(bf16[8,128,512]{2,1,0:T(8,128)(2,1)} %to_pieces.3), calls=%async_computation.1 | async-start | bytes 2097152 | tf_op jit(solution)/shard_map/send_inputs/all_to_all | solution.py:141
  38.9 10.3 %collective-permute-start = (bf16[4,128,512]{2,1,0:T(8,128)(2,1)S(1)}, bf16[4,128,512]{2,1,0:T(8,128)(2,1)S(1)}, u32[]{:S(2)}, u32[]{:S(2)}) collective-permute-start(bf16[4,128,512]{2,1,0:T(8,128)(2,1)S(1)} %all-to-all-done.own_ref), channel_id=1, source_target_pairs={{0,1},{1,0},{2,3},{3,2},{4,5},{5,4},{6,7},{7,6},{8,9},{9,8},{10,11... | collective-permute-start | bytes 1572872 | tf_op jit(solution)/shard_map/gather_value_grad/ppermute | solution.py:149
  40.8 20.3 %collective-permute-start.3 = (bf16[192,512]{1,0:T(8,128)(2,1)S(1)}, bf16[192,512]{1,0:T(8,128)(2,1)S(1)}, u32[]{:S(2)}, u32[]{:S(2)}) collective-permute-start(bf16[192,512]{1,0:T(8,128)(2,1)S(1)} %copy-done.1), channel_id=1, source_target_pairs={{0,192},{64,256},{128,320},{192,384},{256,448},{320,2},{384,66},{4... | collective-permute-start | bytes 589832 | tf_op jit(solution)/shard_map/gather_weight/ppermute | solution.py:157
  42.7 18.3 %collective-permute-start.4 = (bf16[128,512]{1,0:T(8,128)(2,1)S(1)}, bf16[128,512]{1,0:T(8,128)(2,1)S(1)}, u32[]{:S(2)}, u32[]{:S(2)}) collective-permute-start(bf16[128,512]{1,0:T(8,128)(2,1)S(1)} %pad_maximum_fusion.1), channel_id=1, source_target_pairs={{0,322},{64,386},{128,450},{192,0},{256,64},{320,128},{384,192},{4... | collective-permute-start | bytes 393224 | tf_op jit(solution)/shard_map/gather_weight/ppermute | solution.py:157
  56.9 13.3 %all-to-all-start.2 = ((bf16[4,128,512]{2,1,0:T(8,128)(2,1)}), bf16[4,128,512]{2,1,0:T(8,128)(2,1)S(1)}, u32[]{:S(2)}, u32[]{:S(2)}) async-start(bf16[4,128,512]{2,1,0:T(8,128)(2,1)} %bitcast.28), calls=%async_computation.2 | async-start | bytes 1048576 | tf_op jit(solution)/shard_map/sum_y/all_to_all | solution.py:141
  62.0 8.3 %collective-permute-start.5 = (bf16[4,128,512]{2,1,0:T(8,128)(2,1)S(1)}, bf16[4,128,512]{2,1,0:T(8,128)(2,1)S(1)}, u32[]{:S(2)}, u32[]{:S(2)}) collective-permute-start(bf16[4,128,512]{2,1,0:T(8,128)(2,1)S(1)} %get-tuple-element.11), channel_id=1, source_target_pairs={{0,1},{1,0},{2,3},{3,2},{4,5},{5,4},{6,7},{7,6},{8,9},{9,8},{10,11... | collective-permute-start | bytes 1572872 | tf_op jit(solution)/shard_map/input_grad/ppermute | solution.py:149
  71.0 21.4 %all-to-all-start.3 = ((bf16[16,16,512]{2,1,0:T(8,128)(2,1)}), bf16[16,16,512]{2,1,0:T(8,128)(2,1)S(1)}, u32[]{:S(2)}, u32[]{:S(2)}) async-start(bf16[16,16,512]{2,1,0:T(8,128)(2,1)} %bitcast.29), calls=%async_computation.3 | async-start | bytes 524288 | tf_op jit(solution)/shard_map/sum_z/all_to_all | solution.py:141
  79.8 23.6 %collective-permute-start.6 = (bf16[2,128,512]{2,1,0:T(8,128)(2,1)S(1)}, bf16[2,128,512]{2,1,0:T(8,128)(2,1)S(1)}, u32[]{:S(2)}, u32[]{:S(2)}) collective-permute-start(bf16[2,128,512]{2,1,0:T(8,128)(2,1)S(1)} %get-tuple-element.9), channel_id=1, source_target_pairs={{0,16},{16,32},{32,48},{48,0},{1,17},{17,33},{33,49},{49,1},{2,18}... | collective-permute-start | bytes 786440 | tf_op jit(solution)/shard_map/input_grad/ppermute | solution.py:149
  82.5 20.9 %collective-permute-start.7 = (bf16[2,128,512]{2,1,0:T(8,128)(2,1)S(1)}, bf16[2,128,512]{2,1,0:T(8,128)(2,1)S(1)}, u32[]{:S(2)}, u32[]{:S(2)}) collective-permute-start(bf16[2,128,512]{2,1,0:T(8,128)(2,1)S(1)} %get-tuple-element.10), channel_id=1, source_target_pairs={{0,32},{16,48},{32,0},{48,16},{1,33},{17,49},{33,1},{49,17},{2,34}... | collective-permute-start | bytes 786440 | tf_op jit(solution)/shard_map/input_grad/ppermute | solution.py:149
  84.6 18.9 %collective-permute-start.8 = (bf16[2,128,512]{2,1,0:T(8,128)(2,1)S(1)}, bf16[2,128,512]{2,1,0:T(8,128)(2,1)S(1)}, u32[]{:S(2)}, u32[]{:S(2)}) collective-permute-start(bf16[2,128,512]{2,1,0:T(8,128)(2,1)S(1)} %get-tuple-element.7), channel_id=1, source_target_pairs={{0,48},{16,0},{32,16},{48,32},{1,49},{17,1},{33,17},{49,33},{2,50}... | collective-permute-start | bytes 786440 | tf_op jit(solution)/shard_map/input_grad/ppermute | solution.py:149
  93.2 15.3 %all-to-all-start.4 = ((bf16[8,16,512]{2,1,0:T(8,128)(2,1)}), bf16[8,16,512]{2,1,0:T(8,128)(2,1)S(1)}, u32[]{:S(2)}, u32[]{:S(2)}) async-start(bf16[8,16,512]{2,1,0:T(8,128)(2,1)} %broadcast_in_dim.22), calls=%async_computation.4 | async-start | bytes 262144 | tf_op jit(solution)/shard_map/share_rows/all_to_all | solution.py:141

commit v8 on v5

v8 whole, which is shorter than its diff:
```python
import jax
import jax.numpy as jnp
from jax import lax
from jax.experimental import pallas as pl
from jax.experimental.pallas import tpu as pltpu
from jax.sharding import Mesh
from jax.sharding import PartitionSpec as P

ZL, XN, YN, ZH, CN = 8, 4, 4, 2, 2
QN = CN * YN
TOK, WIDTH, KV, HD = 128, 4096, 512, 128
GROUP = 8
SUB = 16
HELD = ZL // CN
BF, F32 = jnp.bfloat16, jnp.float32


def nt(a, b):
    return lax.dot_general(a, b, (((1,), (1,)), ((), ())), preferred_element_type=F32)


def attend_kernel(length_ref, q_ref, k_ref, v_ref, g_ref, _, vg_ref, kg_ref):
    scaling = HD ** (-0.5)
    keys, vals = k_ref[...], v_ref[...]
    length = length_ref[0]
    step = 2
    wide = step * TOK
    pos_s = lax.broadcasted_iota(jnp.int32, (TOK, wide), 0)
    pos_t = lax.broadcasted_iota(jnp.int32, (TOK, wide), 1) & (TOK - 1)
    allowed = pos_s <= pos_t
    live = ((lax.broadcasted_iota(jnp.int32, (1, wide), 1) & (TOK - 1)) < length).astype(F32)
    vg = jnp.zeros((TOK, HD), F32)
    kg = jnp.zeros((TOK, HD), F32)
    for first in range(0, GROUP, step):
        heads = range(first, first + step)
        qs = jnp.concatenate([q_ref[:, h * HD : (h + 1) * HD] for h in heads], axis=0)
        gs = jnp.concatenate([g_ref[:, h * HD : (h + 1) * HD] for h in heads], axis=0)
        scores = jnp.where(allowed, nt(keys, qs) * scaling, F32(-1e30))
        expd = jnp.exp(scores - jnp.max(scores, axis=0, keepdims=True))
        probs = expd * (live / jnp.sum(expd, axis=0, keepdims=True))
        dprob = nt(vals, gs)
        delta = jnp.sum(probs * dprob, axis=0, keepdims=True)
        dscore = probs * (dprob - delta)
        vg += jnp.dot(probs.astype(BF), gs, preferred_element_type=F32)
        kg += jnp.dot(dscore.astype(BF), qs, preferred_element_type=F32)
    vg_ref[...] = vg.astype(BF)
    kg_ref[...] = (kg * scaling).astype(BF)


def attend_back(query, key_rows, value_rows, grad_rows, length, earlier):
    heads = KV // HD
    wide = pl.BlockSpec((TOK, GROUP * HD), lambda g: (0, g))
    thin = pl.BlockSpec((TOK, HD), lambda g: (0, g))
    return pl.pallas_call(
        attend_kernel,
        grid=(heads,),
        in_specs=[pl.BlockSpec(memory_space=pltpu.SMEM), wide, thin, thin, wide, pl.BlockSpec(memory_space=pl.ANY)],
        out_specs=[thin, thin],
        out_shape=[jax.ShapeDtypeStruct((TOK, KV), BF)] * 2,
        cost_estimate=pl.CostEstimate(
            flops=10 * 32 * TOK * TOK * HD, bytes_accessed=3 << 20, transcendentals=32 * TOK * TOK
        ),
        name="attend",
    )(length, query, key_rows, value_rows, grad_rows, earlier)


def swap_groups(tiles):
    lane = lax.broadcasted_iota(jnp.int32, tiles[0].shape, 1)
    for bit in (1, 2, 4):
        shift = bit * SUB
        high = (lane & shift) != 0
        after = list(tiles)
        for i in range(8):
            if i & bit == 0:
                low_tile, high_tile = tiles[i], tiles[i | bit]
                after[i] = jnp.where(high, pltpu.roll(high_tile, shift, 1), low_tile)
                after[i | bit] = jnp.where(high, high_tile, pltpu.roll(low_tile, 128 - shift, 1))
        tiles = after
    return tiles


def to_pieces_kernel(in_ref, out_ref):
    for x in range(XN):
        tiles = [in_ref[:, (zl * XN + x) * 128 : (zl * XN + x + 1) * 128].astype(F32) for zl in range(8)]
        for q, tile in enumerate(swap_groups(tiles)):
            y = q % YN
            out_ref[q // YN * XN + x, :, y * 128 : (y + 1) * 128] = tile.astype(BF)


def from_pieces_kernel(at_ref, *refs):
    out_ref = refs[-1]
    for by in range(XN):
        x = (at_ref[2] + XN - by) % XN
        for which in range(CN):
            for k in range(HELD):
                tile = (at_ref[which] + ZL - k) % ZL * XN + x
                lanes = pl.ds(pl.multiple_of(tile * 128, 128), 128)
                out_ref[:, lanes] = refs[by][which, :, k * 128 : (k + 1) * 128]


def to_pieces(rows):
    part = 32
    return pl.pallas_call(
        to_pieces_kernel,
        grid=(TOK // part,),
        in_specs=[pl.BlockSpec((part, WIDTH), lambda i: (i, 0))],
        out_specs=pl.BlockSpec((QN, part, KV), lambda i: (0, i, 0)),
        out_shape=jax.ShapeDtypeStruct((QN, TOK, KV), BF),
        cost_estimate=pl.CostEstimate(flops=1 << 22, bytes_accessed=2 << 20, transcendentals=0),
        name="to_pieces",
    )(rows)


def from_pieces(pieces, core, zl, x):
    part = 32
    firsts = [(zl + ZL - HELD * c) % ZL for c in (core, 1 - core)]
    return pl.pallas_call(
        from_pieces_kernel,
        grid=(TOK // part,),
        in_specs=[pl.BlockSpec(memory_space=pltpu.SMEM)]
        + [pl.BlockSpec((CN, part, KV), lambda i: (0, i, 0))] * XN,
        out_specs=pl.BlockSpec((part, WIDTH), lambda i: (i, 0)),
        out_shape=jax.ShapeDtypeStruct((TOK, WIDTH), BF),
        cost_estimate=pl.CostEstimate(flops=0, bytes_accessed=2 << 20, transcendentals=0),
        compiler_params=pltpu.CompilerParams(vmem_limit_bytes=16 << 20),
        name="from_pieces",
    )(jnp.stack(firsts + [x]).astype(jnp.int32), *pieces)


def exchange(array, axes):
    return lax.all_to_all(array, axes, 0, 0, tiled=True)


def spread(array, axes, count):
    return exchange(jnp.broadcast_to(array[None], (count,) + array.shape), axes)


def shifted(array, axes, count, by):
    return lax.ppermute(array, axes, [(i, (i + by) % count) for i in range(count)])


def along_z(array, steps):
    pairs = []
    for z in range(ZH * ZL):
        for core, by in enumerate(steps):
            to = (z + by) % (ZH * ZL)
            pairs.append((((z % ZL) * ZH + z // ZL) * CN + core, ((to % ZL) * ZH + to // ZL) * CN + core))
    return lax.ppermute(array, ("zl", "zh", "core"), pairs)


def pair_kernel(core_ref, own_ref, other_ref, out_ref):
    core = core_ref[0]
    out_ref[core] = own_ref[...]
    out_ref[1 - core] = other_ref[...]


def pair(own, other, core):
    vmem = pl.BlockSpec(memory_space=pltpu.VMEM)
    return pl.pallas_call(
        pair_kernel,
        in_specs=[pl.BlockSpec(memory_space=pltpu.SMEM), vmem, vmem],
        out_specs=vmem,
        out_shape=jax.ShapeDtypeStruct((CN,) + own.shape, own.dtype),
        compiler_params=pltpu.CompilerParams(vmem_limit_bytes=16 << 20),
        name="pair",
    )(core[None].astype(jnp.int32), own, other)


def join_kernel(*refs):
    out_ref = refs[-1]
    for i, ref in enumerate(refs[:-2]):
        out_ref[i * 128 : (i + 1) * 128, :] = ref[...]


def join(blocks, earlier):
    vmem = pl.BlockSpec(memory_space=pltpu.VMEM)
    return pl.pallas_call(
        join_kernel,
        in_specs=[vmem] * len(blocks) + [pl.BlockSpec(memory_space=pl.ANY)],
        out_specs=vmem,
        out_shape=jax.ShapeDtypeStruct((len(blocks) * 128, KV), BF),
        compiler_params=pltpu.CompilerParams(vmem_limit_bytes=16 << 20),
        name="join",
    )(*blocks, earlier)


def per_device(inputs, queries, keys, values, out_grad, lengths, value_weight):
    core, x, zl = (lax.axis_index(name) for name in ("core", "x", "zl"))
    with jax.named_scope("cut_inputs"):
        pieces = to_pieces(inputs[0])
    with jax.named_scope("attention"):
        value_grad, key_grad = attend_back(queries[0], keys[0], values[0], out_grad[0], lengths, pieces)
    with jax.named_scope("gather_value_grad"):
        mine = lax.all_gather(value_grad, "x", axis=0)
        other = shifted(mine, "core", CN, 1)
        grads = pair(mine, other, core).reshape(CN * XN * TOK, KV)
    with jax.named_scope("send_inputs"):
        columns = exchange(pieces, ("core", "x"))
    with jax.named_scope("weight_term"):
        term = lax.dot_general(
            columns.reshape(CN * XN * TOK, KV), grads, (((0,), (0,)), ((), ())), preferred_element_type=F32
        ).astype(BF)
    with jax.named_scope("sum_y"):
        got = exchange(term.reshape(YN, ZL * SUB, KV), "y")
        plane = jnp.sum(got.astype(F32), axis=0).astype(BF).reshape(1, ZL, SUB, KV)
    with jax.named_scope("sum_z"):
        both = jnp.broadcast_to(plane, (ZH, ZL, SUB, KV)).reshape(ZH * ZL, SUB, KV)
        got = exchange(both, ("zh", "zl"))
        total = jnp.sum(got.astype(F32), axis=0) * F32(1.0 / 512)
    with jax.named_scope("share_rows"):
        weight_grad = spread(total.astype(BF), ("core", "y"), QN).reshape(QN * SUB, KV).astype(F32)
    with jax.named_scope("gather_weight"):
        weight = join([along_z(value_weight, steps) for steps in ((0, 4), (1, -3), (2, -2), (3, -1))], plane)
    with jax.named_scope("input_grad"):
        parts = nt(grads, weight).astype(BF).reshape(CN, XN, TOK, KV)
        kept = lax.dynamic_index_in_dim(parts, core, 0, False)
        theirs = shifted(lax.dynamic_index_in_dim(parts, 1 - core, 0, False), "core", CN, 1)
        parts = jnp.stack([kept, theirs], axis=1)
        back = []
        for by in range(XN):
            piece = lax.dynamic_index_in_dim(parts, (x + by) % XN, 0, False)
            back.append(shifted(piece, "x", XN, by) if by else piece)
        input_grad = from_pieces(back, core, zl, x)
    return (input_grad[None], key_grad[None], weight_grad)


def solution(mesh):
    names = ("zl", "x", "y", "zh", "core")
    fine = Mesh(mesh.devices.reshape(ZL, XN, YN, ZH, CN), names)
    blk = names[:2]
    rows = P(names, None, None)
    return jax.shard_map(
        per_device,
        mesh=fine,
        in_specs=(rows, rows, rows, rows, rows, P(names), P(blk, None)),
        out_specs=(rows, rows, P(blk, None)),
        check_vma=False,
    )
```

time: 104 us -> 102 us (0.981)
  blocking collectives: 0 us -> 15 us
  starting transfers between devices: 72.6 us -> 58.2 us
  local copies, waits for them, and re-layouts: 2.97 us -> 1.51 us
  Pallas kernels: 14.1 us -> 12.8 us
    all_gather x0 -> x1, blocking collectives: none -> 15 us  [per_device(): mine = lax.all_gather(value_grad, 'x', axis=0)]
    all_to_all x5 -> x4, starting transfers between devices: 36.8 us -> 24.2 us  [exchange(): return lax.all_to_all(array, axes, 0, 0, tiled=True)]
    ppermute x5, waiting for transfers between devices: 1.8 us -> 4.47 us  [shifted(): lax.ppermute(array, axes, [(i, (i + by) % count) for i in range(count)])]
    ppermute x4, starting transfers between devices: 21.4 us -> 19.1 us  [along_z(): return lax.ppermute(array, ('zl', 'zh', 'core'), pairs)]
    all_to_all x5 -> x4, waiting for transfers between devices: 6.09 us -> 4.6 us  [exchange(): return lax.all_to_all(array, axes, 0, 0, tiled=True)]
    ppermute x4, waiting for transfers between devices: 1.31 us -> 0.01 us  [along_z(): return lax.ppermute(array, ('zl', 'zh', 'core'), pairs)]
    pallas_call x1, Pallas kernels: 3.61 us -> 2.4 us  [from_pieces(): pl.pallas_call(from_pieces_kernel, grid=(TOK // part,), in_specs=[pl.Bloc...]
  transfers between devices with their start and end apart: 14 -> 13, of which waited for: 7 -> 5; matrix products, arithmetic and copies ran while one was open for 3% -> 3% of each run, Pallas kernels for 8% -> 8%
where the time goes in v8:
time: 102 us; the launch traced here: 101 us
  starting transfers between devices  58.2 us (57%)
  blocking collectives  15 us (15%)
  Pallas kernels  12.8 us (13%)
  waiting for transfers between devices  9.09 us (9%)
  matrix products  2.29 us (2%)
  between operations  1.54 us (2%)
  local copies, waits for them, and re-layouts  1.51 us (1%)
  other arithmetic  1.03 us (1%)
    all_to_all x4, starting transfers between devices, exchange(): return lax.all_to_all(array, axes, 0, 0, tiled=True)  24.2 us
    ppermute x4, starting transfers between devices, along_z(): return lax.ppermute(array, ('zl', 'zh', 'core'), pairs)  19.1 us
    all_gather x1, blocking collectives, per_device(): mine = lax.all_gather(value_grad, 'x', axis=0)  15 us
    ppermute x5, starting transfers between devices, shifted(): lax.ppermute(array, axes, [(i, (i + by) % count) for i in range(count)])  14.9 us
    pallas_call x1, Pallas kernels, attend_back(): pl.pallas_call(attend_kernel, grid=(heads,), in_specs=[pl.BlockSpec(memor...  5.9 us
    all_to_all x4, waiting for transfers between devices, exchange(): return lax.all_to_all(array, axes, 0, 0, tiled=True)  4.6 us
    ppermute x5, waiting for transfers between devices, shifted(): lax.ppermute(array, axes, [(i, (i + by) % count) for i in range(count)])  4.47 us
    pallas_call x1, Pallas kernels, to_pieces(): pl.pallas_call(to_pieces_kernel, grid=(TOK // part,), in_specs=[pl.BlockS...  4.36 us
  transfers between devices with their start and end apart: 13, of which 5 were waited for; matrix products, arithmetic and copies ran while one was open for 3% of the time, Pallas kernels for 8%

profile of v8, /device:TPU:1, one launch (start us, length us, event | category | flops | bytes accessed | tf_op | source)
XLA Modules:
  0.0 101.5 jit_solution(950573041240939351)
XLA Ops:
  0.6 4.4 %to_pieces.1._ = bf16[8,128,512]{2,1,0:T(8,128)(2,1)} custom-call(bf16[128,4096]{1,0:T(8,128)(2,1)} %bitcast.48), custom_call_target="tpu_custom_call" | custom-call | flops 4194304 | bytes 2097152 | tf_op jit(solution)/shard_map/cut_inputs/to_pieces/pallas_call | solution.py:103
  5.0 10.4 %all-to-all-start = ((bf16[8,128,512]{2,1,0:T(8,128)(2,1)}), bf16[8,128,512]{2,1,0:T(8,128)(2,1)S(1)}, u32[]{:S(2)}, u32[]{:S(2)}) async-start(bf16[8,128,512]{2,1,0:T(8,128)(2,1)} %to_pieces.1._), calls=%async_computation | async-start | bytes 2097152 | tf_op jit(solution)/shard_map/send_inputs/all_to_all | solution.py:131
  16.0 5.9 %attend.1 = (bf16[128,512]{1,0:T(8,128)(2,1)}, bf16[128,512]{1,0:T(8,128)(2,1)}) custom-call(s32[1]{0:T(128)S(6)} %copy.10.length_ref, bf16[128,4096]{1,0:T(8,128)(2,1)} %bitcast.49, bf16[128,512]{1,0:T(8,128)(2,1)} %bitcast.54, bf16[128,512]{1,0:T(8,128)(2,1)} %bitcast.55, bf16[128,4096]{1,0:T(8,128)(2,1)} %bitcast.50, bf16[8,128,512]{2,1,0:T(8,128)(2,1)} %to_pieces.1._), custom_call_target="tpu_custom_call" | custom-call | flops 671088640 | bytes 3145728 | tf_op jit(solution)/shard_map/attention/attend/pallas_call | solution.py:54
  21.9 15.0 %all-gather = bf16[512,512]{1,0:T(8,128)(2,1)S(1)} all-gather(bf16[128,512]{1,0:T(8,128)(2,1)} %get-tuple-element.5), channel_id=2, replica_groups=mesh['zl'=8,'x'=4,'y'=4,'zh'=2,'core'=2] {'x'}, dimensions={0}, use_global_device_ids=true | all-gather | bytes 655360 | tf_op jit(solution)/shard_map/gather_value_grad/all_gather | solution.py:194
  36.9 4.0 %collective-permute-start = (bf16[4,128,512]{2,1,0:T(8,128)(2,1)S(1)}, bf16[4,128,512]{2,1,0:T(8,128)(2,1)S(1)}, u32[]{:S(2)}, u32[]{:S(2)}) collective-permute-start(bf16[4,128,512]{2,1,0:T(8,128)(2,1)S(1)} %bitcast.41), channel_id=1, source_target_pairs={{0,1},{1,0},{2,3},{3,2},{4,5},{5,4},{6,7},{7,6},{8,9},{9,8},{10,11... | collective-permute-start | bytes 1572872 | tf_op jit(solution)/shard_map/gather_value_grad/ppermute | solution.py:139
  41.0 1.5 %collective-permute-done.other_ref = bf16[4,128,512]{2,1,0:T(8,128)(2,1)S(1)} collective-permute-done((bf16[4,128,512]{2,1,0:T(8,128)(2,1)S(1)}, bf16[4,128,512]{2,1,0:T(8,128)(2,1)S(1)}, u32[]{:S(2)}, u32[]{:S(2)}) %collective-permute-start) | collective-permute-done | bytes 524320 | tf_op jit(solution)/shard_map/gather_value_grad/ppermute | solution.py:139
  42.5 0.1 pair.1
  42.6 1.6 %convolution_convert_fusion.1 = bf16[512,512]{0,1:T(8,128)(2,1)} fusion(bf16[1024,512]{1,0:T(8,128)(2,1)S(1)} %bitcast.45, bf16[1024,512]{1,0:T(8,128)(2,1)S(1)} %bitcast.51), kind=kOutput, calls=%fused_computation.9 | convolution fusion | flops 537133056 | bytes 2621440 | tf_op jit(solution)/shard_map/weight_term/dot_general | solution.py:200
  44.2 3.6 %all-to-all-start.1 = ((bf16[4,128,512]{2,1,0:T(8,128)(2,1)}), bf16[4,128,512]{2,1,0:T(8,128)(2,1)S(1)}, u32[]{:S(2)}, u32[]{:S(2)}) async-start(bf16[4,128,512]{2,1,0:T(8,128)(2,1)} %bitcast.13), calls=%async_computation.1 | async-start | bytes 1048576 | tf_op jit(solution)/shard_map/sum_y/all_to_all | solution.py:131
  47.8 4.9 %collective-permute-start.1 = (bf16[128,512]{1,0:T(8,128)(2,1)S(1)}, bf16[128,512]{1,0:T(8,128)(2,1)S(1)}, u32[]{:S(2)}, u32[]{:S(2)}) collective-permute-start(bf16[128,512]{1,0:T(8,128)(2,1)S(1)} %copy-done), channel_id=1, source_target_pairs={{0,0},{1,257},{64,64},{65,321},{128,128},{129,385},{192,192},{193,... | collective-permute-start | bytes 393224 | tf_op jit(solution)/shard_map/gather_weight/ppermute | solution.py:148
  52.7 5.1 %collective-permute-start.2 = (bf16[128,512]{1,0:T(8,128)(2,1)S(1)}, bf16[128,512]{1,0:T(8,128)(2,1)S(1)}, u32[]{:S(2)}, u32[]{:S(2)}) collective-permute-start(bf16[128,512]{1,0:T(8,128)(2,1)S(1)} %copy-done), channel_id=1, source_target_pairs={{0,64},{1,323},{64,128},{65,387},{128,192},{129,451},{192,256},{19... | collective-permute-start | bytes 393224 | tf_op jit(solution)/shard_map/gather_weight/ppermute | solution.py:148
  57.8 6.4 %collective-permute-start.3 = (bf16[128,512]{1,0:T(8,128)(2,1)S(1)}, bf16[128,512]{1,0:T(8,128)(2,1)S(1)}, u32[]{:S(2)}, u32[]{:S(2)}) collective-permute-start(bf16[128,512]{1,0:T(8,128)(2,1)S(1)} %copy-done), channel_id=1, source_target_pairs={{0,128},{1,387},{64,192},{65,451},{128,256},{129,1},{192,320},{193... | collective-permute-start | bytes 393224 | tf_op jit(solution)/shard_map/gather_weight/ppermute | solution.py:148
  64.2 2.6 %collective-permute-start.4 = (bf16[128,512]{1,0:T(8,128)(2,1)S(1)}, bf16[128,512]{1,0:T(8,128)(2,1)S(1)}, u32[]{:S(2)}, u32[]{:S(2)}) collective-permute-start(bf16[128,512]{1,0:T(8,128)(2,1)S(1)} %copy-done), channel_id=1, source_target_pairs={{0,192},{1,451},{64,256},{65,1},{128,320},{129,65},{192,384},{193,... | collective-permute-start | bytes 393224 | tf_op jit(solution)/shard_map/gather_weight/ppermute | solution.py:148
  66.9 0.1 reduce_sum.21
  67.0 0.7 broadcast_in_dim.26
  67.7 5.5 %all-to-all-start.2 = ((bf16[16,16,512]{2,1,0:T(8,128)(2,1)}), bf16[16,16,512]{2,1,0:T(8,128)(2,1)S(1)}, u32[]{:S(2)}, u32[]{:S(2)}) async-start(bf16[16,16,512]{2,1,0:T(8,128)(2,1)} %bitcast.26), calls=%async_computation.2 | async-start | bytes 524288 | tf_op jit(solution)/shard_map/sum_z/all_to_all | solution.py:131
  73.3 0.7 convolution_convert_fusion
  74.1 0.1 dynamic-slice_bitcast_fusion
  74.2 1.9 %collective-permute-start.5 = (bf16[4,128,512]{2,1,0:T(8,128)(2,1)S(1)}, bf16[4,128,512]{2,1,0:T(8,128)(2,1)S(1)}, u32[]{:S(2)}, u32[]{:S(2)}) collective-permute-start(bf16[4,128,512]{2,1,0:T(8,128)(2,1)S(1)} %get-tuple-element.11), channel_id=1, source_target_pairs={{0,1},{1,0},{2,3},{3,2},{4,5},{5,4},{6,7},{7,6},{8,9},{9,8},{10,11... | collective-permute-start | bytes 1572872 | tf_op jit(solution)/shard_map/input_grad/ppermute | solution.py:139
  76.2 1.8 %collective-permute-done.5 = bf16[4,128,512]{2,1,0:T(8,128)(2,1)S(1)} collective-permute-done((bf16[4,128,512]{2,1,0:T(8,128)(2,1)S(1)}, bf16[4,128,512]{2,1,0:T(8,128)(2,1)S(1)}, u32[]{:S(2)}, u32[]{:S(2)}) %collective-permute-start.5) | collective-permute-done | bytes 524320 | tf_op jit(solution)/shard_map/input_grad/ppermute | solution.py:139
  78.0 0.1 fusion.1
  78.1 1.9 %collective-permute-start.6 = (bf16[2,128,512]{2,1,0:T(8,128)(2,1)S(1)}, bf16[2,128,512]{2,1,0:T(8,128)(2,1)S(1)}, u32[]{:S(2)}, u32[]{:S(2)}) collective-permute-start(bf16[2,128,512]{2,1,0:T(8,128)(2,1)S(1)} %get-tuple-element.9), channel_id=1, source_target_pairs={{0,16},{16,32},{32,48},{48,0},{1,17},{17,33},{33,49},{49,1},{2,18}... | collective-permute-start | bytes 786440 | tf_op jit(solution)/shard_map/input_grad/ppermute | solution.py:139
  80.0 4.3 %collective-permute-start.7 = (bf16[2,128,512]{2,1,0:T(8,128)(2,1)S(1)}, bf16[2,128,512]{2,1,0:T(8,128)(2,1)S(1)}, u32[]{:S(2)}, u32[]{:S(2)}) collective-permute-start(bf16[2,128,512]{2,1,0:T(8,128)(2,1)S(1)} %get-tuple-element.10), channel_id=1, source_target_pairs={{0,32},{16,48},{32,0},{48,16},{1,33},{17,49},{33,1},{49,17},{2,34}... | collective-permute-start | bytes 786440 | tf_op jit(solution)/shard_map/input_grad/ppermute | solution.py:139
  84.3 2.8 %collective-permute-start.8 = (bf16[2,128,512]{2,1,0:T(8,128)(2,1)S(1)}, bf16[2,128,512]{2,1,0:T(8,128)(2,1)S(1)}, u32[]{:S(2)}, u32[]{:S(2)}) collective-permute-start(bf16[2,128,512]{2,1,0:T(8,128)(2,1)S(1)} %get-tuple-element.7), channel_id=1, source_target_pairs={{0,48},{16,0},{32,16},{48,32},{1,49},{17,1},{33,17},{49,33},{2,50}... | collective-permute-start | bytes 786440 | tf_op jit(solution)/shard_map/input_grad/ppermute | solution.py:139
  87.1 3.1 %all-to-all-done.2 = bf16[16,16,512]{2,1,0:T(8,128)(2,1)S(1)} async-done(((bf16[16,16,512]{2,1,0:T(8,128)(2,1)}), bf16[16,16,512]{2,1,0:T(8,128)(2,1)S(1)}, u32[]{:S(2)}, u32[]{:S(2)}) %all-to-all-start.2) | async-done | bytes 262176 | tf_op jit(solution)/shard_map/sum_z/all_to_all | solution.py:131
  90.2 0.7 broadcast_in_dim.27
  90.9 4.7 %all-to-all-start.3 = ((bf16[8,16,512]{2,1,0:T(8,128)(2,1)}), bf16[8,16,512]{2,1,0:T(8,128)(2,1)S(1)}, u32[]{:S(2)}, u32[]{:S(2)}) async-start(bf16[8,16,512]{2,1,0:T(8,128)(2,1)} %broadcast_in_dim.27), calls=%async_computation.3 | async-start | bytes 262144 | tf_op jit(solution)/shard_map/share_rows/all_to_all | solution.py:131
  95.6 0.1 pad_add_fusion.at_ref
  95.7 1.1 %collective-permute-done.8.refs_3_ = bf16[2,128,512]{2,1,0:T(8,128)(2,1)S(1)} collective-permute-done((bf16[2,128,512]{2,1,0:T(8,128)(2,1)S(1)}, bf16[2,128,512]{2,1,0:T(8,128)(2,1)S(1)}, u32[]{:S(2)}, u32[]{:S(2)}) %collective-permute-start.8) | collective-permute-done | bytes 262176 | tf_op jit(solution)/shard_map/input_grad/ppermute | solution.py:139
  96.8 2.4 %from_pieces.1 = bf16[128,4096]{1,0:T(8,128)(2,1)} custom-call(s32[3]{0:T(128)S(1)} %pad_add_fusion.at_ref, bf16[2,128,512]{2,1,0:T(8,128)(2,1)S(1)} %get-tuple-element.8.refs_0_, bf16[2,128,512]{2,1,0:T(8,128)(2,1)S(1)} %collective-permute-done.6.refs_1_, bf16[2,128,512]{2,1,0:T(8,128)(2,1)S(1)} %collective-permute-done.7.refs_2_, ...), custom_call_target="tpu_custom_call" | custom-call | bytes 2097152 | tf_op jit(solution)/shard_map/input_grad/from_pieces/pallas_call | solution.py:117
  99.2 1.5 %all-to-all-done.3 = bf16[8,16,512]{2,1,0:T(8,128)(2,1)S(1)} async-done(((bf16[8,16,512]{2,1,0:T(8,128)(2,1)}), bf16[8,16,512]{2,1,0:T(8,128)(2,1)S(1)}, u32[]{:S(2)}, u32[]{:S(2)}) %all-to-all-start.3) | async-done | bytes 131104 | tf_op jit(solution)/shard_map/share_rows/all_to_all | solution.py:131
  100.8 0.7 bitcast_convert_fusion
  (13 shorter events, 0.1 us)
Async XLA Ops:
  5.0 37.6 %all-to-all-start = ((bf16[8,128,512]{2,1,0:T(8,128)(2,1)}), bf16[8,128,512]{2,1,0:T(8,128)(2,1)S(1)}, u32[]{:S(2)}, u32[]{:S(2)}) async-start(bf16[8,128,512]{2,1,0:T(8,128)(2,1)} %to_pieces.1._), calls=%async_computation | async-start | bytes 2097152 | tf_op jit(solution)/shard_map/send_inputs/all_to_all | solution.py:131
  36.9 5.6 %collective-permute-start = (bf16[4,128,512]{2,1,0:T(8,128)(2,1)S(1)}, bf16[4,128,512]{2,1,0:T(8,128)(2,1)S(1)}, u32[]{:S(2)}, u32[]{:S(2)}) collective-permute-start(bf16[4,128,512]{2,1,0:T(8,128)(2,1)S(1)} %bitcast.41), channel_id=1, source_target_pairs={{0,1},{1,0},{2,3},{3,2},{4,5},{5,4},{6,7},{7,6},{8,9},{9,8},{10,11... | collective-permute-start | bytes 1572872 | tf_op jit(solution)/shard_map/gather_value_grad/ppermute | solution.py:139
  44.2 3.6 %copy-start = (bf16[128,512]{1,0:T(8,128)(2,1)S(1)}, bf16[128,512]{1,0:T(8,128)(2,1)}, u32[]{:S(2)}) copy-start(bf16[128,512]{1,0:T(8,128)(2,1)} %param.13) | copy-start | bytes 393220
  44.2 22.7 %all-to-all-start.1 = ((bf16[4,128,512]{2,1,0:T(8,128)(2,1)}), bf16[4,128,512]{2,1,0:T(8,128)(2,1)S(1)}, u32[]{:S(2)}, u32[]{:S(2)}) async-start(bf16[4,128,512]{2,1,0:T(8,128)(2,1)} %bitcast.13), calls=%async_computation.1 | async-start | bytes 1048576 | tf_op jit(solution)/shard_map/sum_y/all_to_all | solution.py:131
  47.8 25.5 %collective-permute-start.1 = (bf16[128,512]{1,0:T(8,128)(2,1)S(1)}, bf16[128,512]{1,0:T(8,128)(2,1)S(1)}, u32[]{:S(2)}, u32[]{:S(2)}) collective-permute-start(bf16[128,512]{1,0:T(8,128)(2,1)S(1)} %copy-done), channel_id=1, source_target_pairs={{0,0},{1,257},{64,64},{65,321},{128,128},{129,385},{192,192},{193,... | collective-permute-start | bytes 393224 | tf_op jit(solution)/shard_map/gather_weight/ppermute | solution.py:148
  52.7 20.5 %collective-permute-start.2 = (bf16[128,512]{1,0:T(8,128)(2,1)S(1)}, bf16[128,512]{1,0:T(8,128)(2,1)S(1)}, u32[]{:S(2)}, u32[]{:S(2)}) collective-permute-start(bf16[128,512]{1,0:T(8,128)(2,1)S(1)} %copy-done), channel_id=1, source_target_pairs={{0,64},{1,323},{64,128},{65,387},{128,192},{129,451},{192,256},{19... | collective-permute-start | bytes 393224 | tf_op jit(solution)/shard_map/gather_weight/ppermute | solution.py:148
  57.8 15.4 %collective-permute-start.3 = (bf16[128,512]{1,0:T(8,128)(2,1)S(1)}, bf16[128,512]{1,0:T(8,128)(2,1)S(1)}, u32[]{:S(2)}, u32[]{:S(2)}) collective-permute-start(bf16[128,512]{1,0:T(8,128)(2,1)S(1)} %copy-done), channel_id=1, source_target_pairs={{0,128},{1,387},{64,192},{65,451},{128,256},{129,1},{192,320},{193... | collective-permute-start | bytes 393224 | tf_op jit(solution)/shard_map/gather_weight/ppermute | solution.py:148
  64.2 9.1 %collective-permute-start.4 = (bf16[128,512]{1,0:T(8,128)(2,1)S(1)}, bf16[128,512]{1,0:T(8,128)(2,1)S(1)}, u32[]{:S(2)}, u32[]{:S(2)}) collective-permute-start(bf16[128,512]{1,0:T(8,128)(2,1)S(1)} %copy-done), channel_id=1, source_target_pairs={{0,192},{1,451},{64,256},{65,1},{128,320},{129,65},{192,384},{193,... | collective-permute-start | bytes 393224 | tf_op jit(solution)/shard_map/gather_weight/ppermute | solution.py:148
  67.7 22.5 %all-to-all-start.2 = ((bf16[16,16,512]{2,1,0:T(8,128)(2,1)}), bf16[16,16,512]{2,1,0:T(8,128)(2,1)S(1)}, u32[]{:S(2)}, u32[]{:S(2)}) async-start(bf16[16,16,512]{2,1,0:T(8,128)(2,1)} %bitcast.26), calls=%async_computation.2 | async-start | bytes 524288 | tf_op jit(solution)/shard_map/sum_z/all_to_all | solution.py:131
  74.2 3.8 %collective-permute-start.5 = (bf16[4,128,512]{2,1,0:T(8,128)(2,1)S(1)}, bf16[4,128,512]{2,1,0:T(8,128)(2,1)S(1)}, u32[]{:S(2)}, u32[]{:S(2)}) collective-permute-start(bf16[4,128,512]{2,1,0:T(8,128)(2,1)S(1)} %get-tuple-element.11), channel_id=1, source_target_pairs={{0,1},{1,0},{2,3},{3,2},{4,5},{5,4},{6,7},{7,6},{8,9},{9,8},{10,11... | collective-permute-start | bytes 1572872 | tf_op jit(solution)/shard_map/input_grad/ppermute | solution.py:139
  78.1 17.6 %collective-permute-start.6 = (bf16[2,128,512]{2,1,0:T(8,128)(2,1)S(1)}, bf16[2,128,512]{2,1,0:T(8,128)(2,1)S(1)}, u32[]{:S(2)}, u32[]{:S(2)}) collective-permute-start(bf16[2,128,512]{2,1,0:T(8,128)(2,1)S(1)} %get-tuple-element.9), channel_id=1, source_target_pairs={{0,16},{16,32},{32,48},{48,0},{1,17},{17,33},{33,49},{49,1},{2,18}... | collective-permute-start | bytes 786440 | tf_op jit(solution)/shard_map/input_grad/ppermute | solution.py:139
  80.0 15.6 %collective-permute-start.7 = (bf16[2,128,512]{2,1,0:T(8,128)(2,1)S(1)}, bf16[2,128,512]{2,1,0:T(8,128)(2,1)S(1)}, u32[]{:S(2)}, u32[]{:S(2)}) collective-permute-start(bf16[2,128,512]{2,1,0:T(8,128)(2,1)S(1)} %get-tuple-element.10), channel_id=1, source_target_pairs={{0,32},{16,48},{32,0},{48,16},{1,33},{17,49},{33,1},{49,17},{2,34}... | collective-permute-start | bytes 786440 | tf_op jit(solution)/shard_map/input_grad/ppermute | solution.py:139
  84.3 12.5 %collective-permute-start.8 = (bf16[2,128,512]{2,1,0:T(8,128)(2,1)S(1)}, bf16[2,128,512]{2,1,0:T(8,128)(2,1)S(1)}, u32[]{:S(2)}, u32[]{:S(2)}) collective-permute-start(bf16[2,128,512]{2,1,0:T(8,128)(2,1)S(1)} %get-tuple-element.7), channel_id=1, source_target_pairs={{0,48},{16,0},{32,16},{48,32},{1,49},{17,1},{33,17},{49,33},{2,50}... | collective-permute-start | bytes 786440 | tf_op jit(solution)/shard_map/input_grad/ppermute | solution.py:139
  90.9 9.9 %all-to-all-start.3 = ((bf16[8,16,512]{2,1,0:T(8,128)(2,1)}), bf16[8,16,512]{2,1,0:T(8,128)(2,1)S(1)}, u32[]{:S(2)}, u32[]{:S(2)}) async-start(bf16[8,16,512]{2,1,0:T(8,128)(2,1)} %broadcast_in_dim.27), calls=%async_computation.3 | async-start | bytes 262144 | tf_op jit(solution)/shard_map/share_rows/all_to_all | solution.py:131

commit v9 on v8

--- a/solution.py
+++ b/solution.py
@@ -10,6 +10,7 @@
 QN = CN * YN
 TOK, WIDTH, KV, HD = 128, 4096, 512, 128
 GROUP = 8
+KV_STEP = 2
 SUB = 16
 HELD = ZL // CN
 BF, F32 = jnp.bfloat16, jnp.float32
@@ -21,39 +22,35 @@
 
 def attend_kernel(length_ref, q_ref, k_ref, v_ref, g_ref, _, vg_ref, kg_ref):
     scaling = HD ** (-0.5)
-    keys, vals = k_ref[...], v_ref[...]
     length = length_ref[0]
-    step = 2
-    wide = step * TOK
+    wide = GROUP * TOK
     pos_s = lax.broadcasted_iota(jnp.int32, (TOK, wide), 0)
     pos_t = lax.broadcasted_iota(jnp.int32, (TOK, wide), 1) & (TOK - 1)
     allowed = pos_s <= pos_t
     live = ((lax.broadcasted_iota(jnp.int32, (1, wide), 1) & (TOK - 1)) < length).astype(F32)
-    vg = jnp.zeros((TOK, HD), F32)
-    kg = jnp.zeros((TOK, HD), F32)
-    for first in range(0, GROUP, step):
-        heads = range(first, first + step)
+    for head in range(KV_STEP):
+        cols = slice(head * HD, (head + 1) * HD)
+        heads = range(head * GROUP, (head + 1) * GROUP)
         qs = jnp.concatenate([q_ref[:, h * HD : (h + 1) * HD] for h in heads], axis=0)
         gs = jnp.concatenate([g_ref[:, h * HD : (h + 1) * HD] for h in heads], axis=0)
-        scores = jnp.where(allowed, nt(keys, qs) * scaling, F32(-1e30))
+        scores = jnp.where(allowed, nt(k_ref[:, cols], qs) * scaling, F32(-1e30))
         expd = jnp.exp(scores - jnp.max(scores, axis=0, keepdims=True))
         probs = expd * (live / jnp.sum(expd, axis=0, keepdims=True))
-        dprob = nt(vals, gs)
+        dprob = nt(v_ref[:, cols], gs)
         delta = jnp.sum(probs * dprob, axis=0, keepdims=True)
         dscore = probs * (dprob - delta)
-        vg += jnp.dot(probs.astype(BF), gs, preferred_element_type=F32)
-        kg += jnp.dot(dscore.astype(BF), qs, preferred_element_type=F32)
-    vg_ref[...] = vg.astype(BF)
-    kg_ref[...] = (kg * scaling).astype(BF)
+        vg = jnp.dot(probs.astype(BF), gs, preferred_element_type=F32)
+        kg = jnp.dot(dscore.astype(BF), qs, preferred_element_type=F32)
+        vg_ref[:, cols] = vg.astype(BF)
+        kg_ref[:, cols] = (kg * scaling).astype(BF)
 
 
 def attend_back(query, key_rows, value_rows, grad_rows, length, earlier):
-    heads = KV // HD
-    wide = pl.BlockSpec((TOK, GROUP * HD), lambda g: (0, g))
-    thin = pl.BlockSpec((TOK, HD), lambda g: (0, g))
+    wide = pl.BlockSpec((TOK, KV_STEP * GROUP * HD), lambda g: (0, g))
+    thin = pl.BlockSpec((TOK, KV_STEP * HD), lambda g: (0, g))
     return pl.pallas_call(
         attend_kernel,
-        grid=(heads,),
+        grid=(KV // HD // KV_STEP,),
         in_specs=[pl.BlockSpec(memory_space=pltpu.SMEM), wide, thin, thin, wide, pl.BlockSpec(memory_space=pl.ANY)],
         out_specs=[thin, thin],
         out_shape=[jax.ShapeDtypeStruct((TOK, KV), BF)] * 2,
@@ -99,7 +96,7 @@
 
 
 def to_pieces(rows):
-    part = 32
+    part = 64
     return pl.pallas_call(
         to_pieces_kernel,
         grid=(TOK // part,),
@@ -112,7 +109,7 @@
 
 
 def from_pieces(pieces, core, zl, x):
-    part = 32
+    part = 64
     firsts = [(zl + ZL - HELD * c) % ZL for c in (core, 1 - core)]
     return pl.pallas_call(
         from_pieces_kernel,

time: 102 us -> 101 us (level)
  Pallas kernels: 12.8 us -> 9.59 us
  blocking collectives: 15 us -> 16.7 us
    pallas_call x1, Pallas kernels: 5.9 us -> 4.26 us  [attend_back(): pl.pallas_call(attend_kernel, grid=(KV // HD // KV_STEP,), in_specs=[pl.B...]
    all_gather x1, blocking collectives: 15 us -> 16.7 us  [per_device(): mine = lax.all_gather(value_grad, 'x', axis=0)]
  transfers between devices with their start and end apart: 13 -> 13, of which waited for: 5 -> 5; matrix products, arithmetic and copies ran while one was open for 3% -> 3% of each run, Pallas kernels for 8% -> 6%
where the time goes in v9:
time: 101 us
  starting transfers between devices  58.2 us (58%)
  blocking collectives  16.7 us (17%)
  waiting for transfers between devices  9.75 us (10%)
  Pallas kernels  9.59 us (9%)
  matrix products  2.29 us (2%)
  between operations  1.54 us (2%)
  local copies, waits for them, and re-layouts  1.51 us (1%)
  other arithmetic  1.03 us (1%)
    all_to_all x4, starting transfers between devices, exchange(): return lax.all_to_all(array, axes, 0, 0, tiled=True)  24.2 us
    ppermute x4, starting transfers between devices, along_z(): return lax.ppermute(array, ('zl', 'zh', 'core'), pairs)  19.1 us
    all_gather x1, blocking collectives, per_device(): mine = lax.all_gather(value_grad, 'x', axis=0)  16.7 us
    ppermute x5, starting transfers between devices, shifted(): lax.ppermute(array, axes, [(i, (i + by) % count) for i in range(count)])  14.9 us
    all_to_all x4, waiting for transfers between devices, exchange(): return lax.all_to_all(array, axes, 0, 0, tiled=True)  5.27 us
    ppermute x5, waiting for transfers between devices, shifted(): lax.ppermute(array, axes, [(i, (i + by) % count) for i in range(count)])  4.47 us
    pallas_call x1, Pallas kernels, attend_back(): pl.pallas_call(attend_kernel, grid=(KV // HD // KV_STEP,), in_specs=[pl.B...  4.26 us
    pallas_call x1, Pallas kernels, to_pieces(): pl.pallas_call(to_pieces_kernel, grid=(TOK // part,), in_specs=[pl.BlockS...  3.49 us
  transfers between devices with their start and end apart: 13, of which 5 were waited for; matrix products, arithmetic and copies ran while one was open for 3% of the time, Pallas kernels for 6%

profile of v9, /device:TPU:1, one launch (start us, length us, event | category | flops | bytes accessed | tf_op | source)
XLA Modules:
  0.0 100.6 jit_solution(2108547572568988238)
XLA Ops:
  0.6 3.5 %to_pieces.1._ = bf16[8,128,512]{2,1,0:T(8,128)(2,1)} custom-call(bf16[128,4096]{1,0:T(8,128)(2,1)} %bitcast.48), custom_call_target="tpu_custom_call" | custom-call | flops 4194304 | bytes 2097152 | tf_op jit(solution)/shard_map/cut_inputs/to_pieces/pallas_call | solution.py:100
  4.1 10.4 %all-to-all-start = ((bf16[8,128,512]{2,1,0:T(8,128)(2,1)}), bf16[8,128,512]{2,1,0:T(8,128)(2,1)S(1)}, u32[]{:S(2)}, u32[]{:S(2)}) async-start(bf16[8,128,512]{2,1,0:T(8,128)(2,1)} %to_pieces.1._), calls=%async_computation | async-start | bytes 2097152 | tf_op jit(solution)/shard_map/send_inputs/all_to_all | solution.py:128
  15.1 4.3 %attend.1 = (bf16[128,512]{1,0:T(8,128)(2,1)}, bf16[128,512]{1,0:T(8,128)(2,1)}) custom-call(s32[1]{0:T(128)S(6)} %copy.10.length_ref, bf16[128,4096]{1,0:T(8,128)(2,1)} %bitcast.49, bf16[128,512]{1,0:T(8,128)(2,1)} %bitcast.54, bf16[128,512]{1,0:T(8,128)(2,1)} %bitcast.55, bf16[128,4096]{1,0:T(8,128)(2,1)} %bitcast.50, bf16[8,128,512]{2,1,0:T(8,128)(2,1)} %to_pieces.1._), custom_call_target="tpu_custom_call" | custom-call | flops 671088640 | bytes 3145728 | tf_op jit(solution)/shard_map/attention/attend/pallas_call | solution.py:51
  19.4 16.7 %all-gather = bf16[512,512]{1,0:T(8,128)(2,1)S(1)} all-gather(bf16[128,512]{1,0:T(8,128)(2,1)} %get-tuple-element.5), channel_id=2, replica_groups=mesh['zl'=8,'x'=4,'y'=4,'zh'=2,'core'=2] {'x'}, dimensions={0}, use_global_device_ids=true | all-gather | bytes 655360 | tf_op jit(solution)/shard_map/gather_value_grad/all_gather | solution.py:191
  36.1 4.0 %collective-permute-start = (bf16[4,128,512]{2,1,0:T(8,128)(2,1)S(1)}, bf16[4,128,512]{2,1,0:T(8,128)(2,1)S(1)}, u32[]{:S(2)}, u32[]{:S(2)}) collective-permute-start(bf16[4,128,512]{2,1,0:T(8,128)(2,1)S(1)} %bitcast.41), channel_id=1, source_target_pairs={{0,1},{1,0},{2,3},{3,2},{4,5},{5,4},{6,7},{7,6},{8,9},{9,8},{10,11... | collective-permute-start | bytes 1572872 | tf_op jit(solution)/shard_map/gather_value_grad/ppermute | solution.py:136
  40.1 1.5 %collective-permute-done.other_ref = bf16[4,128,512]{2,1,0:T(8,128)(2,1)S(1)} collective-permute-done((bf16[4,128,512]{2,1,0:T(8,128)(2,1)S(1)}, bf16[4,128,512]{2,1,0:T(8,128)(2,1)S(1)}, u32[]{:S(2)}, u32[]{:S(2)}) %collective-permute-start) | collective-permute-done | bytes 524320 | tf_op jit(solution)/shard_map/gather_value_grad/ppermute | solution.py:136
  41.6 0.1 pair.1
  41.7 1.6 %convolution_convert_fusion.1 = bf16[512,512]{0,1:T(8,128)(2,1)} fusion(bf16[1024,512]{1,0:T(8,128)(2,1)S(1)} %bitcast.45, bf16[1024,512]{1,0:T(8,128)(2,1)S(1)} %bitcast.51), kind=kOutput, calls=%fused_computation.9 | convolution fusion | flops 537133056 | bytes 2621440 | tf_op jit(solution)/shard_map/weight_term/dot_general | solution.py:197
  43.3 3.6 %all-to-all-start.1 = ((bf16[4,128,512]{2,1,0:T(8,128)(2,1)}), bf16[4,128,512]{2,1,0:T(8,128)(2,1)S(1)}, u32[]{:S(2)}, u32[]{:S(2)}) async-start(bf16[4,128,512]{2,1,0:T(8,128)(2,1)} %bitcast.13), calls=%async_computation.1 | async-start | bytes 1048576 | tf_op jit(solution)/shard_map/sum_y/all_to_all | solution.py:128
  46.9 4.9 %collective-permute-start.1 = (bf16[128,512]{1,0:T(8,128)(2,1)S(1)}, bf16[128,512]{1,0:T(8,128)(2,1)S(1)}, u32[]{:S(2)}, u32[]{:S(2)}) collective-permute-start(bf16[128,512]{1,0:T(8,128)(2,1)S(1)} %copy-done), channel_id=1, source_target_pairs={{0,0},{1,257},{64,64},{65,321},{128,128},{129,385},{192,192},{193,... | collective-permute-start | bytes 393224 | tf_op jit(solution)/shard_map/gather_weight/ppermute | solution.py:145
  51.9 5.1 %collective-permute-start.2 = (bf16[128,512]{1,0:T(8,128)(2,1)S(1)}, bf16[128,512]{1,0:T(8,128)(2,1)S(1)}, u32[]{:S(2)}, u32[]{:S(2)}) collective-permute-start(bf16[128,512]{1,0:T(8,128)(2,1)S(1)} %copy-done), channel_id=1, source_target_pairs={{0,64},{1,323},{64,128},{65,387},{128,192},{129,451},{192,256},{19... | collective-permute-start | bytes 393224 | tf_op jit(solution)/shard_map/gather_weight/ppermute | solution.py:145
  57.0 6.4 %collective-permute-start.3 = (bf16[128,512]{1,0:T(8,128)(2,1)S(1)}, bf16[128,512]{1,0:T(8,128)(2,1)S(1)}, u32[]{:S(2)}, u32[]{:S(2)}) collective-permute-start(bf16[128,512]{1,0:T(8,128)(2,1)S(1)} %copy-done), channel_id=1, source_target_pairs={{0,128},{1,387},{64,192},{65,451},{128,256},{129,1},{192,320},{193... | collective-permute-start | bytes 393224 | tf_op jit(solution)/shard_map/gather_weight/ppermute | solution.py:145
  63.4 2.6 %collective-permute-start.4 = (bf16[128,512]{1,0:T(8,128)(2,1)S(1)}, bf16[128,512]{1,0:T(8,128)(2,1)S(1)}, u32[]{:S(2)}, u32[]{:S(2)}) collective-permute-start(bf16[128,512]{1,0:T(8,128)(2,1)S(1)} %copy-done), channel_id=1, source_target_pairs={{0,192},{1,451},{64,256},{65,1},{128,320},{129,65},{192,384},{193,... | collective-permute-start | bytes 393224 | tf_op jit(solution)/shard_map/gather_weight/ppermute | solution.py:145
  66.0 0.1 reduce_sum.21
  66.1 0.7 broadcast_in_dim.26
  66.8 5.5 %all-to-all-start.2 = ((bf16[16,16,512]{2,1,0:T(8,128)(2,1)}), bf16[16,16,512]{2,1,0:T(8,128)(2,1)S(1)}, u32[]{:S(2)}, u32[]{:S(2)}) async-start(bf16[16,16,512]{2,1,0:T(8,128)(2,1)} %bitcast.26), calls=%async_computation.2 | async-start | bytes 524288 | tf_op jit(solution)/shard_map/sum_z/all_to_all | solution.py:128
  72.5 0.7 convolution_convert_fusion
  73.2 0.1 dynamic-slice_bitcast_fusion
  73.3 1.9 %collective-permute-start.5 = (bf16[4,128,512]{2,1,0:T(8,128)(2,1)S(1)}, bf16[4,128,512]{2,1,0:T(8,128)(2,1)S(1)}, u32[]{:S(2)}, u32[]{:S(2)}) collective-permute-start(bf16[4,128,512]{2,1,0:T(8,128)(2,1)S(1)} %get-tuple-element.11), channel_id=1, source_target_pairs={{0,1},{1,0},{2,3},{3,2},{4,5},{5,4},{6,7},{7,6},{8,9},{9,8},{10,11... | collective-permute-start | bytes 1572872 | tf_op jit(solution)/shard_map/input_grad/ppermute | solution.py:136
  75.3 1.8 %collective-permute-done.5 = bf16[4,128,512]{2,1,0:T(8,128)(2,1)S(1)} collective-permute-done((bf16[4,128,512]{2,1,0:T(8,128)(2,1)S(1)}, bf16[4,128,512]{2,1,0:T(8,128)(2,1)S(1)}, u32[]{:S(2)}, u32[]{:S(2)}) %collective-permute-start.5) | collective-permute-done | bytes 524320 | tf_op jit(solution)/shard_map/input_grad/ppermute | solution.py:136
  77.1 0.1 fusion.1
  77.2 1.9 %collective-permute-start.6 = (bf16[2,128,512]{2,1,0:T(8,128)(2,1)S(1)}, bf16[2,128,512]{2,1,0:T(8,128)(2,1)S(1)}, u32[]{:S(2)}, u32[]{:S(2)}) collective-permute-start(bf16[2,128,512]{2,1,0:T(8,128)(2,1)S(1)} %get-tuple-element.9), channel_id=1, source_target_pairs={{0,16},{16,32},{32,48},{48,0},{1,17},{17,33},{33,49},{49,1},{2,18}... | collective-permute-start | bytes 786440 | tf_op jit(solution)/shard_map/input_grad/ppermute | solution.py:136
  79.2 4.3 %collective-permute-start.7 = (bf16[2,128,512]{2,1,0:T(8,128)(2,1)S(1)}, bf16[2,128,512]{2,1,0:T(8,128)(2,1)S(1)}, u32[]{:S(2)}, u32[]{:S(2)}) collective-permute-start(bf16[2,128,512]{2,1,0:T(8,128)(2,1)S(1)} %get-tuple-element.10), channel_id=1, source_target_pairs={{0,32},{16,48},{32,0},{48,16},{1,33},{17,49},{33,1},{49,17},{2,34}... | collective-permute-start | bytes 786440 | tf_op jit(solution)/shard_map/input_grad/ppermute | solution.py:136
  83.4 2.8 %collective-permute-start.8 = (bf16[2,128,512]{2,1,0:T(8,128)(2,1)S(1)}, bf16[2,128,512]{2,1,0:T(8,128)(2,1)S(1)}, u32[]{:S(2)}, u32[]{:S(2)}) collective-permute-start(bf16[2,128,512]{2,1,0:T(8,128)(2,1)S(1)} %get-tuple-element.7), channel_id=1, source_target_pairs={{0,48},{16,0},{32,16},{48,32},{1,49},{17,1},{33,17},{49,33},{2,50}... | collective-permute-start | bytes 786440 | tf_op jit(solution)/shard_map/input_grad/ppermute | solution.py:136
  86.2 3.1 %all-to-all-done.2 = bf16[16,16,512]{2,1,0:T(8,128)(2,1)S(1)} async-done(((bf16[16,16,512]{2,1,0:T(8,128)(2,1)}), bf16[16,16,512]{2,1,0:T(8,128)(2,1)S(1)}, u32[]{:S(2)}, u32[]{:S(2)}) %all-to-all-start.2) | async-done | bytes 262176 | tf_op jit(solution)/shard_map/sum_z/all_to_all | solution.py:128
  89.4 0.7 broadcast_in_dim.27
  90.0 4.7 %all-to-all-start.3 = ((bf16[8,16,512]{2,1,0:T(8,128)(2,1)}), bf16[8,16,512]{2,1,0:T(8,128)(2,1)S(1)}, u32[]{:S(2)}, u32[]{:S(2)}) async-start(bf16[8,16,512]{2,1,0:T(8,128)(2,1)} %broadcast_in_dim.27), calls=%async_computation.3 | async-start | bytes 262144 | tf_op jit(solution)/shard_map/share_rows/all_to_all | solution.py:128
  94.7 0.1 pad_add_fusion.at_ref
  94.8 1.1 %collective-permute-done.8.refs_3_ = bf16[2,128,512]{2,1,0:T(8,128)(2,1)S(1)} collective-permute-done((bf16[2,128,512]{2,1,0:T(8,128)(2,1)S(1)}, bf16[2,128,512]{2,1,0:T(8,128)(2,1)S(1)}, u32[]{:S(2)}, u32[]{:S(2)}) %collective-permute-start.8) | collective-permute-done | bytes 262176 | tf_op jit(solution)/shard_map/input_grad/ppermute | solution.py:136
  96.0 1.7 %from_pieces.1 = bf16[128,4096]{1,0:T(8,128)(2,1)} custom-call(s32[3]{0:T(128)S(1)} %pad_add_fusion.at_ref, bf16[2,128,512]{2,1,0:T(8,128)(2,1)S(1)} %get-tuple-element.8.refs_0_, bf16[2,128,512]{2,1,0:T(8,128)(2,1)S(1)} %collective-permute-done.6.refs_1_, bf16[2,128,512]{2,1,0:T(8,128)(2,1)S(1)} %collective-permute-done.7.refs_2_, ...), custom_call_target="tpu_custom_call" | custom-call | bytes 2097152 | tf_op jit(solution)/shard_map/input_grad/from_pieces/pallas_call | solution.py:114
  97.7 2.2 %all-to-all-done.3 = bf16[8,16,512]{2,1,0:T(8,128)(2,1)S(1)} async-done(((bf16[8,16,512]{2,1,0:T(8,128)(2,1)}), bf16[8,16,512]{2,1,0:T(8,128)(2,1)S(1)}, u32[]{:S(2)}, u32[]{:S(2)}) %all-to-all-start.3) | async-done | bytes 131104 | tf_op jit(solution)/shard_map/share_rows/all_to_all | solution.py:128
  99.9 0.7 bitcast_convert_fusion
  (13 shorter events, 0.1 us)
Async XLA Ops:
  4.1 37.6 %all-to-all-start = ((bf16[8,128,512]{2,1,0:T(8,128)(2,1)}), bf16[8,128,512]{2,1,0:T(8,128)(2,1)S(1)}, u32[]{:S(2)}, u32[]{:S(2)}) async-start(bf16[8,128,512]{2,1,0:T(8,128)(2,1)} %to_pieces.1._), calls=%async_computation | async-start | bytes 2097152 | tf_op jit(solution)/shard_map/send_inputs/all_to_all | solution.py:128
  36.1 5.6 %collective-permute-start = (bf16[4,128,512]{2,1,0:T(8,128)(2,1)S(1)}, bf16[4,128,512]{2,1,0:T(8,128)(2,1)S(1)}, u32[]{:S(2)}, u32[]{:S(2)}) collective-permute-start(bf16[4,128,512]{2,1,0:T(8,128)(2,1)S(1)} %bitcast.41), channel_id=1, source_target_pairs={{0,1},{1,0},{2,3},{3,2},{4,5},{5,4},{6,7},{7,6},{8,9},{9,8},{10,11... | collective-permute-start | bytes 1572872 | tf_op jit(solution)/shard_map/gather_value_grad/ppermute | solution.py:136
  43.3 3.6 %copy-start = (bf16[128,512]{1,0:T(8,128)(2,1)S(1)}, bf16[128,512]{1,0:T(8,128)(2,1)}, u32[]{:S(2)}) copy-start(bf16[128,512]{1,0:T(8,128)(2,1)} %param.13) | copy-start | bytes 393220
  43.3 22.7 %all-to-all-start.1 = ((bf16[4,128,512]{2,1,0:T(8,128)(2,1)}), bf16[4,128,512]{2,1,0:T(8,128)(2,1)S(1)}, u32[]{:S(2)}, u32[]{:S(2)}) async-start(bf16[4,128,512]{2,1,0:T(8,128)(2,1)} %bitcast.13), calls=%async_computation.1 | async-start | bytes 1048576 | tf_op jit(solution)/shard_map/sum_y/all_to_all | solution.py:128
  46.9 25.5 %collective-permute-start.1 = (bf16[128,512]{1,0:T(8,128)(2,1)S(1)}, bf16[128,512]{1,0:T(8,128)(2,1)S(1)}, u32[]{:S(2)}, u32[]{:S(2)}) collective-permute-start(bf16[128,512]{1,0:T(8,128)(2,1)S(1)} %copy-done), channel_id=1, source_target_pairs={{0,0},{1,257},{64,64},{65,321},{128,128},{129,385},{192,192},{193,... | collective-permute-start | bytes 393224 | tf_op jit(solution)/shard_map/gather_weight/ppermute | solution.py:145
  51.9 20.5 %collective-permute-start.2 = (bf16[128,512]{1,0:T(8,128)(2,1)S(1)}, bf16[128,512]{1,0:T(8,128)(2,1)S(1)}, u32[]{:S(2)}, u32[]{:S(2)}) collective-permute-start(bf16[128,512]{1,0:T(8,128)(2,1)S(1)} %copy-done), channel_id=1, source_target_pairs={{0,64},{1,323},{64,128},{65,387},{128,192},{129,451},{192,256},{19... | collective-permute-start | bytes 393224 | tf_op jit(solution)/shard_map/gather_weight/ppermute | solution.py:145
  57.0 15.4 %collective-permute-start.3 = (bf16[128,512]{1,0:T(8,128)(2,1)S(1)}, bf16[128,512]{1,0:T(8,128)(2,1)S(1)}, u32[]{:S(2)}, u32[]{:S(2)}) collective-permute-start(bf16[128,512]{1,0:T(8,128)(2,1)S(1)} %copy-done), channel_id=1, source_target_pairs={{0,128},{1,387},{64,192},{65,451},{128,256},{129,1},{192,320},{193... | collective-permute-start | bytes 393224 | tf_op jit(solution)/shard_map/gather_weight/ppermute | solution.py:145
  63.4 9.1 %collective-permute-start.4 = (bf16[128,512]{1,0:T(8,128)(2,1)S(1)}, bf16[128,512]{1,0:T(8,128)(2,1)S(1)}, u32[]{:S(2)}, u32[]{:S(2)}) collective-permute-start(bf16[128,512]{1,0:T(8,128)(2,1)S(1)} %copy-done), channel_id=1, source_target_pairs={{0,192},{1,451},{64,256},{65,1},{128,320},{129,65},{192,384},{193,... | collective-permute-start | bytes 393224 | tf_op jit(solution)/shard_map/gather_weight/ppermute | solution.py:145
  66.8 22.5 %all-to-all-start.2 = ((bf16[16,16,512]{2,1,0:T(8,128)(2,1)}), bf16[16,16,512]{2,1,0:T(8,128)(2,1)S(1)}, u32[]{:S(2)}, u32[]{:S(2)}) async-start(bf16[16,16,512]{2,1,0:T(8,128)(2,1)} %bitcast.26), calls=%async_computation.2 | async-start | bytes 524288 | tf_op jit(solution)/shard_map/sum_z/all_to_all | solution.py:128
  73.3 3.8 %collective-permute-start.5 = (bf16[4,128,512]{2,1,0:T(8,128)(2,1)S(1)}, bf16[4,128,512]{2,1,0:T(8,128)(2,1)S(1)}, u32[]{:S(2)}, u32[]{:S(2)}) collective-permute-start(bf16[4,128,512]{2,1,0:T(8,128)(2,1)S(1)} %get-tuple-element.11), channel_id=1, source_target_pairs={{0,1},{1,0},{2,3},{3,2},{4,5},{5,4},{6,7},{7,6},{8,9},{9,8},{10,11... | collective-permute-start | bytes 1572872 | tf_op jit(solution)/shard_map/input_grad/ppermute | solution.py:136
  77.2 17.6 %collective-permute-start.6 = (bf16[2,128,512]{2,1,0:T(8,128)(2,1)S(1)}, bf16[2,128,512]{2,1,0:T(8,128)(2,1)S(1)}, u32[]{:S(2)}, u32[]{:S(2)}) collective-permute-start(bf16[2,128,512]{2,1,0:T(8,128)(2,1)S(1)} %get-tuple-element.9), channel_id=1, source_target_pairs={{0,16},{16,32},{32,48},{48,0},{1,17},{17,33},{33,49},{49,1},{2,18}... | collective-permute-start | bytes 786440 | tf_op jit(solution)/shard_map/input_grad/ppermute | solution.py:136
  79.2 15.6 %collective-permute-start.7 = (bf16[2,128,512]{2,1,0:T(8,128)(2,1)S(1)}, bf16[2,128,512]{2,1,0:T(8,128)(2,1)S(1)}, u32[]{:S(2)}, u32[]{:S(2)}) collective-permute-start(bf16[2,128,512]{2,1,0:T(8,128)(2,1)S(1)} %get-tuple-element.10), channel_id=1, source_target_pairs={{0,32},{16,48},{32,0},{48,16},{1,33},{17,49},{33,1},{49,17},{2,34}... | collective-permute-start | bytes 786440 | tf_op jit(solution)/shard_map/input_grad/ppermute | solution.py:136
  83.4 12.5 %collective-permute-start.8 = (bf16[2,128,512]{2,1,0:T(8,128)(2,1)S(1)}, bf16[2,128,512]{2,1,0:T(8,128)(2,1)S(1)}, u32[]{:S(2)}, u32[]{:S(2)}) collective-permute-start(bf16[2,128,512]{2,1,0:T(8,128)(2,1)S(1)} %get-tuple-element.7), channel_id=1, source_target_pairs={{0,48},{16,0},{32,16},{48,32},{1,49},{17,1},{33,17},{49,33},{2,50}... | collective-permute-start | bytes 786440 | tf_op jit(solution)/shard_map/input_grad/ppermute | solution.py:136
  90.0 9.9 %all-to-all-start.3 = ((bf16[8,16,512]{2,1,0:T(8,128)(2,1)}), bf16[8,16,512]{2,1,0:T(8,128)(2,1)S(1)}, u32[]{:S(2)}, u32[]{:S(2)}) async-start(bf16[8,16,512]{2,1,0:T(8,128)(2,1)} %broadcast_in_dim.27), calls=%async_computation.3 | async-start | bytes 262144 | tf_op jit(solution)/shard_map/share_rows/all_to_all | solution.py:128

commit v10 on v9

--- a/solution.py
+++ b/solution.py
@@ -145,6 +145,22 @@
     return lax.ppermute(array, ("zl", "zh", "core"), pairs)
 
 
+def hold_kernel(in_ref, *refs):
+    refs[-1][...] = in_ref[...]
+
+
+def hold(array, earlier):
+    vmem = pl.BlockSpec(memory_space=pltpu.VMEM)
+    return pl.pallas_call(
+        hold_kernel,
+        in_specs=[vmem] + [pl.BlockSpec(memory_space=pl.ANY)] * len(earlier),
+        out_specs=vmem,
+        out_shape=jax.ShapeDtypeStruct(array.shape, array.dtype),
+        compiler_params=pltpu.CompilerParams(vmem_limit_bytes=16 << 20),
+        name="hold",
+    )(array, *earlier)
+
+
 def pair_kernel(core_ref, own_ref, other_ref, out_ref):
     core = core_ref[0]
     out_ref[core] = own_ref[...]
@@ -188,7 +204,8 @@
     with jax.named_scope("attention"):
         value_grad, key_grad = attend_back(queries[0], keys[0], values[0], out_grad[0], lengths, pieces)
     with jax.named_scope("gather_value_grad"):
-        mine = lax.all_gather(value_grad, "x", axis=0)
+        near = [along_z(value_weight, steps) for steps in ((1, -3), (2, -2))]
+        mine = hold(lax.all_gather(value_grad, "x", axis=0), near)
         other = shifted(mine, "core", CN, 1)
         grads = pair(mine, other, core).reshape(CN * XN * TOK, KV)
     with jax.named_scope("send_inputs"):
@@ -207,7 +224,8 @@
     with jax.named_scope("share_rows"):
         weight_grad = spread(total.astype(BF), ("core", "y"), QN).reshape(QN * SUB, KV).astype(F32)
     with jax.named_scope("gather_weight"):
-        weight = join([along_z(value_weight, steps) for steps in ((0, 4), (1, -3), (2, -2), (3, -1))], plane)
+        first, last = (along_z(value_weight, steps) for steps in ((0, 4), (3, -1)))
+        weight = join([first] + near + [last], plane)
     with jax.named_scope("input_grad"):
         parts = nt(grads, weight).astype(BF).reshape(CN, XN, TOK, KV)
         kept = lax.dynamic_index_in_dim(parts, core, 0, False)

time: 101 us -> 99.8 us (0.988)
  blocking collectives: 16.7 us -> 11.4 us
  starting transfers between devices: 58.2 us -> 63.1 us
  waiting for transfers between devices: 9.75 us -> 8.68 us
    all_to_all x4, starting transfers between devices: 24.2 us -> 29.6 us  [exchange(): return lax.all_to_all(array, axes, 0, 0, tiled=True)]
    all_gather x1, blocking collectives: 16.7 us -> 11.4 us  [per_device(): mine = hold(lax.all_gather(value_grad, 'x', axis=0), near)]
where the time goes in v10:
time: 99.8 us; the launch traced here: 99.1 us
  starting transfers between devices  63.1 us (63%)
  blocking collectives  11.4 us (11%)
  Pallas kernels  9.63 us (10%)
  waiting for transfers between devices  8.68 us (9%)
  matrix products  2.29 us (2%)
  between operations  1.52 us (2%)
  local copies, waits for them, and re-layouts  1.51 us (2%)
  other arithmetic  1.03 us (1%)
    all_to_all x4, starting transfers between devices, exchange(): return lax.all_to_all(array, axes, 0, 0, tiled=True)  29.6 us
    ppermute x4, starting transfers between devices, along_z(): return lax.ppermute(array, ('zl', 'zh', 'core'), pairs)  18.9 us
    ppermute x5, starting transfers between devices, shifted(): lax.ppermute(array, axes, [(i, (i + by) % count) for i in range(count)])  14.6 us
    all_gather x1, blocking collectives, per_device(): mine = hold(lax.all_gather(value_grad, 'x', axis=0), near)  11.4 us
    ppermute x5, waiting for transfers between devices, shifted(): lax.ppermute(array, axes, [(i, (i + by) % count) for i in range(count)])  4.39 us
    all_to_all x4, waiting for transfers between devices, exchange(): return lax.all_to_all(array, axes, 0, 0, tiled=True)  4.28 us
    pallas_call x1, Pallas kernels, attend_back(): pl.pallas_call(attend_kernel, grid=(KV // HD // KV_STEP,), in_specs=[pl.B...  4.25 us
    pallas_call x1, Pallas kernels, to_pieces(): pl.pallas_call(to_pieces_kernel, grid=(TOK // part,), in_specs=[pl.BlockS...  3.49 us
  transfers between devices with their start and end apart: 13, of which 5 were waited for; matrix products, arithmetic and copies ran while one was open for 3% of the time, Pallas kernels for 6%

profile of v10, /device:TPU:1, one launch (start us, length us, event | category | flops | bytes accessed | tf_op | source)
XLA Modules:
  0.0 99.1 jit_solution(5958029147563185227)
XLA Ops:
  0.6 3.5 %to_pieces.1._ = bf16[8,128,512]{2,1,0:T(8,128)(2,1)} custom-call(bf16[128,4096]{1,0:T(8,128)(2,1)} %bitcast.47), custom_call_target="tpu_custom_call" | custom-call | flops 4194304 | bytes 2097152 | tf_op jit(solution)/shard_map/cut_inputs/to_pieces/pallas_call | solution.py:100
  4.1 10.5 %all-to-all-start = ((bf16[8,128,512]{2,1,0:T(8,128)(2,1)}), bf16[8,128,512]{2,1,0:T(8,128)(2,1)S(1)}, u32[]{:S(2)}, u32[]{:S(2)}) async-start(bf16[8,128,512]{2,1,0:T(8,128)(2,1)} %to_pieces.1._), calls=%async_computation | async-start | bytes 2097152 | tf_op jit(solution)/shard_map/send_inputs/all_to_all | solution.py:128
  14.6 7.4 %collective-permute-start = (bf16[128,512]{1,0:T(8,128)(2,1)S(1)}, bf16[128,512]{1,0:T(8,128)(2,1)S(1)}, u32[]{:S(2)}, u32[]{:S(2)}) collective-permute-start(bf16[128,512]{1,0:T(8,128)(2,1)S(1)} %copy-done), channel_id=1, source_target_pairs={{0,64},{1,323},{64,128},{65,387},{128,192},{129,451},{192,256},{19... | collective-permute-start | bytes 393224 | tf_op jit(solution)/shard_map/gather_value_grad/ppermute | solution.py:145
  22.1 4.3 %collective-permute-start.1 = (bf16[128,512]{1,0:T(8,128)(2,1)S(1)}, bf16[128,512]{1,0:T(8,128)(2,1)S(1)}, u32[]{:S(2)}, u32[]{:S(2)}) collective-permute-start(bf16[128,512]{1,0:T(8,128)(2,1)S(1)} %copy-done), channel_id=1, source_target_pairs={{0,128},{1,387},{64,192},{65,451},{128,256},{129,1},{192,320},{193... | collective-permute-start | bytes 393224 | tf_op jit(solution)/shard_map/gather_value_grad/ppermute | solution.py:145
  27.0 4.3 %attend.1 = (bf16[128,512]{1,0:T(8,128)(2,1)}, bf16[128,512]{1,0:T(8,128)(2,1)}) custom-call(s32[1]{0:T(128)S(6)} %copy.10.length_ref, bf16[128,4096]{1,0:T(8,128)(2,1)} %bitcast.48, bf16[128,512]{1,0:T(8,128)(2,1)} %bitcast.54, bf16[128,512]{1,0:T(8,128)(2,1)} %bitcast.55, bf16[128,4096]{1,0:T(8,128)(2,1)} %bitcast.49, bf16[8,128,512]{2,1,0:T(8,128)(2,1)} %to_pieces.1._), custom_call_target="tpu_custom_call" | custom-call | flops 671088640 | bytes 3145728 | tf_op jit(solution)/shard_map/attention/attend/pallas_call | solution.py:51
  31.3 11.4 %all-gather = bf16[512,512]{1,0:T(8,128)(2,1)S(1)} all-gather(bf16[128,512]{1,0:T(8,128)(2,1)} %get-tuple-element.5), channel_id=2, replica_groups=mesh['zl'=8,'x'=4,'y'=4,'zh'=2,'core'=2] {'x'}, dimensions={0}, use_global_device_ids=true | all-gather | bytes 655360 | tf_op jit(solution)/shard_map/gather_value_grad/all_gather | solution.py:208
  42.7 1.9 %collective-permute-start.2 = (bf16[4,128,512]{2,1,0:T(8,128)(2,1)S(1)}, bf16[4,128,512]{2,1,0:T(8,128)(2,1)S(1)}, u32[]{:S(2)}, u32[]{:S(2)}) collective-permute-start(bf16[4,128,512]{2,1,0:T(8,128)(2,1)S(1)} %hold.1.own_ref), channel_id=1, source_target_pairs={{0,1},{1,0},{2,3},{3,2},{4,5},{5,4},{6,7},{7,6},{8,9},{9,8},{10,11... | collective-permute-start | bytes 1572872 | tf_op jit(solution)/shard_map/gather_value_grad/ppermute | solution.py:136
  44.6 1.9 %collective-permute-done.2.other_ref = bf16[4,128,512]{2,1,0:T(8,128)(2,1)S(1)} collective-permute-done((bf16[4,128,512]{2,1,0:T(8,128)(2,1)S(1)}, bf16[4,128,512]{2,1,0:T(8,128)(2,1)S(1)}, u32[]{:S(2)}, u32[]{:S(2)}) %collective-permute-start.2) | collective-permute-done | bytes 524320 | tf_op jit(solution)/shard_map/gather_value_grad/ppermute | solution.py:136
  46.5 0.1 pair.1
  46.6 1.6 %convolution_convert_fusion.1 = bf16[512,512]{0,1:T(8,128)(2,1)} fusion(bf16[1024,512]{1,0:T(8,128)(2,1)S(1)} %bitcast.44, bf16[1024,512]{1,0:T(8,128)(2,1)S(1)} %bitcast.50), kind=kOutput, calls=%fused_computation.9 | convolution fusion | flops 537133056 | bytes 2621440 | tf_op jit(solution)/shard_map/weight_term/dot_general | solution.py:214
  48.2 4.2 %all-to-all-start.1 = ((bf16[4,128,512]{2,1,0:T(8,128)(2,1)}), bf16[4,128,512]{2,1,0:T(8,128)(2,1)S(1)}, u32[]{:S(2)}, u32[]{:S(2)}) async-start(bf16[4,128,512]{2,1,0:T(8,128)(2,1)} %bitcast.53), calls=%async_computation.1 | async-start | bytes 1048576 | tf_op jit(solution)/shard_map/sum_y/all_to_all | solution.py:128
  52.3 4.2 %collective-permute-start.3 = (bf16[128,512]{1,0:T(8,128)(2,1)S(1)}, bf16[128,512]{1,0:T(8,128)(2,1)S(1)}, u32[]{:S(2)}, u32[]{:S(2)}) collective-permute-start(bf16[128,512]{1,0:T(8,128)(2,1)S(1)} %copy-done), channel_id=1, source_target_pairs={{0,0},{1,257},{64,64},{65,321},{128,128},{129,385},{192,192},{193,... | collective-permute-start | bytes 393224 | tf_op jit(solution)/shard_map/gather_weight/ppermute | solution.py:145
  56.6 2.9 %collective-permute-start.4 = (bf16[128,512]{1,0:T(8,128)(2,1)S(1)}, bf16[128,512]{1,0:T(8,128)(2,1)S(1)}, u32[]{:S(2)}, u32[]{:S(2)}) collective-permute-start(bf16[128,512]{1,0:T(8,128)(2,1)S(1)} %copy-done), channel_id=1, source_target_pairs={{0,192},{1,451},{64,256},{65,1},{128,320},{129,65},{192,384},{193,... | collective-permute-start | bytes 393224 | tf_op jit(solution)/shard_map/gather_weight/ppermute | solution.py:145
  59.5 2.0 %all-to-all-done.1 = bf16[4,128,512]{2,1,0:T(8,128)(2,1)S(1)} async-done(((bf16[4,128,512]{2,1,0:T(8,128)(2,1)}), bf16[4,128,512]{2,1,0:T(8,128)(2,1)S(1)}, u32[]{:S(2)}, u32[]{:S(2)}) %all-to-all-start.1) | async-done | bytes 524320 | tf_op jit(solution)/shard_map/sum_y/all_to_all | solution.py:128
  61.5 0.1 reduce_sum.21
  61.6 0.7 broadcast_in_dim.26
  62.3 7.3 %all-to-all-start.2 = ((bf16[16,16,512]{2,1,0:T(8,128)(2,1)}), bf16[16,16,512]{2,1,0:T(8,128)(2,1)S(1)}, u32[]{:S(2)}, u32[]{:S(2)}) async-start(bf16[16,16,512]{2,1,0:T(8,128)(2,1)} %bitcast.26), calls=%async_computation.2 | async-start | bytes 524288 | tf_op jit(solution)/shard_map/sum_z/all_to_all | solution.py:128
  69.7 0.7 convolution_convert_fusion
  70.5 0.1 dynamic-slice_bitcast_fusion
  70.6 3.7 %collective-permute-start.5 = (bf16[4,128,512]{2,1,0:T(8,128)(2,1)S(1)}, bf16[4,128,512]{2,1,0:T(8,128)(2,1)S(1)}, u32[]{:S(2)}, u32[]{:S(2)}) collective-permute-start(bf16[4,128,512]{2,1,0:T(8,128)(2,1)S(1)} %get-tuple-element.11), channel_id=1, source_target_pairs={{0,1},{1,0},{2,3},{3,2},{4,5},{5,4},{6,7},{7,6},{8,9},{9,8},{10,11... | collective-permute-start | bytes 1572872 | tf_op jit(solution)/shard_map/input_grad/ppermute | solution.py:136
  74.4 1.5 %collective-permute-done.5 = bf16[4,128,512]{2,1,0:T(8,128)(2,1)S(1)} collective-permute-done((bf16[4,128,512]{2,1,0:T(8,128)(2,1)S(1)}, bf16[4,128,512]{2,1,0:T(8,128)(2,1)S(1)}, u32[]{:S(2)}, u32[]{:S(2)}) %collective-permute-start.5) | collective-permute-done | bytes 524320 | tf_op jit(solution)/shard_map/input_grad/ppermute | solution.py:136
  75.8 0.1 fusion.1
  75.9 2.6 %collective-permute-start.6 = (bf16[2,128,512]{2,1,0:T(8,128)(2,1)S(1)}, bf16[2,128,512]{2,1,0:T(8,128)(2,1)S(1)}, u32[]{:S(2)}, u32[]{:S(2)}) collective-permute-start(bf16[2,128,512]{2,1,0:T(8,128)(2,1)S(1)} %get-tuple-element.9), channel_id=1, source_target_pairs={{0,16},{16,32},{32,48},{48,0},{1,17},{17,33},{33,49},{49,1},{2,18}... | collective-permute-start | bytes 786440 | tf_op jit(solution)/shard_map/input_grad/ppermute | solution.py:136
  78.5 4.3 %collective-permute-start.7 = (bf16[2,128,512]{2,1,0:T(8,128)(2,1)S(1)}, bf16[2,128,512]{2,1,0:T(8,128)(2,1)S(1)}, u32[]{:S(2)}, u32[]{:S(2)}) collective-permute-start(bf16[2,128,512]{2,1,0:T(8,128)(2,1)S(1)} %get-tuple-element.10), channel_id=1, source_target_pairs={{0,32},{16,48},{32,0},{48,16},{1,33},{17,49},{33,1},{49,17},{2,34}... | collective-permute-start | bytes 786440 | tf_op jit(solution)/shard_map/input_grad/ppermute | solution.py:136
  82.8 2.1 %collective-permute-start.8 = (bf16[2,128,512]{2,1,0:T(8,128)(2,1)S(1)}, bf16[2,128,512]{2,1,0:T(8,128)(2,1)S(1)}, u32[]{:S(2)}, u32[]{:S(2)}) collective-permute-start(bf16[2,128,512]{2,1,0:T(8,128)(2,1)S(1)} %get-tuple-element.7), channel_id=1, source_target_pairs={{0,48},{16,0},{32,16},{48,32},{1,49},{17,1},{33,17},{49,33},{2,50}... | collective-permute-start | bytes 786440 | tf_op jit(solution)/shard_map/input_grad/ppermute | solution.py:136
  85.0 0.7 broadcast_in_dim.27
  85.7 7.6 %all-to-all-start.3 = ((bf16[8,16,512]{2,1,0:T(8,128)(2,1)}), bf16[8,16,512]{2,1,0:T(8,128)(2,1)S(1)}, u32[]{:S(2)}, u32[]{:S(2)}) async-start(bf16[8,16,512]{2,1,0:T(8,128)(2,1)} %broadcast_in_dim.27), calls=%async_computation.3 | async-start | bytes 262144 | tf_op jit(solution)/shard_map/share_rows/all_to_all | solution.py:128
  93.2 0.1 pad_add_fusion.at_ref
  93.3 1.1 %collective-permute-done.8.refs_3_ = bf16[2,128,512]{2,1,0:T(8,128)(2,1)S(1)} collective-permute-done((bf16[2,128,512]{2,1,0:T(8,128)(2,1)S(1)}, bf16[2,128,512]{2,1,0:T(8,128)(2,1)S(1)}, u32[]{:S(2)}, u32[]{:S(2)}) %collective-permute-start.8) | collective-permute-done | bytes 262176 | tf_op jit(solution)/shard_map/input_grad/ppermute | solution.py:136
  94.4 1.7 %from_pieces.1 = bf16[128,4096]{1,0:T(8,128)(2,1)} custom-call(s32[3]{0:T(128)S(1)} %pad_add_fusion.at_ref, bf16[2,128,512]{2,1,0:T(8,128)(2,1)S(1)} %get-tuple-element.8.refs_0_, bf16[2,128,512]{2,1,0:T(8,128)(2,1)S(1)} %collective-permute-done.6.refs_1_, bf16[2,128,512]{2,1,0:T(8,128)(2,1)S(1)} %collective-permute-done.7.refs_2_, ...), custom_call_target="tpu_custom_call" | custom-call | bytes 2097152 | tf_op jit(solution)/shard_map/input_grad/from_pieces/pallas_call | solution.py:114
  96.1 2.3 %all-to-all-done.3 = bf16[8,16,512]{2,1,0:T(8,128)(2,1)S(1)} async-done(((bf16[8,16,512]{2,1,0:T(8,128)(2,1)}), bf16[8,16,512]{2,1,0:T(8,128)(2,1)S(1)}, u32[]{:S(2)}, u32[]{:S(2)}) %all-to-all-start.3) | async-done | bytes 131104 | tf_op jit(solution)/shard_map/share_rows/all_to_all | solution.py:128
  98.4 0.7 bitcast_convert_fusion
  (14 shorter events, 0.1 us)
Async XLA Ops:
  4.1 10.5 %copy-start = (bf16[128,512]{1,0:T(8,128)(2,1)S(1)}, bf16[128,512]{1,0:T(8,128)(2,1)}, u32[]{:S(2)}) copy-start(bf16[128,512]{1,0:T(8,128)(2,1)} %param.13) | copy-start | bytes 393220
  4.1 42.5 %all-to-all-start = ((bf16[8,128,512]{2,1,0:T(8,128)(2,1)}), bf16[8,128,512]{2,1,0:T(8,128)(2,1)S(1)}, u32[]{:S(2)}, u32[]{:S(2)}) async-start(bf16[8,128,512]{2,1,0:T(8,128)(2,1)} %to_pieces.1._), calls=%async_computation | async-start | bytes 2097152 | tf_op jit(solution)/shard_map/send_inputs/all_to_all | solution.py:128
  14.6 28.0 %collective-permute-start = (bf16[128,512]{1,0:T(8,128)(2,1)S(1)}, bf16[128,512]{1,0:T(8,128)(2,1)S(1)}, u32[]{:S(2)}, u32[]{:S(2)}) collective-permute-start(bf16[128,512]{1,0:T(8,128)(2,1)S(1)} %copy-done), channel_id=1, source_target_pairs={{0,64},{1,323},{64,128},{65,387},{128,192},{129,451},{192,256},{19... | collective-permute-start | bytes 393224 | tf_op jit(solution)/shard_map/gather_value_grad/ppermute | solution.py:145
  22.1 20.6 %collective-permute-start.1 = (bf16[128,512]{1,0:T(8,128)(2,1)S(1)}, bf16[128,512]{1,0:T(8,128)(2,1)S(1)}, u32[]{:S(2)}, u32[]{:S(2)}) collective-permute-start(bf16[128,512]{1,0:T(8,128)(2,1)S(1)} %copy-done), channel_id=1, source_target_pairs={{0,128},{1,387},{64,192},{65,451},{128,256},{129,1},{192,320},{193... | collective-permute-start | bytes 393224 | tf_op jit(solution)/shard_map/gather_value_grad/ppermute | solution.py:145
  42.7 3.8 %collective-permute-start.2 = (bf16[4,128,512]{2,1,0:T(8,128)(2,1)S(1)}, bf16[4,128,512]{2,1,0:T(8,128)(2,1)S(1)}, u32[]{:S(2)}, u32[]{:S(2)}) collective-permute-start(bf16[4,128,512]{2,1,0:T(8,128)(2,1)S(1)} %hold.1.own_ref), channel_id=1, source_target_pairs={{0,1},{1,0},{2,3},{3,2},{4,5},{5,4},{6,7},{7,6},{8,9},{9,8},{10,11... | collective-permute-start | bytes 1572872 | tf_op jit(solution)/shard_map/gather_value_grad/ppermute | solution.py:136
  48.2 13.3 %all-to-all-start.1 = ((bf16[4,128,512]{2,1,0:T(8,128)(2,1)}), bf16[4,128,512]{2,1,0:T(8,128)(2,1)S(1)}, u32[]{:S(2)}, u32[]{:S(2)}) async-start(bf16[4,128,512]{2,1,0:T(8,128)(2,1)} %bitcast.53), calls=%async_computation.1 | async-start | bytes 1048576 | tf_op jit(solution)/shard_map/sum_y/all_to_all | solution.py:128
  52.3 17.3 %collective-permute-start.3 = (bf16[128,512]{1,0:T(8,128)(2,1)S(1)}, bf16[128,512]{1,0:T(8,128)(2,1)S(1)}, u32[]{:S(2)}, u32[]{:S(2)}) collective-permute-start(bf16[128,512]{1,0:T(8,128)(2,1)S(1)} %copy-done), channel_id=1, source_target_pairs={{0,0},{1,257},{64,64},{65,321},{128,128},{129,385},{192,192},{193,... | collective-permute-start | bytes 393224 | tf_op jit(solution)/shard_map/gather_weight/ppermute | solution.py:145
  56.6 13.1 %collective-permute-start.4 = (bf16[128,512]{1,0:T(8,128)(2,1)S(1)}, bf16[128,512]{1,0:T(8,128)(2,1)S(1)}, u32[]{:S(2)}, u32[]{:S(2)}) collective-permute-start(bf16[128,512]{1,0:T(8,128)(2,1)S(1)} %copy-done), channel_id=1, source_target_pairs={{0,192},{1,451},{64,256},{65,1},{128,320},{129,65},{192,384},{193,... | collective-permute-start | bytes 393224 | tf_op jit(solution)/shard_map/gather_weight/ppermute | solution.py:145
  62.3 22.6 %all-to-all-start.2 = ((bf16[16,16,512]{2,1,0:T(8,128)(2,1)}), bf16[16,16,512]{2,1,0:T(8,128)(2,1)S(1)}, u32[]{:S(2)}, u32[]{:S(2)}) async-start(bf16[16,16,512]{2,1,0:T(8,128)(2,1)} %bitcast.26), calls=%async_computation.2 | async-start | bytes 524288 | tf_op jit(solution)/shard_map/sum_z/all_to_all | solution.py:128
  70.6 5.2 %collective-permute-start.5 = (bf16[4,128,512]{2,1,0:T(8,128)(2,1)S(1)}, bf16[4,128,512]{2,1,0:T(8,128)(2,1)S(1)}, u32[]{:S(2)}, u32[]{:S(2)}) collective-permute-start(bf16[4,128,512]{2,1,0:T(8,128)(2,1)S(1)} %get-tuple-element.11), channel_id=1, source_target_pairs={{0,1},{1,0},{2,3},{3,2},{4,5},{5,4},{6,7},{7,6},{8,9},{9,8},{10,11... | collective-permute-start | bytes 1572872 | tf_op jit(solution)/shard_map/input_grad/ppermute | solution.py:136
  75.9 17.4 %collective-permute-start.6 = (bf16[2,128,512]{2,1,0:T(8,128)(2,1)S(1)}, bf16[2,128,512]{2,1,0:T(8,128)(2,1)S(1)}, u32[]{:S(2)}, u32[]{:S(2)}) collective-permute-start(bf16[2,128,512]{2,1,0:T(8,128)(2,1)S(1)} %get-tuple-element.9), channel_id=1, source_target_pairs={{0,16},{16,32},{32,48},{48,0},{1,17},{17,33},{33,49},{49,1},{2,18}... | collective-permute-start | bytes 786440 | tf_op jit(solution)/shard_map/input_grad/ppermute | solution.py:136
  78.5 14.8 %collective-permute-start.7 = (bf16[2,128,512]{2,1,0:T(8,128)(2,1)S(1)}, bf16[2,128,512]{2,1,0:T(8,128)(2,1)S(1)}, u32[]{:S(2)}, u32[]{:S(2)}) collective-permute-start(bf16[2,128,512]{2,1,0:T(8,128)(2,1)S(1)} %get-tuple-element.10), channel_id=1, source_target_pairs={{0,32},{16,48},{32,0},{48,16},{1,33},{17,49},{33,1},{49,17},{2,34}... | collective-permute-start | bytes 786440 | tf_op jit(solution)/shard_map/input_grad/ppermute | solution.py:136
  82.8 11.5 %collective-permute-start.8 = (bf16[2,128,512]{2,1,0:T(8,128)(2,1)S(1)}, bf16[2,128,512]{2,1,0:T(8,128)(2,1)S(1)}, u32[]{:S(2)}, u32[]{:S(2)}) collective-permute-start(bf16[2,128,512]{2,1,0:T(8,128)(2,1)S(1)} %get-tuple-element.7), channel_id=1, source_target_pairs={{0,48},{16,0},{32,16},{48,32},{1,49},{17,1},{33,17},{49,33},{2,50}... | collective-permute-start | bytes 786440 | tf_op jit(solution)/shard_map/input_grad/ppermute | solution.py:136
  85.7 12.7 %all-to-all-start.3 = ((bf16[8,16,512]{2,1,0:T(8,128)(2,1)}), bf16[8,16,512]{2,1,0:T(8,128)(2,1)S(1)}, u32[]{:S(2)}, u32[]{:S(2)}) async-start(bf16[8,16,512]{2,1,0:T(8,128)(2,1)} %broadcast_in_dim.27), calls=%async_computation.3 | async-start | bytes 262144 | tf_op jit(solution)/shard_map/share_rows/all_to_all | solution.py:128

commit v11 on v10

--- a/solution.py
+++ b/solution.py
@@ -204,7 +204,8 @@
     with jax.named_scope("attention"):
         value_grad, key_grad = attend_back(queries[0], keys[0], values[0], out_grad[0], lengths, pieces)
     with jax.named_scope("gather_value_grad"):
-        near = [along_z(value_weight, steps) for steps in ((1, -3), (2, -2))]
+        block = hold(value_weight, [value_grad])
+        near = [along_z(block, steps) for steps in ((1, -3), (2, -2))]
         mine = hold(lax.all_gather(value_grad, "x", axis=0), near)
         other = shifted(mine, "core", CN, 1)
         grads = pair(mine, other, core).reshape(CN * XN * TOK, KV)

time: 99.8 us -> 101 us (1.012)
  no operation moved by 1% of the time
where the time goes in v11:
time: 101 us; the launch traced here: 99.8 us
  starting transfers between devices  63 us (62%)
  blocking collectives  11.2 us (11%)
  Pallas kernels  9.67 us (10%)
  waiting for transfers between devices  8.7 us (9%)
  local copies, waits for them, and re-layouts  2.41 us (2%)
  matrix products  2.29 us (2%)
  between operations  1.53 us (2%)
  other arithmetic  1.03 us (1%)
    all_to_all x4, starting transfers between devices, exchange(): return lax.all_to_all(array, axes, 0, 0, tiled=True)  29.5 us
    ppermute x4, starting transfers between devices, along_z(): return lax.ppermute(array, ('zl', 'zh', 'core'), pairs)  18.9 us
    ppermute x5, starting transfers between devices, shifted(): lax.ppermute(array, axes, [(i, (i + by) % count) for i in range(count)])  14.6 us
    all_gather x1, blocking collectives, per_device(): mine = hold(lax.all_gather(value_grad, 'x', axis=0), near)  11.2 us
    ppermute x5, waiting for transfers between devices, shifted(): lax.ppermute(array, axes, [(i, (i + by) % count) for i in range(count)])  4.39 us
    all_to_all x4, waiting for transfers between devices, exchange(): return lax.all_to_all(array, axes, 0, 0, tiled=True)  4.3 us
    pallas_call x1, Pallas kernels, attend_back(): pl.pallas_call(attend_kernel, grid=(KV // HD // KV_STEP,), in_specs=[pl.B...  4.29 us
    pallas_call x1, Pallas kernels, to_pieces(): pl.pallas_call(to_pieces_kernel, grid=(TOK // part,), in_specs=[pl.BlockS...  3.49 us
  transfers between devices with their start and end apart: 13, of which 5 were waited for; matrix products, arithmetic and copies ran while one was open for 3% of the time, Pallas kernels for 6%

profile of v11, /device:TPU:1, one launch (start us, length us, event | category | flops | bytes accessed | tf_op | source)
XLA Modules:
  0.0 99.8 jit_solution(8863995983657061544)
XLA Ops:
  0.6 3.5 %to_pieces.1._ = bf16[8,128,512]{2,1,0:T(8,128)(2,1)} custom-call(bf16[128,4096]{1,0:T(8,128)(2,1)} %bitcast.47), custom_call_target="tpu_custom_call" | custom-call | flops 4194304 | bytes 2097152 | tf_op jit(solution)/shard_map/cut_inputs/to_pieces/pallas_call | solution.py:100
  4.1 10.4 %all-to-all-start = ((bf16[8,128,512]{2,1,0:T(8,128)(2,1)}), bf16[8,128,512]{2,1,0:T(8,128)(2,1)S(1)}, u32[]{:S(2)}, u32[]{:S(2)}) async-start(bf16[8,128,512]{2,1,0:T(8,128)(2,1)} %to_pieces.1._), calls=%async_computation | async-start | bytes 2097152 | tf_op jit(solution)/shard_map/send_inputs/all_to_all | solution.py:128
  15.1 4.3 %attend.1 = (bf16[128,512]{1,0:T(8,128)(2,1)}, bf16[128,512]{1,0:T(8,128)(2,1)}) custom-call(s32[1]{0:T(128)S(6)} %copy.10.length_ref, bf16[128,4096]{1,0:T(8,128)(2,1)} %bitcast.48, bf16[128,512]{1,0:T(8,128)(2,1)} %bitcast.54, bf16[128,512]{1,0:T(8,128)(2,1)} %bitcast.55, bf16[128,4096]{1,0:T(8,128)(2,1)} %bitcast.49, bf16[8,128,512]{2,1,0:T(8,128)(2,1)} %to_pieces.1._), custom_call_target="tpu_custom_call" | custom-call | flops 671088640 | bytes 3145728 | tf_op jit(solution)/shard_map/attention/attend/pallas_call | solution.py:51
  19.4 0.9 copy-done
  20.4 7.5 %collective-permute-start = (bf16[128,512]{1,0:T(8,128)(2,1)S(1)}, bf16[128,512]{1,0:T(8,128)(2,1)S(1)}, u32[]{:S(2)}, u32[]{:S(2)}) collective-permute-start(bf16[128,512]{1,0:T(8,128)(2,1)S(1)} %hold.2), channel_id=1, source_target_pairs={{0,64},{1,323},{64,128},{65,387},{128,192},{129,451},{192,256},{19... | collective-permute-start | bytes 393224 | tf_op jit(solution)/shard_map/gather_value_grad/ppermute | solution.py:145
  27.8 4.3 %collective-permute-start.1 = (bf16[128,512]{1,0:T(8,128)(2,1)S(1)}, bf16[128,512]{1,0:T(8,128)(2,1)S(1)}, u32[]{:S(2)}, u32[]{:S(2)}) collective-permute-start(bf16[128,512]{1,0:T(8,128)(2,1)S(1)} %hold.2), channel_id=1, source_target_pairs={{0,128},{1,387},{64,192},{65,451},{128,256},{129,1},{192,320},{193... | collective-permute-start | bytes 393224 | tf_op jit(solution)/shard_map/gather_value_grad/ppermute | solution.py:145
  32.1 11.2 %all-gather = bf16[512,512]{1,0:T(8,128)(2,1)S(1)} all-gather(bf16[128,512]{1,0:T(8,128)(2,1)S(1)} %copy-done), channel_id=2, replica_groups=mesh['zl'=8,'x'=4,'y'=4,'zh'=2,'core'=2] {'x'}, dimensions={0}, use_global_device_ids=true | all-gather | bytes 655360 | tf_op jit(solution)/shard_map/gather_value_grad/all_gather | solution.py:209
  43.4 1.9 %collective-permute-start.2 = (bf16[4,128,512]{2,1,0:T(8,128)(2,1)S(1)}, bf16[4,128,512]{2,1,0:T(8,128)(2,1)S(1)}, u32[]{:S(2)}, u32[]{:S(2)}) collective-permute-start(bf16[4,128,512]{2,1,0:T(8,128)(2,1)S(1)} %hold.3.own_ref), channel_id=1, source_target_pairs={{0,1},{1,0},{2,3},{3,2},{4,5},{5,4},{6,7},{7,6},{8,9},{9,8},{10,11... | collective-permute-start | bytes 1572872 | tf_op jit(solution)/shard_map/gather_value_grad/ppermute | solution.py:136
  45.3 1.9 %collective-permute-done.2.other_ref = bf16[4,128,512]{2,1,0:T(8,128)(2,1)S(1)} collective-permute-done((bf16[4,128,512]{2,1,0:T(8,128)(2,1)S(1)}, bf16[4,128,512]{2,1,0:T(8,128)(2,1)S(1)}, u32[]{:S(2)}, u32[]{:S(2)}) %collective-permute-start.2) | collective-permute-done | bytes 524320 | tf_op jit(solution)/shard_map/gather_value_grad/ppermute | solution.py:136
  47.2 1.6 %convolution_convert_fusion.1 = bf16[512,512]{0,1:T(8,128)(2,1)} fusion(bf16[1024,512]{1,0:T(8,128)(2,1)S(1)} %bitcast.44, bf16[1024,512]{1,0:T(8,128)(2,1)S(1)} %bitcast.50), kind=kOutput, calls=%fused_computation.9 | convolution fusion | flops 537133056 | bytes 2621440 | tf_op jit(solution)/shard_map/weight_term/dot_general | solution.py:215
  48.8 4.2 %all-to-all-start.1 = ((bf16[4,128,512]{2,1,0:T(8,128)(2,1)}), bf16[4,128,512]{2,1,0:T(8,128)(2,1)S(1)}, u32[]{:S(2)}, u32[]{:S(2)}) async-start(bf16[4,128,512]{2,1,0:T(8,128)(2,1)} %bitcast.53), calls=%async_computation.1 | async-start | bytes 1048576 | tf_op jit(solution)/shard_map/sum_y/all_to_all | solution.py:128
  53.0 4.2 %collective-permute-start.3 = (bf16[128,512]{1,0:T(8,128)(2,1)S(1)}, bf16[128,512]{1,0:T(8,128)(2,1)S(1)}, u32[]{:S(2)}, u32[]{:S(2)}) collective-permute-start(bf16[128,512]{1,0:T(8,128)(2,1)S(1)} %copy-done.1), channel_id=1, source_target_pairs={{0,0},{1,257},{64,64},{65,321},{128,128},{129,385},{192,192},{193,... | collective-permute-start | bytes 393224 | tf_op jit(solution)/shard_map/gather_weight/ppermute | solution.py:145
  57.2 2.9 %collective-permute-start.4 = (bf16[128,512]{1,0:T(8,128)(2,1)S(1)}, bf16[128,512]{1,0:T(8,128)(2,1)S(1)}, u32[]{:S(2)}, u32[]{:S(2)}) collective-permute-start(bf16[128,512]{1,0:T(8,128)(2,1)S(1)} %copy-done.1), channel_id=1, source_target_pairs={{0,192},{1,451},{64,256},{65,1},{128,320},{129,65},{192,384},{193,... | collective-permute-start | bytes 393224 | tf_op jit(solution)/shard_map/gather_weight/ppermute | solution.py:145
  60.1 2.0 %all-to-all-done.1 = bf16[4,128,512]{2,1,0:T(8,128)(2,1)S(1)} async-done(((bf16[4,128,512]{2,1,0:T(8,128)(2,1)}), bf16[4,128,512]{2,1,0:T(8,128)(2,1)S(1)}, u32[]{:S(2)}, u32[]{:S(2)}) %all-to-all-start.1) | async-done | bytes 524320 | tf_op jit(solution)/shard_map/sum_y/all_to_all | solution.py:128
  62.1 0.1 reduce_sum.21
  62.2 0.7 broadcast_in_dim.26
  63.0 7.4 %all-to-all-start.2 = ((bf16[16,16,512]{2,1,0:T(8,128)(2,1)}), bf16[16,16,512]{2,1,0:T(8,128)(2,1)S(1)}, u32[]{:S(2)}, u32[]{:S(2)}) async-start(bf16[16,16,512]{2,1,0:T(8,128)(2,1)} %bitcast.26), calls=%async_computation.2 | async-start | bytes 524288 | tf_op jit(solution)/shard_map/sum_z/all_to_all | solution.py:128
  70.4 0.7 convolution_convert_fusion
  71.2 0.1 dynamic-slice_bitcast_fusion
  71.3 3.7 %collective-permute-start.5 = (bf16[4,128,512]{2,1,0:T(8,128)(2,1)S(1)}, bf16[4,128,512]{2,1,0:T(8,128)(2,1)S(1)}, u32[]{:S(2)}, u32[]{:S(2)}) collective-permute-start(bf16[4,128,512]{2,1,0:T(8,128)(2,1)S(1)} %get-tuple-element.11), channel_id=1, source_target_pairs={{0,1},{1,0},{2,3},{3,2},{4,5},{5,4},{6,7},{7,6},{8,9},{9,8},{10,11... | collective-permute-start | bytes 1572872 | tf_op jit(solution)/shard_map/input_grad/ppermute | solution.py:136
  75.0 1.5 %collective-permute-done.5 = bf16[4,128,512]{2,1,0:T(8,128)(2,1)S(1)} collective-permute-done((bf16[4,128,512]{2,1,0:T(8,128)(2,1)S(1)}, bf16[4,128,512]{2,1,0:T(8,128)(2,1)S(1)}, u32[]{:S(2)}, u32[]{:S(2)}) %collective-permute-start.5) | collective-permute-done | bytes 524320 | tf_op jit(solution)/shard_map/input_grad/ppermute | solution.py:136
  76.5 0.1 fusion.1
  76.6 2.2 %collective-permute-start.6 = (bf16[2,128,512]{2,1,0:T(8,128)(2,1)S(1)}, bf16[2,128,512]{2,1,0:T(8,128)(2,1)S(1)}, u32[]{:S(2)}, u32[]{:S(2)}) collective-permute-start(bf16[2,128,512]{2,1,0:T(8,128)(2,1)S(1)} %get-tuple-element.9), channel_id=1, source_target_pairs={{0,16},{16,32},{32,48},{48,0},{1,17},{17,33},{33,49},{49,1},{2,18}... | collective-permute-start | bytes 786440 | tf_op jit(solution)/shard_map/input_grad/ppermute | solution.py:136
  78.8 4.3 %collective-permute-start.7 = (bf16[2,128,512]{2,1,0:T(8,128)(2,1)S(1)}, bf16[2,128,512]{2,1,0:T(8,128)(2,1)S(1)}, u32[]{:S(2)}, u32[]{:S(2)}) collective-permute-start(bf16[2,128,512]{2,1,0:T(8,128)(2,1)S(1)} %get-tuple-element.10), channel_id=1, source_target_pairs={{0,32},{16,48},{32,0},{48,16},{1,33},{17,49},{33,1},{49,17},{2,34}... | collective-permute-start | bytes 786440 | tf_op jit(solution)/shard_map/input_grad/ppermute | solution.py:136
  83.1 2.5 %collective-permute-start.8 = (bf16[2,128,512]{2,1,0:T(8,128)(2,1)S(1)}, bf16[2,128,512]{2,1,0:T(8,128)(2,1)S(1)}, u32[]{:S(2)}, u32[]{:S(2)}) collective-permute-start(bf16[2,128,512]{2,1,0:T(8,128)(2,1)S(1)} %get-tuple-element.7), channel_id=1, source_target_pairs={{0,48},{16,0},{32,16},{48,32},{1,49},{17,1},{33,17},{49,33},{2,50}... | collective-permute-start | bytes 786440 | tf_op jit(solution)/shard_map/input_grad/ppermute | solution.py:136
  85.7 0.7 broadcast_in_dim.27
  86.3 7.6 %all-to-all-start.3 = ((bf16[8,16,512]{2,1,0:T(8,128)(2,1)}), bf16[8,16,512]{2,1,0:T(8,128)(2,1)S(1)}, u32[]{:S(2)}, u32[]{:S(2)}) async-start(bf16[8,16,512]{2,1,0:T(8,128)(2,1)} %broadcast_in_dim.27), calls=%async_computation.3 | async-start | bytes 262144 | tf_op jit(solution)/shard_map/share_rows/all_to_all | solution.py:128
  93.9 0.1 pad_add_fusion.at_ref
  94.0 1.1 %collective-permute-done.8.refs_3_ = bf16[2,128,512]{2,1,0:T(8,128)(2,1)S(1)} collective-permute-done((bf16[2,128,512]{2,1,0:T(8,128)(2,1)S(1)}, bf16[2,128,512]{2,1,0:T(8,128)(2,1)S(1)}, u32[]{:S(2)}, u32[]{:S(2)}) %collective-permute-start.8) | collective-permute-done | bytes 262176 | tf_op jit(solution)/shard_map/input_grad/ppermute | solution.py:136
  95.1 1.7 %from_pieces.1 = bf16[128,4096]{1,0:T(8,128)(2,1)} custom-call(s32[3]{0:T(128)S(1)} %pad_add_fusion.at_ref, bf16[2,128,512]{2,1,0:T(8,128)(2,1)S(1)} %get-tuple-element.8.refs_0_, bf16[2,128,512]{2,1,0:T(8,128)(2,1)S(1)} %collective-permute-done.6.refs_1_, bf16[2,128,512]{2,1,0:T(8,128)(2,1)S(1)} %collective-permute-done.7.refs_2_, ...), custom_call_target="tpu_custom_call" | custom-call | bytes 2097152 | tf_op jit(solution)/shard_map/input_grad/from_pieces/pallas_call | solution.py:114
  96.8 2.3 %all-to-all-done.3 = bf16[8,16,512]{2,1,0:T(8,128)(2,1)S(1)} async-done(((bf16[8,16,512]{2,1,0:T(8,128)(2,1)}), bf16[8,16,512]{2,1,0:T(8,128)(2,1)S(1)}, u32[]{:S(2)}, u32[]{:S(2)}) %all-to-all-start.3) | async-done | bytes 131104 | tf_op jit(solution)/shard_map/share_rows/all_to_all | solution.py:128
  99.1 0.7 bitcast_convert_fusion
  (17 shorter events, 0.2 us)
Async XLA Ops:
  4.1 43.1 %all-to-all-start = ((bf16[8,128,512]{2,1,0:T(8,128)(2,1)}), bf16[8,128,512]{2,1,0:T(8,128)(2,1)S(1)}, u32[]{:S(2)}, u32[]{:S(2)}) async-start(bf16[8,128,512]{2,1,0:T(8,128)(2,1)} %to_pieces.1._), calls=%async_computation | async-start | bytes 2097152 | tf_op jit(solution)/shard_map/send_inputs/all_to_all | solution.py:128
  15.1 4.3 %copy-start.1 = (bf16[128,512]{1,0:T(8,128)(2,1)S(1)}, bf16[128,512]{1,0:T(8,128)(2,1)}, u32[]{:S(2)}) copy-start(bf16[128,512]{1,0:T(8,128)(2,1)} %in_ref.1) | copy-start | bytes 393220
  19.4 0.9 copy-start
  20.4 23.0 %collective-permute-start = (bf16[128,512]{1,0:T(8,128)(2,1)S(1)}, bf16[128,512]{1,0:T(8,128)(2,1)S(1)}, u32[]{:S(2)}, u32[]{:S(2)}) collective-permute-start(bf16[128,512]{1,0:T(8,128)(2,1)S(1)} %hold.2), channel_id=1, source_target_pairs={{0,64},{1,323},{64,128},{65,387},{128,192},{129,451},{192,256},{19... | collective-permute-start | bytes 393224 | tf_op jit(solution)/shard_map/gather_value_grad/ppermute | solution.py:145
  27.8 15.5 %collective-permute-start.1 = (bf16[128,512]{1,0:T(8,128)(2,1)S(1)}, bf16[128,512]{1,0:T(8,128)(2,1)S(1)}, u32[]{:S(2)}, u32[]{:S(2)}) collective-permute-start(bf16[128,512]{1,0:T(8,128)(2,1)S(1)} %hold.2), channel_id=1, source_target_pairs={{0,128},{1,387},{64,192},{65,451},{128,256},{129,1},{192,320},{193... | collective-permute-start | bytes 393224 | tf_op jit(solution)/shard_map/gather_value_grad/ppermute | solution.py:145
  43.4 3.8 %collective-permute-start.2 = (bf16[4,128,512]{2,1,0:T(8,128)(2,1)S(1)}, bf16[4,128,512]{2,1,0:T(8,128)(2,1)S(1)}, u32[]{:S(2)}, u32[]{:S(2)}) collective-permute-start(bf16[4,128,512]{2,1,0:T(8,128)(2,1)S(1)} %hold.3.own_ref), channel_id=1, source_target_pairs={{0,1},{1,0},{2,3},{3,2},{4,5},{5,4},{6,7},{7,6},{8,9},{9,8},{10,11... | collective-permute-start | bytes 1572872 | tf_op jit(solution)/shard_map/gather_value_grad/ppermute | solution.py:136
  48.8 13.3 %all-to-all-start.1 = ((bf16[4,128,512]{2,1,0:T(8,128)(2,1)}), bf16[4,128,512]{2,1,0:T(8,128)(2,1)S(1)}, u32[]{:S(2)}, u32[]{:S(2)}) async-start(bf16[4,128,512]{2,1,0:T(8,128)(2,1)} %bitcast.53), calls=%async_computation.1 | async-start | bytes 1048576 | tf_op jit(solution)/shard_map/sum_y/all_to_all | solution.py:128
  53.0 17.4 %collective-permute-start.3 = (bf16[128,512]{1,0:T(8,128)(2,1)S(1)}, bf16[128,512]{1,0:T(8,128)(2,1)S(1)}, u32[]{:S(2)}, u32[]{:S(2)}) collective-permute-start(bf16[128,512]{1,0:T(8,128)(2,1)S(1)} %copy-done.1), channel_id=1, source_target_pairs={{0,0},{1,257},{64,64},{65,321},{128,128},{129,385},{192,192},{193,... | collective-permute-start | bytes 393224 | tf_op jit(solution)/shard_map/gather_weight/ppermute | solution.py:145
  57.2 13.1 %collective-permute-start.4 = (bf16[128,512]{1,0:T(8,128)(2,1)S(1)}, bf16[128,512]{1,0:T(8,128)(2,1)S(1)}, u32[]{:S(2)}, u32[]{:S(2)}) collective-permute-start(bf16[128,512]{1,0:T(8,128)(2,1)S(1)} %copy-done.1), channel_id=1, source_target_pairs={{0,192},{1,451},{64,256},{65,1},{128,320},{129,65},{192,384},{193,... | collective-permute-start | bytes 393224 | tf_op jit(solution)/shard_map/gather_weight/ppermute | solution.py:145
  63.0 22.6 %all-to-all-start.2 = ((bf16[16,16,512]{2,1,0:T(8,128)(2,1)}), bf16[16,16,512]{2,1,0:T(8,128)(2,1)S(1)}, u32[]{:S(2)}, u32[]{:S(2)}) async-start(bf16[16,16,512]{2,1,0:T(8,128)(2,1)} %bitcast.26), calls=%async_computation.2 | async-start | bytes 524288 | tf_op jit(solution)/shard_map/sum_z/all_to_all | solution.py:128
  71.3 5.2 %collective-permute-start.5 = (bf16[4,128,512]{2,1,0:T(8,128)(2,1)S(1)}, bf16[4,128,512]{2,1,0:T(8,128)(2,1)S(1)}, u32[]{:S(2)}, u32[]{:S(2)}) collective-permute-start(bf16[4,128,512]{2,1,0:T(8,128)(2,1)S(1)} %get-tuple-element.11), channel_id=1, source_target_pairs={{0,1},{1,0},{2,3},{3,2},{4,5},{5,4},{6,7},{7,6},{8,9},{9,8},{10,11... | collective-permute-start | bytes 1572872 | tf_op jit(solution)/shard_map/input_grad/ppermute | solution.py:136
  76.6 17.4 %collective-permute-start.6 = (bf16[2,128,512]{2,1,0:T(8,128)(2,1)S(1)}, bf16[2,128,512]{2,1,0:T(8,128)(2,1)S(1)}, u32[]{:S(2)}, u32[]{:S(2)}) collective-permute-start(bf16[2,128,512]{2,1,0:T(8,128)(2,1)S(1)} %get-tuple-element.9), channel_id=1, source_target_pairs={{0,16},{16,32},{32,48},{48,0},{1,17},{17,33},{33,49},{49,1},{2,18}... | collective-permute-start | bytes 786440 | tf_op jit(solution)/shard_map/input_grad/ppermute | solution.py:136
  78.8 15.2 %collective-permute-start.7 = (bf16[2,128,512]{2,1,0:T(8,128)(2,1)S(1)}, bf16[2,128,512]{2,1,0:T(8,128)(2,1)S(1)}, u32[]{:S(2)}, u32[]{:S(2)}) collective-permute-start(bf16[2,128,512]{2,1,0:T(8,128)(2,1)S(1)} %get-tuple-element.10), channel_id=1, source_target_pairs={{0,32},{16,48},{32,0},{48,16},{1,33},{17,49},{33,1},{49,17},{2,34}... | collective-permute-start | bytes 786440 | tf_op jit(solution)/shard_map/input_grad/ppermute | solution.py:136
  83.1 12.0 %collective-permute-start.8 = (bf16[2,128,512]{2,1,0:T(8,128)(2,1)S(1)}, bf16[2,128,512]{2,1,0:T(8,128)(2,1)S(1)}, u32[]{:S(2)}, u32[]{:S(2)}) collective-permute-start(bf16[2,128,512]{2,1,0:T(8,128)(2,1)S(1)} %get-tuple-element.7), channel_id=1, source_target_pairs={{0,48},{16,0},{32,16},{48,32},{1,49},{17,1},{33,17},{49,33},{2,50}... | collective-permute-start | bytes 786440 | tf_op jit(solution)/shard_map/input_grad/ppermute | solution.py:136
  86.3 12.7 %all-to-all-start.3 = ((bf16[8,16,512]{2,1,0:T(8,128)(2,1)}), bf16[8,16,512]{2,1,0:T(8,128)(2,1)S(1)}, u32[]{:S(2)}, u32[]{:S(2)}) async-start(bf16[8,16,512]{2,1,0:T(8,128)(2,1)} %broadcast_in_dim.27), calls=%async_computation.3 | async-start | bytes 262144 | tf_op jit(solution)/shard_map/share_rows/all_to_all | solution.py:128

commit v12 on v10

--- a/solution.py
+++ b/solution.py
@@ -204,8 +204,8 @@
     with jax.named_scope("attention"):
         value_grad, key_grad = attend_back(queries[0], keys[0], values[0], out_grad[0], lengths, pieces)
     with jax.named_scope("gather_value_grad"):
-        near = [along_z(value_weight, steps) for steps in ((1, -3), (2, -2))]
-        mine = hold(lax.all_gather(value_grad, "x", axis=0), near)
+        early = along_z(value_weight, (2, -2))
+        mine = hold(lax.all_gather(value_grad, "x", axis=0), [early])
         other = shifted(mine, "core", CN, 1)
         grads = pair(mine, other, core).reshape(CN * XN * TOK, KV)
     with jax.named_scope("send_inputs"):
@@ -224,8 +224,8 @@
     with jax.named_scope("share_rows"):
         weight_grad = spread(total.astype(BF), ("core", "y"), QN).reshape(QN * SUB, KV).astype(F32)
     with jax.named_scope("gather_weight"):
-        first, last = (along_z(value_weight, steps) for steps in ((0, 4), (3, -1)))
-        weight = join([first] + near + [last], plane)
+        first, second, last = (along_z(value_weight, steps) for steps in ((0, 4), (1, -3), (3, -1)))
+        weight = join([first, second, early, last], plane)
     with jax.named_scope("input_grad"):
         parts = nt(grads, weight).astype(BF).reshape(CN, XN, TOK, KV)
         kept = lax.dynamic_index_in_dim(parts, core, 0, False)

time: 99.8 us -> 98.8 us (0.990)
  starting transfers between devices: 63.1 us -> 60.4 us
  waiting for transfers between devices: 8.68 us -> 10.4 us
    all_to_all x4, starting transfers between devices: 29.6 us -> 27.6 us  [exchange(): return lax.all_to_all(array, axes, 0, 0, tiled=True)]
    ppermute x5, starting transfers between devices: 14.6 us -> 13.2 us  [shifted(): lax.ppermute(array, axes, [(i, (i + by) % count) for i in range(count)])]
    all_to_all x4, waiting for transfers between devices: 4.28 us -> 5.55 us  [exchange(): return lax.all_to_all(array, axes, 0, 0, tiled=True)]
where the time goes in v12:
time: 98.8 us; the launch traced here: 98.1 us
  starting transfers between devices  60.4 us (61%)
  blocking collectives  11.3 us (11%)
  waiting for transfers between devices  10.4 us (11%)
  Pallas kernels  9.63 us (10%)
  matrix products  2.29 us (2%)
  between operations  1.52 us (2%)
  local copies, waits for them, and re-layouts  1.51 us (2%)
  other arithmetic  1.03 us (1%)
    all_to_all x4, starting transfers between devices, exchange(): return lax.all_to_all(array, axes, 0, 0, tiled=True)  27.6 us
    ppermute x4, starting transfers between devices, along_z(): return lax.ppermute(array, ('zl', 'zh', 'core'), pairs)  19.5 us
    ppermute x5, starting transfers between devices, shifted(): lax.ppermute(array, axes, [(i, (i + by) % count) for i in range(count)])  13.2 us
    all_gather x1, blocking collectives, per_device(): mine = hold(lax.all_gather(value_grad, 'x', axis=0), [early])  11.3 us
    all_to_all x4, waiting for transfers between devices, exchange(): return lax.all_to_all(array, axes, 0, 0, tiled=True)  5.55 us
    ppermute x5, waiting for transfers between devices, shifted(): lax.ppermute(array, axes, [(i, (i + by) % count) for i in range(count)])  4.86 us
    pallas_call x1, Pallas kernels, attend_back(): pl.pallas_call(attend_kernel, grid=(KV // HD // KV_STEP,), in_specs=[pl.B...  4.25 us
    pallas_call x1, Pallas kernels, to_pieces(): pl.pallas_call(to_pieces_kernel, grid=(TOK // part,), in_specs=[pl.BlockS...  3.49 us
  transfers between devices with their start and end apart: 13, of which 5 were waited for; matrix products, arithmetic and copies ran while one was open for 3% of the time, Pallas kernels for 6%

profile of v12, /device:TPU:1, one launch (start us, length us, event | category | flops | bytes accessed | tf_op | source)
XLA Modules:
  0.0 98.1 jit_solution(6758921358321807645)
XLA Ops:
  0.6 3.5 %to_pieces.1._ = bf16[8,128,512]{2,1,0:T(8,128)(2,1)} custom-call(bf16[128,4096]{1,0:T(8,128)(2,1)} %bitcast.47), custom_call_target="tpu_custom_call" | custom-call | flops 4194304 | bytes 2097152 | tf_op jit(solution)/shard_map/cut_inputs/to_pieces/pallas_call | solution.py:100
  4.1 10.5 %all-to-all-start = ((bf16[8,128,512]{2,1,0:T(8,128)(2,1)}), bf16[8,128,512]{2,1,0:T(8,128)(2,1)S(1)}, u32[]{:S(2)}, u32[]{:S(2)}) async-start(bf16[8,128,512]{2,1,0:T(8,128)(2,1)} %to_pieces.1._), calls=%async_computation | async-start | bytes 2097152 | tf_op jit(solution)/shard_map/send_inputs/all_to_all | solution.py:128
  14.6 7.0 %collective-permute-start = (bf16[128,512]{1,0:T(8,128)(2,1)S(1)}, bf16[128,512]{1,0:T(8,128)(2,1)S(1)}, u32[]{:S(2)}, u32[]{:S(2)}) collective-permute-start(bf16[128,512]{1,0:T(8,128)(2,1)S(1)} %copy-done), channel_id=1, source_target_pairs={{0,128},{1,387},{64,192},{65,451},{128,256},{129,1},{192,320},{193... | collective-permute-start | bytes 393224 | tf_op jit(solution)/shard_map/gather_value_grad/ppermute | solution.py:145
  22.3 4.3 %attend.1 = (bf16[128,512]{1,0:T(8,128)(2,1)}, bf16[128,512]{1,0:T(8,128)(2,1)}) custom-call(s32[1]{0:T(128)S(6)} %copy.10.length_ref, bf16[128,4096]{1,0:T(8,128)(2,1)} %bitcast.48, bf16[128,512]{1,0:T(8,128)(2,1)} %bitcast.53, bf16[128,512]{1,0:T(8,128)(2,1)} %bitcast.54, bf16[128,4096]{1,0:T(8,128)(2,1)} %bitcast.49, bf16[8,128,512]{2,1,0:T(8,128)(2,1)} %to_pieces.1._), custom_call_target="tpu_custom_call" | custom-call | flops 671088640 | bytes 3145728 | tf_op jit(solution)/shard_map/attention/attend/pallas_call | solution.py:51
  26.5 11.3 %all-gather = bf16[512,512]{1,0:T(8,128)(2,1)S(1)} all-gather(bf16[128,512]{1,0:T(8,128)(2,1)} %get-tuple-element.5), channel_id=2, replica_groups=mesh['zl'=8,'x'=4,'y'=4,'zh'=2,'core'=2] {'x'}, dimensions={0}, use_global_device_ids=true | all-gather | bytes 655360 | tf_op jit(solution)/shard_map/gather_value_grad/all_gather | solution.py:208
  37.9 2.3 %collective-permute-start.1 = (bf16[4,128,512]{2,1,0:T(8,128)(2,1)S(1)}, bf16[4,128,512]{2,1,0:T(8,128)(2,1)S(1)}, u32[]{:S(2)}, u32[]{:S(2)}) collective-permute-start(bf16[4,128,512]{2,1,0:T(8,128)(2,1)S(1)} %hold.1.own_ref), channel_id=1, source_target_pairs={{0,1},{1,0},{2,3},{3,2},{4,5},{5,4},{6,7},{7,6},{8,9},{9,8},{10,11... | collective-permute-start | bytes 1572872 | tf_op jit(solution)/shard_map/gather_value_grad/ppermute | solution.py:136
  40.2 1.5 %collective-permute-done.1.other_ref = bf16[4,128,512]{2,1,0:T(8,128)(2,1)S(1)} collective-permute-done((bf16[4,128,512]{2,1,0:T(8,128)(2,1)S(1)}, bf16[4,128,512]{2,1,0:T(8,128)(2,1)S(1)}, u32[]{:S(2)}, u32[]{:S(2)}) %collective-permute-start.1) | collective-permute-done | bytes 524320 | tf_op jit(solution)/shard_map/gather_value_grad/ppermute | solution.py:136
  41.7 0.1 pair.1
  41.8 1.6 %convolution_convert_fusion.1 = bf16[512,512]{0,1:T(8,128)(2,1)} fusion(bf16[1024,512]{1,0:T(8,128)(2,1)S(1)} %bitcast.44, bf16[1024,512]{1,0:T(8,128)(2,1)S(1)} %bitcast.50), kind=kOutput, calls=%fused_computation.9 | convolution fusion | flops 537133056 | bytes 2621440 | tf_op jit(solution)/shard_map/weight_term/dot_general | solution.py:214
  43.4 3.7 %all-to-all-start.1 = ((bf16[4,128,512]{2,1,0:T(8,128)(2,1)}), bf16[4,128,512]{2,1,0:T(8,128)(2,1)S(1)}, u32[]{:S(2)}, u32[]{:S(2)}) async-start(bf16[4,128,512]{2,1,0:T(8,128)(2,1)} %bitcast.13), calls=%async_computation.1 | async-start | bytes 1048576 | tf_op jit(solution)/shard_map/sum_y/all_to_all | solution.py:128
  47.1 5.2 %collective-permute-start.2 = (bf16[128,512]{1,0:T(8,128)(2,1)S(1)}, bf16[128,512]{1,0:T(8,128)(2,1)S(1)}, u32[]{:S(2)}, u32[]{:S(2)}) collective-permute-start(bf16[128,512]{1,0:T(8,128)(2,1)S(1)} %copy-done), channel_id=1, source_target_pairs={{0,0},{1,257},{64,64},{65,321},{128,128},{129,385},{192,192},{193,... | collective-permute-start | bytes 393224 | tf_op jit(solution)/shard_map/gather_weight/ppermute | solution.py:145
  52.3 4.7 %collective-permute-start.3 = (bf16[128,512]{1,0:T(8,128)(2,1)S(1)}, bf16[128,512]{1,0:T(8,128)(2,1)S(1)}, u32[]{:S(2)}, u32[]{:S(2)}) collective-permute-start(bf16[128,512]{1,0:T(8,128)(2,1)S(1)} %copy-done), channel_id=1, source_target_pairs={{0,64},{1,323},{64,128},{65,387},{128,192},{129,451},{192,256},{19... | collective-permute-start | bytes 393224 | tf_op jit(solution)/shard_map/gather_weight/ppermute | solution.py:145
  57.0 2.6 %collective-permute-start.4 = (bf16[128,512]{1,0:T(8,128)(2,1)S(1)}, bf16[128,512]{1,0:T(8,128)(2,1)S(1)}, u32[]{:S(2)}, u32[]{:S(2)}) collective-permute-start(bf16[128,512]{1,0:T(8,128)(2,1)S(1)} %copy-done), channel_id=1, source_target_pairs={{0,192},{1,451},{64,256},{65,1},{128,320},{129,65},{192,384},{193,... | collective-permute-start | bytes 393224 | tf_op jit(solution)/shard_map/gather_weight/ppermute | solution.py:145
  59.7 0.1 reduce_sum.21
  59.8 0.7 broadcast_in_dim.26
  60.5 9.7 %all-to-all-start.2 = ((bf16[16,16,512]{2,1,0:T(8,128)(2,1)}), bf16[16,16,512]{2,1,0:T(8,128)(2,1)S(1)}, u32[]{:S(2)}, u32[]{:S(2)}) async-start(bf16[16,16,512]{2,1,0:T(8,128)(2,1)} %bitcast.26), calls=%async_computation.2 | async-start | bytes 524288 | tf_op jit(solution)/shard_map/sum_z/all_to_all | solution.py:128
  70.3 0.7 convolution_convert_fusion
  71.1 0.1 dynamic-slice_bitcast_fusion
  71.2 1.9 %collective-permute-start.5 = (bf16[4,128,512]{2,1,0:T(8,128)(2,1)S(1)}, bf16[4,128,512]{2,1,0:T(8,128)(2,1)S(1)}, u32[]{:S(2)}, u32[]{:S(2)}) collective-permute-start(bf16[4,128,512]{2,1,0:T(8,128)(2,1)S(1)} %get-tuple-element.11), channel_id=1, source_target_pairs={{0,1},{1,0},{2,3},{3,2},{4,5},{5,4},{6,7},{7,6},{8,9},{9,8},{10,11... | collective-permute-start | bytes 1572872 | tf_op jit(solution)/shard_map/input_grad/ppermute | solution.py:136
  73.2 1.8 %collective-permute-done.5 = bf16[4,128,512]{2,1,0:T(8,128)(2,1)S(1)} collective-permute-done((bf16[4,128,512]{2,1,0:T(8,128)(2,1)S(1)}, bf16[4,128,512]{2,1,0:T(8,128)(2,1)S(1)}, u32[]{:S(2)}, u32[]{:S(2)}) %collective-permute-start.5) | collective-permute-done | bytes 524320 | tf_op jit(solution)/shard_map/input_grad/ppermute | solution.py:136
  75.0 0.1 fusion.1
  75.1 1.9 %collective-permute-start.6 = (bf16[2,128,512]{2,1,0:T(8,128)(2,1)S(1)}, bf16[2,128,512]{2,1,0:T(8,128)(2,1)S(1)}, u32[]{:S(2)}, u32[]{:S(2)}) collective-permute-start(bf16[2,128,512]{2,1,0:T(8,128)(2,1)S(1)} %get-tuple-element.9), channel_id=1, source_target_pairs={{0,16},{16,32},{32,48},{48,0},{1,17},{17,33},{33,49},{49,1},{2,18}... | collective-permute-start | bytes 786440 | tf_op jit(solution)/shard_map/input_grad/ppermute | solution.py:136
  77.0 4.2 %collective-permute-start.7 = (bf16[2,128,512]{2,1,0:T(8,128)(2,1)S(1)}, bf16[2,128,512]{2,1,0:T(8,128)(2,1)S(1)}, u32[]{:S(2)}, u32[]{:S(2)}) collective-permute-start(bf16[2,128,512]{2,1,0:T(8,128)(2,1)S(1)} %get-tuple-element.10), channel_id=1, source_target_pairs={{0,32},{16,48},{32,0},{48,16},{1,33},{17,49},{33,1},{49,17},{2,34}... | collective-permute-start | bytes 786440 | tf_op jit(solution)/shard_map/input_grad/ppermute | solution.py:136
  81.3 2.8 %collective-permute-start.8 = (bf16[2,128,512]{2,1,0:T(8,128)(2,1)S(1)}, bf16[2,128,512]{2,1,0:T(8,128)(2,1)S(1)}, u32[]{:S(2)}, u32[]{:S(2)}) collective-permute-start(bf16[2,128,512]{2,1,0:T(8,128)(2,1)S(1)} %get-tuple-element.7), channel_id=1, source_target_pairs={{0,48},{16,0},{32,16},{48,32},{1,49},{17,1},{33,17},{49,33},{2,50}... | collective-permute-start | bytes 786440 | tf_op jit(solution)/shard_map/input_grad/ppermute | solution.py:136
  84.1 3.7 %all-to-all-done.2 = bf16[16,16,512]{2,1,0:T(8,128)(2,1)S(1)} async-done(((bf16[16,16,512]{2,1,0:T(8,128)(2,1)}), bf16[16,16,512]{2,1,0:T(8,128)(2,1)S(1)}, u32[]{:S(2)}, u32[]{:S(2)}) %all-to-all-start.2) | async-done | bytes 262176 | tf_op jit(solution)/shard_map/sum_z/all_to_all | solution.py:128
  87.9 0.7 broadcast_in_dim.27
  88.6 3.6 %all-to-all-start.3 = ((bf16[8,16,512]{2,1,0:T(8,128)(2,1)}), bf16[8,16,512]{2,1,0:T(8,128)(2,1)S(1)}, u32[]{:S(2)}, u32[]{:S(2)}) async-start(bf16[8,16,512]{2,1,0:T(8,128)(2,1)} %broadcast_in_dim.27), calls=%async_computation.3 | async-start | bytes 262144 | tf_op jit(solution)/shard_map/share_rows/all_to_all | solution.py:128
  92.2 0.1 pad_add_fusion.at_ref
  92.3 1.5 %collective-permute-done.8.refs_3_ = bf16[2,128,512]{2,1,0:T(8,128)(2,1)S(1)} collective-permute-done((bf16[2,128,512]{2,1,0:T(8,128)(2,1)S(1)}, bf16[2,128,512]{2,1,0:T(8,128)(2,1)S(1)}, u32[]{:S(2)}, u32[]{:S(2)}) %collective-permute-start.8) | collective-permute-done | bytes 262176 | tf_op jit(solution)/shard_map/input_grad/ppermute | solution.py:136
  93.8 1.7 %from_pieces.1 = bf16[128,4096]{1,0:T(8,128)(2,1)} custom-call(s32[3]{0:T(128)S(1)} %pad_add_fusion.at_ref, bf16[2,128,512]{2,1,0:T(8,128)(2,1)S(1)} %get-tuple-element.8.refs_0_, bf16[2,128,512]{2,1,0:T(8,128)(2,1)S(1)} %collective-permute-done.6.refs_1_, bf16[2,128,512]{2,1,0:T(8,128)(2,1)S(1)} %collective-permute-done.7.refs_2_, ...), custom_call_target="tpu_custom_call" | custom-call | bytes 2097152 | tf_op jit(solution)/shard_map/input_grad/from_pieces/pallas_call | solution.py:114
  95.6 1.8 %all-to-all-done.3 = bf16[8,16,512]{2,1,0:T(8,128)(2,1)S(1)} async-done(((bf16[8,16,512]{2,1,0:T(8,128)(2,1)}), bf16[8,16,512]{2,1,0:T(8,128)(2,1)S(1)}, u32[]{:S(2)}, u32[]{:S(2)}) %all-to-all-start.3) | async-done | bytes 131104 | tf_op jit(solution)/shard_map/share_rows/all_to_all | solution.py:128
  97.4 0.7 bitcast_convert_fusion
  (14 shorter events, 0.1 us)
Async XLA Ops:
  4.1 10.5 %copy-start = (bf16[128,512]{1,0:T(8,128)(2,1)S(1)}, bf16[128,512]{1,0:T(8,128)(2,1)}, u32[]{:S(2)}) copy-start(bf16[128,512]{1,0:T(8,128)(2,1)} %param.13) | copy-start | bytes 393220
  4.1 37.7 %all-to-all-start = ((bf16[8,128,512]{2,1,0:T(8,128)(2,1)}), bf16[8,128,512]{2,1,0:T(8,128)(2,1)S(1)}, u32[]{:S(2)}, u32[]{:S(2)}) async-start(bf16[8,128,512]{2,1,0:T(8,128)(2,1)} %to_pieces.1._), calls=%async_computation | async-start | bytes 2097152 | tf_op jit(solution)/shard_map/send_inputs/all_to_all | solution.py:128
  14.6 23.2 %collective-permute-start = (bf16[128,512]{1,0:T(8,128)(2,1)S(1)}, bf16[128,512]{1,0:T(8,128)(2,1)S(1)}, u32[]{:S(2)}, u32[]{:S(2)}) collective-permute-start(bf16[128,512]{1,0:T(8,128)(2,1)S(1)} %copy-done), channel_id=1, source_target_pairs={{0,128},{1,387},{64,192},{65,451},{128,256},{129,1},{192,320},{193... | collective-permute-start | bytes 393224 | tf_op jit(solution)/shard_map/gather_value_grad/ppermute | solution.py:145
  37.9 3.8 %collective-permute-start.1 = (bf16[4,128,512]{2,1,0:T(8,128)(2,1)S(1)}, bf16[4,128,512]{2,1,0:T(8,128)(2,1)S(1)}, u32[]{:S(2)}, u32[]{:S(2)}) collective-permute-start(bf16[4,128,512]{2,1,0:T(8,128)(2,1)S(1)} %hold.1.own_ref), channel_id=1, source_target_pairs={{0,1},{1,0},{2,3},{3,2},{4,5},{5,4},{6,7},{7,6},{8,9},{9,8},{10,11... | collective-permute-start | bytes 1572872 | tf_op jit(solution)/shard_map/gather_value_grad/ppermute | solution.py:136
  43.4 16.3 %all-to-all-start.1 = ((bf16[4,128,512]{2,1,0:T(8,128)(2,1)}), bf16[4,128,512]{2,1,0:T(8,128)(2,1)S(1)}, u32[]{:S(2)}, u32[]{:S(2)}) async-start(bf16[4,128,512]{2,1,0:T(8,128)(2,1)} %bitcast.13), calls=%async_computation.1 | async-start | bytes 1048576 | tf_op jit(solution)/shard_map/sum_y/all_to_all | solution.py:128
  47.1 23.2 %collective-permute-start.2 = (bf16[128,512]{1,0:T(8,128)(2,1)S(1)}, bf16[128,512]{1,0:T(8,128)(2,1)S(1)}, u32[]{:S(2)}, u32[]{:S(2)}) collective-permute-start(bf16[128,512]{1,0:T(8,128)(2,1)S(1)} %copy-done), channel_id=1, source_target_pairs={{0,0},{1,257},{64,64},{65,321},{128,128},{129,385},{192,192},{193,... | collective-permute-start | bytes 393224 | tf_op jit(solution)/shard_map/gather_weight/ppermute | solution.py:145
  52.3 18.0 %collective-permute-start.3 = (bf16[128,512]{1,0:T(8,128)(2,1)S(1)}, bf16[128,512]{1,0:T(8,128)(2,1)S(1)}, u32[]{:S(2)}, u32[]{:S(2)}) collective-permute-start(bf16[128,512]{1,0:T(8,128)(2,1)S(1)} %copy-done), channel_id=1, source_target_pairs={{0,64},{1,323},{64,128},{65,387},{128,192},{129,451},{192,256},{19... | collective-permute-start | bytes 393224 | tf_op jit(solution)/shard_map/gather_weight/ppermute | solution.py:145
  57.0 13.2 %collective-permute-start.4 = (bf16[128,512]{1,0:T(8,128)(2,1)S(1)}, bf16[128,512]{1,0:T(8,128)(2,1)S(1)}, u32[]{:S(2)}, u32[]{:S(2)}) collective-permute-start(bf16[128,512]{1,0:T(8,128)(2,1)S(1)} %copy-done), channel_id=1, source_target_pairs={{0,192},{1,451},{64,256},{65,1},{128,320},{129,65},{192,384},{193,... | collective-permute-start | bytes 393224 | tf_op jit(solution)/shard_map/gather_weight/ppermute | solution.py:145
  60.5 27.3 %all-to-all-start.2 = ((bf16[16,16,512]{2,1,0:T(8,128)(2,1)}), bf16[16,16,512]{2,1,0:T(8,128)(2,1)S(1)}, u32[]{:S(2)}, u32[]{:S(2)}) async-start(bf16[16,16,512]{2,1,0:T(8,128)(2,1)} %bitcast.26), calls=%async_computation.2 | async-start | bytes 524288 | tf_op jit(solution)/shard_map/sum_z/all_to_all | solution.py:128
  71.2 3.8 %collective-permute-start.5 = (bf16[4,128,512]{2,1,0:T(8,128)(2,1)S(1)}, bf16[4,128,512]{2,1,0:T(8,128)(2,1)S(1)}, u32[]{:S(2)}, u32[]{:S(2)}) collective-permute-start(bf16[4,128,512]{2,1,0:T(8,128)(2,1)S(1)} %get-tuple-element.11), channel_id=1, source_target_pairs={{0,1},{1,0},{2,3},{3,2},{4,5},{5,4},{6,7},{7,6},{8,9},{9,8},{10,11... | collective-permute-start | bytes 1572872 | tf_op jit(solution)/shard_map/input_grad/ppermute | solution.py:136
  75.1 17.2 %collective-permute-start.6 = (bf16[2,128,512]{2,1,0:T(8,128)(2,1)S(1)}, bf16[2,128,512]{2,1,0:T(8,128)(2,1)S(1)}, u32[]{:S(2)}, u32[]{:S(2)}) collective-permute-start(bf16[2,128,512]{2,1,0:T(8,128)(2,1)S(1)} %get-tuple-element.9), channel_id=1, source_target_pairs={{0,16},{16,32},{32,48},{48,0},{1,17},{17,33},{33,49},{49,1},{2,18}... | collective-permute-start | bytes 786440 | tf_op jit(solution)/shard_map/input_grad/ppermute | solution.py:136
  77.0 15.3 %collective-permute-start.7 = (bf16[2,128,512]{2,1,0:T(8,128)(2,1)S(1)}, bf16[2,128,512]{2,1,0:T(8,128)(2,1)S(1)}, u32[]{:S(2)}, u32[]{:S(2)}) collective-permute-start(bf16[2,128,512]{2,1,0:T(8,128)(2,1)S(1)} %get-tuple-element.10), channel_id=1, source_target_pairs={{0,32},{16,48},{32,0},{48,16},{1,33},{17,49},{33,1},{49,17},{2,34}... | collective-permute-start | bytes 786440 | tf_op jit(solution)/shard_map/input_grad/ppermute | solution.py:136
  81.3 12.5 %collective-permute-start.8 = (bf16[2,128,512]{2,1,0:T(8,128)(2,1)S(1)}, bf16[2,128,512]{2,1,0:T(8,128)(2,1)S(1)}, u32[]{:S(2)}, u32[]{:S(2)}) collective-permute-start(bf16[2,128,512]{2,1,0:T(8,128)(2,1)S(1)} %get-tuple-element.7), channel_id=1, source_target_pairs={{0,48},{16,0},{32,16},{48,32},{1,49},{17,1},{33,17},{49,33},{2,50}... | collective-permute-start | bytes 786440 | tf_op jit(solution)/shard_map/input_grad/ppermute | solution.py:136
  88.6 8.8 %all-to-all-start.3 = ((bf16[8,16,512]{2,1,0:T(8,128)(2,1)}), bf16[8,16,512]{2,1,0:T(8,128)(2,1)S(1)}, u32[]{:S(2)}, u32[]{:S(2)}) async-start(bf16[8,16,512]{2,1,0:T(8,128)(2,1)} %broadcast_in_dim.27), calls=%async_computation.3 | async-start | bytes 262144 | tf_op jit(solution)/shard_map/share_rows/all_to_all | solution.py:128

commit v13 on v12

--- a/solution.py
+++ b/solution.py
@@ -204,7 +204,7 @@
     with jax.named_scope("attention"):
         value_grad, key_grad = attend_back(queries[0], keys[0], values[0], out_grad[0], lengths, pieces)
     with jax.named_scope("gather_value_grad"):
-        early = along_z(value_weight, (2, -2))
+        early = along_z(value_weight, (0, 4))
         mine = hold(lax.all_gather(value_grad, "x", axis=0), [early])
         other = shifted(mine, "core", CN, 1)
         grads = pair(mine, other, core).reshape(CN * XN * TOK, KV)
@@ -224,8 +224,8 @@
     with jax.named_scope("share_rows"):
         weight_grad = spread(total.astype(BF), ("core", "y"), QN).reshape(QN * SUB, KV).astype(F32)
     with jax.named_scope("gather_weight"):
-        first, second, last = (along_z(value_weight, steps) for steps in ((0, 4), (1, -3), (3, -1)))
-        weight = join([first, second, early, last], plane)
+        later = [along_z(value_weight, steps) for steps in ((1, -3), (2, -2), (3, -1))]
+        weight = join([early] + later, plane)
     with jax.named_scope("input_grad"):
         parts = nt(grads, weight).astype(BF).reshape(CN, XN, TOK, KV)
         kept = lax.dynamic_index_in_dim(parts, core, 0, False)

time: 98.8 us -> 98 us (level)
  waiting for transfers between devices: 10.4 us -> 6.33 us
  starting transfers between devices: 60.4 us -> 62.6 us
  blocking collectives: 11.3 us -> 12.4 us
    ppermute x5, starting transfers between devices: 13.2 us -> 17.1 us  [shifted(): lax.ppermute(array, axes, [(i, (i + by) % count) for i in range(count)])]
    all_to_all x4, waiting for transfers between devices: 5.55 us -> 2.03 us  [exchange(): return lax.all_to_all(array, axes, 0, 0, tiled=True)]
    all_to_all x4, starting transfers between devices: 27.6 us -> 26.1 us  [exchange(): return lax.all_to_all(array, axes, 0, 0, tiled=True)]
    all_gather x1, blocking collectives: 11.3 us -> 12.4 us  [per_device(): mine = hold(lax.all_gather(value_grad, 'x', axis=0), [early])]
  transfers between devices with their start and end apart: 13 -> 13, of which waited for: 5 -> 4; matrix products, arithmetic and copies ran while one was open for 3% -> 3% of each run, Pallas kernels for 6% -> 6%
where the time goes in v13:
time: 98 us; the launch traced here: 97.4 us
  starting transfers between devices  62.6 us (64%)
  blocking collectives  12.4 us (13%)
  Pallas kernels  9.63 us (10%)
  waiting for transfers between devices  6.33 us (6%)
  matrix products  2.29 us (2%)
  between operations  1.54 us (2%)
  local copies, waits for them, and re-layouts  1.51 us (2%)
  other arithmetic  1.04 us (1%)
    all_to_all x4, starting transfers between devices, exchange(): return lax.all_to_all(array, axes, 0, 0, tiled=True)  26.1 us
    ppermute x4, starting transfers between devices, along_z(): return lax.ppermute(array, ('zl', 'zh', 'core'), pairs)  19.3 us
    ppermute x5, starting transfers between devices, shifted(): lax.ppermute(array, axes, [(i, (i + by) % count) for i in range(count)])  17.1 us
    all_gather x1, blocking collectives, per_device(): mine = hold(lax.all_gather(value_grad, 'x', axis=0), [early])  12.4 us
    ppermute x5, waiting for transfers between devices, shifted(): lax.ppermute(array, axes, [(i, (i + by) % count) for i in range(count)])  4.28 us
    pallas_call x1, Pallas kernels, attend_back(): pl.pallas_call(attend_kernel, grid=(KV // HD // KV_STEP,), in_specs=[pl.B...  4.26 us
    pallas_call x1, Pallas kernels, to_pieces(): pl.pallas_call(to_pieces_kernel, grid=(TOK // part,), in_specs=[pl.BlockS...  3.49 us
    all_to_all x4, waiting for transfers between devices, exchange(): return lax.all_to_all(array, axes, 0, 0, tiled=True)  2.03 us
  transfers between devices with their start and end apart: 13, of which 4 were waited for; matrix products, arithmetic and copies ran while one was open for 3% of the time, Pallas kernels for 6%

profile of v13, /device:TPU:1, one launch (start us, length us, event | category | flops | bytes accessed | tf_op | source)
XLA Modules:
  0.0 97.4 jit_solution(15690500507933566987)
XLA Ops:
  0.6 3.5 %to_pieces.1._ = bf16[8,128,512]{2,1,0:T(8,128)(2,1)} custom-call(bf16[128,4096]{1,0:T(8,128)(2,1)} %bitcast.47), custom_call_target="tpu_custom_call" | custom-call | flops 4194304 | bytes 2097152 | tf_op jit(solution)/shard_map/cut_inputs/to_pieces/pallas_call | solution.py:100
  4.1 10.5 %all-to-all-start = ((bf16[8,128,512]{2,1,0:T(8,128)(2,1)}), bf16[8,128,512]{2,1,0:T(8,128)(2,1)S(1)}, u32[]{:S(2)}, u32[]{:S(2)}) async-start(bf16[8,128,512]{2,1,0:T(8,128)(2,1)} %to_pieces.1._), calls=%async_computation | async-start | bytes 2097152 | tf_op jit(solution)/shard_map/send_inputs/all_to_all | solution.py:128
  14.6 4.2 %collective-permute-start = (bf16[128,512]{1,0:T(8,128)(2,1)S(1)}, bf16[128,512]{1,0:T(8,128)(2,1)S(1)}, u32[]{:S(2)}, u32[]{:S(2)}) collective-permute-start(bf16[128,512]{1,0:T(8,128)(2,1)S(1)} %copy-done), channel_id=1, source_target_pairs={{0,0},{1,257},{64,64},{65,321},{128,128},{129,385},{192,192},{193,... | collective-permute-start | bytes 393224 | tf_op jit(solution)/shard_map/gather_value_grad/ppermute | solution.py:145
  19.5 4.3 %attend.1 = (bf16[128,512]{1,0:T(8,128)(2,1)}, bf16[128,512]{1,0:T(8,128)(2,1)}) custom-call(s32[1]{0:T(128)S(6)} %copy.10.length_ref, bf16[128,4096]{1,0:T(8,128)(2,1)} %bitcast.48, bf16[128,512]{1,0:T(8,128)(2,1)} %bitcast.53, bf16[128,512]{1,0:T(8,128)(2,1)} %bitcast.54, bf16[128,4096]{1,0:T(8,128)(2,1)} %bitcast.49, bf16[8,128,512]{2,1,0:T(8,128)(2,1)} %to_pieces.1._), custom_call_target="tpu_custom_call" | custom-call | flops 671088640 | bytes 3145728 | tf_op jit(solution)/shard_map/attention/attend/pallas_call | solution.py:51
  23.8 12.4 %all-gather = bf16[512,512]{1,0:T(8,128)(2,1)S(1)} all-gather(bf16[128,512]{1,0:T(8,128)(2,1)} %get-tuple-element.5), channel_id=2, replica_groups=mesh['zl'=8,'x'=4,'y'=4,'zh'=2,'core'=2] {'x'}, dimensions={0}, use_global_device_ids=true | all-gather | bytes 655360 | tf_op jit(solution)/shard_map/gather_value_grad/all_gather | solution.py:208
  36.2 0.0 collective-permute-done.refs_0_
  36.3 4.1 %collective-permute-start.1 = (bf16[4,128,512]{2,1,0:T(8,128)(2,1)S(1)}, bf16[4,128,512]{2,1,0:T(8,128)(2,1)S(1)}, u32[]{:S(2)}, u32[]{:S(2)}) collective-permute-start(bf16[4,128,512]{2,1,0:T(8,128)(2,1)S(1)} %hold.1.own_ref), channel_id=1, source_target_pairs={{0,1},{1,0},{2,3},{3,2},{4,5},{5,4},{6,7},{7,6},{8,9},{9,8},{10,11... | collective-permute-start | bytes 1572872 | tf_op jit(solution)/shard_map/gather_value_grad/ppermute | solution.py:136
  40.3 1.5 %collective-permute-done.1.other_ref = bf16[4,128,512]{2,1,0:T(8,128)(2,1)S(1)} collective-permute-done((bf16[4,128,512]{2,1,0:T(8,128)(2,1)S(1)}, bf16[4,128,512]{2,1,0:T(8,128)(2,1)S(1)}, u32[]{:S(2)}, u32[]{:S(2)}) %collective-permute-start.1) | collective-permute-done | bytes 524320 | tf_op jit(solution)/shard_map/gather_value_grad/ppermute | solution.py:136
  41.8 0.1 pair.1
  41.9 1.6 %convolution_convert_fusion.1 = bf16[512,512]{0,1:T(8,128)(2,1)} fusion(bf16[1024,512]{1,0:T(8,128)(2,1)S(1)} %bitcast.44, bf16[1024,512]{1,0:T(8,128)(2,1)S(1)} %bitcast.50), kind=kOutput, calls=%fused_computation.9 | convolution fusion | flops 537133056 | bytes 2621440 | tf_op jit(solution)/shard_map/weight_term/dot_general | solution.py:214
  43.5 3.5 %all-to-all-start.1 = ((bf16[4,128,512]{2,1,0:T(8,128)(2,1)}), bf16[4,128,512]{2,1,0:T(8,128)(2,1)S(1)}, u32[]{:S(2)}, u32[]{:S(2)}) async-start(bf16[4,128,512]{2,1,0:T(8,128)(2,1)} %bitcast.13), calls=%async_computation.1 | async-start | bytes 1048576 | tf_op jit(solution)/shard_map/sum_y/all_to_all | solution.py:128
  47.0 8.1 %collective-permute-start.2 = (bf16[128,512]{1,0:T(8,128)(2,1)S(1)}, bf16[128,512]{1,0:T(8,128)(2,1)S(1)}, u32[]{:S(2)}, u32[]{:S(2)}) collective-permute-start(bf16[128,512]{1,0:T(8,128)(2,1)S(1)} %copy-done), channel_id=1, source_target_pairs={{0,64},{1,323},{64,128},{65,387},{128,192},{129,451},{192,256},{19... | collective-permute-start | bytes 393224 | tf_op jit(solution)/shard_map/gather_weight/ppermute | solution.py:145
  55.1 4.3 %collective-permute-start.3 = (bf16[128,512]{1,0:T(8,128)(2,1)S(1)}, bf16[128,512]{1,0:T(8,128)(2,1)S(1)}, u32[]{:S(2)}, u32[]{:S(2)}) collective-permute-start(bf16[128,512]{1,0:T(8,128)(2,1)S(1)} %copy-done), channel_id=1, source_target_pairs={{0,128},{1,387},{64,192},{65,451},{128,256},{129,1},{192,320},{193... | collective-permute-start | bytes 393224 | tf_op jit(solution)/shard_map/gather_weight/ppermute | solution.py:145
  59.4 2.6 %collective-permute-start.4 = (bf16[128,512]{1,0:T(8,128)(2,1)S(1)}, bf16[128,512]{1,0:T(8,128)(2,1)S(1)}, u32[]{:S(2)}, u32[]{:S(2)}) collective-permute-start(bf16[128,512]{1,0:T(8,128)(2,1)S(1)} %copy-done), channel_id=1, source_target_pairs={{0,192},{1,451},{64,256},{65,1},{128,320},{129,65},{192,384},{193,... | collective-permute-start | bytes 393224 | tf_op jit(solution)/shard_map/gather_weight/ppermute | solution.py:145
  62.1 0.1 reduce_sum.21
  62.1 0.7 broadcast_in_dim.26
  62.9 4.9 %all-to-all-start.2 = ((bf16[16,16,512]{2,1,0:T(8,128)(2,1)}), bf16[16,16,512]{2,1,0:T(8,128)(2,1)S(1)}, u32[]{:S(2)}, u32[]{:S(2)}) async-start(bf16[16,16,512]{2,1,0:T(8,128)(2,1)} %bitcast.26), calls=%async_computation.2 | async-start | bytes 524288 | tf_op jit(solution)/shard_map/sum_z/all_to_all | solution.py:128
  67.8 0.7 convolution_convert_fusion
  68.6 0.1 dynamic-slice_bitcast_fusion
  68.7 4.1 %collective-permute-start.5 = (bf16[4,128,512]{2,1,0:T(8,128)(2,1)S(1)}, bf16[4,128,512]{2,1,0:T(8,128)(2,1)S(1)}, u32[]{:S(2)}, u32[]{:S(2)}) collective-permute-start(bf16[4,128,512]{2,1,0:T(8,128)(2,1)S(1)} %get-tuple-element.11), channel_id=1, source_target_pairs={{0,1},{1,0},{2,3},{3,2},{4,5},{5,4},{6,7},{7,6},{8,9},{9,8},{10,11... | collective-permute-start | bytes 1572872 | tf_op jit(solution)/shard_map/input_grad/ppermute | solution.py:136
  72.9 1.5 %collective-permute-done.5 = bf16[4,128,512]{2,1,0:T(8,128)(2,1)S(1)} collective-permute-done((bf16[4,128,512]{2,1,0:T(8,128)(2,1)S(1)}, bf16[4,128,512]{2,1,0:T(8,128)(2,1)S(1)}, u32[]{:S(2)}, u32[]{:S(2)}) %collective-permute-start.5) | collective-permute-done | bytes 524320 | tf_op jit(solution)/shard_map/input_grad/ppermute | solution.py:136
  74.3 0.1 fusion.1
  74.4 1.9 %collective-permute-start.6 = (bf16[2,128,512]{2,1,0:T(8,128)(2,1)S(1)}, bf16[2,128,512]{2,1,0:T(8,128)(2,1)S(1)}, u32[]{:S(2)}, u32[]{:S(2)}) collective-permute-start(bf16[2,128,512]{2,1,0:T(8,128)(2,1)S(1)} %get-tuple-element.9), channel_id=1, source_target_pairs={{0,16},{16,32},{32,48},{48,0},{1,17},{17,33},{33,49},{49,1},{2,18}... | collective-permute-start | bytes 786440 | tf_op jit(solution)/shard_map/input_grad/ppermute | solution.py:136
  76.3 4.2 %collective-permute-start.7 = (bf16[2,128,512]{2,1,0:T(8,128)(2,1)S(1)}, bf16[2,128,512]{2,1,0:T(8,128)(2,1)S(1)}, u32[]{:S(2)}, u32[]{:S(2)}) collective-permute-start(bf16[2,128,512]{2,1,0:T(8,128)(2,1)S(1)} %get-tuple-element.10), channel_id=1, source_target_pairs={{0,32},{16,48},{32,0},{48,16},{1,33},{17,49},{33,1},{49,17},{2,34}... | collective-permute-start | bytes 786440 | tf_op jit(solution)/shard_map/input_grad/ppermute | solution.py:136
  80.6 2.8 %collective-permute-start.8 = (bf16[2,128,512]{2,1,0:T(8,128)(2,1)S(1)}, bf16[2,128,512]{2,1,0:T(8,128)(2,1)S(1)}, u32[]{:S(2)}, u32[]{:S(2)}) collective-permute-start(bf16[2,128,512]{2,1,0:T(8,128)(2,1)S(1)} %get-tuple-element.7), channel_id=1, source_target_pairs={{0,48},{16,0},{32,16},{48,32},{1,49},{17,1},{33,17},{49,33},{2,50}... | collective-permute-start | bytes 786440 | tf_op jit(solution)/shard_map/input_grad/ppermute | solution.py:136
  83.5 0.7 broadcast_in_dim.27
  84.1 7.3 %all-to-all-start.3 = ((bf16[8,16,512]{2,1,0:T(8,128)(2,1)}), bf16[8,16,512]{2,1,0:T(8,128)(2,1)S(1)}, u32[]{:S(2)}, u32[]{:S(2)}) async-start(bf16[8,16,512]{2,1,0:T(8,128)(2,1)} %broadcast_in_dim.27), calls=%async_computation.3 | async-start | bytes 262144 | tf_op jit(solution)/shard_map/share_rows/all_to_all | solution.py:128
  91.5 0.1 pad_add_fusion.at_ref
  91.6 1.3 %collective-permute-done.8.refs_3_ = bf16[2,128,512]{2,1,0:T(8,128)(2,1)S(1)} collective-permute-done((bf16[2,128,512]{2,1,0:T(8,128)(2,1)S(1)}, bf16[2,128,512]{2,1,0:T(8,128)(2,1)S(1)}, u32[]{:S(2)}, u32[]{:S(2)}) %collective-permute-start.8) | collective-permute-done | bytes 262176 | tf_op jit(solution)/shard_map/input_grad/ppermute | solution.py:136
  92.9 1.7 %from_pieces.1 = bf16[128,4096]{1,0:T(8,128)(2,1)} custom-call(s32[3]{0:T(128)S(1)} %pad_add_fusion.at_ref, bf16[2,128,512]{2,1,0:T(8,128)(2,1)S(1)} %get-tuple-element.8.refs_0_, bf16[2,128,512]{2,1,0:T(8,128)(2,1)S(1)} %collective-permute-done.6.refs_1_, bf16[2,128,512]{2,1,0:T(8,128)(2,1)S(1)} %collective-permute-done.7.refs_2_, ...), custom_call_target="tpu_custom_call" | custom-call | bytes 2097152 | tf_op jit(solution)/shard_map/input_grad/from_pieces/pallas_call | solution.py:114
  94.6 2.0 %all-to-all-done.3 = bf16[8,16,512]{2,1,0:T(8,128)(2,1)S(1)} async-done(((bf16[8,16,512]{2,1,0:T(8,128)(2,1)}), bf16[8,16,512]{2,1,0:T(8,128)(2,1)S(1)}, u32[]{:S(2)}, u32[]{:S(2)}) %all-to-all-start.3) | async-done | bytes 131104 | tf_op jit(solution)/shard_map/share_rows/all_to_all | solution.py:128
  96.6 0.7 bitcast_convert_fusion
  (14 shorter events, 0.1 us)
Async XLA Ops:
  4.1 10.5 %copy-start = (bf16[128,512]{1,0:T(8,128)(2,1)S(1)}, bf16[128,512]{1,0:T(8,128)(2,1)}, u32[]{:S(2)}) copy-start(bf16[128,512]{1,0:T(8,128)(2,1)} %param.13) | copy-start | bytes 393220
  4.1 37.8 %all-to-all-start = ((bf16[8,128,512]{2,1,0:T(8,128)(2,1)}), bf16[8,128,512]{2,1,0:T(8,128)(2,1)S(1)}, u32[]{:S(2)}, u32[]{:S(2)}) async-start(bf16[8,128,512]{2,1,0:T(8,128)(2,1)} %to_pieces.1._), calls=%async_computation | async-start | bytes 2097152 | tf_op jit(solution)/shard_map/send_inputs/all_to_all | solution.py:128
  14.6 21.6 %collective-permute-start = (bf16[128,512]{1,0:T(8,128)(2,1)S(1)}, bf16[128,512]{1,0:T(8,128)(2,1)S(1)}, u32[]{:S(2)}, u32[]{:S(2)}) collective-permute-start(bf16[128,512]{1,0:T(8,128)(2,1)S(1)} %copy-done), channel_id=1, source_target_pairs={{0,0},{1,257},{64,64},{65,321},{128,128},{129,385},{192,192},{193,... | collective-permute-start | bytes 393224 | tf_op jit(solution)/shard_map/gather_value_grad/ppermute | solution.py:145
  36.3 5.6 %collective-permute-start.1 = (bf16[4,128,512]{2,1,0:T(8,128)(2,1)S(1)}, bf16[4,128,512]{2,1,0:T(8,128)(2,1)S(1)}, u32[]{:S(2)}, u32[]{:S(2)}) collective-permute-start(bf16[4,128,512]{2,1,0:T(8,128)(2,1)S(1)} %hold.1.own_ref), channel_id=1, source_target_pairs={{0,1},{1,0},{2,3},{3,2},{4,5},{5,4},{6,7},{7,6},{8,9},{9,8},{10,11... | collective-permute-start | bytes 1572872 | tf_op jit(solution)/shard_map/gather_value_grad/ppermute | solution.py:136
  43.5 18.6 %all-to-all-start.1 = ((bf16[4,128,512]{2,1,0:T(8,128)(2,1)}), bf16[4,128,512]{2,1,0:T(8,128)(2,1)S(1)}, u32[]{:S(2)}, u32[]{:S(2)}) async-start(bf16[4,128,512]{2,1,0:T(8,128)(2,1)} %bitcast.13), calls=%async_computation.1 | async-start | bytes 1048576 | tf_op jit(solution)/shard_map/sum_y/all_to_all | solution.py:128
  47.0 20.8 %collective-permute-start.2 = (bf16[128,512]{1,0:T(8,128)(2,1)S(1)}, bf16[128,512]{1,0:T(8,128)(2,1)S(1)}, u32[]{:S(2)}, u32[]{:S(2)}) collective-permute-start(bf16[128,512]{1,0:T(8,128)(2,1)S(1)} %copy-done), channel_id=1, source_target_pairs={{0,64},{1,323},{64,128},{65,387},{128,192},{129,451},{192,256},{19... | collective-permute-start | bytes 393224 | tf_op jit(solution)/shard_map/gather_weight/ppermute | solution.py:145
  55.1 12.7 %collective-permute-start.3 = (bf16[128,512]{1,0:T(8,128)(2,1)S(1)}, bf16[128,512]{1,0:T(8,128)(2,1)S(1)}, u32[]{:S(2)}, u32[]{:S(2)}) collective-permute-start(bf16[128,512]{1,0:T(8,128)(2,1)S(1)} %copy-done), channel_id=1, source_target_pairs={{0,128},{1,387},{64,192},{65,451},{128,256},{129,1},{192,320},{193... | collective-permute-start | bytes 393224 | tf_op jit(solution)/shard_map/gather_weight/ppermute | solution.py:145
  59.4 8.4 %collective-permute-start.4 = (bf16[128,512]{1,0:T(8,128)(2,1)S(1)}, bf16[128,512]{1,0:T(8,128)(2,1)S(1)}, u32[]{:S(2)}, u32[]{:S(2)}) collective-permute-start(bf16[128,512]{1,0:T(8,128)(2,1)S(1)} %copy-done), channel_id=1, source_target_pairs={{0,192},{1,451},{64,256},{65,1},{128,320},{129,65},{192,384},{193,... | collective-permute-start | bytes 393224 | tf_op jit(solution)/shard_map/gather_weight/ppermute | solution.py:145
  62.9 20.5 %all-to-all-start.2 = ((bf16[16,16,512]{2,1,0:T(8,128)(2,1)}), bf16[16,16,512]{2,1,0:T(8,128)(2,1)S(1)}, u32[]{:S(2)}, u32[]{:S(2)}) async-start(bf16[16,16,512]{2,1,0:T(8,128)(2,1)} %bitcast.26), calls=%async_computation.2 | async-start | bytes 524288 | tf_op jit(solution)/shard_map/sum_z/all_to_all | solution.py:128
  68.7 5.6 %collective-permute-start.5 = (bf16[4,128,512]{2,1,0:T(8,128)(2,1)S(1)}, bf16[4,128,512]{2,1,0:T(8,128)(2,1)S(1)}, u32[]{:S(2)}, u32[]{:S(2)}) collective-permute-start(bf16[4,128,512]{2,1,0:T(8,128)(2,1)S(1)} %get-tuple-element.11), channel_id=1, source_target_pairs={{0,1},{1,0},{2,3},{3,2},{4,5},{5,4},{6,7},{7,6},{8,9},{9,8},{10,11... | collective-permute-start | bytes 1572872 | tf_op jit(solution)/shard_map/input_grad/ppermute | solution.py:136
  74.4 17.1 %collective-permute-start.6 = (bf16[2,128,512]{2,1,0:T(8,128)(2,1)S(1)}, bf16[2,128,512]{2,1,0:T(8,128)(2,1)S(1)}, u32[]{:S(2)}, u32[]{:S(2)}) collective-permute-start(bf16[2,128,512]{2,1,0:T(8,128)(2,1)S(1)} %get-tuple-element.9), channel_id=1, source_target_pairs={{0,16},{16,32},{32,48},{48,0},{1,17},{17,33},{33,49},{49,1},{2,18}... | collective-permute-start | bytes 786440 | tf_op jit(solution)/shard_map/input_grad/ppermute | solution.py:136
  76.3 15.2 %collective-permute-start.7 = (bf16[2,128,512]{2,1,0:T(8,128)(2,1)S(1)}, bf16[2,128,512]{2,1,0:T(8,128)(2,1)S(1)}, u32[]{:S(2)}, u32[]{:S(2)}) collective-permute-start(bf16[2,128,512]{2,1,0:T(8,128)(2,1)S(1)} %get-tuple-element.10), channel_id=1, source_target_pairs={{0,32},{16,48},{32,0},{48,16},{1,33},{17,49},{33,1},{49,17},{2,34}... | collective-permute-start | bytes 786440 | tf_op jit(solution)/shard_map/input_grad/ppermute | solution.py:136
  80.6 12.3 %collective-permute-start.8 = (bf16[2,128,512]{2,1,0:T(8,128)(2,1)S(1)}, bf16[2,128,512]{2,1,0:T(8,128)(2,1)S(1)}, u32[]{:S(2)}, u32[]{:S(2)}) collective-permute-start(bf16[2,128,512]{2,1,0:T(8,128)(2,1)S(1)} %get-tuple-element.7), channel_id=1, source_target_pairs={{0,48},{16,0},{32,16},{48,32},{1,49},{17,1},{33,17},{49,33},{2,50}... | collective-permute-start | bytes 786440 | tf_op jit(solution)/shard_map/input_grad/ppermute | solution.py:136
  84.1 12.5 %all-to-all-start.3 = ((bf16[8,16,512]{2,1,0:T(8,128)(2,1)}), bf16[8,16,512]{2,1,0:T(8,128)(2,1)S(1)}, u32[]{:S(2)}, u32[]{:S(2)}) async-start(bf16[8,16,512]{2,1,0:T(8,128)(2,1)} %broadcast_in_dim.27), calls=%async_computation.3 | async-start | bytes 262144 | tf_op jit(solution)/shard_map/share_rows/all_to_all | solution.py:128
